TPU v7x, 32 devices: a whole 2x2x4 slice. The times are simulated.
32 devices in a mesh: expert: 16 (over z, y, x), dp: 2 (over core).
Axes of the slice: x: 2, y: 2, z: 4, core: 2. Of those that a mesh axis runs over, the one named last changes fastest.
Arguments:
- tokens: bfloat16 [2048, 2048], P(('expert', 'dp')), may hold values from -6 to 6
- grad_out: bfloat16 [2048, 2048], P(('expert', 'dp')), may hold values from -6 to 6
- expert_ids: int32 [2048, 8], P(('expert', 'dp')), may hold values from 0 to 15, all different within a row; in each aligned block of 64 rows (0 to 63, 64 to 127, ...) at most 48 rows name the same one
- router_weights: float32 [2048, 8], P(('expert', 'dp')), may hold values from 0.02 to 0.25
- codes_in: int32 [16, 2, 2048, 256], P('expert', None, 'dp'), may hold values from 0 to 4095
- codes_out: int32 [16, 256, 2048], P('expert', None, 'dp'), may hold values from 0 to 4095
- clip_in: float32 [16, 2, 2, 16, 768], P('expert'), may hold values from -1 to 3
- range_in: float32 [16, 2, 2, 16, 768], P('expert'), may hold values from 0.01 to 0.06
- clip_out: float32 [16, 2, 6, 2048], P('expert'), may hold values from -1 to 3
- range_out: float32 [16, 2, 6, 2048], P('expert'), may hold values from 0.018 to 0.1
Outputs:
- grad_tokens: bfloat16 [2048, 2048], P(('expert', 'dp'))
- grad_clip_in: float32 [16, 2, 2, 16, 768], P('expert', None, None, 'dp')
- grad_clip_out: float32 [16, 2, 6, 2048], P('expert', None, None, 'dp')
Inputs may be any that keep to these rules, and one draw needn't show every extreme that they name: `expert_ids`: each row names 8 different experts; among the rows of one device no expert is named by more than 48 rows, and in some device some expert is named by exactly 48 rows.
All inputs are finite; a program needn't handle non-finite values.
Results may differ from a plain program's by a relative error of at most 0.0082.
Values may be sent and summed in bfloat16 or wider, within the bound.
No kernel may reach another device: no remote copies, remote signals or barrier semaphores. Data moves between devices by JAX's collectives and lax.ppermute only.
A program may use at most 128 MiB of HBM per device.

v0:
```python
import functools

import jax
import jax.numpy as jnp
from jax import lax
from jax.experimental import pallas as pl
from jax.experimental.pallas import tpu as pltpu
from jax.sharding import PartitionSpec as P

GROUP = 128
PACK = 3
CHUNK = 16
TILE = 256
LIMIT = 24 * 1024 * 1024
SMALL = 8 * 1024 * 1024
F32 = jnp.float32
BF16 = jnp.bfloat16


def dot_nn(a, b):
    return lax.dot_general(a, b, (((1,), (0,)), ((), ())), preferred_element_type=F32)


def dot_nt(a, b):
    return lax.dot_general(a, b, (((1,), (1,)), ((), ())), preferred_element_type=F32)


def dot_tn(a, b):
    return lax.dot_general(a, b, (((0,), (0,)), ((), ())), preferred_element_type=F32)


def sigmoid(v):
    return 1.0 / (1.0 + jnp.exp(-v))


def plane_order(size, back=False):
    third = size // PACK
    row = lax.broadcasted_iota(jnp.int32, (size, size), 1 if back else 0)
    col = lax.broadcasted_iota(jnp.int32, (size, size), 0 if back else 1)
    plane = jnp.zeros_like(col)
    for j in range(1, PACK):
        plane = plane + (col >= j * third).astype(jnp.int32)
    return (row == PACK * (col - plane * third) + plane).astype(F32).astype(BF16)


def three_parts(a):
    high = a.astype(BF16)
    rest = a - high.astype(F32)
    middle = rest.astype(BF16)
    low = (rest - middle.astype(F32)).astype(BF16)
    return high, middle, low


def placed(a, order):
    parts = [dot_nn(part, order) for part in three_parts(a)]
    return parts[0] + parts[1] + parts[2]


ANYWHERE = pl.BlockSpec(memory_space=pl.ANY)
INSIDE = pl.BlockSpec(memory_space=pltpu.VMEM)


class Calls:
    def __init__(self, keep):
        self.keep = keep

    def pin(self, array):
        return pltpu.with_memory_space_constraint(array, pltpu.VMEM) if self.keep else array

    def out(self, shape, dtype):
        return pltpu.VMEM(shape, dtype) if self.keep else jax.ShapeDtypeStruct(shape, dtype)

    def run(self, kernel, name, inputs, outputs, after=(), alias=None, limit=LIMIT, flops=0, free=()):
        count = len(inputs)

        def wrapped(*refs):
            kernel(*refs[:count], *refs[count + len(after) :])

        return pl.pallas_call(
            wrapped,
            in_specs=[INSIDE] * count + [ANYWHERE] * len(after),
            out_specs=[INSIDE] * len(outputs),
            out_shape=[
                jax.ShapeDtypeStruct(shape, dtype) if i in free else self.out(shape, dtype)
                for i, (shape, dtype) in enumerate(outputs)
            ],
            input_output_aliases=alias or {},
            compiler_params=pltpu.CompilerParams(vmem_limit_bytes=limit),
            cost_estimate=pl.CostEstimate(flops=flops, bytes_accessed=10**6, transcendentals=0),
            name=name,
        )(*[self.pin(a) for a in inputs], *after)


def pack_kernel(experts, token_ref, grad_ref, ids_ref, weights_ref, out_ref):
    rows, width = grad_ref.shape
    extra = out_ref.shape[1] - 2 * width
    out_ref[:, :width] = token_ref[...]
    out_ref[:, width : 2 * width] = grad_ref[...]
    line = lax.broadcasted_iota(jnp.int32, (extra, rows), 0)
    part = sum((line >= i * experts).astype(jnp.int32) for i in range(1, 4))
    expert = jnp.where(part < 3, line - part * experts, -1)
    table = jnp.zeros((extra, rows), F32)
    for k in range(ids_ref.shape[0]):
        table = table + jnp.where(ids_ref[k : k + 1, :] == expert, weights_ref[k : k + 1, :], 0.0)
    high, middle, low = three_parts(table)
    split = jnp.where(
        part == 0,
        high.astype(F32),
        jnp.where(part == 1, middle.astype(F32), low.astype(F32)),
    ).astype(BF16)
    same = lax.broadcasted_iota(jnp.int32, (extra, extra), 0) == lax.broadcasted_iota(jnp.int32, (extra, extra), 1)
    out_ref[:, 2 * width :] = dot_tn(split, same.astype(F32).astype(BF16)).astype(BF16)


def weight_kernel(codes_in, codes_out, clip_in, range_in, clip_out, range_out, gu_ref, d_ref):
    dp = lax.axis_index("dp")
    depth, third = codes_in.shape[1:]
    hidden = clip_in.shape[3]
    groups = depth // GROUP
    own = pl.ds(pl.multiple_of(dp * groups, groups), groups)
    order = plane_order(hidden)
    for p in range(2):
        upper = sigmoid(clip_in[p, 0, own, :]) * range_in[p, 0, own, :]
        lower = sigmoid(clip_in[p, 1, own, :]) * range_in[p, 1, own, :]
        ends = placed(jnp.concatenate([(upper + lower) / 15.0, lower], axis=0), order)
        for g in range(groups):
            packed = codes_in[p, g * GROUP : (g + 1) * GROUP, :]
            for j in range(PACK):
                code = jnp.bitwise_and(jnp.right_shift(packed, 4 * j), 15).astype(F32)
                cols = slice(j * third, (j + 1) * third)
                gu_ref[p, g * GROUP : (g + 1) * GROUP, cols] = (
                    ends[g : g + 1, cols] * code - ends[groups + g : groups + g + 1, cols]
                ).astype(BF16)
    own = pl.ds(pl.multiple_of(dp * depth, depth), depth)
    step, lower = [], []
    for g in range(clip_out.shape[0]):
        upper_end = sigmoid(clip_out[g, 0:1, own]) * range_out[g, 0:1, own]
        lower_end = sigmoid(clip_out[g, 1:2, own]) * range_out[g, 1:2, own]
        step.append((upper_end + lower_end) / 15.0)
        lower.append(lower_end)
    row = lax.broadcasted_iota(jnp.int32, (CHUNK, 1), 0)
    for start in range(0, third, CHUNK):
        packed = codes_out[start : start + CHUNK, :]
        for j in range(PACK):
            first = (PACK * start + j) // GROUP
            last = (PACK * (start + CHUNK - 1) + j) // GROUP
            step_rows, lower_rows = step[first], lower[first]
            for g in range(first + 1, last + 1):
                late = PACK * (row + start) + j >= g * GROUP
                step_rows = jnp.where(late, step[g], step_rows)
                lower_rows = jnp.where(late, lower[g], lower_rows)
            code = jnp.bitwise_and(jnp.right_shift(packed, 4 * j), 15).astype(F32)
            d_ref[j * third + start : j * third + start + CHUNK, :] = (
                step_rows * code - lower_rows
            ).astype(BF16)


def set_kernel(experts, first, *refs):
    blocks = refs[0:4]
    gu_sides, d_sides = refs[4:6], refs[6:8]
    refs = refs[8:] if first == 0 else refs[12:]
    partials = refs[0:4]
    x_ref, s_ref, h_ref, g_ref = refs[4:8]
    rows, width = partials[0].shape
    half = width // 2
    hidden = h_ref.shape[1]
    third = hidden // PACK
    dp, mine = lax.axis_index("dp"), lax.axis_index("expert")
    spans = (
        pl.ds(pl.multiple_of(dp * half, half), half),
        pl.ds(pl.multiple_of((1 - dp) * half, half), half),
    )
    here = slice(first, first + 4 * rows)
    for i in range(4):
        span = slice(first + i * rows, first + (i + 1) * rows)
        x_ref[span, :] = blocks[i][:, :width]
        beside = blocks[i][:, 2 * width :].astype(F32)
        lane = lax.broadcasted_iota(jnp.int32, beside.shape, 1)
        keep = (lane == mine) | (lane == mine + experts) | (lane == mine + 2 * experts)
        scale = jnp.sum(jnp.where(keep, beside, 0.0), axis=1, keepdims=True)
        s_ref[span, :] = (scale * blocks[i][:, width : 2 * width].astype(F32)).astype(BF16)
    for j in range(PACK):
        cols = slice(j * third, (j + 1) * third)
        gate_pre = dot_nn(x_ref[here, spans[0]], gu_sides[0][0, :, cols]) + dot_nn(
            x_ref[here, spans[1]], gu_sides[1][0, :, cols]
        )
        up_pre = dot_nn(x_ref[here, spans[0]], gu_sides[0][1, :, cols]) + dot_nn(
            x_ref[here, spans[1]], gu_sides[1][1, :, cols]
        )
        grad_hidden = dot_nt(s_ref[here, spans[0]], d_sides[0][cols, :]) + dot_nt(
            s_ref[here, spans[1]], d_sides[1][cols, :]
        )
        sig = sigmoid(gate_pre)
        act = gate_pre * sig
        h_ref[here, cols] = (act * up_pre).astype(BF16)
        g_ref[0, here, cols] = (grad_hidden * up_pre * sig * (1.0 + gate_pre * (1.0 - sig))).astype(BF16)
        g_ref[1, here, cols] = (grad_hidden * act).astype(BF16)
    for side in range(2):
        base = jnp.where(side == 0, dp, 1 - dp) * half

        @pl.loop(0, half // TILE)
        def _(n):
            depth = pl.ds(pl.multiple_of(n * TILE, TILE), TILE)
            part = dot_nt(g_ref[0, here, :], gu_sides[side][0, depth, :]) + dot_nt(
                g_ref[1, here, :], gu_sides[side][1, depth, :]
            )
            cols = pl.ds(pl.multiple_of(base + n * TILE, TILE), TILE)
            for i in range(4):
                partials[i][:, cols] = part[i * rows : (i + 1) * rows, :].astype(BF16)


def run_set(calls, blocks, weights, experts, pair, after):
    rows, width = blocks[0].shape[0], 2 * weights[2].shape[1]
    hidden = weights[2].shape[0]
    both = 8 * rows
    stored = [((both, width), BF16), ((both, width), BF16), ((both, hidden), BF16), ((2, both, hidden), BF16)]
    out = calls.run(
        functools.partial(set_kernel, experts, 0 if pair is None else 4 * rows),
        "expert_set",
        [*blocks, *weights, *(pair or ())],
        [((rows, width), BF16)] * 4 + stored,
        after=after,
        alias=None if pair is None else {8 + i: 4 + i for i in range(4)},
        flops=40 * rows * width * hidden,
    )
    return list(out[:4]), list(out[4:])


def group_marks(size, count, span, planes):
    row = lax.broadcasted_iota(jnp.int32, (size, count), 0)
    group = lax.broadcasted_iota(jnp.int32, (size, count), 1)
    if planes > 1:
        third = size // planes
        plane = jnp.zeros_like(row)
        for j in range(1, planes):
            plane = plane + (row >= j * third).astype(jnp.int32)
        row = planes * (row - plane * third) + plane
    return ((row >= group * span) & (row < (group + 1) * span)).astype(F32).astype(BF16)


def two_parts(a):
    high = a.astype(BF16)
    return high, (a - high.astype(F32)).astype(BF16)


def sums_kernel(other, more, x_ref, s_ref, h_ref, g_ref, weights_in, weights_out, *refs):
    old_in, old_out = refs[:2] if more else (None, None)
    sums_in, sums_out = refs[-2:]
    width = x_ref.shape[1]
    half = width // 2
    hidden = h_ref.shape[1]
    third = hidden // PACK
    share = sums_in.shape[2]
    groups_out = sums_out.shape[1]
    dp = lax.axis_index("dp")
    base = (1 - dp if other else dp) * half
    span = pl.ds(pl.multiple_of(base, half), half)

    def since(old, found, *where):
        return old[where] + found if more else found

    row_sums = two_parts(dot_nn(x_ref[:, span], group_marks(half, share, GROUP, 1)))
    for p in range(2):
        found = dot_tn(row_sums[0], g_ref[p]) + dot_tn(row_sums[1], g_ref[p])
        sums_in[p, 1] = since(old_in, found, p, 1)
    hidden_sums = two_parts(dot_nn(h_ref[...], group_marks(hidden, groups_out, GROUP, PACK)))
    found = dot_tn(hidden_sums[0], s_ref[:, span]) + dot_tn(hidden_sums[1], s_ref[:, span])
    sums_out[1] = since(old_out, found, 1)

    @pl.loop(0, half // TILE)
    def _(t):
        rows = pl.ds(pl.multiple_of(t * TILE, TILE), TILE)
        span = pl.ds(pl.multiple_of(base + t * TILE, TILE), TILE)
        x_cols = x_ref[:, span]
        for p in range(2):
            weighted = dot_tn(x_cols, g_ref[p]) * weights_in[p, rows, :].astype(F32)
            for g in range(TILE // GROUP):
                spot = pl.ds(t * (TILE // GROUP) + g, 1)
                found = jnp.sum(weighted[g * GROUP : (g + 1) * GROUP], axis=0, keepdims=True)
                sums_in[p, 0, spot, :] = since(old_in, found, p, 0, spot, slice(None))
        weighted = dot_tn(h_ref[...], s_ref[:, span]) * weights_out[:, rows].astype(F32)
        for g in range(groups_out):
            found = None
            for j in range(PACK):
                low = -((j - GROUP * g) // PACK)
                high = -((j - GROUP * (g + 1)) // PACK)
                inner, outer = -(-low // 8) * 8, high // 8 * 8
                part = jnp.sum(weighted[j * third + inner : j * third + outer], axis=0, keepdims=True)
                found = part if found is None else found + part
                for start in sorted(({low // 8 * 8} if low % 8 else set()) | ({outer} if high % 8 else set())):
                    block = weighted[j * third + start : j * third + start + 8]
                    row = lax.broadcasted_iota(jnp.int32, block.shape, 0) + start
                    inside = (row >= low) & (row < high)
                    found = found + jnp.sum(jnp.where(inside, block, 0.0), axis=0, keepdims=True)
            sums_out[0, g : g + 1, rows] = since(old_out, found, 0, slice(g, g + 1), rows)


def run_sums(calls, stored, weights, other, before, shapes, after):
    both, width = stored[0].shape
    hidden = stored[2].shape[1]
    side = weights[1::2] if other else weights[0::2]
    return calls.run(
        functools.partial(sums_kernel, other, before is not None),
        "group_sums",
        [*stored, *side, *(before or ())],
        [(shape, F32) for shape in shapes],
        after=after,
        flops=3 * both * width * hidden,
    )


def clip_kernel(mine_in, got_in, mine_out, got_out, clip_in, range_in, clip_out, range_out, in_ref, out_ref):
    dp = lax.axis_index("dp")
    hidden = clip_in.shape[3]
    groups = in_ref.shape[2]
    share = out_ref.shape[2]
    back = plane_order(hidden, True)

    def finish(weighted, plain, clip, span):
        sig_upper, sig_lower = sigmoid(clip[0]), sigmoid(clip[1])
        upper, lower = sig_upper * span[0], sig_lower * span[1]
        upper_sum = (weighted + lower * plain) / (upper + lower)
        lower_sum = upper_sum - plain
        return (
            upper_sum * span[0] * sig_upper * (1.0 - sig_upper),
            lower_sum * span[1] * sig_lower * (1.0 - sig_lower),
        )

    own = pl.ds(pl.multiple_of(dp * groups, groups), groups)
    for p in range(2):
        sums = jnp.concatenate(
            [mine_in[p, 0] + got_in[p, 0], mine_in[p, 1] + got_in[p, 1]], axis=0
        )
        natural = placed(sums, back)
        in_ref[p, 0], in_ref[p, 1] = finish(
            natural[:groups],
            natural[groups:],
            [clip_in[p, i, own, :] for i in range(2)],
            [range_in[p, i, own, :] for i in range(2)],
        )
    own = pl.ds(pl.multiple_of(dp * share, share), share)
    for g in range(out_ref.shape[0]):
        out_ref[g, 0:1, :], out_ref[g, 1:2, :] = finish(
            mine_out[0, g : g + 1, :] + got_out[0, g : g + 1, :],
            mine_out[1, g : g + 1, :] + got_out[1, g : g + 1, :],
            [clip_out[g, i : i + 1, own] for i in range(2)],
            [range_out[g, i : i + 1, own] for i in range(2)],
        )


def add_kernel(*refs):
    total = refs[0][...].astype(F32)
    for ref in refs[1:-1]:
        total = total + ref[...].astype(F32)
    refs[-1][...] = total.astype(refs[-1].dtype)


def body(
    tokens,
    grad_out,
    expert_ids,
    router_weights,
    codes_in,
    codes_out,
    clip_in,
    range_in,
    clip_out,
    range_out,
):
    experts = lax.axis_size("expert")
    rows, width = tokens.shape
    hidden = clip_in.shape[4]
    depth = codes_in.shape[2]
    extra = -(-3 * experts // 128) * 128
    sets = experts // 4
    calls = Calls(experts * rows * (3 * width + extra) * 2 < 2**24)

    def swap(array, mask):
        return lax.ppermute(array, "expert", [(i, i ^ mask) for i in range(experts)])

    def swap_core(array):
        return lax.ppermute(array, "dp", [(0, 1), (1, 0)])

    def added(*parts, after=(), free=()):
        return calls.run(
            add_kernel, "add_rows", list(parts), [(parts[0].shape, BF16)], after=after, limit=SMALL, free=free
        )[0]

    packed = calls.run(
        functools.partial(pack_kernel, experts),
        "pack_rows",
        [tokens, grad_out, expert_ids.T, router_weights.T],
        [((rows, 2 * width + extra), BF16)],
        limit=SMALL,
    )[0]

    order = [0] + [r for r in range(sets) if r % 4 > 1] + [r for r in range(1, sets) if r % 4 < 2]
    blocks, heads = {}, {0: packed}
    for r in order:
        if r not in heads:
            heads[r] = swap(packed, 4 * r) if r % 2 == 0 or r == 1 else swap(heads[r - 1], 4)
        own = heads[r]
        over_x, over_y = swap(own, 1), swap(own, 2)
        if r % 2 == 1:
            diagonal = swap(blocks[r - 1][3], 4)
        elif r % 4 == 0:
            diagonal = swap(over_x, 2)
        else:
            diagonal = swap(over_y, 1)
        blocks[r] = (own, over_x, over_y, diagonal)

    clips = (clip_in[0], range_in[0], clip_out[0].transpose(1, 0, 2), range_out[0].transpose(1, 0, 2))
    gu_mine, d_mine = calls.run(
        weight_kernel,
        "make_weights",
        [codes_in[0], codes_out[0], *clips],
        [((2, depth, hidden), BF16), ((hidden, depth), BF16)],
        after=(blocks[0][1],),
    )
    weights = (gu_mine, swap_core(gu_mine), d_mine, swap_core(d_mine))

    shapes = ((2, 2, depth // GROUP, hidden), (2, clip_out.shape[2], depth))
    partials, sums, after = {}, {True: None, False: None}, ()
    for first, second in zip(order[0::2], order[1::2]):
        partials[first], stored = run_set(calls, blocks[first], weights, experts, None, after)
        partials[second], stored = run_set(calls, blocks[second], weights, experts, stored, ())
        for other in (True, False):
            sums[other] = run_sums(calls, stored, weights, other, sums[other], shapes, ())
        after = (sums[False][0],)

    final = []
    for r in order[1:]:
        own, p_x, p_y, p_d = partials[r]
        if r == 1:
            partials[0][3] = added(partials[0][3], swap(p_d, 4))
        elif r % 4 in (0, 3):
            p_x = added(p_x, swap(p_d, 2))
        else:
            p_y = added(p_y, swap(p_d, 1))
        final.append(swap(added(own, swap(p_x, 1), swap(p_y, 2)), 4 * r))
    own, p_x, p_y, p_d = partials[0]
    p_x = added(p_x, swap(p_d, 2))
    grad_tokens = added(own, swap(p_x, 1), swap(p_y, 2), *final, free=(0,))

    mine_in, mine_out = sums[False]
    got_in, got_out = (swap_core(a) for a in sums[True])
    grad_in, grad_clip_out = calls.run(
        clip_kernel,
        "clip_gradients",
        [mine_in, got_in, mine_out, got_out, *clips],
        [((2, 2, depth // GROUP, hidden), F32), ((clip_out.shape[2], 2, depth), F32)],
        limit=SMALL,
        free=(0, 1),
    )
    return grad_tokens, grad_in[None], grad_clip_out.transpose(1, 0, 2)[None]


def solution(mesh):
    return jax.shard_map(
        body,
        mesh=mesh,
        in_specs=(
            P(("expert", "dp"), None),
            P(("expert", "dp"), None),
            P(("expert", "dp"), None),
            P(("expert", "dp"), None),
            P("expert", None, "dp", None),
            P("expert", None, "dp"),
            P("expert", None, None, None, None),
            P("expert", None, None, None, None),
            P("expert", None, None, None),
            P("expert", None, None, None),
        ),
        out_specs=(
            P(("expert", "dp"), None),
            P("expert", None, None, "dp", None),
            P("expert", None, None, "dp"),
        ),
        check_vma=False,
    )
```

profile of v0, /device:TPU:0, one launch (start us, length us, event | category | flops | bytes accessed | tf_op | source)
XLA Modules:
  0.0 182.5 jit_solution(5286279982129090976)
XLA Ops:
  0.6 0.9 copy-done.10
  1.6 0.9 copy-done.11
  2.5 0.7 copy-done.12
  3.2 0.7 copy-done.13
  3.9 0.2 pack_rows.1.refs_0_
  4.1 2.9 %collective-permute-start = (bf16[64,4224]{1,0:T(8,128)(2,1)S(1)}, bf16[64,4224]{1,0:T(8,128)(2,1)S(1)}, u32[]{:S(2)}, u32[]{:S(2)}) collective-permute-start(bf16[64,4224]{1,0:T(8,128)(2,1)S(1)} %pack_rows.1.refs_0_), channel_id=1, source_target_pairs={{0,2},{2,0},{4,6},{6,4},{8,10},{10,8},{12,14},{14,12},{16,18},{18,... | collective-permute-start | bytes 1622024 | tf_op jit(solution)/shard_map/ppermute | solution.py:379
  7.0 12.3 %collective-permute-done.refs_6_.refs_1_ = bf16[64,4224]{1,0:T(8,128)(2,1)S(1)} collective-permute-done((bf16[64,4224]{1,0:T(8,128)(2,1)S(1)}, bf16[64,4224]{1,0:T(8,128)(2,1)S(1)}, u32[]{:S(2)}, u32[]{:S(2)}) %collective-permute-start) | collective-permute-done | bytes 540704 | tf_op jit(solution)/shard_map/ppermute | solution.py:379
  19.3 1.6 copy-done
  20.9 1.2 copy-done.1
  22.1 0.9 copy-done.2
  23.1 0.9 copy-done.4
  24.0 0.9 copy-done.6
  24.9 0.9 copy-done.8
  25.8 2.6 %make_weights.1 = (bf16[2,1024,768]{2,1,0:T(8,128)(2,1)S(1)}, bf16[768,1024]{1,0:T(8,128)(2,1)S(1)}) custom-call(s32[2,1024,256]{2,1,0:T(8,128)S(1)} %bitcast.16, s32[256,1024]{1,0:T(8,128)S(1)} %bitcast.17, f32[2,2,16,768]{3,2,1,0:T(8,128)S(1)} %bitcast.18, f32[2,2,16,768]{3,2,1,0:T(8,128)S(1)} %bitcast.20, f32[6,2,2048]{2,1,0:T(2,128)S(1)} %bitcast.22, ...), custom_call_target="tpu_custom_call" | custom-call | bytes 1000000 | tf_op jit(solution)/shard_map/make_weights/pallas_call | solution.py:79
  28.4 0.5 collective-permute-start.4
  28.9 1.8 collective-permute-start.1
  30.7 2.6 %collective-permute-start.9 = (bf16[64,4224]{1,0:T(8,128)(2,1)S(1)}, bf16[64,4224]{1,0:T(8,128)(2,1)S(1)}, u32[]{:S(2)}, u32[]{:S(2)}) collective-permute-start(bf16[64,4224]{1,0:T(8,128)(2,1)S(1)} %pack_rows.1.refs_0_), channel_id=1, source_target_pairs={{0,16},{2,18},{4,20},{6,22},{8,24},{10,26},{12,28},{14,30},{16,0},... | collective-permute-start | bytes 1622024 | tf_op jit(solution)/shard_map/ppermute | solution.py:379
  33.3 1.6 collective-permute-start.5
  34.9 8.3 %collective-permute-done.1.refs_2_ = bf16[64,4224]{1,0:T(8,128)(2,1)S(1)} collective-permute-done((bf16[64,4224]{1,0:T(8,128)(2,1)S(1)}, bf16[64,4224]{1,0:T(8,128)(2,1)S(1)}, u32[]{:S(2)}, u32[]{:S(2)}) %collective-permute-start.1) | collective-permute-done | bytes 540704 | tf_op jit(solution)/shard_map/ppermute | solution.py:379
  43.2 1.7 collective-permute-start.2
  45.0 12.3 %collective-permute-done.9.refs_0_ = bf16[64,4224]{1,0:T(8,128)(2,1)S(1)} collective-permute-done((bf16[64,4224]{1,0:T(8,128)(2,1)S(1)}, bf16[64,4224]{1,0:T(8,128)(2,1)S(1)}, u32[]{:S(2)}, u32[]{:S(2)}) %collective-permute-start.9) | collective-permute-done | bytes 540704 | tf_op jit(solution)/shard_map/ppermute | solution.py:379
  57.3 0.5 collective-permute-start.13
  57.7 1.2 collective-permute-start.10
  58.9 1.5 collective-permute-start.16
  60.4 10.0 %collective-permute-done.13.refs_2_ = bf16[64,4224]{1,0:T(8,128)(2,1)S(1)} collective-permute-done((bf16[64,4224]{1,0:T(8,128)(2,1)S(1)}, bf16[64,4224]{1,0:T(8,128)(2,1)S(1)}, u32[]{:S(2)}, u32[]{:S(2)}) %collective-permute-start.13) | collective-permute-done | bytes 540704 | tf_op jit(solution)/shard_map/ppermute | solution.py:379
  70.4 1.5 collective-permute-start.14
  71.9 0.5 collective-permute-start.6
  72.4 1.2 collective-permute-start.7
  73.6 0.8 collective-permute-start.11
  74.4 6.3 %expert_set.4 = (bf16[64,2048]{1,0:T(8,128)(2,1)S(1)}, bf16[64,2048]{1,0:T(8,128)(2,1)S(1)}, bf16[64,2048]{1,0:T(8,128)(2,1)S(1)}, bf16[64,2048]{1,0:T(8,128)(2,...) custom-call(bf16[64,4224]{1,0:T(8,128)(2,1)S(1)} %pack_rows.1.refs_0, ...), custom_call_target="tpu_custom_call" | custom-call | flops 4026531840 | bytes 1000000 | tf_op jit(solution)/shard_map/expert_set/pallas_call | solution.py:79
  80.7 1.6 collective-permute-start.12
  82.3 3.3 %collective-permute-done.14.refs_3_ = bf16[64,4224]{1,0:T(8,128)(2,1)S(1)} collective-permute-done((bf16[64,4224]{1,0:T(8,128)(2,1)S(1)}, bf16[64,4224]{1,0:T(8,128)(2,1)S(1)}, u32[]{:S(2)}, u32[]{:S(2)}) %collective-permute-start.14) | collective-permute-done | bytes 540704 | tf_op jit(solution)/shard_map/ppermute | solution.py:379
  85.6 1.7 collective-permute-start.15
  87.3 6.1 %expert_set.5 = (bf16[64,2048]{1,0:T(8,128)(2,1)S(1)}, bf16[64,2048]{1,0:T(8,128)(2,1)S(1)}, bf16[64,2048]{1,0:T(8,128)(2,1)S(1)}, bf16[64,2048]{1,0:T(8,128)(2,...) custom-call(bf16[64,4224]{1,0:T(8,128)(2,1)S(1)} %collective-permute, ...), custom_call_target="tpu_custom_call", output_to_operand_aliasing={{4}: (8, {}), {5}: (9, {}), {6}: (10, {}), {7}: (11, {})} | custom-call | flops 4026531840 | bytes 1000000 | tf_op jit(solution)/shard_map/expert_set/pallas_call | solution.py:79
  93.4 13.4 %collective-permute-done.11.refs_1_ = bf16[64,4224]{1,0:T(8,128)(2,1)S(1)} collective-permute-done((bf16[64,4224]{1,0:T(8,128)(2,1)S(1)}, bf16[64,4224]{1,0:T(8,128)(2,1)S(1)}, u32[]{:S(2)}, u32[]{:S(2)}) %collective-permute-start.11) | collective-permute-done | bytes 540704 | tf_op jit(solution)/shard_map/ppermute | solution.py:379
  106.8 1.8 collective-permute-start.8
  108.6 5.4 %group_sums.4 = (f32[2,2,8,768]{3,2,1,0:T(8,128)S(1)}, f32[2,6,1024]{2,1,0:T(8,128)S(1)}) custom-call(bf16[512,2048]{1,0:T(8,128)(2,1)S(1)} %get-tuple-element.56.refs_0_, bf16[512,2048]{1,0:T(8,128)(2,1)S(1)} %get-tuple-element.57.refs_1_, bf16[512,768]{1,0:T(8,128)(2,1)S(1)} %get-tuple-element.58.refs_2_, ...), custom_call_target="tpu_custom_call" | custom-call | flops 2415919104 | bytes 1000000 | tf_op jit(solution)/shard_map/group_sums/pallas_call | solution.py:79
  114.0 6.1 %expert_set.6 = (bf16[64,2048]{1,0:T(8,128)(2,1)S(1)}, bf16[64,2048]{1,0:T(8,128)(2,1)S(1)}, bf16[64,2048]{1,0:T(8,128)(2,1)S(1)}, bf16[64,2048]{1,0:T(8,128)(2,...) custom-call(bf16[64,4224]{1,0:T(8,128)(2,1)S(1)} %collective-permute, ...), custom_call_target="tpu_custom_call" | custom-call | flops 4026531840 | bytes 1000000 | tf_op jit(solution)/shard_map/expert_set/pallas_call | solution.py:79
  120.1 0.6 collective-permute-start.25
  120.7 1.5 collective-permute-start.22
  122.2 6.3 %expert_set.7 = (bf16[64,2048]{1,0:T(8,128)(2,1)S(1)}, bf16[64,2048]{1,0:T(8,128)(2,1)S(1)}, bf16[64,2048]{1,0:T(8,128)(2,1)S(1)}, bf16[64,2048]{1,0:T(8,128)(2,...) custom-call(bf16[64,4224]{1,0:T(8,128)(2,1)S(1)} %collective-permute, ...), custom_call_target="tpu_custom_call", output_to_operand_aliasing={{4}: (8, {}), {5}: (9, {}), {6}: (10, {}), {7}: (11, {})} | custom-call | flops 4026531840 | bytes 1000000 | tf_op jit(solution)/shard_map/expert_set/pallas_call | solution.py:79
  128.5 1.3 collective-permute-start.17
  129.8 0.5 collective-permute-start.29
  130.4 0.5 collective-permute-start.30
  130.9 1.5 collective-permute-start.27
  132.4 5.4 %group_sums.6 = (f32[2,2,8,768]{3,2,1,0:T(8,128)S(1)}, f32[2,6,1024]{2,1,0:T(8,128)S(1)}) custom-call(bf16[512,2048]{1,0:T(8,128)(2,1)S(1)} %get-tuple-element.56.refs_0_, bf16[512,2048]{1,0:T(8,128)(2,1)S(1)} %get-tuple-element.57.refs_1_, bf16[512,768]{1,0:T(8,128)(2,1)S(1)} %get-tuple-element.58.refs_2_, ...), custom_call_target="tpu_custom_call" | custom-call | flops 2415919104 | bytes 1000000 | tf_op jit(solution)/shard_map/group_sums/pallas_call | solution.py:79
  137.9 1.6 collective-permute-start.21
  139.5 0.6 collective-permute-start.26
  140.2 0.6 collective-permute-start.23
  140.8 1.5 collective-permute-start.18
  142.3 5.4 %group_sums.7 = (f32[2,2,8,768]{3,2,1,0:T(8,128)S(1)}, f32[2,6,1024]{2,1,0:T(8,128)S(1)}) custom-call(bf16[512,2048]{1,0:T(8,128)(2,1)S(1)} %get-tuple-element.78.refs_0_, bf16[512,2048]{1,0:T(8,128)(2,1)S(1)} %get-tuple-element.79.refs_1_, bf16[512,768]{1,0:T(8,128)(2,1)S(1)} %get-tuple-element.80.refs_2_, ...), custom_call_target="tpu_custom_call" | custom-call | flops 2415919104 | bytes 1000000 | tf_op jit(solution)/shard_map/group_sums/pallas_call | solution.py:79
  147.7 4.8 %collective-permute-done.18.refs_1_ = bf16[64,2048]{1,0:T(8,128)(2,1)S(1)} collective-permute-done((bf16[64,2048]{1,0:T(8,128)(2,1)S(1)}, bf16[64,2048]{1,0:T(8,128)(2,1)S(1)}, u32[]{:S(2)}, u32[]{:S(2)}) %collective-permute-start.18) | collective-permute-done | bytes 262176 | tf_op jit(solution)/shard_map/ppermute | solution.py:379
  152.6 0.1 add_rows.14
  152.7 0.4 collective-permute-start.20
  153.2 0.1 add_rows.13
  153.3 1.7 collective-permute-start.31
  155.0 3.3 %collective-permute-start.28 = (bf16[64,2048]{1,0:T(8,128)(2,1)S(1)}, bf16[64,2048]{1,0:T(8,128)(2,1)S(1)}, u32[]{:S(2)}, u32[]{:S(2)}) collective-permute-start(bf16[64,2048]{1,0:T(8,128)(2,1)S(1)} %add_rows.13), channel_id=1, source_target_pairs={{0,24},{2,26},{4,28},{6,30},{8,16},{10,18},{12,20},{14,22},{16,8},... | collective-permute-start | bytes 786440 | tf_op jit(solution)/shard_map/ppermute | solution.py:379
  158.4 0.1 collective-permute-start.24
  158.6 1.5 collective-permute-start.19
  160.1 5.4 %group_sums.5 = (f32[2,2,8,768]{3,2,1,0:T(8,128)S(1)}, f32[2,6,1024]{2,1,0:T(8,128)S(1)}) custom-call(bf16[512,2048]{1,0:T(8,128)(2,1)S(1)} %get-tuple-element.78.refs_0_, bf16[512,2048]{1,0:T(8,128)(2,1)S(1)} %get-tuple-element.79.refs_1_, bf16[512,768]{1,0:T(8,128)(2,1)S(1)} %get-tuple-element.80.refs_2_, ...), custom_call_target="tpu_custom_call" | custom-call | flops 2415919104 | bytes 1000000 | tf_op jit(solution)/shard_map/group_sums/pallas_call | solution.py:79
  165.5 1.7 clip_gradients.1
  167.2 3.9 %collective-permute-done.28.refs_4_ = bf16[64,2048]{1,0:T(8,128)(2,1)S(1)} collective-permute-done((bf16[64,2048]{1,0:T(8,128)(2,1)S(1)}, bf16[64,2048]{1,0:T(8,128)(2,1)S(1)}, u32[]{:S(2)}, u32[]{:S(2)}) %collective-permute-start.28) | collective-permute-done | bytes 262176 | tf_op jit(solution)/shard_map/ppermute | solution.py:379
  171.2 10.5 %collective-permute-done.24.refs_3_ = bf16[64,2048]{1,0:T(8,128)(2,1)S(1)} collective-permute-done((bf16[64,2048]{1,0:T(8,128)(2,1)S(1)}, bf16[64,2048]{1,0:T(8,128)(2,1)S(1)}, u32[]{:S(2)}, u32[]{:S(2)}) %collective-permute-start.24) | collective-permute-done | bytes 262176 | tf_op jit(solution)/shard_map/ppermute | solution.py:379
  181.6 0.9 add_rows.15
  (51 shorter events, 0.6 us)
Async XLA Ops:
  0.6 1.0 copy-start.10
  1.6 0.9 copy-start.11
  2.5 0.7 copy-start.12
  3.2 0.7 copy-start.13
  4.1 15.2 %collective-permute-start = (bf16[64,4224]{1,0:T(8,128)(2,1)S(1)}, bf16[64,4224]{1,0:T(8,128)(2,1)S(1)}, u32[]{:S(2)}, u32[]{:S(2)}) collective-permute-start(bf16[64,4224]{1,0:T(8,128)(2,1)S(1)} %pack_rows.1.refs_0_), channel_id=1, source_target_pairs={{0,2},{2,0},{4,6},{6,4},{8,10},{10,8},{12,14},{14,12},{16,18},{18,... | collective-permute-start | bytes 1622024 | tf_op jit(solution)/shard_map/ppermute | solution.py:379
  19.3 1.6 copy-start
  20.9 1.2 copy-start.1
  22.1 0.9 copy-start.2
  23.1 0.9 copy-start.4
  24.0 0.9 copy-start.6
  24.9 0.9 copy-start.8
  28.4 45.3 %collective-permute-start.3 = (bf16[2,1024,768]{2,1,0:T(8,128)(2,1)S(1)}, bf16[2,1024,768]{2,1,0:T(8,128)(2,1)S(1)}, u32[]{:S(2)}, u32[]{:S(2)}) collective-permute-start(bf16[2,1024,768]{2,1,0:T(8,128)(2,1)S(1)} %get-tuple-element.47.refs_4_), channel_id=1, source_target_pairs={{0,1},{1,0},{2,3},{3,2},{4,5},{5,4},{6,7},{7,6},{8,9},{9,8},{10,11... | collective-permute-start | bytes 9437192 | tf_op jit(solution)/shard_map/ppermute | solution.py:382
  28.4 44.0 %collective-permute-start.4 = (bf16[768,1024]{1,0:T(8,128)(2,1)S(1)}, bf16[768,1024]{1,0:T(8,128)(2,1)S(1)}, u32[]{:S(2)}, u32[]{:S(2)}) collective-permute-start(bf16[768,1024]{1,0:T(8,128)(2,1)S(1)} %get-tuple-element.48.refs_6_.refs_5_), channel_id=1, source_target_pairs={{0,1},{1,0},{2,3},{3,2},{4,5},{5,4},{6,7},{7,6},{8,9},{9,8},{10,11... | collective-permute-start | bytes 4718600 | tf_op jit(solution)/shard_map/ppermute | solution.py:382
  28.9 14.3 %collective-permute-start.1 = (bf16[64,4224]{1,0:T(8,128)(2,1)S(1)}, bf16[64,4224]{1,0:T(8,128)(2,1)S(1)}, u32[]{:S(2)}, u32[]{:S(2)}) collective-permute-start(bf16[64,4224]{1,0:T(8,128)(2,1)S(1)} %pack_rows.1.refs_0_), channel_id=1, source_target_pairs={{0,4},{2,6},{4,0},{6,2},{8,12},{10,14},{12,8},{14,10},{16,20},{18,... | collective-permute-start | bytes 1622024 | tf_op jit(solution)/shard_map/ppermute | solution.py:379
  30.7 26.6 %collective-permute-start.9 = (bf16[64,4224]{1,0:T(8,128)(2,1)S(1)}, bf16[64,4224]{1,0:T(8,128)(2,1)S(1)}, u32[]{:S(2)}, u32[]{:S(2)}) collective-permute-start(bf16[64,4224]{1,0:T(8,128)(2,1)S(1)} %pack_rows.1.refs_0_), channel_id=1, source_target_pairs={{0,16},{2,18},{4,20},{6,22},{8,24},{10,26},{12,28},{14,30},{16,0},... | collective-permute-start | bytes 1622024 | tf_op jit(solution)/shard_map/ppermute | solution.py:379
  33.3 24.4 %collective-permute-start.5 = (bf16[64,4224]{1,0:T(8,128)(2,1)S(1)}, bf16[64,4224]{1,0:T(8,128)(2,1)S(1)}, u32[]{:S(2)}, u32[]{:S(2)}) collective-permute-start(bf16[64,4224]{1,0:T(8,128)(2,1)S(1)} %pack_rows.1.refs_0_), channel_id=1, source_target_pairs={{0,8},{2,10},{4,12},{6,14},{8,0},{10,2},{12,4},{14,6},{16,24},{18,... | collective-permute-start | bytes 1622024 | tf_op jit(solution)/shard_map/ppermute | solution.py:379
  43.2 15.7 %collective-permute-start.2 = (bf16[64,4224]{1,0:T(8,128)(2,1)S(1)}, bf16[64,4224]{1,0:T(8,128)(2,1)S(1)}, u32[]{:S(2)}, u32[]{:S(2)}) collective-permute-start(bf16[64,4224]{1,0:T(8,128)(2,1)S(1)} %collective-permute-done.refs_6_.refs_1_), channel_id=1, source_target_pairs={{0,4},{2,6},{4,0},{6,2},{8,12},{10,14},{12,8},{14,10},{16,20},{18,... | collective-permute-start | bytes 1622024 | tf_op jit(solution)/shard_map/ppermute | solution.py:379
  57.3 13.1 %collective-permute-start.13 = (bf16[64,4224]{1,0:T(8,128)(2,1)S(1)}, bf16[64,4224]{1,0:T(8,128)(2,1)S(1)}, u32[]{:S(2)}, u32[]{:S(2)}) collective-permute-start(bf16[64,4224]{1,0:T(8,128)(2,1)S(1)} %collective-permute-done.9.refs_0_), channel_id=1, source_target_pairs={{0,4},{2,6},{4,0},{6,2},{8,12},{10,14},{12,8},{14,10},{16,20},{18,... | collective-permute-start | bytes 1622024 | tf_op jit(solution)/shard_map/ppermute | solution.py:379
  57.7 14.1 %collective-permute-start.10 = (bf16[64,4224]{1,0:T(8,128)(2,1)S(1)}, bf16[64,4224]{1,0:T(8,128)(2,1)S(1)}, u32[]{:S(2)}, u32[]{:S(2)}) collective-permute-start(bf16[64,4224]{1,0:T(8,128)(2,1)S(1)} %collective-permute-done.9.refs_0_), channel_id=1, source_target_pairs={{0,8},{2,10},{4,12},{6,14},{8,0},{10,2},{12,4},{14,6},{16,24},{18,... | collective-permute-start | bytes 1622024 | tf_op jit(solution)/shard_map/ppermute | solution.py:379
  58.9 21.8 %collective-permute-start.16 = (bf16[64,4224]{1,0:T(8,128)(2,1)S(1)}, bf16[64,4224]{1,0:T(8,128)(2,1)S(1)}, u32[]{:S(2)}, u32[]{:S(2)}) collective-permute-start(bf16[64,4224]{1,0:T(8,128)(2,1)S(1)} %collective-permute-done.9.refs_0_), channel_id=1, source_target_pairs={{0,2},{2,0},{4,6},{6,4},{8,10},{10,8},{12,14},{14,12},{16,18},{18,... | collective-permute-start | bytes 1622024 | tf_op jit(solution)/shard_map/ppermute | solution.py:379
  70.4 15.2 %collective-permute-start.14 = (bf16[64,4224]{1,0:T(8,128)(2,1)S(1)}, bf16[64,4224]{1,0:T(8,128)(2,1)S(1)}, u32[]{:S(2)}, u32[]{:S(2)}) collective-permute-start(bf16[64,4224]{1,0:T(8,128)(2,1)S(1)} %collective-permute-done.13.refs_2_), channel_id=1, source_target_pairs={{0,2},{2,0},{4,6},{6,4},{8,10},{10,8},{12,14},{14,12},{16,18},{18,... | collective-permute-start | bytes 1622024 | tf_op jit(solution)/shard_map/ppermute | solution.py:379
  71.9 50.3 %collective-permute-start.6 = (bf16[64,4224]{1,0:T(8,128)(2,1)S(1)}, bf16[64,4224]{1,0:T(8,128)(2,1)S(1)}, u32[]{:S(2)}, u32[]{:S(2)}) collective-permute-start(bf16[64,4224]{1,0:T(8,128)(2,1)S(1)} %collective-permute-done.5.refs_0_), channel_id=1, source_target_pairs={{0,2},{2,0},{4,6},{6,4},{8,10},{10,8},{12,14},{14,12},{16,18},{18,... | collective-permute-start | bytes 1622024 | tf_op jit(solution)/shard_map/ppermute | solution.py:379
  72.4 49.8 %collective-permute-start.7 = (bf16[64,4224]{1,0:T(8,128)(2,1)S(1)}, bf16[64,4224]{1,0:T(8,128)(2,1)S(1)}, u32[]{:S(2)}, u32[]{:S(2)}) collective-permute-start(bf16[64,4224]{1,0:T(8,128)(2,1)S(1)} %collective-permute-done.5.refs_0_), channel_id=1, source_target_pairs={{0,4},{2,6},{4,0},{6,2},{8,12},{10,14},{12,8},{14,10},{16,20},{18,... | collective-permute-start | bytes 1622024 | tf_op jit(solution)/shard_map/ppermute | solution.py:379
  73.6 33.1 %collective-permute-start.11 = (bf16[64,4224]{1,0:T(8,128)(2,1)S(1)}, bf16[64,4224]{1,0:T(8,128)(2,1)S(1)}, u32[]{:S(2)}, u32[]{:S(2)}) collective-permute-start(bf16[64,4224]{1,0:T(8,128)(2,1)S(1)} %collective-permute-done.10.refs_0_), channel_id=1, source_target_pairs={{0,2},{2,0},{4,6},{6,4},{8,10},{10,8},{12,14},{14,12},{16,18},{18,... | collective-permute-start | bytes 1622024 | tf_op jit(solution)/shard_map/ppermute | solution.py:379
  80.7 33.3 %collective-permute-start.12 = (bf16[64,4224]{1,0:T(8,128)(2,1)S(1)}, bf16[64,4224]{1,0:T(8,128)(2,1)S(1)}, u32[]{:S(2)}, u32[]{:S(2)}) collective-permute-start(bf16[64,4224]{1,0:T(8,128)(2,1)S(1)} %collective-permute-done.10.refs_0_), channel_id=1, source_target_pairs={{0,4},{2,6},{4,0},{6,2},{8,12},{10,14},{12,8},{14,10},{16,20},{18,... | collective-permute-start | bytes 1622024 | tf_op jit(solution)/shard_map/ppermute | solution.py:379
  85.6 28.4 %collective-permute-start.15 = (bf16[64,4224]{1,0:T(8,128)(2,1)S(1)}, bf16[64,4224]{1,0:T(8,128)(2,1)S(1)}, u32[]{:S(2)}, u32[]{:S(2)}) collective-permute-start(bf16[64,4224]{1,0:T(8,128)(2,1)S(1)} %collective-permute-done.14.refs_3_), channel_id=1, source_target_pairs={{0,8},{2,10},{4,12},{6,14},{8,0},{10,2},{12,4},{14,6},{16,24},{18,... | collective-permute-start | bytes 1622024 | tf_op jit(solution)/shard_map/ppermute | solution.py:379
  106.8 15.4 %collective-permute-start.8 = (bf16[64,4224]{1,0:T(8,128)(2,1)S(1)}, bf16[64,4224]{1,0:T(8,128)(2,1)S(1)}, u32[]{:S(2)}, u32[]{:S(2)}) collective-permute-start(bf16[64,4224]{1,0:T(8,128)(2,1)S(1)} %collective-permute-done.2.refs_3_), channel_id=1, source_target_pairs={{0,8},{2,10},{4,12},{6,14},{8,0},{10,2},{12,4},{14,6},{16,24},{18,... | collective-permute-start | bytes 1622024 | tf_op jit(solution)/shard_map/ppermute | solution.py:379
  120.1 10.8 %collective-permute-start.25 = (bf16[64,2048]{1,0:T(8,128)(2,1)S(1)}, bf16[64,2048]{1,0:T(8,128)(2,1)S(1)}, u32[]{:S(2)}, u32[]{:S(2)}) collective-permute-start(bf16[64,2048]{1,0:T(8,128)(2,1)S(1)} %get-tuple-element.73), channel_id=1, source_target_pairs={{0,4},{2,6},{4,0},{6,2},{8,12},{10,14},{12,8},{14,10},{16,20},{18,... | collective-permute-start | bytes 786440 | tf_op jit(solution)/shard_map/ppermute | solution.py:379
  120.7 17.2 %collective-permute-start.22 = (bf16[64,2048]{1,0:T(8,128)(2,1)S(1)}, bf16[64,2048]{1,0:T(8,128)(2,1)S(1)}, u32[]{:S(2)}, u32[]{:S(2)}) collective-permute-start(bf16[64,2048]{1,0:T(8,128)(2,1)S(1)} %get-tuple-element.70), channel_id=1, source_target_pairs={{0,2},{2,0},{4,6},{6,4},{8,10},{10,8},{12,14},{14,12},{16,18},{18,... | collective-permute-start | bytes 786440 | tf_op jit(solution)/shard_map/ppermute | solution.py:379
  128.5 11.0 %collective-permute-start.17 = (bf16[64,2048]{1,0:T(8,128)(2,1)S(1)}, bf16[64,2048]{1,0:T(8,128)(2,1)S(1)}, u32[]{:S(2)}, u32[]{:S(2)}) collective-permute-start(bf16[64,2048]{1,0:T(8,128)(2,1)S(1)} %get-tuple-element.65), channel_id=1, source_target_pairs={{0,8},{2,10},{4,12},{6,14},{8,0},{10,2},{12,4},{14,6},{16,24},{18,... | collective-permute-start | bytes 786440 | tf_op jit(solution)/shard_map/ppermute | solution.py:379
  129.8 10.3 %collective-permute-start.29 = (bf16[64,2048]{1,0:T(8,128)(2,1)S(1)}, bf16[64,2048]{1,0:T(8,128)(2,1)S(1)}, u32[]{:S(2)}, u32[]{:S(2)}) collective-permute-start(bf16[64,2048]{1,0:T(8,128)(2,1)S(1)} %get-tuple-element.76), channel_id=1, source_target_pairs={{0,2},{2,0},{4,6},{6,4},{8,10},{10,8},{12,14},{14,12},{16,18},{18,... | collective-permute-start | bytes 786440 | tf_op jit(solution)/shard_map/ppermute | solution.py:379
  130.4 10.4 %collective-permute-start.30 = (bf16[64,2048]{1,0:T(8,128)(2,1)S(1)}, bf16[64,2048]{1,0:T(8,128)(2,1)S(1)}, u32[]{:S(2)}, u32[]{:S(2)}) collective-permute-start(bf16[64,2048]{1,0:T(8,128)(2,1)S(1)} %get-tuple-element.77), channel_id=1, source_target_pairs={{0,4},{2,6},{4,0},{6,2},{8,12},{10,14},{12,8},{14,10},{16,20},{18,... | collective-permute-start | bytes 786440 | tf_op jit(solution)/shard_map/ppermute | solution.py:379
  130.9 16.8 %collective-permute-start.27 = (bf16[64,2048]{1,0:T(8,128)(2,1)S(1)}, bf16[64,2048]{1,0:T(8,128)(2,1)S(1)}, u32[]{:S(2)}, u32[]{:S(2)}) collective-permute-start(bf16[64,2048]{1,0:T(8,128)(2,1)S(1)} %get-tuple-element.74), channel_id=1, source_target_pairs={{0,4},{2,6},{4,0},{6,2},{8,12},{10,14},{12,8},{14,10},{16,20},{18,... | collective-permute-start | bytes 786440 | tf_op jit(solution)/shard_map/ppermute | solution.py:379
  137.9 15.4 %collective-permute-start.21 = (bf16[64,2048]{1,0:T(8,128)(2,1)S(1)}, bf16[64,2048]{1,0:T(8,128)(2,1)S(1)}, u32[]{:S(2)}, u32[]{:S(2)}) collective-permute-start(bf16[64,2048]{1,0:T(8,128)(2,1)S(1)} %get-tuple-element.68), channel_id=1, source_target_pairs={{0,2},{2,0},{4,6},{6,4},{8,10},{10,8},{12,14},{14,12},{16,18},{18,... | collective-permute-start | bytes 786440 | tf_op jit(solution)/shard_map/ppermute | solution.py:379
  139.5 13.2 %collective-permute-start.26 = (bf16[64,2048]{1,0:T(8,128)(2,1)S(1)}, bf16[64,2048]{1,0:T(8,128)(2,1)S(1)}, u32[]{:S(2)}, u32[]{:S(2)}) collective-permute-start(bf16[64,2048]{1,0:T(8,128)(2,1)S(1)} %add_rows.12), channel_id=1, source_target_pairs={{0,2},{2,0},{4,6},{6,4},{8,10},{10,8},{12,14},{14,12},{16,18},{18,... | collective-permute-start | bytes 786440 | tf_op jit(solution)/shard_map/ppermute | solution.py:379
  140.2 14.8 %collective-permute-start.23 = (bf16[64,2048]{1,0:T(8,128)(2,1)S(1)}, bf16[64,2048]{1,0:T(8,128)(2,1)S(1)}, u32[]{:S(2)}, u32[]{:S(2)}) collective-permute-start(bf16[64,2048]{1,0:T(8,128)(2,1)S(1)} %add_rows.10), channel_id=1, source_target_pairs={{0,4},{2,6},{4,0},{6,2},{8,12},{10,14},{12,8},{14,10},{16,20},{18,... | collective-permute-start | bytes 786440 | tf_op jit(solution)/shard_map/ppermute | solution.py:379
  140.8 11.8 %collective-permute-start.18 = (bf16[64,2048]{1,0:T(8,128)(2,1)S(1)}, bf16[64,2048]{1,0:T(8,128)(2,1)S(1)}, u32[]{:S(2)}, u32[]{:S(2)}) collective-permute-start(bf16[64,2048]{1,0:T(8,128)(2,1)S(1)} %add_rows.8), channel_id=1, source_target_pairs={{0,4},{2,6},{4,0},{6,2},{8,12},{10,14},{12,8},{14,10},{16,20},{18,... | collective-permute-start | bytes 786440 | tf_op jit(solution)/shard_map/ppermute | solution.py:379
  147.7 10.9 %collective-permute-start.32 = (f32[2,2,8,768]{3,2,1,0:T(8,128)S(1)}, f32[2,2,8,768]{3,2,1,0:T(8,128)S(1)}, u32[]{:S(2)}, u32[]{:S(2)}) collective-permute-start(f32[2,2,8,768]{3,2,1,0:T(8,128)S(1)} %get-tuple-element.86), channel_id=1, source_target_pairs={{0,1},{1,0},{2,3},{3,2},{4,5},{5,4},{6,7},{7,6},{8,9},{9,8},{10,11... | collective-permute-start | bytes 294920 | tf_op jit(solution)/shard_map/ppermute | solution.py:382
  152.6 5.9 %collective-permute-start.33 = (f32[2,6,1024]{2,1,0:T(8,128)S(1)}, f32[2,6,1024]{2,1,0:T(8,128)S(1)}, u32[]{:S(2)}, u32[]{:S(2)}) collective-permute-start(f32[2,6,1024]{2,1,0:T(8,128)S(1)} %get-tuple-element.88), channel_id=1, source_target_pairs={{0,1},{1,0},{2,3},{3,2},{4,5},{5,4},{6,7},{7,6},{8,9},{9,8},{10,11... | collective-permute-start | bytes 147464 | tf_op jit(solution)/shard_map/ppermute | solution.py:382
  152.7 14.5 %collective-permute-start.20 = (bf16[64,2048]{1,0:T(8,128)(2,1)S(1)}, bf16[64,2048]{1,0:T(8,128)(2,1)S(1)}, u32[]{:S(2)}, u32[]{:S(2)}) collective-permute-start(bf16[64,2048]{1,0:T(8,128)(2,1)S(1)} %get-tuple-element.66), channel_id=1, source_target_pairs={{0,4},{2,6},{4,0},{6,2},{8,12},{10,14},{12,8},{14,10},{16,20},{18,... | collective-permute-start | bytes 786440 | tf_op jit(solution)/shard_map/ppermute | solution.py:379
  153.3 14.0 %collective-permute-start.31 = (bf16[64,2048]{1,0:T(8,128)(2,1)S(1)}, bf16[64,2048]{1,0:T(8,128)(2,1)S(1)}, u32[]{:S(2)}, u32[]{:S(2)}) collective-permute-start(bf16[64,2048]{1,0:T(8,128)(2,1)S(1)} %add_rows.14), channel_id=1, source_target_pairs={{0,8},{2,10},{4,12},{6,14},{8,0},{10,2},{12,4},{14,6},{16,24},{18,... | collective-permute-start | bytes 786440 | tf_op jit(solution)/shard_map/ppermute | solution.py:379
  155.0 16.2 %collective-permute-start.28 = (bf16[64,2048]{1,0:T(8,128)(2,1)S(1)}, bf16[64,2048]{1,0:T(8,128)(2,1)S(1)}, u32[]{:S(2)}, u32[]{:S(2)}) collective-permute-start(bf16[64,2048]{1,0:T(8,128)(2,1)S(1)} %add_rows.13), channel_id=1, source_target_pairs={{0,24},{2,26},{4,28},{6,30},{8,16},{10,18},{12,20},{14,22},{16,8},... | collective-permute-start | bytes 786440 | tf_op jit(solution)/shard_map/ppermute | solution.py:379
  158.4 23.2 %collective-permute-start.24 = (bf16[64,2048]{1,0:T(8,128)(2,1)S(1)}, bf16[64,2048]{1,0:T(8,128)(2,1)S(1)}, u32[]{:S(2)}, u32[]{:S(2)}) collective-permute-start(bf16[64,2048]{1,0:T(8,128)(2,1)S(1)} %add_rows.11), channel_id=1, source_target_pairs={{0,16},{2,18},{4,20},{6,22},{8,24},{10,26},{12,28},{14,30},{16,0},... | collective-permute-start | bytes 786440 | tf_op jit(solution)/shard_map/ppermute | solution.py:379
  158.6 23.1 %collective-permute-start.19 = (bf16[64,2048]{1,0:T(8,128)(2,1)S(1)}, bf16[64,2048]{1,0:T(8,128)(2,1)S(1)}, u32[]{:S(2)}, u32[]{:S(2)}) collective-permute-start(bf16[64,2048]{1,0:T(8,128)(2,1)S(1)} %add_rows.9), channel_id=1, source_target_pairs={{0,2},{2,0},{4,6},{6,4},{8,10},{10,8},{12,14},{14,12},{16,18},{18,... | collective-permute-start | bytes 786440 | tf_op jit(solution)/shard_map/ppermute | solution.py:379
  160.1 5.4 %copy-start.3 = (f32[1,2,2,16,768]{4,3,2,1,0:T(8,128)S(1)}, f32[1,2,2,16,768]{4,3,2,1,0:T(8,128)}, u32[]{:S(2)}) copy-start(f32[1,2,2,16,768]{4,3,2,1,0:T(8,128)} %param.16) | copy-start | bytes 589828
  160.1 5.4 %copy-start.5 = (f32[1,2,2,16,768]{4,3,2,1,0:T(8,128)S(1)}, f32[1,2,2,16,768]{4,3,2,1,0:T(8,128)}, u32[]{:S(2)}) copy-start(f32[1,2,2,16,768]{4,3,2,1,0:T(8,128)} %param.17) | copy-start | bytes 589828
  160.1 5.4 %copy-start.7 = (f32[1,2,6,2048]{3,1,2,0:T(2,128)S(1)}, f32[1,2,6,2048]{3,1,2,0:T(2,128)}, u32[]{:S(2)}) copy-start(f32[1,2,6,2048]{3,1,2,0:T(2,128)} %param.18) | copy-start | bytes 294916
  160.1 5.4 %copy-start.9 = (f32[1,2,6,2048]{3,1,2,0:T(2,128)S(1)}, f32[1,2,6,2048]{3,1,2,0:T(2,128)}, u32[]{:S(2)}) copy-start(f32[1,2,6,2048]{3,1,2,0:T(2,128)} %param.19) | copy-start | bytes 294916
where the time goes:
time: 183 us
  waiting for transfers between devices  78.9 us (43%)
  Pallas kernels  52.3 us (29%)
  starting transfers between devices  40.8 us (22%)
  local copies, waits for them, and re-layouts  9.73 us (5%)
    ppermute x30, waiting for transfers between devices, swap(): lax.ppermute(array, 'expert', [(i, i ^ mask) for i in range(experts)])  78.8 us
    pallas_call x19, Pallas kernels, run(): pl.pallas_call(wrapped, in_specs=[INSIDE] * count + [ANYWHERE] * len(afte...  52.3 us
    ppermute x30, starting transfers between devices, swap(): lax.ppermute(array, 'expert', [(i, i ^ mask) for i in range(experts)])  40.1 us
    unnamed x28, local copies, waits for them, and re-layouts  9.73 us
  transfers between devices with their start and end apart: 34, of which 9 were waited for; matrix products, arithmetic and copies ran while one was open for 0% of the time, Pallas kernels for 27%

commit v1 on v0

--- a/solution.py
+++ b/solution.py
@@ -70,7 +70,8 @@
     def out(self, shape, dtype):
         return pltpu.VMEM(shape, dtype) if self.keep else jax.ShapeDtypeStruct(shape, dtype)
 
-    def run(self, kernel, name, inputs, outputs, after=(), alias=None, limit=LIMIT, flops=0, free=()):
+    def run(self, kernel, name, inputs, outputs, after=(), alias=None, limit=LIMIT, raw=(), free=()):
+        inputs = [*raw, *map(self.pin, inputs)]
         count = len(inputs)
 
         def wrapped(*refs):
@@ -86,9 +87,9 @@
             ],
             input_output_aliases=alias or {},
             compiler_params=pltpu.CompilerParams(vmem_limit_bytes=limit),
-            cost_estimate=pl.CostEstimate(flops=flops, bytes_accessed=10**6, transcendentals=0),
+            cost_estimate=pl.CostEstimate(flops=0, bytes_accessed=0, transcendentals=0),
             name=name,
-        )(*[self.pin(a) for a in inputs], *after)
+        )(*inputs, *after)
 
 
 def pack_kernel(experts, token_ref, grad_ref, ids_ref, weights_ref, out_ref):
@@ -112,7 +113,7 @@
     out_ref[:, 2 * width :] = dot_tn(split, same.astype(F32).astype(BF16)).astype(BF16)
 
 
-def weight_kernel(codes_in, codes_out, clip_in, range_in, clip_out, range_out, gu_ref, d_ref):
+def weight_kernel(codes_in, codes_out, clip_in, range_in, clip_out, range_out, w_ref):
     dp = lax.axis_index("dp")
     depth, third = codes_in.shape[1:]
     hidden = clip_in.shape[3]
@@ -128,7 +129,7 @@
             for j in range(PACK):
                 code = jnp.bitwise_and(jnp.right_shift(packed, 4 * j), 15).astype(F32)
                 cols = slice(j * third, (j + 1) * third)
-                gu_ref[p, g * GROUP : (g + 1) * GROUP, cols] = (
+                w_ref[p, g * GROUP : (g + 1) * GROUP, cols] = (
                     ends[g : g + 1, cols] * code - ends[groups + g : groups + g + 1, cols]
                 ).astype(BF16)
     own = pl.ds(pl.multiple_of(dp * depth, depth), depth)
@@ -150,15 +151,18 @@
                 step_rows = jnp.where(late, step[g], step_rows)
                 lower_rows = jnp.where(late, lower[g], lower_rows)
             code = jnp.bitwise_and(jnp.right_shift(packed, 4 * j), 15).astype(F32)
-            d_ref[j * third + start : j * third + start + CHUNK, :] = (
-                step_rows * code - lower_rows
-            ).astype(BF16)
-
-
-def set_kernel(experts, first, *refs):
+            down = (step_rows * code - lower_rows).astype(BF16)
+            for q in range(depth // third):
+                w_ref[2, q * third + start : q * third + start + CHUNK, j * third : (j + 1) * third] = down[
+                    :, q * third : (q + 1) * third
+                ]
+
+
+def set_kernel(experts, first, keep, *refs):
     blocks = refs[0:4]
-    gu_sides, d_sides = refs[4:6], refs[6:8]
-    refs = refs[8:] if first == 0 else refs[12:]
+    sides = refs[4:6]
+    earlier = refs[6:10]
+    refs = refs[6:] if first == 0 else refs[10:]
     partials = refs[0:4]
     x_ref, s_ref, h_ref, g_ref = refs[4:8]
     rows, width = partials[0].shape
@@ -171,6 +175,9 @@
         pl.ds(pl.multiple_of((1 - dp) * half, half), half),
     )
     here = slice(first, first + 4 * rows)
+    if first and not keep:
+        for old, new in zip(earlier, refs[4:8]):
+            new[..., :first, :] = old[..., :first, :]
     for i in range(4):
         span = slice(first + i * rows, first + (i + 1) * rows)
         x_ref[span, :] = blocks[i][:, :width]
@@ -181,15 +188,19 @@
         s_ref[span, :] = (scale * blocks[i][:, width : 2 * width].astype(F32)).astype(BF16)
     for j in range(PACK):
         cols = slice(j * third, (j + 1) * third)
-        gate_pre = dot_nn(x_ref[here, spans[0]], gu_sides[0][0, :, cols]) + dot_nn(
-            x_ref[here, spans[1]], gu_sides[1][0, :, cols]
-        )
-        up_pre = dot_nn(x_ref[here, spans[0]], gu_sides[0][1, :, cols]) + dot_nn(
-            x_ref[here, spans[1]], gu_sides[1][1, :, cols]
-        )
-        grad_hidden = dot_nt(s_ref[here, spans[0]], d_sides[0][cols, :]) + dot_nt(
-            s_ref[here, spans[1]], d_sides[1][cols, :]
-        )
+        gate_pre = dot_nn(x_ref[here, spans[0]], sides[0][0, :, cols]) + dot_nn(
+            x_ref[here, spans[1]], sides[1][0, :, cols]
+        )
+        up_pre = dot_nn(x_ref[here, spans[0]], sides[0][1, :, cols]) + dot_nn(
+            x_ref[here, spans[1]], sides[1][1, :, cols]
+        )
+        grad_hidden = 0.0
+        for side in range(2):
+            for q in range(half // third):
+                tile = pl.ds(pl.multiple_of((dp if side == 0 else 1 - dp) * half + q * third, third), third)
+                grad_hidden = grad_hidden + dot_nt(
+                    s_ref[here, tile], sides[side][2, q * third : (q + 1) * third, cols]
+                )
         sig = sigmoid(gate_pre)
         act = gate_pre * sig
         h_ref[here, cols] = (act * up_pre).astype(BF16)
@@ -201,27 +212,26 @@
         @pl.loop(0, half // TILE)
         def _(n):
             depth = pl.ds(pl.multiple_of(n * TILE, TILE), TILE)
-            part = dot_nt(g_ref[0, here, :], gu_sides[side][0, depth, :]) + dot_nt(
-                g_ref[1, here, :], gu_sides[side][1, depth, :]
+            part = dot_nt(g_ref[0, here, :], sides[side][0, depth, :]) + dot_nt(
+                g_ref[1, here, :], sides[side][1, depth, :]
             )
             cols = pl.ds(pl.multiple_of(base + n * TILE, TILE), TILE)
             for i in range(4):
                 partials[i][:, cols] = part[i * rows : (i + 1) * rows, :].astype(BF16)
 
 
-def run_set(calls, blocks, weights, experts, pair, after):
-    rows, width = blocks[0].shape[0], 2 * weights[2].shape[1]
-    hidden = weights[2].shape[0]
+def run_set(calls, blocks, weights, experts, pair=None, after=()):
+    rows, width = blocks[0].shape[0], 2 * weights[0].shape[1]
+    hidden = weights[0].shape[2]
     both = 8 * rows
     stored = [((both, width), BF16), ((both, width), BF16), ((both, hidden), BF16), ((2, both, hidden), BF16)]
     out = calls.run(
-        functools.partial(set_kernel, experts, 0 if pair is None else 4 * rows),
+        functools.partial(set_kernel, experts, 0 if pair is None else 4 * rows, calls.keep),
         "expert_set",
         [*blocks, *weights, *(pair or ())],
         [((rows, width), BF16)] * 4 + stored,
         after=after,
-        alias=None if pair is None else {8 + i: 4 + i for i in range(4)},
-        flops=40 * rows * width * hidden,
+        alias=None if pair is None else {6 + i: 4 + i for i in range(4)},
     )
     return list(out[:4]), list(out[4:])
 
@@ -243,7 +253,7 @@
     return high, (a - high.astype(F32)).astype(BF16)
 
 
-def sums_kernel(other, more, x_ref, s_ref, h_ref, g_ref, weights_in, weights_out, *refs):
+def sums_kernel(other, more, x_ref, s_ref, h_ref, g_ref, weights, *refs):
     old_in, old_out = refs[:2] if more else (None, None)
     sums_in, sums_out = refs[-2:]
     width = x_ref.shape[1]
@@ -267,18 +277,19 @@
     found = dot_tn(hidden_sums[0], s_ref[:, span]) + dot_tn(hidden_sums[1], s_ref[:, span])
     sums_out[1] = since(old_out, found, 1)
 
-    @pl.loop(0, half // TILE)
+    @pl.loop(0, half // third)
     def _(t):
-        rows = pl.ds(pl.multiple_of(t * TILE, TILE), TILE)
-        span = pl.ds(pl.multiple_of(base + t * TILE, TILE), TILE)
+        rows = pl.ds(pl.multiple_of(t * third, third), third)
+        span = pl.ds(pl.multiple_of(base + t * third, third), third)
         x_cols = x_ref[:, span]
         for p in range(2):
-            weighted = dot_tn(x_cols, g_ref[p]) * weights_in[p, rows, :].astype(F32)
-            for g in range(TILE // GROUP):
-                spot = pl.ds(t * (TILE // GROUP) + g, 1)
+            weighted = dot_tn(x_cols, g_ref[p]) * weights[p, rows, :].astype(F32)
+            for g in range(third // GROUP):
+                spot = pl.ds(t * (third // GROUP) + g, 1)
                 found = jnp.sum(weighted[g * GROUP : (g + 1) * GROUP], axis=0, keepdims=True)
                 sums_in[p, 0, spot, :] = since(old_in, found, p, 0, spot, slice(None))
-        weighted = dot_tn(h_ref[...], s_ref[:, span]) * weights_out[:, rows].astype(F32)
+        down = jnp.concatenate([weights[2, rows, j * third : (j + 1) * third] for j in range(PACK)], axis=0)
+        weighted = dot_tn(h_ref[...], s_ref[:, span]) * down.astype(F32)
         for g in range(groups_out):
             found = None
             for j in range(PACK):
@@ -295,21 +306,18 @@
             sums_out[0, g : g + 1, rows] = since(old_out, found, 0, slice(g, g + 1), rows)
 
 
-def run_sums(calls, stored, weights, other, before, shapes, after):
-    both, width = stored[0].shape
-    hidden = stored[2].shape[1]
-    side = weights[1::2] if other else weights[0::2]
+def run_sums(calls, stored, weights, other, before, shapes, after=()):
+    side = weights[1] if other else weights[0]
     return calls.run(
         functools.partial(sums_kernel, other, before is not None),
         "group_sums",
-        [*stored, *side, *(before or ())],
+        [*stored, side, *(before or ())],
         [(shape, F32) for shape in shapes],
         after=after,
-        flops=3 * both * width * hidden,
     )
 
 
-def clip_kernel(mine_in, got_in, mine_out, got_out, clip_in, range_in, clip_out, range_out, in_ref, out_ref):
+def clip_kernel(clip_in, range_in, clip_out, range_out, mine_in, got_in, mine_out, got_out, in_ref, out_ref):
     dp = lax.axis_index("dp")
     hidden = clip_in.shape[3]
     groups = in_ref.shape[2]
@@ -353,6 +361,10 @@
     for ref in refs[1:-1]:
         total = total + ref[...].astype(F32)
     refs[-1][...] = total.astype(refs[-1].dtype)
+
+
+def hold_kernel(*refs):
+    pass
 
 
 def body(
@@ -372,7 +384,6 @@
     hidden = clip_in.shape[4]
     depth = codes_in.shape[2]
     extra = -(-3 * experts // 128) * 128
-    sets = experts // 4
     calls = Calls(experts * rows * (3 * width + extra) * 2 < 2**24)
 
     def swap(array, mask):
@@ -386,69 +397,86 @@
             add_kernel, "add_rows", list(parts), [(parts[0].shape, BF16)], after=after, limit=SMALL, free=free
         )[0]
 
+    def held(array, *after):
+        return pl.pallas_call(
+            hold_kernel,
+            in_specs=[ANYWHERE] * (1 + len(after)),
+            out_specs=ANYWHERE,
+            out_shape=calls.out(array.shape, array.dtype),
+            input_output_aliases={0: 0},
+            name="hold",
+        )(calls.pin(array), *after)
+
     packed = calls.run(
         functools.partial(pack_kernel, experts),
         "pack_rows",
-        [tokens, grad_out, expert_ids.T, router_weights.T],
+        [],
         [((rows, 2 * width + extra), BF16)],
+        raw=(tokens, grad_out, expert_ids.T, router_weights.T),
         limit=SMALL,
     )[0]
 
-    order = [0] + [r for r in range(sets) if r % 4 > 1] + [r for r in range(1, sets) if r % 4 < 2]
-    blocks, heads = {}, {0: packed}
-    for r in order:
-        if r not in heads:
-            heads[r] = swap(packed, 4 * r) if r % 2 == 0 or r == 1 else swap(heads[r - 1], 4)
-        own = heads[r]
-        over_x, over_y = swap(own, 1), swap(own, 2)
-        if r % 2 == 1:
-            diagonal = swap(blocks[r - 1][3], 4)
-        elif r % 4 == 0:
-            diagonal = swap(over_x, 2)
-        else:
-            diagonal = swap(over_y, 1)
-        blocks[r] = (own, over_x, over_y, diagonal)
-
     clips = (clip_in[0], range_in[0], clip_out[0].transpose(1, 0, 2), range_out[0].transpose(1, 0, 2))
-    gu_mine, d_mine = calls.run(
+    (own_weights,) = calls.run(
         weight_kernel,
         "make_weights",
-        [codes_in[0], codes_out[0], *clips],
-        [((2, depth, hidden), BF16), ((hidden, depth), BF16)],
-        after=(blocks[0][1],),
+        [],
+        [((3, depth, hidden), BF16)],
+        raw=(codes_in[0], codes_out[0], *clips),
+        after=(packed,),
     )
-    weights = (gu_mine, swap_core(gu_mine), d_mine, swap_core(d_mine))
+    weights = (own_weights, swap_core(own_weights))
 
     shapes = ((2, 2, depth // GROUP, hidden), (2, clip_out.shape[2], depth))
-    partials, sums, after = {}, {True: None, False: None}, ()
-    for first, second in zip(order[0::2], order[1::2]):
-        partials[first], stored = run_set(calls, blocks[first], weights, experts, None, after)
-        partials[second], stored = run_set(calls, blocks[second], weights, experts, stored, ())
-        for other in (True, False):
-            sums[other] = run_sums(calls, stored, weights, other, sums[other], shapes, ())
+    sums = {True: None, False: None}
+
+    def quad(head, after):
+        near, far = swap(head, 4), swap(head, 8)
+        x0, y0 = swap(head, 1), swap(head, 2)
+        d0 = swap(x0, 2)
+        last = swap(far, 4)
+        ready = held(far, weights[1], x0, y0, d0, near)
+        x2, y2 = swap(ready, 1), swap(ready, 2)
+        d2 = swap(y2, 1)
+        d1, d3 = swap(d0, 4), swap(d2, 4)
+        p0, stored = run_set(calls, (head, x0, y0, d0), weights, experts, after=after)
+        y3 = swap(held(last, x2, y2), 2)
+        x3 = swap(held(last, d2, p0[0]), 1)
+        p2, stored = run_set(calls, (far, x2, y2, d2), weights, experts, stored)
+        other = run_sums(calls, stored, weights, True, sums[True], shapes)
+        y1 = swap(held(near, y3), 2)
+        x1 = swap(held(near, x3, p2[0]), 1)
+        p3, later = run_set(calls, (last, x3, y3, d3), weights, experts, after=(other[0],))
+        x_sum0 = added(p0[1], swap(p0[3], 2))
+        x_sum2 = added(p2[1], swap(p2[3], 2))
+        mine = run_sums(calls, stored, weights, False, sums[False], shapes, (p3[0],))
+        p1, later = run_set(
+            calls, (near, x1, y1, d1), weights, experts, later, (x_sum0, x_sum2, mine[0])
+        )
+        x_sum3 = added(p3[1], swap(p3[3], 2))
+        sums[True] = run_sums(calls, later, weights, True, other, shapes, (x_sum3,))
+        total3 = added(p3[0], swap(x_sum3, 1), swap(p3[2], 2))
+        sums[False] = run_sums(calls, later, weights, False, mine, shapes, (total3,))
+        y_sum1 = added(p1[2], swap(p1[3], 1))
+        total1 = added(p1[0], swap(p1[1], 1), swap(y_sum1, 2))
+        total2 = added(p2[0], swap(x_sum2, 1), swap(p2[2], 2), swap(total3, 4))
+        return p0[0], swap(x_sum0, 1), swap(p0[2], 2), swap(total1, 4), swap(total2, 8)
+
+    final, after = [], ()
+    for base in range(0, experts, 16):
+        parts = quad(swap(packed, base) if base else packed, after)
+        final += [swap(added(*parts), base)] if base else parts
         after = (sums[False][0],)
-
-    final = []
-    for r in order[1:]:
-        own, p_x, p_y, p_d = partials[r]
-        if r == 1:
-            partials[0][3] = added(partials[0][3], swap(p_d, 4))
-        elif r % 4 in (0, 3):
-            p_x = added(p_x, swap(p_d, 2))
-        else:
-            p_y = added(p_y, swap(p_d, 1))
-        final.append(swap(added(own, swap(p_x, 1), swap(p_y, 2)), 4 * r))
-    own, p_x, p_y, p_d = partials[0]
-    p_x = added(p_x, swap(p_d, 2))
-    grad_tokens = added(own, swap(p_x, 1), swap(p_y, 2), *final, free=(0,))
+    grad_tokens = added(*final, free=(0,))
 
     mine_in, mine_out = sums[False]
     got_in, got_out = (swap_core(a) for a in sums[True])
     grad_in, grad_clip_out = calls.run(
         clip_kernel,
         "clip_gradients",
-        [mine_in, got_in, mine_out, got_out, *clips],
+        [mine_in, got_in, mine_out, got_out],
         [((2, 2, depth // GROUP, hidden), F32), ((clip_out.shape[2], 2, depth), F32)],
+        raw=clips,
         limit=SMALL,
         free=(0, 1),
     )

time: 183 us -> 199 us (1.087)
  local copies, waits for them, and re-layouts: 9.73 us -> 51 us
  waiting for transfers between devices: 78.9 us -> 41.6 us
  Pallas kernels: 52.3 us -> 67.8 us
  starting transfers between devices: 40.8 us -> 36.8 us
    unnamed x28 -> x127, local copies, waits for them, and re-layouts: 9.73 us -> 51 us
    ppermute x30, waiting for transfers between devices: 78.8 us -> 40.4 us  [swap(): lax.ppermute(array, 'expert', [(i, i ^ mask) for i in range(experts)])]
    pallas_call x19, Pallas kernels: 52.3 us -> 67.8 us  [run(): pl.pallas_call(wrapped, in_specs=[INSIDE] * count + [ANYWHERE] * len(afte...]
    ppermute x30, starting transfers between devices: 40.1 us -> 36.1 us  [swap(): lax.ppermute(array, 'expert', [(i, i ^ mask) for i in range(experts)])]
  transfers between devices with their start and end apart: 34 -> 33, of which waited for: 9 -> 11; matrix products, arithmetic and copies ran while one was open for 0% -> 3% of each run, Pallas kernels for 27% -> 32%
where the time goes in v1:
time: 199 us; the launch traced here: 198 us
  Pallas kernels  67.8 us (34%)
  local copies, waits for them, and re-layouts  51 us (26%)
  waiting for transfers between devices  41.6 us (21%)
  starting transfers between devices  36.8 us (18%)
    pallas_call x19, Pallas kernels, run(): pl.pallas_call(wrapped, in_specs=[INSIDE] * count + [ANYWHERE] * len(afte...  67.8 us
    unnamed x127, local copies, waits for them, and re-layouts  51 us
    ppermute x30, waiting for transfers between devices, swap(): lax.ppermute(array, 'expert', [(i, i ^ mask) for i in range(experts)])  40.4 us
    ppermute x30, starting transfers between devices, swap(): lax.ppermute(array, 'expert', [(i, i ^ mask) for i in range(experts)])  36.1 us
  transfers between devices with their start and end apart: 33, of which 11 were waited for; matrix products, arithmetic and copies ran while one was open for 3% of the time, Pallas kernels for 32%

profile of v1, /device:TPU:0, one launch (start us, length us, event | category | flops | bytes accessed | tf_op | source)
XLA Modules:
  0.0 198.3 jit_solution(14335363326751267089)
XLA Ops:
  0.6 0.9 copy-done.49
  1.6 0.9 copy-done.50
  4.1 1.6 copy-done.33
  5.7 1.2 copy-done.34
  6.9 0.9 copy-done.39
  7.9 0.9 copy-done.41
  8.8 0.9 copy-done.43
  9.7 0.9 copy-done.45
  10.6 2.6 %make_weights.1.refs_4_ = bf16[3,1024,768]{2,1,0:T(8,128)(2,1)S(1)} custom-call(s32[2,1024,256]{2,1,0:T(8,128)S(1)} %bitcast.18, s32[256,1024]{1,0:T(8,128)S(1)} %bitcast.19, f32[2,2,16,768]{3,2,1,0:T(8,128)S(1)} %bitcast.20, f32[2,2,16,768]{3,2,1,0:T(8,128)S(1)} %bitcast.22, f32[6,2,2048]{2,1,0:T(2,128)S(1)} %bitcast.24, f32[6,2,2048]{2,1,0:T(2,128)S(1)} %bitcast.26, ...), custom_call_target="tpu_custom_call" | custom-call | tf_op jit(solution)/shard_map/make_weights/pallas_call | solution.py:80
  13.7 2.2 %copy-done = bf16[3,1024,768]{2,1,0:T(8,128)(2,1)} copy-done((bf16[3,1024,768]{2,1,0:T(8,128)(2,1)}, bf16[3,1024,768]{2,1,0:T(8,128)(2,1)S(1)}, u32[]{:S(2)}) %copy-start) | copy-done | bytes 4718616
  15.8 2.5 %collective-permute-start = (bf16[64,4224]{1,0:T(8,128)(2,1)S(1)}, bf16[64,4224]{1,0:T(8,128)(2,1)S(1)}, u32[]{:S(2)}, u32[]{:S(2)}) collective-permute-start(bf16[64,4224]{1,0:T(8,128)(2,1)S(1)} %pack_rows.1.refs_6_.refs_0_), channel_id=1, source_target_pairs={{0,2},{2,0},{4,6},{6,4},{8,10},{10,8},{12,14},{14,12},{16,18},{18,... | collective-permute-start | bytes 1622024 | tf_op jit(solution)/shard_map/ppermute | solution.py:390
  18.3 2.6 %collective-permute-start.8 = (bf16[64,4224]{1,0:T(8,128)(2,1)S(1)}, bf16[64,4224]{1,0:T(8,128)(2,1)S(1)}, u32[]{:S(2)}, u32[]{:S(2)}) collective-permute-start(bf16[64,4224]{1,0:T(8,128)(2,1)S(1)} %pack_rows.1.refs_6_.refs_0_), channel_id=1, source_target_pairs={{0,16},{2,18},{4,20},{6,22},{8,24},{10,26},{12,28},{14,30},{16,0},... | collective-permute-start | bytes 1622024 | tf_op jit(solution)/shard_map/ppermute | solution.py:390
  20.9 1.5 collective-permute-start.1
  22.4 1.6 collective-permute-start.7
  24.0 7.2 %collective-permute-done.refs_1_.refs_2_ = bf16[64,4224]{1,0:T(8,128)(2,1)S(1)} collective-permute-done((bf16[64,4224]{1,0:T(8,128)(2,1)S(1)}, bf16[64,4224]{1,0:T(8,128)(2,1)S(1)}, u32[]{:S(2)}, u32[]{:S(2)}) %collective-permute-start) | collective-permute-done | bytes 540704 | tf_op jit(solution)/shard_map/ppermute | solution.py:390
  31.3 1.8 collective-permute-start.2
  33.0 12.3 %collective-permute-done.8.refs_0_ = bf16[64,4224]{1,0:T(8,128)(2,1)S(1)} collective-permute-done((bf16[64,4224]{1,0:T(8,128)(2,1)S(1)}, bf16[64,4224]{1,0:T(8,128)(2,1)S(1)}, u32[]{:S(2)}, u32[]{:S(2)}) %collective-permute-start.8) | collective-permute-done | bytes 540704 | tf_op jit(solution)/shard_map/ppermute | solution.py:390
  47.8 1.5 collective-permute-start.10
  49.3 1.2 collective-permute-start.9
  51.1 10.5 %collective-permute-done.10.refs_2_ = bf16[64,4224]{1,0:T(8,128)(2,1)} collective-permute-done((bf16[64,4224]{1,0:T(8,128)(2,1)}, bf16[64,4224]{1,0:T(8,128)(2,1)}, u32[]{:S(2)}, u32[]{:S(2)}) %collective-permute-start.10) | collective-permute-done | bytes 540704 | tf_op jit(solution)/shard_map/ppermute | solution.py:390
  63.4 1.2 collective-permute-done.13.refs_1_
  66.2 2.3 %copy-done.1 = bf16[3,1024,768]{2,1,0:T(8,128)(2,1)S(1)} copy-done((bf16[3,1024,768]{2,1,0:T(8,128)(2,1)S(1)}, bf16[3,1024,768]{2,1,0:T(8,128)(2,1)}, u32[]{:S(2)}) %copy-start.1) | copy-done | bytes 4718616
  68.6 1.0 copy-done.28
  69.6 1.0 copy-done.30
  70.7 1.0 copy-done.32
  71.7 8.6 %expert_set.4 = (bf16[64,2048]{1,0:T(8,128)(2,1)S(1)}, bf16[64,2048]{1,0:T(8,128)(2,1)S(1)}, bf16[64,2048]{1,0:T(8,128)(2,1)S(1)}, bf16[64,2048]{1,0:T(8,128)(2,...) custom-call(bf16[64,4224]{1,0:T(8,128)(2,1)S(1)} %pack_rows.1.refs_6, ...), custom_call_target="tpu_custom_call" | custom-call | tf_op jit(solution)/shard_map/expert_set/pallas_call | solution.py:80
  80.3 1.3 copy-done.3
  81.7 1.2 copy-done.8
  82.9 0.9 copy-done.15
  85.8 1.4 collective-permute-start.12
  87.3 1.3 collective-permute-start.18
  88.6 1.9 copy.32.refs_0_
  90.4 1.9 copy.34.refs_0_
  93.7 2.3 %copy-done.2 = bf16[3,1024,768]{2,1,0:T(8,128)(2,1)S(1)} copy-done((bf16[3,1024,768]{2,1,0:T(8,128)(2,1)S(1)}, bf16[3,1024,768]{2,1,0:T(8,128)(2,1)}, u32[]{:S(2)}) %copy-start.2) | copy-done | bytes 4718616
  96.0 1.6 copy-done.4
  97.6 1.4 copy-done.9
  99.0 1.1 copy-done.16
  100.2 1.0 copy-done.23
  101.2 1.0 copy-done.25
  102.3 8.8 %expert_set.5 = (bf16[64,2048]{1,0:T(8,128)(2,1)S(1)}, bf16[64,2048]{1,0:T(8,128)(2,1)S(1)}, bf16[64,2048]{1,0:T(8,128)(2,1)S(1)}, bf16[64,2048]{1,0:T(8,128)(2,...) custom-call(bf16[64,4224]{1,0:T(8,128)(2,1)S(1)} %copy-done.23, ...), custom_call_target="tpu_custom_call", output_to_operand_aliasing={{4}: (6, {}), {5}: (7, {}), {6}: (8, {}), {7}: (9, {})} | custom-call | tf_op jit(solution)/shard_map/expert_set/pallas_call | solution.py:80
  111.1 1.3 copy-done.5
  112.4 1.1 copy-done.10
  117.3 2.1 %collective-permute-start.14 = (bf16[64,4224]{1,0:T(8,128)(2,1)S(1)}, bf16[64,4224]{1,0:T(8,128)(2,1)S(1)}, u32[]{:S(2)}, u32[]{:S(2)}) collective-permute-start(bf16[64,4224]{1,0:T(8,128)(2,1)S(1)} %hold.7), channel_id=1, source_target_pairs={{0,2},{2,0},{4,6},{6,4},{8,10},{10,8},{12,14},{14,12},{16,18},{18,... | collective-permute-start | bytes 1622024 | tf_op jit(solution)/shard_map/ppermute | solution.py:390
  119.4 2.0 %collective-permute-start.19 = (bf16[64,2048]{1,0:T(8,128)(2,1)}, bf16[64,2048]{1,0:T(8,128)(2,1)S(1)}, u32[]{:S(2)}, u32[]{:S(2)}) collective-permute-start(bf16[64,2048]{1,0:T(8,128)(2,1)} %copy-done.58), channel_id=1, source_target_pairs={{0,4},{2,6},{4,0},{6,2},{8,12},{10,14},{12,8},{14,10},{16,20},{18,... | collective-permute-start | bytes 786440 | tf_op jit(solution)/shard_map/ppermute | solution.py:390
  121.4 1.6 copy-done.6
  123.0 1.4 copy-done.11
  124.4 1.1 copy-done.18
  125.5 7.9 %group_sums.4 = (f32[2,2,8,768]{3,2,1,0:T(8,128)S(1)}, f32[2,6,1024]{2,1,0:T(8,128)S(1)}) custom-call(bf16[512,2048]{1,0:T(8,128)(2,1)S(1)} %get-tuple-element.54.refs_0_, bf16[512,2048]{1,0:T(8,128)(2,1)S(1)} %copy-done.6, bf16[512,768]{1,0:T(8,128)(2,1)S(1)} %copy-done.18, bf16[2,512,768]{2,1,0:T(8,128)(2,1)S(1)} %copy-done.11, ...), custom_call_target="tpu_custom_call" | custom-call | tf_op jit(solution)/shard_map/group_sums/pallas_call | solution.py:80
  133.5 9.1 %expert_set.6 = (bf16[64,2048]{1,0:T(8,128)(2,1)S(1)}, bf16[64,2048]{1,0:T(8,128)(2,1)S(1)}, bf16[64,2048]{1,0:T(8,128)(2,1)S(1)}, bf16[64,2048]{1,0:T(8,128)(2,...) custom-call(bf16[64,4224]{1,0:T(8,128)(2,1)S(1)} %copy-done.21, ...), custom_call_target="tpu_custom_call" | custom-call | tf_op jit(solution)/shard_map/expert_set/pallas_call | solution.py:80
  142.8 1.1 copy-done.12
  144.0 5.6 %group_sums.5 = (f32[2,2,8,768]{3,2,1,0:T(8,128)S(1)}, f32[2,6,1024]{2,1,0:T(8,128)S(1)}) custom-call(bf16[512,2048]{1,0:T(8,128)(2,1)S(1)} %get-tuple-element.54.refs_0_, bf16[512,2048]{1,0:T(8,128)(2,1)S(1)} %copy-done.7, bf16[512,768]{1,0:T(8,128)(2,1)S(1)} %copy-done.19, bf16[2,512,768]{2,1,0:T(8,128)(2,1)S(1)} %copy-done.12, ...), custom_call_target="tpu_custom_call" | custom-call | tf_op jit(solution)/shard_map/group_sums/pallas_call | solution.py:80
  149.6 1.0 collective-permute-start.28
  151.3 8.8 %expert_set.7 = (bf16[64,2048]{1,0:T(8,128)(2,1)S(1)}, bf16[64,2048]{1,0:T(8,128)(2,1)S(1)}, bf16[64,2048]{1,0:T(8,128)(2,1)S(1)}, bf16[64,2048]{1,0:T(8,128)(2,...) custom-call(bf16[64,4224]{1,0:T(8,128)(2,1)S(1)} %copy-done.14, ...), custom_call_target="tpu_custom_call", output_to_operand_aliasing={{4}: (6, {}), {5}: (7, {}), {6}: (8, {}), {7}: (9, {})} | custom-call | tf_op jit(solution)/shard_map/expert_set/pallas_call | solution.py:80
  160.1 1.9 collective-permute-start.21
  163.2 1.3 collective-permute-start.29
  165.1 4.3 %collective-permute-done.21.refs_1_ = bf16[64,2048]{1,0:T(8,128)(2,1)S(1)} collective-permute-done((bf16[64,2048]{1,0:T(8,128)(2,1)S(1)}, bf16[64,2048]{1,0:T(8,128)(2,1)S(1)}, u32[]{:S(2)}, u32[]{:S(2)}) %collective-permute-start.21) | collective-permute-done | bytes 262176 | tf_op jit(solution)/shard_map/ppermute | solution.py:390
  169.5 1.0 collective-permute-start.22
  172.0 2.9 %collective-permute-done.24.refs_1_ = bf16[64,2048]{1,0:T(8,128)(2,1)S(1)} collective-permute-done((bf16[64,2048]{1,0:T(8,128)(2,1)S(1)}, bf16[64,2048]{1,0:T(8,128)(2,1)S(1)}, u32[]{:S(2)}, u32[]{:S(2)}) %collective-permute-start.24) | collective-permute-done | bytes 262176 | tf_op jit(solution)/shard_map/ppermute | solution.py:390
  175.6 3.8 %collective-permute-start.30 = (bf16[64,2048]{1,0:T(8,128)(2,1)S(1)}, bf16[64,2048]{1,0:T(8,128)(2,1)S(1)}, u32[]{:S(2)}, u32[]{:S(2)}) collective-permute-start(bf16[64,2048]{1,0:T(8,128)(2,1)S(1)} %add_rows.14), channel_id=1, source_target_pairs={{0,16},{2,18},{4,20},{6,22},{8,24},{10,26},{12,28},{14,30},{16,0},... | collective-permute-start | bytes 786440 | tf_op jit(solution)/shard_map/ppermute | solution.py:390
  179.6 1.5 collective-permute-start.23
  181.0 7.7 %group_sums.7 = (f32[2,2,8,768]{3,2,1,0:T(8,128)S(1)}, f32[2,6,1024]{2,1,0:T(8,128)S(1)}) custom-call(bf16[512,2048]{1,0:T(8,128)(2,1)S(1)} %get-tuple-element.75.refs_0_, bf16[512,2048]{1,0:T(8,128)(2,1)S(1)} %get-tuple-element.76.refs_1_, bf16[512,768]{1,0:T(8,128)(2,1)S(1)} %get-tuple-element.77.refs_2_, ...), custom_call_target="tpu_custom_call" | custom-call | tf_op jit(solution)/shard_map/group_sums/pallas_call | solution.py:80
  188.8 1.2 collective-permute-done.32.refs_7_
  190.3 5.4 %group_sums.6 = (f32[2,2,8,768]{3,2,1,0:T(8,128)S(1)}, f32[2,6,1024]{2,1,0:T(8,128)S(1)}) custom-call(bf16[512,2048]{1,0:T(8,128)(2,1)S(1)} %get-tuple-element.75.refs_0_, bf16[512,2048]{1,0:T(8,128)(2,1)S(1)} %get-tuple-element.76.refs_1_, bf16[512,768]{1,0:T(8,128)(2,1)S(1)} %get-tuple-element.77.refs_2_, ...), custom_call_target="tpu_custom_call" | custom-call | tf_op jit(solution)/shard_map/group_sums/pallas_call | solution.py:80
  195.7 1.7 clip_gradients.1
  (154 shorter events, 22.0 us)
Async XLA Ops:
  4.1 1.6 copy-start.33
  5.7 1.2 copy-start.34
  13.2 33.8 %collective-permute-start.3 = (bf16[3,1024,768]{2,1,0:T(8,128)(2,1)S(1)}, bf16[3,1024,768]{2,1,0:T(8,128)(2,1)}, u32[]{:S(2)}, u32[]{:S(2)}) collective-permute-start(bf16[3,1024,768]{2,1,0:T(8,128)(2,1)S(1)} %make_weights.1.refs_4_), channel_id=1, source_target_pairs={{0,1},{1,0},{2,3},{3,2},{4,5},{5,4},{6,7},{7,6},{8,9},{9,8},{10,11... | collective-permute-start | bytes 14155784 | tf_op jit(solution)/shard_map/ppermute | solution.py:393
  13.7 2.2 %copy-start = (bf16[3,1024,768]{2,1,0:T(8,128)(2,1)}, bf16[3,1024,768]{2,1,0:T(8,128)(2,1)S(1)}, u32[]{:S(2)}) copy-start(bf16[3,1024,768]{2,1,0:T(8,128)(2,1)S(1)} %make_weights.1.refs_4_) | copy-start | bytes 14155780
  15.8 15.4 %collective-permute-start = (bf16[64,4224]{1,0:T(8,128)(2,1)S(1)}, bf16[64,4224]{1,0:T(8,128)(2,1)S(1)}, u32[]{:S(2)}, u32[]{:S(2)}) collective-permute-start(bf16[64,4224]{1,0:T(8,128)(2,1)S(1)} %pack_rows.1.refs_6_.refs_0_), channel_id=1, source_target_pairs={{0,2},{2,0},{4,6},{6,4},{8,10},{10,8},{12,14},{14,12},{16,18},{18,... | collective-permute-start | bytes 1622024 | tf_op jit(solution)/shard_map/ppermute | solution.py:390
  18.3 27.0 %collective-permute-start.8 = (bf16[64,4224]{1,0:T(8,128)(2,1)S(1)}, bf16[64,4224]{1,0:T(8,128)(2,1)S(1)}, u32[]{:S(2)}, u32[]{:S(2)}) collective-permute-start(bf16[64,4224]{1,0:T(8,128)(2,1)S(1)} %pack_rows.1.refs_6_.refs_0_), channel_id=1, source_target_pairs={{0,16},{2,18},{4,20},{6,22},{8,24},{10,26},{12,28},{14,30},{16,0},... | collective-permute-start | bytes 1622024 | tf_op jit(solution)/shard_map/ppermute | solution.py:390
  20.9 25.2 %collective-permute-start.1 = (bf16[64,4224]{1,0:T(8,128)(2,1)S(1)}, bf16[64,4224]{1,0:T(8,128)(2,1)S(1)}, u32[]{:S(2)}, u32[]{:S(2)}) collective-permute-start(bf16[64,4224]{1,0:T(8,128)(2,1)S(1)} %pack_rows.1.refs_6_.refs_0_), channel_id=1, source_target_pairs={{0,4},{2,6},{4,0},{6,2},{8,12},{10,14},{12,8},{14,10},{16,20},{18,... | collective-permute-start | bytes 1622024 | tf_op jit(solution)/shard_map/ppermute | solution.py:390
  22.4 24.3 %collective-permute-start.7 = (bf16[64,4224]{1,0:T(8,128)(2,1)S(1)}, bf16[64,4224]{1,0:T(8,128)(2,1)S(1)}, u32[]{:S(2)}, u32[]{:S(2)}) collective-permute-start(bf16[64,4224]{1,0:T(8,128)(2,1)S(1)} %pack_rows.1.refs_6_.refs_0_), channel_id=1, source_target_pairs={{0,8},{2,10},{4,12},{6,14},{8,0},{10,2},{12,4},{14,6},{16,24},{18,... | collective-permute-start | bytes 1622024 | tf_op jit(solution)/shard_map/ppermute | solution.py:390
  31.3 15.5 %copy-start.29 = (bf16[64,4224]{1,0:T(8,128)(2,1)}, bf16[64,4224]{1,0:T(8,128)(2,1)S(1)}, u32[]{:S(2)}) copy-start(bf16[64,4224]{1,0:T(8,128)(2,1)S(1)} %collective-permute-done.refs_1_.refs_2_) | copy-start | bytes 1622020
  31.3 15.5 %collective-permute-start.2 = (bf16[64,4224]{1,0:T(8,128)(2,1)S(1)}, bf16[64,4224]{1,0:T(8,128)(2,1)S(1)}, u32[]{:S(2)}, u32[]{:S(2)}) collective-permute-start(bf16[64,4224]{1,0:T(8,128)(2,1)S(1)} %collective-permute-done.refs_1_.refs_2_), channel_id=1, source_target_pairs={{0,4},{2,6},{4,0},{6,2},{8,12},{10,14},{12,8},{14,10},{16,20},{18,... | collective-permute-start | bytes 1622024 | tf_op jit(solution)/shard_map/ppermute | solution.py:390
  45.3 4.0 %copy-start.22 = (bf16[64,4224]{1,0:T(8,128)(2,1)}, bf16[64,4224]{1,0:T(8,128)(2,1)S(1)}, u32[]{:S(2)}) copy-start(bf16[64,4224]{1,0:T(8,128)(2,1)S(1)} %collective-permute-done.8.refs_0_) | copy-start | bytes 1622020
  47.8 13.8 %collective-permute-start.10 = (bf16[64,4224]{1,0:T(8,128)(2,1)}, bf16[64,4224]{1,0:T(8,128)(2,1)}, u32[]{:S(2)}, u32[]{:S(2)}) collective-permute-start(bf16[64,4224]{1,0:T(8,128)(2,1)} %hold.5), channel_id=1, source_target_pairs={{0,4},{2,6},{4,0},{6,2},{8,12},{10,14},{12,8},{14,10},{16,20},{18,... | collective-permute-start | bytes 1622024 | tf_op jit(solution)/shard_map/ppermute | solution.py:390
  49.3 13.2 %collective-permute-start.9 = (bf16[64,4224]{1,0:T(8,128)(2,1)S(1)}, bf16[64,4224]{1,0:T(8,128)(2,1)S(1)}, u32[]{:S(2)}, u32[]{:S(2)}) collective-permute-start(bf16[64,4224]{1,0:T(8,128)(2,1)S(1)} %collective-permute-done.8.refs_0_), channel_id=1, source_target_pairs={{0,8},{2,10},{4,12},{6,14},{8,0},{10,2},{12,4},{14,6},{16,24},{18,... | collective-permute-start | bytes 1622024 | tf_op jit(solution)/shard_map/ppermute | solution.py:390
  50.5 14.0 %collective-permute-start.13 = (bf16[64,4224]{1,0:T(8,128)(2,1)}, bf16[64,4224]{1,0:T(8,128)(2,1)S(1)}, u32[]{:S(2)}, u32[]{:S(2)}) collective-permute-start(bf16[64,4224]{1,0:T(8,128)(2,1)} %hold.5), channel_id=1, source_target_pairs={{0,2},{2,0},{4,6},{6,4},{8,10},{10,8},{12,14},{14,12},{16,18},{18,... | collective-permute-start | bytes 1622024 | tf_op jit(solution)/shard_map/ppermute | solution.py:390
  61.6 24.2 %collective-permute-start.11 = (bf16[64,4224]{1,0:T(8,128)(2,1)}, bf16[64,4224]{1,0:T(8,128)(2,1)}, u32[]{:S(2)}, u32[]{:S(2)}) collective-permute-start(bf16[64,4224]{1,0:T(8,128)(2,1)} %collective-permute-done.10.refs_2_), channel_id=1, source_target_pairs={{0,2},{2,0},{4,6},{6,4},{8,10},{10,8},{12,14},{14,12},{16,18},{18,... | collective-permute-start | bytes 1622024 | tf_op jit(solution)/shard_map/ppermute | solution.py:390
  62.5 2.9 %copy-start.20 = (bf16[64,4224]{1,0:T(8,128)(2,1)}, bf16[64,4224]{1,0:T(8,128)(2,1)S(1)}, u32[]{:S(2)}) copy-start(bf16[64,4224]{1,0:T(8,128)(2,1)S(1)} %collective-permute-done.9.refs_0_) | copy-start | bytes 1622020
  65.4 27.7 %collective-permute-start.15 = (bf16[64,4224]{1,0:T(8,128)(2,1)}, bf16[64,4224]{1,0:T(8,128)(2,1)}, u32[]{:S(2)}, u32[]{:S(2)}) collective-permute-start(bf16[64,4224]{1,0:T(8,128)(2,1)} %hold.8), channel_id=1, source_target_pairs={{0,4},{2,6},{4,0},{6,2},{8,12},{10,14},{12,8},{14,10},{16,20},{18,... | collective-permute-start | bytes 1622024 | tf_op jit(solution)/shard_map/ppermute | solution.py:390
  66.2 2.3 %copy-start.1 = (bf16[3,1024,768]{2,1,0:T(8,128)(2,1)S(1)}, bf16[3,1024,768]{2,1,0:T(8,128)(2,1)}, u32[]{:S(2)}) copy-start(bf16[3,1024,768]{2,1,0:T(8,128)(2,1)} %copy-done) | copy-start | bytes 14155780
  80.3 1.4 copy-start.3
  85.8 31.4 %collective-permute-start.12 = (bf16[64,4224]{1,0:T(8,128)(2,1)}, bf16[64,4224]{1,0:T(8,128)(2,1)}, u32[]{:S(2)}, u32[]{:S(2)}) collective-permute-start(bf16[64,4224]{1,0:T(8,128)(2,1)} %hold.6), channel_id=1, source_target_pairs={{0,2},{2,0},{4,6},{6,4},{8,10},{10,8},{12,14},{14,12},{16,18},{18,... | collective-permute-start | bytes 1622024 | tf_op jit(solution)/shard_map/ppermute | solution.py:390
  87.3 32.1 %collective-permute-start.18 = (bf16[64,4224]{1,0:T(8,128)(2,1)}, bf16[64,4224]{1,0:T(8,128)(2,1)}, u32[]{:S(2)}, u32[]{:S(2)}) collective-permute-start(bf16[64,4224]{1,0:T(8,128)(2,1)} %collective-permute-done.11.refs_1_.refs_3_), channel_id=1, source_target_pairs={{0,8},{2,10},{4,12},{6,14},{8,0},{10,2},{12,4},{14,6},{16,24},{18,... | collective-permute-start | bytes 1622024 | tf_op jit(solution)/shard_map/ppermute | solution.py:390
  92.4 58.9 %collective-permute-start.17 = (bf16[64,4224]{1,0:T(8,128)(2,1)}, bf16[64,4224]{1,0:T(8,128)(2,1)}, u32[]{:S(2)}, u32[]{:S(2)}) collective-permute-start(bf16[64,4224]{1,0:T(8,128)(2,1)} %copy-done.27), channel_id=1, source_target_pairs={{0,8},{2,10},{4,12},{6,14},{8,0},{10,2},{12,4},{14,6},{16,24},{18,... | collective-permute-start | bytes 1622024 | tf_op jit(solution)/shard_map/ppermute | solution.py:390
  93.1 58.1 %collective-permute-start.16 = (bf16[64,4224]{1,0:T(8,128)(2,1)}, bf16[64,4224]{1,0:T(8,128)(2,1)}, u32[]{:S(2)}, u32[]{:S(2)}) collective-permute-start(bf16[64,4224]{1,0:T(8,128)(2,1)} %hold.9), channel_id=1, source_target_pairs={{0,4},{2,6},{4,0},{6,2},{8,12},{10,14},{12,8},{14,10},{16,20},{18,... | collective-permute-start | bytes 1622024 | tf_op jit(solution)/shard_map/ppermute | solution.py:390
  93.7 2.3 %copy-start.2 = (bf16[3,1024,768]{2,1,0:T(8,128)(2,1)S(1)}, bf16[3,1024,768]{2,1,0:T(8,128)(2,1)}, u32[]{:S(2)}) copy-start(bf16[3,1024,768]{2,1,0:T(8,128)(2,1)} %copy-done) | copy-start | bytes 14155780
  96.0 1.6 copy-start.4
  97.6 1.4 copy-start.9
  102.3 15.0 %copy-start.26 = (bf16[64,4224]{1,0:T(8,128)(2,1)S(1)}, bf16[64,4224]{1,0:T(8,128)(2,1)}, u32[]{:S(2)}) copy-start(bf16[64,4224]{1,0:T(8,128)(2,1)} %copy.32.refs_0_) | copy-start | bytes 1622020
  111.1 1.3 copy-start.5
  117.3 16.1 %slice-start = ((s8[4718592]{0:T(1024)(128)(4,1)}), s8[524288]{0:T(1024)(128)(4,1)S(1)}, s32[]{:S(2)}) async-start(s8[4718592]{0:T(1024)(128)(4,1)} %bitcast.16), calls=%async_computation | async-start | bytes 1048576
  117.3 34.0 %collective-permute-start.14 = (bf16[64,4224]{1,0:T(8,128)(2,1)S(1)}, bf16[64,4224]{1,0:T(8,128)(2,1)S(1)}, u32[]{:S(2)}, u32[]{:S(2)}) collective-permute-start(bf16[64,4224]{1,0:T(8,128)(2,1)S(1)} %hold.7), channel_id=1, source_target_pairs={{0,2},{2,0},{4,6},{6,4},{8,10},{10,8},{12,14},{14,12},{16,18},{18,... | collective-permute-start | bytes 1622024 | tf_op jit(solution)/shard_map/ppermute | solution.py:390
  119.4 23.2 %collective-permute-start.4 = (bf16[64,2048]{1,0:T(8,128)(2,1)}, bf16[64,2048]{1,0:T(8,128)(2,1)S(1)}, u32[]{:S(2)}, u32[]{:S(2)}) collective-permute-start(bf16[64,2048]{1,0:T(8,128)(2,1)} %copy-done.57), channel_id=1, source_target_pairs={{0,4},{2,6},{4,0},{6,2},{8,12},{10,14},{12,8},{14,10},{16,20},{18,... | collective-permute-start | bytes 786440 | tf_op jit(solution)/shard_map/ppermute | solution.py:390
  119.4 23.4 %collective-permute-start.19 = (bf16[64,2048]{1,0:T(8,128)(2,1)}, bf16[64,2048]{1,0:T(8,128)(2,1)S(1)}, u32[]{:S(2)}, u32[]{:S(2)}) collective-permute-start(bf16[64,2048]{1,0:T(8,128)(2,1)} %copy-done.58), channel_id=1, source_target_pairs={{0,4},{2,6},{4,0},{6,2},{8,12},{10,14},{12,8},{14,10},{16,20},{18,... | collective-permute-start | bytes 786440 | tf_op jit(solution)/shard_map/ppermute | solution.py:390
  121.4 1.6 copy-start.6
  123.0 1.4 copy-start.11
  125.5 7.9 %slice-start.1 = ((s8[4718592]{0:T(1024)(128)(4,1)}), s8[4194304]{0:T(1024)(128)(4,1)S(1)}, s32[]{:S(2)}) async-start(s8[4718592]{0:T(1024)(128)(4,1)} %bitcast.16), calls=%async_computation.1 | async-start | bytes 8388608
  125.5 7.9 %copy-start.21 = (bf16[64,4224]{1,0:T(8,128)(2,1)S(1)}, bf16[64,4224]{1,0:T(8,128)(2,1)}, u32[]{:S(2)}) copy-start(bf16[64,4224]{1,0:T(8,128)(2,1)} %copy-done.20) | copy-start | bytes 1622020
  133.4 9.3 %copy-start.48 = (bf16[64,2048]{1,0:T(8,128)(2,1)S(1)}, bf16[64,2048]{1,0:T(8,128)(2,1)}, u32[]{:S(2)}) copy-start(bf16[64,2048]{1,0:T(8,128)(2,1)} %copy-done.47) | copy-start | bytes 786436
  133.5 9.4 %copy-start.7 = (bf16[512,2048]{1,0:T(8,128)(2,1)S(1)}, bf16[512,2048]{1,0:T(8,128)(2,1)}, u32[]{:S(2)}) copy-start(bf16[512,2048]{1,0:T(8,128)(2,1)} %copy-done.5) | copy-start | bytes 6291460
  133.5 9.4 %copy-start.19 = (bf16[512,768]{1,0:T(8,128)(2,1)S(1)}, bf16[512,768]{1,0:T(8,128)(2,1)}, u32[]{:S(2)}) copy-start(bf16[512,768]{1,0:T(8,128)(2,1)} %copy-done.17) | copy-start | bytes 2359300
  142.6 1.4 copy-start.12
  142.6 8.3 %collective-permute-start.26 = (bf16[64,2048]{1,0:T(8,128)(2,1)S(1)}, bf16[64,2048]{1,0:T(8,128)(2,1)S(1)}, u32[]{:S(2)}, u32[]{:S(2)}) collective-permute-start(bf16[64,2048]{1,0:T(8,128)(2,1)S(1)} %get-tuple-element.73), channel_id=1, source_target_pairs={{0,4},{2,6},{4,0},{6,2},{8,12},{10,14},{12,8},{14,10},{16,20},{18,... | collective-permute-start | bytes 786440 | tf_op jit(solution)/shard_map/ppermute | solution.py:390
  144.0 7.3 %copy-start.14 = (bf16[64,4224]{1,0:T(8,128)(2,1)S(1)}, bf16[64,4224]{1,0:T(8,128)(2,1)}, u32[]{:S(2)}) copy-start(bf16[64,4224]{1,0:T(8,128)(2,1)} %copy-done.13) | copy-start | bytes 1622020
  149.6 13.5 %collective-permute-start.28 = (bf16[64,2048]{1,0:T(8,128)(2,1)S(1)}, bf16[64,2048]{1,0:T(8,128)(2,1)S(1)}, u32[]{:S(2)}, u32[]{:S(2)}) collective-permute-start(bf16[64,2048]{1,0:T(8,128)(2,1)S(1)} %get-tuple-element.74), channel_id=1, source_target_pairs={{0,4},{2,6},{4,0},{6,2},{8,12},{10,14},{12,8},{14,10},{16,20},{18,... | collective-permute-start | bytes 786440 | tf_op jit(solution)/shard_map/ppermute | solution.py:390
  150.9 12.2 %collective-permute-start.27 = (bf16[64,2048]{1,0:T(8,128)(2,1)S(1)}, bf16[64,2048]{1,0:T(8,128)(2,1)S(1)}, u32[]{:S(2)}, u32[]{:S(2)}) collective-permute-start(bf16[64,2048]{1,0:T(8,128)(2,1)S(1)} %add_rows.12.refs_7_), channel_id=1, source_target_pairs={{0,2},{2,0},{4,6},{6,4},{8,10},{10,8},{12,14},{14,12},{16,18},{18,... | collective-permute-start | bytes 786440 | tf_op jit(solution)/shard_map/ppermute | solution.py:390
  151.2 10.7 %copy-start.56 = (bf16[64,2048]{1,0:T(8,128)(2,1)S(1)}, bf16[64,2048]{1,0:T(8,128)(2,1)}, u32[]{:S(2)}) copy-start(bf16[64,2048]{1,0:T(8,128)(2,1)} %copy-done.55) | copy-start | bytes 786436
  151.2 20.0 %copy-start.54 = (bf16[64,2048]{1,0:T(8,128)(2,1)S(1)}, bf16[64,2048]{1,0:T(8,128)(2,1)}, u32[]{:S(2)}) copy-start(bf16[64,2048]{1,0:T(8,128)(2,1)} %copy-done.53) | copy-start | bytes 786436
  151.3 24.3 %copy-start.36 = (bf16[64,2048]{1,0:T(8,128)(2,1)S(1)}, bf16[64,2048]{1,0:T(8,128)(2,1)}, u32[]{:S(2)}) copy-start(bf16[64,2048]{1,0:T(8,128)(2,1)} %copy-done.35) | copy-start | bytes 786436
  160.1 9.3 %collective-permute-start.21 = (bf16[64,2048]{1,0:T(8,128)(2,1)S(1)}, bf16[64,2048]{1,0:T(8,128)(2,1)S(1)}, u32[]{:S(2)}, u32[]{:S(2)}) collective-permute-start(bf16[64,2048]{1,0:T(8,128)(2,1)S(1)} %get-tuple-element.70), channel_id=1, source_target_pairs={{0,2},{2,0},{4,6},{6,4},{8,10},{10,8},{12,14},{14,12},{16,18},{18,... | collective-permute-start | bytes 786440 | tf_op jit(solution)/shard_map/ppermute | solution.py:390
  162.0 9.2 %collective-permute-start.25 = (bf16[64,2048]{1,0:T(8,128)(2,1)S(1)}, bf16[64,2048]{1,0:T(8,128)(2,1)S(1)}, u32[]{:S(2)}, u32[]{:S(2)}) collective-permute-start(bf16[64,2048]{1,0:T(8,128)(2,1)S(1)} %copy-done.56), channel_id=1, source_target_pairs={{0,4},{2,6},{4,0},{6,2},{8,12},{10,14},{12,8},{14,10},{16,20},{18,... | collective-permute-start | bytes 786440 | tf_op jit(solution)/shard_map/ppermute | solution.py:390
  162.8 12.2 %collective-permute-start.24 = (bf16[64,2048]{1,0:T(8,128)(2,1)S(1)}, bf16[64,2048]{1,0:T(8,128)(2,1)S(1)}, u32[]{:S(2)}, u32[]{:S(2)}) collective-permute-start(bf16[64,2048]{1,0:T(8,128)(2,1)S(1)} %add_rows.9.refs_11_), channel_id=1, source_target_pairs={{0,2},{2,0},{4,6},{6,4},{8,10},{10,8},{12,14},{14,12},{16,18},{18,... | collective-permute-start | bytes 786440 | tf_op jit(solution)/shard_map/ppermute | solution.py:390
  163.2 12.3 %collective-permute-start.29 = (bf16[64,2048]{1,0:T(8,128)(2,1)S(1)}, bf16[64,2048]{1,0:T(8,128)(2,1)S(1)}, u32[]{:S(2)}, u32[]{:S(2)}) collective-permute-start(bf16[64,2048]{1,0:T(8,128)(2,1)S(1)} %add_rows.13.refs_7_), channel_id=1, source_target_pairs={{0,8},{2,10},{4,12},{6,14},{8,0},{10,2},{12,4},{14,6},{16,24},{18,... | collective-permute-start | bytes 786440 | tf_op jit(solution)/shard_map/ppermute | solution.py:390
  164.6 14.9 %collective-permute-start.20 = (bf16[64,2048]{1,0:T(8,128)(2,1)S(1)}, bf16[64,2048]{1,0:T(8,128)(2,1)S(1)}, u32[]{:S(2)}, u32[]{:S(2)}) collective-permute-start(bf16[64,2048]{1,0:T(8,128)(2,1)S(1)} %get-tuple-element.68), channel_id=1, source_target_pairs={{0,2},{2,0},{4,6},{6,4},{8,10},{10,8},{12,14},{14,12},{16,18},{18,... | collective-permute-start | bytes 786440 | tf_op jit(solution)/shard_map/ppermute | solution.py:390
  169.5 10.0 %collective-permute-start.22 = (bf16[64,2048]{1,0:T(8,128)(2,1)S(1)}, bf16[64,2048]{1,0:T(8,128)(2,1)S(1)}, u32[]{:S(2)}, u32[]{:S(2)}) collective-permute-start(bf16[64,2048]{1,0:T(8,128)(2,1)S(1)} %add_rows.10), channel_id=1, source_target_pairs={{0,4},{2,6},{4,0},{6,2},{8,12},{10,14},{12,8},{14,10},{16,20},{18,... | collective-permute-start | bytes 786440 | tf_op jit(solution)/shard_map/ppermute | solution.py:390
  171.2 26.2 %collective-permute-start.6 = (bf16[64,2048]{1,0:T(8,128)(2,1)S(1)}, bf16[64,2048]{1,0:T(8,128)(2,1)S(1)}, u32[]{:S(2)}, u32[]{:S(2)}) collective-permute-start(bf16[64,2048]{1,0:T(8,128)(2,1)S(1)} %copy-done.54), channel_id=1, source_target_pairs={{0,4},{2,6},{4,0},{6,2},{8,12},{10,14},{12,8},{14,10},{16,20},{18,... | collective-permute-start | bytes 786440 | tf_op jit(solution)/shard_map/ppermute | solution.py:390
  175.0 22.4 %collective-permute-start.5 = (bf16[64,2048]{1,0:T(8,128)(2,1)S(1)}, bf16[64,2048]{1,0:T(8,128)(2,1)S(1)}, u32[]{:S(2)}, u32[]{:S(2)}) collective-permute-start(bf16[64,2048]{1,0:T(8,128)(2,1)S(1)} %add_rows.8.refs_10_), channel_id=1, source_target_pairs={{0,2},{2,0},{4,6},{6,4},{8,10},{10,8},{12,14},{14,12},{16,18},{18,... | collective-permute-start | bytes 786440 | tf_op jit(solution)/shard_map/ppermute | solution.py:390
  175.6 21.7 %collective-permute-start.30 = (bf16[64,2048]{1,0:T(8,128)(2,1)S(1)}, bf16[64,2048]{1,0:T(8,128)(2,1)S(1)}, u32[]{:S(2)}, u32[]{:S(2)}) collective-permute-start(bf16[64,2048]{1,0:T(8,128)(2,1)S(1)} %add_rows.14), channel_id=1, source_target_pairs={{0,16},{2,18},{4,20},{6,22},{8,24},{10,26},{12,28},{14,30},{16,0},... | collective-permute-start | bytes 786440 | tf_op jit(solution)/shard_map/ppermute | solution.py:390
  179.6 17.8 %collective-permute-start.23 = (bf16[64,2048]{1,0:T(8,128)(2,1)S(1)}, bf16[64,2048]{1,0:T(8,128)(2,1)S(1)}, u32[]{:S(2)}, u32[]{:S(2)}) collective-permute-start(bf16[64,2048]{1,0:T(8,128)(2,1)S(1)} %add_rows.11), channel_id=1, source_target_pairs={{0,8},{2,10},{4,12},{6,14},{8,0},{10,2},{12,4},{14,6},{16,24},{18,... | collective-permute-start | bytes 786440 | tf_op jit(solution)/shard_map/ppermute | solution.py:390
  188.8 1.3 collective-permute-start.32
  190.1 5.6 %collective-permute-start.31 = (f32[2,2,8,768]{3,2,1,0:T(8,128)S(1)}, f32[2,2,8,768]{3,2,1,0:T(8,128)S(1)}, u32[]{:S(2)}, u32[]{:S(2)}) collective-permute-start(f32[2,2,8,768]{3,2,1,0:T(8,128)S(1)} %get-tuple-element.82), channel_id=1, source_target_pairs={{0,1},{1,0},{2,3},{3,2},{4,5},{5,4},{6,7},{7,6},{8,9},{9,8},{10,11... | collective-permute-start | bytes 294920 | tf_op jit(solution)/shard_map/ppermute | solution.py:393
  190.2 5.4 %copy-start.40 = (f32[1,2,2,16,768]{4,3,2,1,0:T(8,128)S(1)}, f32[1,2,2,16,768]{4,3,2,1,0:T(8,128)}, u32[]{:S(2)}) copy-start(f32[1,2,2,16,768]{4,3,2,1,0:T(8,128)} %param.16) | copy-start | bytes 589828
  190.2 5.4 %copy-start.42 = (f32[1,2,2,16,768]{4,3,2,1,0:T(8,128)S(1)}, f32[1,2,2,16,768]{4,3,2,1,0:T(8,128)}, u32[]{:S(2)}) copy-start(f32[1,2,2,16,768]{4,3,2,1,0:T(8,128)} %param.17) | copy-start | bytes 589828
  190.2 5.4 %copy-start.44 = (f32[1,2,6,2048]{3,1,2,0:T(2,128)S(1)}, f32[1,2,6,2048]{3,1,2,0:T(2,128)}, u32[]{:S(2)}) copy-start(f32[1,2,6,2048]{3,1,2,0:T(2,128)} %param.18) | copy-start | bytes 294916
  190.2 5.4 %copy-start.46 = (f32[1,2,6,2048]{3,1,2,0:T(2,128)S(1)}, f32[1,2,6,2048]{3,1,2,0:T(2,128)}, u32[]{:S(2)}) copy-start(f32[1,2,6,2048]{3,1,2,0:T(2,128)} %param.19) | copy-start | bytes 294916
  190.2 7.2 %copy-start.38 = (bf16[64,2048]{1,0:T(8,128)(2,1)S(1)}, bf16[64,2048]{1,0:T(8,128)(2,1)}, u32[]{:S(2)}) copy-start(bf16[64,2048]{1,0:T(8,128)(2,1)} %copy-done.37) | copy-start | bytes 786436
  (30 other events, 26.7 us)

commit v2 on v1

--- a/solution.py
+++ b/solution.py
@@ -13,6 +13,7 @@
 TILE = 256
 LIMIT = 24 * 1024 * 1024
 SMALL = 8 * 1024 * 1024
+TINY = 1024 * 1024
 F32 = jnp.float32
 BF16 = jnp.bfloat16
 
@@ -71,25 +72,35 @@
         return pltpu.VMEM(shape, dtype) if self.keep else jax.ShapeDtypeStruct(shape, dtype)
 
     def run(self, kernel, name, inputs, outputs, after=(), alias=None, limit=LIMIT, raw=(), free=()):
-        inputs = [*raw, *map(self.pin, inputs)]
-        count = len(inputs)
+        count, given = len(inputs), len(raw)
 
         def wrapped(*refs):
-            kernel(*refs[:count], *refs[count + len(after) :])
-
+            outs = refs[given + count + len(after) : given + count + len(after) + len(outputs)]
+            scratch = refs[len(refs) - given - 1 : len(refs) - 1] if raw else ()
+            copies = [
+                pltpu.make_async_copy(refs[i], scratch[i], refs[-1].at[i]) for i in range(given)
+            ]
+            for copy in copies:
+                copy.start()
+            for copy in copies:
+                copy.wait()
+            kernel(*scratch, *refs[given : given + count], *outs)
+
+        scratch = [pltpu.VMEM(a.shape, a.dtype) for a in raw]
         return pl.pallas_call(
             wrapped,
-            in_specs=[INSIDE] * count + [ANYWHERE] * len(after),
+            in_specs=[ANYWHERE] * given + [INSIDE] * count + [ANYWHERE] * len(after),
             out_specs=[INSIDE] * len(outputs),
             out_shape=[
                 jax.ShapeDtypeStruct(shape, dtype) if i in free else self.out(shape, dtype)
                 for i, (shape, dtype) in enumerate(outputs)
             ],
+            scratch_shapes=scratch + ([pltpu.SemaphoreType.DMA((given,))] if raw else []),
             input_output_aliases=alias or {},
             compiler_params=pltpu.CompilerParams(vmem_limit_bytes=limit),
             cost_estimate=pl.CostEstimate(flops=0, bytes_accessed=0, transcendentals=0),
             name=name,
-        )(*inputs, *after)
+        )(*[pltpu.with_memory_space_constraint(a, pltpu.HBM) for a in raw], *[self.pin(a) for a in inputs], *after)
 
 
 def pack_kernel(experts, token_ref, grad_ref, ids_ref, weights_ref, out_ref):
@@ -404,6 +415,8 @@
             out_specs=ANYWHERE,
             out_shape=calls.out(array.shape, array.dtype),
             input_output_aliases={0: 0},
+            compiler_params=pltpu.CompilerParams(vmem_limit_bytes=TINY),
+            cost_estimate=pl.CostEstimate(flops=0, bytes_accessed=0, transcendentals=0),
             name="hold",
         )(calls.pin(array), *after)
 

time: 199 us -> 145 us (0.73)
  local copies, waits for them, and re-layouts: 51 us -> 0.19 us
  waiting for transfers between devices: 41.6 us -> 53.8 us
  Pallas kernels: 67.8 us -> 56.5 us
  starting transfers between devices: 36.8 us -> 33.5 us
    unnamed x127 -> x5, local copies, waits for them, and re-layouts: 51 us -> 0.19 us
    ppermute x30, waiting for transfers between devices: 40.4 us -> 52.5 us  [swap(): lax.ppermute(array, 'expert', [(i, i ^ mask) for i in range(experts)])]
    pallas_call x19, Pallas kernels: 67.8 us -> 56.5 us  [run(): pl.pallas_call(wrapped, in_specs=[ANYWHERE] * given + [INSIDE] * count +...]
    ppermute x30, starting transfers between devices: 36.1 us -> 32.7 us  [swap(): lax.ppermute(array, 'expert', [(i, i ^ mask) for i in range(experts)])]
  transfers between devices with their start and end apart: 33 -> 33, of which waited for: 11 -> 14; matrix products, arithmetic and copies ran while one was open for 3% -> 0% of each run, Pallas kernels for 32% -> 34%
where the time goes in v2:
time: 145 us
  Pallas kernels  56.5 us (39%)
  waiting for transfers between devices  53.8 us (37%)
  starting transfers between devices  33.5 us (23%)
    pallas_call x19, Pallas kernels, run(): pl.pallas_call(wrapped, in_specs=[ANYWHERE] * given + [INSIDE] * count +...  56.5 us
    ppermute x30, waiting for transfers between devices, swap(): lax.ppermute(array, 'expert', [(i, i ^ mask) for i in range(experts)])  52.5 us
    ppermute x30, starting transfers between devices, swap(): lax.ppermute(array, 'expert', [(i, i ^ mask) for i in range(experts)])  32.7 us
  transfers between devices with their start and end apart: 33, of which 14 were waited for; matrix products, arithmetic and copies ran while one was open for 0% of the time, Pallas kernels for 34%

profile of v2, /device:TPU:0, one launch (start us, length us, event | category | flops | bytes accessed | tf_op | source)
XLA Modules:
  0.0 144.9 jit_solution(1239095892667516332)
XLA Ops:
  0.6 1.3 pack_rows.1.refs_6_.refs_0_
  1.9 4.7 %make_weights.1.refs_4_ = bf16[3,1024,768]{2,1,0:T(8,128)(2,1)S(1)} custom-call(s32[2,1024,256]{2,1,0:T(8,128)} %bitcast.16, s32[256,1024]{1,0:T(8,128)} %bitcast.17, f32[2,2,16,768]{3,2,1,0:T(8,128)} %bitcast.18, f32[2,2,16,768]{3,2,1,0:T(8,128)} %bitcast.20, f32[6,2,2048]{2,1,0:T(2,128)} %bitcast.22, f32[6,2,2048]{2,1,0:T(2,128)} %bitcast.24, ...), custom_call_target="tpu_custom_call" | custom-call | tf_op jit(solution)/shard_map/make_weights/pallas_call | solution.py:90
  6.6 0.5 collective-permute-start.3
  7.1 2.6 %collective-permute-start = (bf16[64,4224]{1,0:T(8,128)(2,1)S(1)}, bf16[64,4224]{1,0:T(8,128)(2,1)S(1)}, u32[]{:S(2)}, u32[]{:S(2)}) collective-permute-start(bf16[64,4224]{1,0:T(8,128)(2,1)S(1)} %pack_rows.1.refs_6_.refs_0_), channel_id=1, source_target_pairs={{0,2},{2,0},{4,6},{6,4},{8,10},{10,8},{12,14},{14,12},{16,18},{18,... | collective-permute-start | bytes 1622024 | tf_op jit(solution)/shard_map/ppermute | solution.py:401
  9.7 2.6 %collective-permute-start.8 = (bf16[64,4224]{1,0:T(8,128)(2,1)S(1)}, bf16[64,4224]{1,0:T(8,128)(2,1)S(1)}, u32[]{:S(2)}, u32[]{:S(2)}) collective-permute-start(bf16[64,4224]{1,0:T(8,128)(2,1)S(1)} %pack_rows.1.refs_6_.refs_0_), channel_id=1, source_target_pairs={{0,16},{2,18},{4,20},{6,22},{8,24},{10,26},{12,28},{14,30},{16,0},... | collective-permute-start | bytes 1622024 | tf_op jit(solution)/shard_map/ppermute | solution.py:401
  12.3 1.5 %collective-permute-start.1 = (bf16[64,4224]{1,0:T(8,128)(2,1)S(1)}, bf16[64,4224]{1,0:T(8,128)(2,1)S(1)}, u32[]{:S(2)}, u32[]{:S(2)}) collective-permute-start(bf16[64,4224]{1,0:T(8,128)(2,1)S(1)} %pack_rows.1.refs_6_.refs_0_), channel_id=1, source_target_pairs={{0,4},{2,6},{4,0},{6,2},{8,12},{10,14},{12,8},{14,10},{16,20},{18,... | collective-permute-start | bytes 1622024 | tf_op jit(solution)/shard_map/ppermute | solution.py:401
  13.8 1.6 %collective-permute-start.7 = (bf16[64,4224]{1,0:T(8,128)(2,1)S(1)}, bf16[64,4224]{1,0:T(8,128)(2,1)S(1)}, u32[]{:S(2)}, u32[]{:S(2)}) collective-permute-start(bf16[64,4224]{1,0:T(8,128)(2,1)S(1)} %pack_rows.1.refs_6_.refs_0_), channel_id=1, source_target_pairs={{0,8},{2,10},{4,12},{6,14},{8,0},{10,2},{12,4},{14,6},{16,24},{18,... | collective-permute-start | bytes 1622024 | tf_op jit(solution)/shard_map/ppermute | solution.py:401
  15.4 7.2 %collective-permute-done.refs_1_.refs_2_ = bf16[64,4224]{1,0:T(8,128)(2,1)S(1)} collective-permute-done((bf16[64,4224]{1,0:T(8,128)(2,1)S(1)}, bf16[64,4224]{1,0:T(8,128)(2,1)S(1)}, u32[]{:S(2)}, u32[]{:S(2)}) %collective-permute-start) | collective-permute-done | bytes 540704 | tf_op jit(solution)/shard_map/ppermute | solution.py:401
  22.6 1.8 %collective-permute-start.2 = (bf16[64,4224]{1,0:T(8,128)(2,1)S(1)}, bf16[64,4224]{1,0:T(8,128)(2,1)S(1)}, u32[]{:S(2)}, u32[]{:S(2)}) collective-permute-start(bf16[64,4224]{1,0:T(8,128)(2,1)S(1)} %collective-permute-done.refs_1_.refs_2_), channel_id=1, source_target_pairs={{0,4},{2,6},{4,0},{6,2},{8,12},{10,14},{12,8},{14,10},{16,20},{18,... | collective-permute-start | bytes 1622024 | tf_op jit(solution)/shard_map/ppermute | solution.py:401
  24.3 12.3 %collective-permute-done.8.refs_0_ = bf16[64,4224]{1,0:T(8,128)(2,1)S(1)} collective-permute-done((bf16[64,4224]{1,0:T(8,128)(2,1)S(1)}, bf16[64,4224]{1,0:T(8,128)(2,1)S(1)}, u32[]{:S(2)}, u32[]{:S(2)}) %collective-permute-start.8) | collective-permute-done | bytes 540704 | tf_op jit(solution)/shard_map/ppermute | solution.py:401
  36.7 1.4 collective-permute-done.7.refs_5_.refs_0_
  38.1 1.4 collective-permute-start.10
  39.5 1.6 %collective-permute-start.9 = (bf16[64,4224]{1,0:T(8,128)(2,1)S(1)}, bf16[64,4224]{1,0:T(8,128)(2,1)S(1)}, u32[]{:S(2)}, u32[]{:S(2)}) collective-permute-start(bf16[64,4224]{1,0:T(8,128)(2,1)S(1)} %collective-permute-done.8.refs_0_), channel_id=1, source_target_pairs={{0,8},{2,10},{4,12},{6,14},{8,0},{10,2},{12,4},{14,6},{16,24},{18,... | collective-permute-start | bytes 1622024 | tf_op jit(solution)/shard_map/ppermute | solution.py:401
  41.0 0.5 collective-permute-start.13
  41.6 9.6 %collective-permute-done.10.refs_2_ = bf16[64,4224]{1,0:T(8,128)(2,1)S(1)} collective-permute-done((bf16[64,4224]{1,0:T(8,128)(2,1)S(1)}, bf16[64,4224]{1,0:T(8,128)(2,1)S(1)}, u32[]{:S(2)}, u32[]{:S(2)}) %collective-permute-start.10) | collective-permute-done | bytes 540704 | tf_op jit(solution)/shard_map/ppermute | solution.py:401
  51.1 0.6 collective-permute-start.11
  51.7 0.6 collective-permute-done.9.refs_0_
  52.4 3.2 %collective-permute-done.13.refs_1_ = bf16[64,4224]{1,0:T(8,128)(2,1)S(1)} collective-permute-done((bf16[64,4224]{1,0:T(8,128)(2,1)S(1)}, bf16[64,4224]{1,0:T(8,128)(2,1)S(1)}, u32[]{:S(2)}, u32[]{:S(2)}) %collective-permute-start.13) | collective-permute-done | bytes 540704 | tf_op jit(solution)/shard_map/ppermute | solution.py:401
  55.7 6.3 %expert_set.4 = (bf16[64,2048]{1,0:T(8,128)(2,1)S(1)}, bf16[64,2048]{1,0:T(8,128)(2,1)S(1)}, bf16[64,2048]{1,0:T(8,128)(2,1)S(1)}, bf16[64,2048]{1,0:T(8,128)(2,...) custom-call(bf16[64,4224]{1,0:T(8,128)(2,1)S(1)} %pack_rows.1.refs_6, ...), custom_call_target="tpu_custom_call" | custom-call | tf_op jit(solution)/shard_map/expert_set/pallas_call | solution.py:90
  62.0 3.3 %collective-permute-done.11.refs_1_.refs_3_ = bf16[64,4224]{1,0:T(8,128)(2,1)S(1)} collective-permute-done((bf16[64,4224]{1,0:T(8,128)(2,1)S(1)}, bf16[64,4224]{1,0:T(8,128)(2,1)S(1)}, u32[]{:S(2)}, u32[]{:S(2)}) %collective-permute-start.11) | collective-permute-done | bytes 540704 | tf_op jit(solution)/shard_map/ppermute | solution.py:401
  65.3 0.6 collective-permute-start.12
  65.9 0.4 collective-permute-start.18
  66.4 1.6 %collective-permute-start.17 = (bf16[64,4224]{1,0:T(8,128)(2,1)S(1)}, bf16[64,4224]{1,0:T(8,128)(2,1)S(1)}, u32[]{:S(2)}, u32[]{:S(2)}) collective-permute-start(bf16[64,4224]{1,0:T(8,128)(2,1)S(1)} %collective-permute-done.2.refs_3_.refs_4_), channel_id=1, source_target_pairs={{0,8},{2,10},{4,12},{6,14},{8,0},{10,2},{12,4},{14,6},{16,24},{18,... | collective-permute-start | bytes 1622024 | tf_op jit(solution)/shard_map/ppermute | solution.py:401
  68.0 0.5 collective-permute-start.16
  68.5 6.1 %expert_set.5 = (bf16[64,2048]{1,0:T(8,128)(2,1)S(1)}, bf16[64,2048]{1,0:T(8,128)(2,1)S(1)}, bf16[64,2048]{1,0:T(8,128)(2,1)S(1)}, bf16[64,2048]{1,0:T(8,128)(2,...) custom-call(bf16[64,4224]{1,0:T(8,128)(2,1)S(1)} %collective-permute, ...), custom_call_target="tpu_custom_call", output_to_operand_aliasing={{4}: (6, {}), {5}: (7, {}), {6}: (8, {}), {7}: (9, {})} | custom-call | tf_op jit(solution)/shard_map/expert_set/pallas_call | solution.py:90
  74.6 3.1 %collective-permute-done.12.refs_1_ = bf16[64,4224]{1,0:T(8,128)(2,1)S(1)} collective-permute-done((bf16[64,4224]{1,0:T(8,128)(2,1)S(1)}, bf16[64,4224]{1,0:T(8,128)(2,1)S(1)}, u32[]{:S(2)}, u32[]{:S(2)}) %collective-permute-start.12) | collective-permute-done | bytes 540704 | tf_op jit(solution)/shard_map/ppermute | solution.py:401
  77.7 0.6 collective-permute-start.14
  78.3 0.5 collective-permute-start.4
  78.8 2.3 %collective-permute-done.18.refs_3_ = bf16[64,4224]{1,0:T(8,128)(2,1)S(1)} collective-permute-done((bf16[64,4224]{1,0:T(8,128)(2,1)S(1)}, bf16[64,4224]{1,0:T(8,128)(2,1)S(1)}, u32[]{:S(2)}, u32[]{:S(2)}) %collective-permute-start.18) | collective-permute-done | bytes 540704 | tf_op jit(solution)/shard_map/ppermute | solution.py:401
  81.1 0.5 collective-permute-start.19
  81.6 5.4 %group_sums.4 = (f32[2,2,8,768]{3,2,1,0:T(8,128)S(1)}, f32[2,6,1024]{2,1,0:T(8,128)S(1)}) custom-call(bf16[512,2048]{1,0:T(8,128)(2,1)S(1)} %get-tuple-element.54.refs_0_, bf16[512,2048]{1,0:T(8,128)(2,1)S(1)} %get-tuple-element.55.refs_1_, bf16[512,768]{1,0:T(8,128)(2,1)S(1)} %get-tuple-element.56.refs_2_, ...), custom_call_target="tpu_custom_call" | custom-call | tf_op jit(solution)/shard_map/group_sums/pallas_call | solution.py:90
  87.0 6.1 %expert_set.6 = (bf16[64,2048]{1,0:T(8,128)(2,1)S(1)}, bf16[64,2048]{1,0:T(8,128)(2,1)S(1)}, bf16[64,2048]{1,0:T(8,128)(2,1)S(1)}, bf16[64,2048]{1,0:T(8,128)(2,...) custom-call(bf16[64,4224]{1,0:T(8,128)(2,1)S(1)} %collective-permute, ...), custom_call_target="tpu_custom_call" | custom-call | tf_op jit(solution)/shard_map/expert_set/pallas_call | solution.py:90
  93.1 1.6 %collective-permute-start.26 = (bf16[64,2048]{1,0:T(8,128)(2,1)S(1)}, bf16[64,2048]{1,0:T(8,128)(2,1)S(1)}, u32[]{:S(2)}, u32[]{:S(2)}) collective-permute-start(bf16[64,2048]{1,0:T(8,128)(2,1)S(1)} %get-tuple-element.73), channel_id=1, source_target_pairs={{0,4},{2,6},{4,0},{6,2},{8,12},{10,14},{12,8},{14,10},{16,20},{18,... | collective-permute-start | bytes 786440 | tf_op jit(solution)/shard_map/ppermute | solution.py:401
  94.7 0.1 add_rows.8.refs_10_
  94.7 0.1 add_rows.9.refs_11_
  94.8 5.6 %group_sums.5 = (f32[2,2,8,768]{3,2,1,0:T(8,128)S(1)}, f32[2,6,1024]{2,1,0:T(8,128)S(1)}) custom-call(bf16[512,2048]{1,0:T(8,128)(2,1)S(1)} %get-tuple-element.54.refs_0_, bf16[512,2048]{1,0:T(8,128)(2,1)S(1)} %get-tuple-element.55.refs_1_, bf16[512,768]{1,0:T(8,128)(2,1)S(1)} %get-tuple-element.56.refs_2_, ...), custom_call_target="tpu_custom_call" | custom-call | tf_op jit(solution)/shard_map/group_sums/pallas_call | solution.py:90
  100.4 0.6 collective-permute-start.28
  101.0 1.0 collective-permute-done.26.refs_1_
  102.0 0.1 add_rows.12.refs_7_
  102.1 1.7 %collective-permute-start.27 = (bf16[64,2048]{1,0:T(8,128)(2,1)S(1)}, bf16[64,2048]{1,0:T(8,128)(2,1)S(1)}, u32[]{:S(2)}, u32[]{:S(2)}) collective-permute-start(bf16[64,2048]{1,0:T(8,128)(2,1)S(1)} %add_rows.12.refs_7_), channel_id=1, source_target_pairs={{0,2},{2,0},{4,6},{6,4},{8,10},{10,8},{12,14},{14,12},{16,18},{18,... | collective-permute-start | bytes 786440 | tf_op jit(solution)/shard_map/ppermute | solution.py:401
  103.8 6.1 %expert_set.7 = (bf16[64,2048]{1,0:T(8,128)(2,1)S(1)}, bf16[64,2048]{1,0:T(8,128)(2,1)S(1)}, bf16[64,2048]{1,0:T(8,128)(2,1)S(1)}, bf16[64,2048]{1,0:T(8,128)(2,...) custom-call(bf16[64,4224]{1,0:T(8,128)(2,1)S(1)} %collective-permute, ...), custom_call_target="tpu_custom_call", output_to_operand_aliasing={{4}: (6, {}), {5}: (7, {}), {6}: (8, {}), {7}: (9, {})} | custom-call | tf_op jit(solution)/shard_map/expert_set/pallas_call | solution.py:90
  109.9 0.5 collective-permute-start.21
  110.3 1.5 %collective-permute-start.25 = (bf16[64,2048]{1,0:T(8,128)(2,1)S(1)}, bf16[64,2048]{1,0:T(8,128)(2,1)S(1)}, u32[]{:S(2)}, u32[]{:S(2)}) collective-permute-start(bf16[64,2048]{1,0:T(8,128)(2,1)S(1)} %get-tuple-element.71), channel_id=1, source_target_pairs={{0,4},{2,6},{4,0},{6,2},{8,12},{10,14},{12,8},{14,10},{16,20},{18,... | collective-permute-start | bytes 786440 | tf_op jit(solution)/shard_map/ppermute | solution.py:401
  111.9 1.6 %collective-permute-start.24 = (bf16[64,2048]{1,0:T(8,128)(2,1)S(1)}, bf16[64,2048]{1,0:T(8,128)(2,1)S(1)}, u32[]{:S(2)}, u32[]{:S(2)}) collective-permute-start(bf16[64,2048]{1,0:T(8,128)(2,1)S(1)} %add_rows.9.refs_11_), channel_id=1, source_target_pairs={{0,2},{2,0},{4,6},{6,4},{8,10},{10,8},{12,14},{14,12},{16,18},{18,... | collective-permute-start | bytes 786440 | tf_op jit(solution)/shard_map/ppermute | solution.py:401
  113.5 0.1 add_rows.13.refs_7_
  113.6 0.2 collective-permute-start.29
  113.8 0.6 collective-permute-start.20
  114.4 4.8 %collective-permute-done.21.refs_1_ = bf16[64,2048]{1,0:T(8,128)(2,1)S(1)} collective-permute-done((bf16[64,2048]{1,0:T(8,128)(2,1)S(1)}, bf16[64,2048]{1,0:T(8,128)(2,1)S(1)}, u32[]{:S(2)}, u32[]{:S(2)}) %collective-permute-start.21) | collective-permute-done | bytes 262176 | tf_op jit(solution)/shard_map/ppermute | solution.py:401
  119.3 1.6 %collective-permute-start.22 = (bf16[64,2048]{1,0:T(8,128)(2,1)S(1)}, bf16[64,2048]{1,0:T(8,128)(2,1)S(1)}, u32[]{:S(2)}, u32[]{:S(2)}) collective-permute-start(bf16[64,2048]{1,0:T(8,128)(2,1)S(1)} %add_rows.10), channel_id=1, source_target_pairs={{0,4},{2,6},{4,0},{6,2},{8,12},{10,14},{12,8},{14,10},{16,20},{18,... | collective-permute-start | bytes 786440 | tf_op jit(solution)/shard_map/ppermute | solution.py:401
  120.9 0.5 collective-permute-start.6
  121.4 3.5 %collective-permute-done.24.refs_1_ = bf16[64,2048]{1,0:T(8,128)(2,1)S(1)} collective-permute-done((bf16[64,2048]{1,0:T(8,128)(2,1)S(1)}, bf16[64,2048]{1,0:T(8,128)(2,1)S(1)}, u32[]{:S(2)}, u32[]{:S(2)}) %collective-permute-start.24) | collective-permute-done | bytes 262176 | tf_op jit(solution)/shard_map/ppermute | solution.py:401
  124.8 0.4 collective-permute-start.5
  125.2 0.1 add_rows.14
  125.3 2.3 %collective-permute-start.30 = (bf16[64,2048]{1,0:T(8,128)(2,1)S(1)}, bf16[64,2048]{1,0:T(8,128)(2,1)S(1)}, u32[]{:S(2)}, u32[]{:S(2)}) collective-permute-start(bf16[64,2048]{1,0:T(8,128)(2,1)S(1)} %add_rows.14), channel_id=1, source_target_pairs={{0,16},{2,18},{4,20},{6,22},{8,24},{10,26},{12,28},{14,30},{16,0},... | collective-permute-start | bytes 786440 | tf_op jit(solution)/shard_map/ppermute | solution.py:401
  127.6 0.4 collective-permute-done.20.refs_1_
  128.0 0.1 add_rows.11
  128.1 0.8 collective-permute-start.23
  128.8 5.4 %group_sums.7 = (f32[2,2,8,768]{3,2,1,0:T(8,128)S(1)}, f32[2,6,1024]{2,1,0:T(8,128)S(1)}) custom-call(bf16[512,2048]{1,0:T(8,128)(2,1)S(1)} %get-tuple-element.75.refs_0_, bf16[512,2048]{1,0:T(8,128)(2,1)S(1)} %get-tuple-element.76.refs_1_, bf16[512,768]{1,0:T(8,128)(2,1)S(1)} %get-tuple-element.77.refs_2_, ...), custom_call_target="tpu_custom_call" | custom-call | tf_op jit(solution)/shard_map/group_sums/pallas_call | solution.py:90
  134.2 0.1 collective-permute-start.32
  134.3 1.2 collective-permute-done.32.refs_7_
  135.5 0.2 collective-permute-start.31
  135.7 5.4 %group_sums.6 = (f32[2,2,8,768]{3,2,1,0:T(8,128)S(1)}, f32[2,6,1024]{2,1,0:T(8,128)S(1)}) custom-call(bf16[512,2048]{1,0:T(8,128)(2,1)S(1)} %get-tuple-element.75.refs_0_, bf16[512,2048]{1,0:T(8,128)(2,1)S(1)} %get-tuple-element.76.refs_1_, bf16[512,768]{1,0:T(8,128)(2,1)S(1)} %get-tuple-element.77.refs_2_, ...), custom_call_target="tpu_custom_call" | custom-call | tf_op jit(solution)/shard_map/group_sums/pallas_call | solution.py:90
  141.1 2.9 %clip_gradients.1 = (f32[2,2,8,768]{3,2,1,0:T(8,128)}, f32[6,2,1024]{2,1,0:T(2,128)}) custom-call(f32[2,2,16,768]{3,2,1,0:T(8,128)} %bitcast.19, f32[2,2,16,768]{3,2,1,0:T(8,128)} %bitcast.21, f32[6,2,2048]{2,1,0:T(2,128)} %bitcast.23, f32[6,2,2048]{2,1,0:T(2,128)} %bitcast.25, f32[2,2,8,768]{3,2,1,0:T(8,128)S(1)} %get-tuple-element.80.refs_4_, ...), custom_call_target="tpu_custom_call" | custom-call | tf_op jit(solution)/shard_map/clip_gradients/pallas_call | solution.py:90
  144.0 0.9 add_rows.15
  (31 shorter events, 0.3 us)
Async XLA Ops:
  6.6 31.5 %collective-permute-start.3 = (bf16[3,1024,768]{2,1,0:T(8,128)(2,1)S(1)}, bf16[3,1024,768]{2,1,0:T(8,128)(2,1)S(1)}, u32[]{:S(2)}, u32[]{:S(2)}) collective-permute-start(bf16[3,1024,768]{2,1,0:T(8,128)(2,1)S(1)} %make_weights.1.refs_4_), channel_id=1, source_target_pairs={{0,1},{1,0},{2,3},{3,2},{4,5},{5,4},{6,7},{7,6},{8,9},{9,8},{10,11... | collective-permute-start | bytes 14155784 | tf_op jit(solution)/shard_map/ppermute | solution.py:404
  7.1 15.4 %collective-permute-start = (bf16[64,4224]{1,0:T(8,128)(2,1)S(1)}, bf16[64,4224]{1,0:T(8,128)(2,1)S(1)}, u32[]{:S(2)}, u32[]{:S(2)}) collective-permute-start(bf16[64,4224]{1,0:T(8,128)(2,1)S(1)} %pack_rows.1.refs_6_.refs_0_), channel_id=1, source_target_pairs={{0,2},{2,0},{4,6},{6,4},{8,10},{10,8},{12,14},{14,12},{16,18},{18,... | collective-permute-start | bytes 1622024 | tf_op jit(solution)/shard_map/ppermute | solution.py:401
  9.7 26.9 %collective-permute-start.8 = (bf16[64,4224]{1,0:T(8,128)(2,1)S(1)}, bf16[64,4224]{1,0:T(8,128)(2,1)S(1)}, u32[]{:S(2)}, u32[]{:S(2)}) collective-permute-start(bf16[64,4224]{1,0:T(8,128)(2,1)S(1)} %pack_rows.1.refs_6_.refs_0_), channel_id=1, source_target_pairs={{0,16},{2,18},{4,20},{6,22},{8,24},{10,26},{12,28},{14,30},{16,0},... | collective-permute-start | bytes 1622024 | tf_op jit(solution)/shard_map/ppermute | solution.py:401
  12.3 24.4 %collective-permute-start.1 = (bf16[64,4224]{1,0:T(8,128)(2,1)S(1)}, bf16[64,4224]{1,0:T(8,128)(2,1)S(1)}, u32[]{:S(2)}, u32[]{:S(2)}) collective-permute-start(bf16[64,4224]{1,0:T(8,128)(2,1)S(1)} %pack_rows.1.refs_6_.refs_0_), channel_id=1, source_target_pairs={{0,4},{2,6},{4,0},{6,2},{8,12},{10,14},{12,8},{14,10},{16,20},{18,... | collective-permute-start | bytes 1622024 | tf_op jit(solution)/shard_map/ppermute | solution.py:401
  13.8 24.3 %collective-permute-start.7 = (bf16[64,4224]{1,0:T(8,128)(2,1)S(1)}, bf16[64,4224]{1,0:T(8,128)(2,1)S(1)}, u32[]{:S(2)}, u32[]{:S(2)}) collective-permute-start(bf16[64,4224]{1,0:T(8,128)(2,1)S(1)} %pack_rows.1.refs_6_.refs_0_), channel_id=1, source_target_pairs={{0,8},{2,10},{4,12},{6,14},{8,0},{10,2},{12,4},{14,6},{16,24},{18,... | collective-permute-start | bytes 1622024 | tf_op jit(solution)/shard_map/ppermute | solution.py:401
  22.6 15.5 %collective-permute-start.2 = (bf16[64,4224]{1,0:T(8,128)(2,1)S(1)}, bf16[64,4224]{1,0:T(8,128)(2,1)S(1)}, u32[]{:S(2)}, u32[]{:S(2)}) collective-permute-start(bf16[64,4224]{1,0:T(8,128)(2,1)S(1)} %collective-permute-done.refs_1_.refs_2_), channel_id=1, source_target_pairs={{0,4},{2,6},{4,0},{6,2},{8,12},{10,14},{12,8},{14,10},{16,20},{18,... | collective-permute-start | bytes 1622024 | tf_op jit(solution)/shard_map/ppermute | solution.py:401
  38.1 13.1 %collective-permute-start.10 = (bf16[64,4224]{1,0:T(8,128)(2,1)S(1)}, bf16[64,4224]{1,0:T(8,128)(2,1)S(1)}, u32[]{:S(2)}, u32[]{:S(2)}) collective-permute-start(bf16[64,4224]{1,0:T(8,128)(2,1)S(1)} %hold.5), channel_id=1, source_target_pairs={{0,4},{2,6},{4,0},{6,2},{8,12},{10,14},{12,8},{14,10},{16,20},{18,... | collective-permute-start | bytes 1622024 | tf_op jit(solution)/shard_map/ppermute | solution.py:401
  39.5 12.9 %collective-permute-start.9 = (bf16[64,4224]{1,0:T(8,128)(2,1)S(1)}, bf16[64,4224]{1,0:T(8,128)(2,1)S(1)}, u32[]{:S(2)}, u32[]{:S(2)}) collective-permute-start(bf16[64,4224]{1,0:T(8,128)(2,1)S(1)} %collective-permute-done.8.refs_0_), channel_id=1, source_target_pairs={{0,8},{2,10},{4,12},{6,14},{8,0},{10,2},{12,4},{14,6},{16,24},{18,... | collective-permute-start | bytes 1622024 | tf_op jit(solution)/shard_map/ppermute | solution.py:401
  41.0 14.6 %collective-permute-start.13 = (bf16[64,4224]{1,0:T(8,128)(2,1)S(1)}, bf16[64,4224]{1,0:T(8,128)(2,1)S(1)}, u32[]{:S(2)}, u32[]{:S(2)}) collective-permute-start(bf16[64,4224]{1,0:T(8,128)(2,1)S(1)} %hold.5), channel_id=1, source_target_pairs={{0,2},{2,0},{4,6},{6,4},{8,10},{10,8},{12,14},{14,12},{16,18},{18,... | collective-permute-start | bytes 1622024 | tf_op jit(solution)/shard_map/ppermute | solution.py:401
  51.1 14.1 %collective-permute-start.11 = (bf16[64,4224]{1,0:T(8,128)(2,1)S(1)}, bf16[64,4224]{1,0:T(8,128)(2,1)S(1)}, u32[]{:S(2)}, u32[]{:S(2)}) collective-permute-start(bf16[64,4224]{1,0:T(8,128)(2,1)S(1)} %collective-permute-done.10.refs_2_), channel_id=1, source_target_pairs={{0,2},{2,0},{4,6},{6,4},{8,10},{10,8},{12,14},{14,12},{16,18},{18,... | collective-permute-start | bytes 1622024 | tf_op jit(solution)/shard_map/ppermute | solution.py:401
  55.6 12.4 %collective-permute-start.15 = (bf16[64,4224]{1,0:T(8,128)(2,1)S(1)}, bf16[64,4224]{1,0:T(8,128)(2,1)S(1)}, u32[]{:S(2)}, u32[]{:S(2)}) collective-permute-start(bf16[64,4224]{1,0:T(8,128)(2,1)S(1)} %hold.8), channel_id=1, source_target_pairs={{0,4},{2,6},{4,0},{6,2},{8,12},{10,14},{12,8},{14,10},{16,20},{18,... | collective-permute-start | bytes 1622024 | tf_op jit(solution)/shard_map/ppermute | solution.py:401
  65.3 12.4 %collective-permute-start.12 = (bf16[64,4224]{1,0:T(8,128)(2,1)S(1)}, bf16[64,4224]{1,0:T(8,128)(2,1)S(1)}, u32[]{:S(2)}, u32[]{:S(2)}) collective-permute-start(bf16[64,4224]{1,0:T(8,128)(2,1)S(1)} %hold.6), channel_id=1, source_target_pairs={{0,2},{2,0},{4,6},{6,4},{8,10},{10,8},{12,14},{14,12},{16,18},{18,... | collective-permute-start | bytes 1622024 | tf_op jit(solution)/shard_map/ppermute | solution.py:401
  65.9 15.2 %collective-permute-start.18 = (bf16[64,4224]{1,0:T(8,128)(2,1)S(1)}, bf16[64,4224]{1,0:T(8,128)(2,1)S(1)}, u32[]{:S(2)}, u32[]{:S(2)}) collective-permute-start(bf16[64,4224]{1,0:T(8,128)(2,1)S(1)} %collective-permute-done.11.refs_1_.refs_3_), channel_id=1, source_target_pairs={{0,8},{2,10},{4,12},{6,14},{8,0},{10,2},{12,4},{14,6},{16,24},{18,... | collective-permute-start | bytes 1622024 | tf_op jit(solution)/shard_map/ppermute | solution.py:401
  66.4 37.4 %collective-permute-start.17 = (bf16[64,4224]{1,0:T(8,128)(2,1)S(1)}, bf16[64,4224]{1,0:T(8,128)(2,1)S(1)}, u32[]{:S(2)}, u32[]{:S(2)}) collective-permute-start(bf16[64,4224]{1,0:T(8,128)(2,1)S(1)} %collective-permute-done.2.refs_3_.refs_4_), channel_id=1, source_target_pairs={{0,8},{2,10},{4,12},{6,14},{8,0},{10,2},{12,4},{14,6},{16,24},{18,... | collective-permute-start | bytes 1622024 | tf_op jit(solution)/shard_map/ppermute | solution.py:401
  68.0 35.8 %collective-permute-start.16 = (bf16[64,4224]{1,0:T(8,128)(2,1)S(1)}, bf16[64,4224]{1,0:T(8,128)(2,1)S(1)}, u32[]{:S(2)}, u32[]{:S(2)}) collective-permute-start(bf16[64,4224]{1,0:T(8,128)(2,1)S(1)} %hold.9), channel_id=1, source_target_pairs={{0,4},{2,6},{4,0},{6,2},{8,12},{10,14},{12,8},{14,10},{16,20},{18,... | collective-permute-start | bytes 1622024 | tf_op jit(solution)/shard_map/ppermute | solution.py:401
  77.7 26.1 %collective-permute-start.14 = (bf16[64,4224]{1,0:T(8,128)(2,1)S(1)}, bf16[64,4224]{1,0:T(8,128)(2,1)S(1)}, u32[]{:S(2)}, u32[]{:S(2)}) collective-permute-start(bf16[64,4224]{1,0:T(8,128)(2,1)S(1)} %hold.7), channel_id=1, source_target_pairs={{0,2},{2,0},{4,6},{6,4},{8,10},{10,8},{12,14},{14,12},{16,18},{18,... | collective-permute-start | bytes 1622024 | tf_op jit(solution)/shard_map/ppermute | solution.py:401
  78.3 14.8 %collective-permute-start.4 = (bf16[64,2048]{1,0:T(8,128)(2,1)S(1)}, bf16[64,2048]{1,0:T(8,128)(2,1)S(1)}, u32[]{:S(2)}, u32[]{:S(2)}) collective-permute-start(bf16[64,2048]{1,0:T(8,128)(2,1)S(1)} %get-tuple-element.47), channel_id=1, source_target_pairs={{0,4},{2,6},{4,0},{6,2},{8,12},{10,14},{12,8},{14,10},{16,20},{18,... | collective-permute-start | bytes 786440 | tf_op jit(solution)/shard_map/ppermute | solution.py:401
  81.1 13.7 %collective-permute-start.19 = (bf16[64,2048]{1,0:T(8,128)(2,1)S(1)}, bf16[64,2048]{1,0:T(8,128)(2,1)S(1)}, u32[]{:S(2)}, u32[]{:S(2)}) collective-permute-start(bf16[64,2048]{1,0:T(8,128)(2,1)S(1)} %get-tuple-element.64), channel_id=1, source_target_pairs={{0,4},{2,6},{4,0},{6,2},{8,12},{10,14},{12,8},{14,10},{16,20},{18,... | collective-permute-start | bytes 786440 | tf_op jit(solution)/shard_map/ppermute | solution.py:401
  93.1 8.9 %collective-permute-start.26 = (bf16[64,2048]{1,0:T(8,128)(2,1)S(1)}, bf16[64,2048]{1,0:T(8,128)(2,1)S(1)}, u32[]{:S(2)}, u32[]{:S(2)}) collective-permute-start(bf16[64,2048]{1,0:T(8,128)(2,1)S(1)} %get-tuple-element.73), channel_id=1, source_target_pairs={{0,4},{2,6},{4,0},{6,2},{8,12},{10,14},{12,8},{14,10},{16,20},{18,... | collective-permute-start | bytes 786440 | tf_op jit(solution)/shard_map/ppermute | solution.py:401
  100.4 13.1 %collective-permute-start.28 = (bf16[64,2048]{1,0:T(8,128)(2,1)S(1)}, bf16[64,2048]{1,0:T(8,128)(2,1)S(1)}, u32[]{:S(2)}, u32[]{:S(2)}) collective-permute-start(bf16[64,2048]{1,0:T(8,128)(2,1)S(1)} %get-tuple-element.74), channel_id=1, source_target_pairs={{0,4},{2,6},{4,0},{6,2},{8,12},{10,14},{12,8},{14,10},{16,20},{18,... | collective-permute-start | bytes 786440 | tf_op jit(solution)/shard_map/ppermute | solution.py:401
  102.1 11.4 %collective-permute-start.27 = (bf16[64,2048]{1,0:T(8,128)(2,1)S(1)}, bf16[64,2048]{1,0:T(8,128)(2,1)S(1)}, u32[]{:S(2)}, u32[]{:S(2)}) collective-permute-start(bf16[64,2048]{1,0:T(8,128)(2,1)S(1)} %add_rows.12.refs_7_), channel_id=1, source_target_pairs={{0,2},{2,0},{4,6},{6,4},{8,10},{10,8},{12,14},{14,12},{16,18},{18,... | collective-permute-start | bytes 786440 | tf_op jit(solution)/shard_map/ppermute | solution.py:401
  109.9 9.3 %collective-permute-start.21 = (bf16[64,2048]{1,0:T(8,128)(2,1)S(1)}, bf16[64,2048]{1,0:T(8,128)(2,1)S(1)}, u32[]{:S(2)}, u32[]{:S(2)}) collective-permute-start(bf16[64,2048]{1,0:T(8,128)(2,1)S(1)} %get-tuple-element.70), channel_id=1, source_target_pairs={{0,2},{2,0},{4,6},{6,4},{8,10},{10,8},{12,14},{14,12},{16,18},{18,... | collective-permute-start | bytes 786440 | tf_op jit(solution)/shard_map/ppermute | solution.py:401
  110.3 10.5 %collective-permute-start.25 = (bf16[64,2048]{1,0:T(8,128)(2,1)S(1)}, bf16[64,2048]{1,0:T(8,128)(2,1)S(1)}, u32[]{:S(2)}, u32[]{:S(2)}) collective-permute-start(bf16[64,2048]{1,0:T(8,128)(2,1)S(1)} %get-tuple-element.71), channel_id=1, source_target_pairs={{0,4},{2,6},{4,0},{6,2},{8,12},{10,14},{12,8},{14,10},{16,20},{18,... | collective-permute-start | bytes 786440 | tf_op jit(solution)/shard_map/ppermute | solution.py:401
  111.9 13.0 %collective-permute-start.24 = (bf16[64,2048]{1,0:T(8,128)(2,1)S(1)}, bf16[64,2048]{1,0:T(8,128)(2,1)S(1)}, u32[]{:S(2)}, u32[]{:S(2)}) collective-permute-start(bf16[64,2048]{1,0:T(8,128)(2,1)S(1)} %add_rows.9.refs_11_), channel_id=1, source_target_pairs={{0,2},{2,0},{4,6},{6,4},{8,10},{10,8},{12,14},{14,12},{16,18},{18,... | collective-permute-start | bytes 786440 | tf_op jit(solution)/shard_map/ppermute | solution.py:401
  113.6 11.6 %collective-permute-start.29 = (bf16[64,2048]{1,0:T(8,128)(2,1)S(1)}, bf16[64,2048]{1,0:T(8,128)(2,1)S(1)}, u32[]{:S(2)}, u32[]{:S(2)}) collective-permute-start(bf16[64,2048]{1,0:T(8,128)(2,1)S(1)} %add_rows.13.refs_7_), channel_id=1, source_target_pairs={{0,8},{2,10},{4,12},{6,14},{8,0},{10,2},{12,4},{14,6},{16,24},{18,... | collective-permute-start | bytes 786440 | tf_op jit(solution)/shard_map/ppermute | solution.py:401
  113.8 14.1 %collective-permute-start.20 = (bf16[64,2048]{1,0:T(8,128)(2,1)S(1)}, bf16[64,2048]{1,0:T(8,128)(2,1)S(1)}, u32[]{:S(2)}, u32[]{:S(2)}) collective-permute-start(bf16[64,2048]{1,0:T(8,128)(2,1)S(1)} %get-tuple-element.68), channel_id=1, source_target_pairs={{0,2},{2,0},{4,6},{6,4},{8,10},{10,8},{12,14},{14,12},{16,18},{18,... | collective-permute-start | bytes 786440 | tf_op jit(solution)/shard_map/ppermute | solution.py:401
  119.3 8.7 %collective-permute-start.22 = (bf16[64,2048]{1,0:T(8,128)(2,1)S(1)}, bf16[64,2048]{1,0:T(8,128)(2,1)S(1)}, u32[]{:S(2)}, u32[]{:S(2)}) collective-permute-start(bf16[64,2048]{1,0:T(8,128)(2,1)S(1)} %add_rows.10), channel_id=1, source_target_pairs={{0,4},{2,6},{4,0},{6,2},{8,12},{10,14},{12,8},{14,10},{16,20},{18,... | collective-permute-start | bytes 786440 | tf_op jit(solution)/shard_map/ppermute | solution.py:401
  120.9 23.1 %collective-permute-start.6 = (bf16[64,2048]{1,0:T(8,128)(2,1)S(1)}, bf16[64,2048]{1,0:T(8,128)(2,1)S(1)}, u32[]{:S(2)}, u32[]{:S(2)}) collective-permute-start(bf16[64,2048]{1,0:T(8,128)(2,1)S(1)} %get-tuple-element.48), channel_id=1, source_target_pairs={{0,4},{2,6},{4,0},{6,2},{8,12},{10,14},{12,8},{14,10},{16,20},{18,... | collective-permute-start | bytes 786440 | tf_op jit(solution)/shard_map/ppermute | solution.py:401
  124.8 19.1 %collective-permute-start.5 = (bf16[64,2048]{1,0:T(8,128)(2,1)S(1)}, bf16[64,2048]{1,0:T(8,128)(2,1)S(1)}, u32[]{:S(2)}, u32[]{:S(2)}) collective-permute-start(bf16[64,2048]{1,0:T(8,128)(2,1)S(1)} %add_rows.8.refs_10_), channel_id=1, source_target_pairs={{0,2},{2,0},{4,6},{6,4},{8,10},{10,8},{12,14},{14,12},{16,18},{18,... | collective-permute-start | bytes 786440 | tf_op jit(solution)/shard_map/ppermute | solution.py:401
  125.3 18.6 %collective-permute-start.30 = (bf16[64,2048]{1,0:T(8,128)(2,1)S(1)}, bf16[64,2048]{1,0:T(8,128)(2,1)S(1)}, u32[]{:S(2)}, u32[]{:S(2)}) collective-permute-start(bf16[64,2048]{1,0:T(8,128)(2,1)S(1)} %add_rows.14), channel_id=1, source_target_pairs={{0,16},{2,18},{4,20},{6,22},{8,24},{10,26},{12,28},{14,30},{16,0},... | collective-permute-start | bytes 786440 | tf_op jit(solution)/shard_map/ppermute | solution.py:401
  128.1 15.9 %collective-permute-start.23 = (bf16[64,2048]{1,0:T(8,128)(2,1)S(1)}, bf16[64,2048]{1,0:T(8,128)(2,1)S(1)}, u32[]{:S(2)}, u32[]{:S(2)}) collective-permute-start(bf16[64,2048]{1,0:T(8,128)(2,1)S(1)} %add_rows.11), channel_id=1, source_target_pairs={{0,8},{2,10},{4,12},{6,14},{8,0},{10,2},{12,4},{14,6},{16,24},{18,... | collective-permute-start | bytes 786440 | tf_op jit(solution)/shard_map/ppermute | solution.py:401
  134.2 1.3 collective-permute-start.32
  135.5 5.5 %collective-permute-start.31 = (f32[2,2,8,768]{3,2,1,0:T(8,128)S(1)}, f32[2,2,8,768]{3,2,1,0:T(8,128)S(1)}, u32[]{:S(2)}, u32[]{:S(2)}) collective-permute-start(f32[2,2,8,768]{3,2,1,0:T(8,128)S(1)} %get-tuple-element.82), channel_id=1, source_target_pairs={{0,1},{1,0},{2,3},{3,2},{4,5},{5,4},{6,7},{7,6},{8,9},{9,8},{10,11... | collective-permute-start | bytes 294920 | tf_op jit(solution)/shard_map/ppermute | solution.py:404

commit v3 on v2

--- a/solution.py
+++ b/solution.py
@@ -71,7 +71,7 @@
     def out(self, shape, dtype):
         return pltpu.VMEM(shape, dtype) if self.keep else jax.ShapeDtypeStruct(shape, dtype)
 
-    def run(self, kernel, name, inputs, outputs, after=(), alias=None, limit=LIMIT, raw=(), free=()):
+    def run(self, kernel, name, inputs, outputs, after=(), alias=None, limit=LIMIT, raw=(), late=0, free=()):
         count, given = len(inputs), len(raw)
 
         def wrapped(*refs):
@@ -82,9 +82,10 @@
             ]
             for copy in copies:
                 copy.start()
-            for copy in copies:
+            for copy in copies[late:]:
                 copy.wait()
-            kernel(*scratch, *refs[given : given + count], *outs)
+            waits = [copy.wait for copy in copies[:late]]
+            kernel(*waits, *scratch, *refs[given : given + count], *outs)
 
         scratch = [pltpu.VMEM(a.shape, a.dtype) for a in raw]
         return pl.pallas_call(
@@ -124,7 +125,7 @@
     out_ref[:, 2 * width :] = dot_tn(split, same.astype(F32).astype(BF16)).astype(BF16)
 
 
-def weight_kernel(codes_in, codes_out, clip_in, range_in, clip_out, range_out, w_ref):
+def weight_kernel(wait_in, wait_out, codes_in, codes_out, clip_in, range_in, clip_out, range_out, w_ref):
     dp = lax.axis_index("dp")
     depth, third = codes_in.shape[1:]
     hidden = clip_in.shape[3]
@@ -135,6 +136,8 @@
         upper = sigmoid(clip_in[p, 0, own, :]) * range_in[p, 0, own, :]
         lower = sigmoid(clip_in[p, 1, own, :]) * range_in[p, 1, own, :]
         ends = placed(jnp.concatenate([(upper + lower) / 15.0, lower], axis=0), order)
+        if p == 0:
+            wait_in()
         for g in range(groups):
             packed = codes_in[p, g * GROUP : (g + 1) * GROUP, :]
             for j in range(PACK):
@@ -151,6 +154,7 @@
         step.append((upper_end + lower_end) / 15.0)
         lower.append(lower_end)
     row = lax.broadcasted_iota(jnp.int32, (CHUNK, 1), 0)
+    wait_out()
     for start in range(0, third, CHUNK):
         packed = codes_out[start : start + CHUNK, :]
         for j in range(PACK):
@@ -169,11 +173,10 @@
                 ]
 
 
-def set_kernel(experts, first, keep, *refs):
-    blocks = refs[0:4]
-    sides = refs[4:6]
-    earlier = refs[6:10]
-    refs = refs[6:] if first == 0 else refs[10:]
+def set_kernel(experts, first, keep, count, *refs):
+    blocks, sides = refs[:count], refs[count : count + 2]
+    earlier = refs[count + 2 : count + 6]
+    refs = refs[count + 2 :] if first == 0 else refs[count + 6 :]
     partials = refs[0:4]
     x_ref, s_ref, h_ref, g_ref = refs[4:8]
     rows, width = partials[0].shape
@@ -189,14 +192,16 @@
     if first and not keep:
         for old, new in zip(earlier, refs[4:8]):
             new[..., :first, :] = old[..., :first, :]
-    for i in range(4):
-        span = slice(first + i * rows, first + (i + 1) * rows)
-        x_ref[span, :] = blocks[i][:, :width]
-        beside = blocks[i][:, 2 * width :].astype(F32)
+    start = first
+    for block in blocks:
+        span = slice(start, start + block.shape[0])
+        start = span.stop
+        x_ref[span, :] = block[:, :width]
+        beside = block[:, 2 * width :].astype(F32)
         lane = lax.broadcasted_iota(jnp.int32, beside.shape, 1)
         keep = (lane == mine) | (lane == mine + experts) | (lane == mine + 2 * experts)
         scale = jnp.sum(jnp.where(keep, beside, 0.0), axis=1, keepdims=True)
-        s_ref[span, :] = (scale * blocks[i][:, width : 2 * width].astype(F32)).astype(BF16)
+        s_ref[span, :] = (scale * block[:, width : 2 * width].astype(F32)).astype(BF16)
     for j in range(PACK):
         cols = slice(j * third, (j + 1) * third)
         gate_pre = dot_nn(x_ref[here, spans[0]], sides[0][0, :, cols]) + dot_nn(
@@ -237,12 +242,12 @@
     both = 8 * rows
     stored = [((both, width), BF16), ((both, width), BF16), ((both, hidden), BF16), ((2, both, hidden), BF16)]
     out = calls.run(
-        functools.partial(set_kernel, experts, 0 if pair is None else 4 * rows, calls.keep),
+        functools.partial(set_kernel, experts, 0 if pair is None else 4 * rows, calls.keep, len(blocks)),
         "expert_set",
         [*blocks, *weights, *(pair or ())],
         [((rows, width), BF16)] * 4 + stored,
         after=after,
-        alias=None if pair is None else {6 + i: 4 + i for i in range(4)},
+        alias=None if pair is None else {len(blocks) + 2 + i: 4 + i for i in range(4)},
     )
     return list(out[:4]), list(out[4:])
 
@@ -430,54 +435,70 @@
     )[0]
 
     clips = (clip_in[0], range_in[0], clip_out[0].transpose(1, 0, 2), range_out[0].transpose(1, 0, 2))
-    (own_weights,) = calls.run(
-        weight_kernel,
-        "make_weights",
-        [],
-        [((3, depth, hidden), BF16)],
-        raw=(codes_in[0], codes_out[0], *clips),
-        after=(packed,),
-    )
-    weights = (own_weights, swap_core(own_weights))
-
     shapes = ((2, 2, depth // GROUP, hidden), (2, clip_out.shape[2], depth))
     sums = {True: None, False: None}
 
-    def quad(head, after):
+    def dequantized(*after):
+        (own_weights,) = calls.run(
+            weight_kernel,
+            "make_weights",
+            [],
+            [((3, depth, hidden), BF16)],
+            raw=(codes_in[0], codes_out[0], *clips),
+            late=2,
+            after=after,
+        )
+        return own_weights, swap_core(own_weights)
+
+    cut = rows // 2
+
+    def crossed(over_x, over_y):
+        return swap(over_x[:cut], 2), swap(over_y[cut:], 1)
+
+    def quad(head, weights, after):
         near, far = swap(head, 4), swap(head, 8)
         x0, y0 = swap(head, 1), swap(head, 2)
-        d0 = swap(x0, 2)
+        if weights is None:
+            weights = dequantized(head)
+        d0 = crossed(x0, y0)
         last = swap(far, 4)
-        ready = held(far, weights[1], x0, y0, d0, near)
+        ready = held(near, x0, y0, weights[1])
+        x1, y1 = swap(ready, 1), swap(ready, 2)
+        d1 = tuple(swap(part, 4) for part in d0)
+        ready = held(far, x1, y1, *d0, *d1)
         x2, y2 = swap(ready, 1), swap(ready, 2)
-        d2 = swap(y2, 1)
-        d1, d3 = swap(d0, 4), swap(d2, 4)
-        p0, stored = run_set(calls, (head, x0, y0, d0), weights, experts, after=after)
-        y3 = swap(held(last, x2, y2), 2)
-        x3 = swap(held(last, d2, p0[0]), 1)
-        p2, stored = run_set(calls, (far, x2, y2, d2), weights, experts, stored)
+        d2 = crossed(x2, y2)
+        d3 = tuple(swap(part, 4) for part in d2)
+        p0, stored = run_set(calls, (head, x0, y0, *d0), weights, experts, after=after)
+        p1, stored = run_set(calls, (near, x1, y1, *d1), weights, experts, stored)
+        ready = held(last, x2, y2, p0[0], p1[0])
+        x3, y3 = swap(ready, 1), swap(ready, 2)
         other = run_sums(calls, stored, weights, True, sums[True], shapes)
-        y1 = swap(held(near, y3), 2)
-        x1 = swap(held(near, x3, p2[0]), 1)
-        p3, later = run_set(calls, (last, x3, y3, d3), weights, experts, after=(other[0],))
-        x_sum0 = added(p0[1], swap(p0[3], 2))
+        p2, later = run_set(calls, (far, x2, y2, *d2), weights, experts, after=(other[0],))
+        p3, later = run_set(calls, (last, x3, y3, *d3), weights, experts, later)
+        sums[True] = run_sums(calls, later, weights, True, other, shapes)
+        y_sum3 = added(p3[2], swap(p3[3], 1), after=(sums[True][0],))
+        mine = run_sums(calls, stored, weights, False, sums[False], shapes, (y_sum3,))
         x_sum2 = added(p2[1], swap(p2[3], 2))
-        mine = run_sums(calls, stored, weights, False, sums[False], shapes, (p3[0],))
-        p1, later = run_set(
-            calls, (near, x1, y1, d1), weights, experts, later, (x_sum0, x_sum2, mine[0])
-        )
-        x_sum3 = added(p3[1], swap(p3[3], 2))
-        sums[True] = run_sums(calls, later, weights, True, other, shapes, (x_sum3,))
-        total3 = added(p3[0], swap(x_sum3, 1), swap(p3[2], 2))
+        total2 = added(p2[0], swap(x_sum2, 1), swap(p2[2], 2))
+        total3 = added(p3[0], swap(p3[1], 1), swap(y_sum3, 2), after=(mine[0],))
         sums[False] = run_sums(calls, later, weights, False, mine, shapes, (total3,))
         y_sum1 = added(p1[2], swap(p1[3], 1))
         total1 = added(p1[0], swap(p1[1], 1), swap(y_sum1, 2))
-        total2 = added(p2[0], swap(x_sum2, 1), swap(p2[2], 2), swap(total3, 4))
-        return p0[0], swap(x_sum0, 1), swap(p0[2], 2), swap(total1, 4), swap(total2, 8)
-
-    final, after = [], ()
+        x_sum0 = added(p0[1], swap(p0[3], 2))
+        parts = (
+            p0[0],
+            swap(x_sum0, 1),
+            swap(p0[2], 2),
+            swap(total1, 4),
+            swap(total2, 8),
+            swap(total3, 12),
+        )
+        return parts, weights
+
+    final, after, weights = [], (), None
     for base in range(0, experts, 16):
-        parts = quad(swap(packed, base) if base else packed, after)
+        parts, weights = quad(swap(packed, base) if base else packed, weights, after)
         final += [swap(added(*parts), base)] if base else parts
         after = (sums[False][0],)
     grad_tokens = added(*final, free=(0,))

time: 145 us -> 159 us (1.097); the launches traced: 145 us -> 157 us
  starting transfers between devices: 33.5 us -> 41 us
  waiting for transfers between devices: 53.8 us -> 56.9 us
    ppermute x30 -> x34, starting transfers between devices: 32.7 us -> 40.5 us  [swap(): lax.ppermute(array, 'expert', [(i, i ^ mask) for i in range(experts)])]
    ppermute x30 -> x34, waiting for transfers between devices: 52.5 us -> 56.9 us  [swap(): lax.ppermute(array, 'expert', [(i, i ^ mask) for i in range(experts)])]
  transfers between devices with their start and end apart: 33 -> 37, of which waited for: 14 -> 10; matrix products, arithmetic and copies ran while one was open for 0% -> 0% of each run, Pallas kernels for 34% -> 32%
where the time goes in v3:
time: 159 us; the launch traced here: 157 us
  Pallas kernels  57.5 us (36%)
  waiting for transfers between devices  56.9 us (36%)
  starting transfers between devices  41 us (26%)
    pallas_call x19, Pallas kernels, run(): pl.pallas_call(wrapped, in_specs=[ANYWHERE] * given + [INSIDE] * count +...  57.5 us
    ppermute x34, waiting for transfers between devices, swap(): lax.ppermute(array, 'expert', [(i, i ^ mask) for i in range(experts)])  56.9 us
    ppermute x34, starting transfers between devices, swap(): lax.ppermute(array, 'expert', [(i, i ^ mask) for i in range(experts)])  40.5 us
  transfers between devices with their start and end apart: 37, of which 10 were waited for; matrix products, arithmetic and copies ran while one was open for 0% of the time, Pallas kernels for 32%

profile of v3, /device:TPU:0, one launch (start us, length us, event | category | flops | bytes accessed | tf_op | source)
XLA Modules:
  0.0 156.6 jit_solution(18420645944125592867)
XLA Ops:
  0.6 1.3 pack_rows.1.refs_6_.refs_0_
  1.9 5.6 %make_weights.1.refs_5_.refs_4_ = bf16[3,1024,768]{2,1,0:T(8,128)(2,1)S(1)} custom-call(s32[2,1024,256]{2,1,0:T(8,128)} %bitcast.16, s32[256,1024]{1,0:T(8,128)} %bitcast.17, f32[2,2,16,768]{3,2,1,0:T(8,128)} %bitcast.18, f32[2,2,16,768]{3,2,1,0:T(8,128)} %bitcast.20, f32[6,2,2048]{2,1,0:T(2,128)} %bitcast.22, f32[6,2,2048]{2,1,0:T(2,128)} %bitcast.24, ...), custom_call_target="tpu_custom_call" | custom-call | tf_op jit(solution)/shard_map/make_weights/pallas_call | solution.py:91
  7.6 0.5 collective-permute-start.4
  8.1 2.6 %collective-permute-start.1 = (bf16[64,4224]{1,0:T(8,128)(2,1)S(1)}, bf16[64,4224]{1,0:T(8,128)(2,1)S(1)}, u32[]{:S(2)}, u32[]{:S(2)}) collective-permute-start(bf16[64,4224]{1,0:T(8,128)(2,1)S(1)} %pack_rows.1.refs_6_.refs_0_), channel_id=1, source_target_pairs={{0,4},{2,6},{4,0},{6,2},{8,12},{10,14},{12,8},{14,10},{16,20},{18,... | collective-permute-start | bytes 1622024 | tf_op jit(solution)/shard_map/ppermute | solution.py:406
  10.7 1.5 collective-permute-start
  12.2 1.6 %collective-permute-start.8 = (bf16[64,4224]{1,0:T(8,128)(2,1)S(1)}, bf16[64,4224]{1,0:T(8,128)(2,1)S(1)}, u32[]{:S(2)}, u32[]{:S(2)}) collective-permute-start(bf16[64,4224]{1,0:T(8,128)(2,1)S(1)} %pack_rows.1.refs_6_.refs_0_), channel_id=1, source_target_pairs={{0,8},{2,10},{4,12},{6,14},{8,0},{10,2},{12,4},{14,6},{16,24},{18,... | collective-permute-start | bytes 1622024 | tf_op jit(solution)/shard_map/ppermute | solution.py:406
  13.8 2.6 %collective-permute-start.17 = (bf16[64,4224]{1,0:T(8,128)(2,1)S(1)}, bf16[64,4224]{1,0:T(8,128)(2,1)S(1)}, u32[]{:S(2)}, u32[]{:S(2)}) collective-permute-start(bf16[64,4224]{1,0:T(8,128)(2,1)S(1)} %pack_rows.1.refs_6_.refs_0_), channel_id=1, source_target_pairs={{0,16},{2,18},{4,20},{6,22},{8,24},{10,26},{12,28},{14,30},{16,0},... | collective-permute-start | bytes 1622024 | tf_op jit(solution)/shard_map/ppermute | solution.py:406
  16.4 7.2 %collective-permute-done.1.refs_2_ = bf16[64,4224]{1,0:T(8,128)(2,1)S(1)} collective-permute-done((bf16[64,4224]{1,0:T(8,128)(2,1)S(1)}, bf16[64,4224]{1,0:T(8,128)(2,1)S(1)}, u32[]{:S(2)}, u32[]{:S(2)}) %collective-permute-start.1) | collective-permute-done | bytes 540704 | tf_op jit(solution)/shard_map/ppermute | solution.py:406
  23.6 1.8 %collective-permute-start.3 = (bf16[32,4224]{1,0:T(8,128)(2,1)S(1)}, bf16[32,4224]{1,0:T(8,128)(2,1)S(1)}, u32[]{:S(2)}, u32[]{:S(2)}) collective-permute-start(bf16[32,4224]{1,0:T(8,128)(2,1)S(1)} %slice.17), channel_id=1, source_target_pairs={{0,2},{2,0},{4,6},{6,4},{8,10},{10,8},{12,14},{14,12},{16,18},{18,... | collective-permute-start | bytes 811016 | tf_op jit(solution)/shard_map/ppermute | solution.py:406
  25.4 0.0 collective-permute-done.refs_1_
  25.4 1.6 %collective-permute-start.2 = (bf16[32,4224]{1,0:T(8,128)(2,1)S(1)}, bf16[32,4224]{1,0:T(8,128)(2,1)S(1)}, u32[]{:S(2)}, u32[]{:S(2)}) collective-permute-start(bf16[32,4224]{1,0:T(8,128)(2,1)S(1)} %slice.16), channel_id=1, source_target_pairs={{0,4},{2,6},{4,0},{6,2},{8,12},{10,14},{12,8},{14,10},{16,20},{18,... | collective-permute-start | bytes 811016 | tf_op jit(solution)/shard_map/ppermute | solution.py:406
  27.0 10.7 %collective-permute-done.8.refs_0_ = bf16[64,4224]{1,0:T(8,128)(2,1)S(1)} collective-permute-done((bf16[64,4224]{1,0:T(8,128)(2,1)S(1)}, bf16[64,4224]{1,0:T(8,128)(2,1)S(1)}, u32[]{:S(2)}, u32[]{:S(2)}) %collective-permute-start.8) | collective-permute-done | bytes 540704 | tf_op jit(solution)/shard_map/ppermute | solution.py:406
  37.8 0.6 collective-permute-start.10
  38.4 0.4 collective-permute-start.9
  38.8 2.0 %collective-permute-start.11 = (bf16[32,4224]{1,0:T(8,128)(2,1)S(1)}, bf16[32,4224]{1,0:T(8,128)(2,1)S(1)}, u32[]{:S(2)}, u32[]{:S(2)}) collective-permute-start(bf16[32,4224]{1,0:T(8,128)(2,1)S(1)} %collective-permute-done.2.refs_3_), channel_id=1, source_target_pairs={{0,8},{2,10},{4,12},{6,14},{8,0},{10,2},{12,4},{14,6},{16,24},{18,... | collective-permute-start | bytes 811016 | tf_op jit(solution)/shard_map/ppermute | solution.py:406
  40.8 7.3 %collective-permute-done.12.refs_4_.refs_6_ = bf16[32,4224]{1,0:T(8,128)(2,1)S(1)} collective-permute-done((bf16[32,4224]{1,0:T(8,128)(2,1)S(1)}, bf16[32,4224]{1,0:T(8,128)(2,1)S(1)}, u32[]{:S(2)}, u32[]{:S(2)}) %collective-permute-start.12) | collective-permute-done | bytes 270368 | tf_op jit(solution)/shard_map/ppermute | solution.py:406
  48.2 3.5 %collective-permute-done.11.refs_3_.refs_5_ = bf16[32,4224]{1,0:T(8,128)(2,1)S(1)} collective-permute-done((bf16[32,4224]{1,0:T(8,128)(2,1)S(1)}, bf16[32,4224]{1,0:T(8,128)(2,1)S(1)}, u32[]{:S(2)}, u32[]{:S(2)}) %collective-permute-start.11) | collective-permute-done | bytes 270368 | tf_op jit(solution)/shard_map/ppermute | solution.py:406
  51.7 1.4 collective-permute-start.19
  53.1 0.3 collective-permute-start.26
  53.4 1.5 collective-permute-start.18
  54.9 8.9 %collective-permute-done.19.refs_2_ = bf16[64,4224]{1,0:T(8,128)(2,1)S(1)} collective-permute-done((bf16[64,4224]{1,0:T(8,128)(2,1)S(1)}, bf16[64,4224]{1,0:T(8,128)(2,1)S(1)}, u32[]{:S(2)}, u32[]{:S(2)}) %collective-permute-start.19) | collective-permute-done | bytes 540704 | tf_op jit(solution)/shard_map/ppermute | solution.py:406
  63.8 1.1 collective-permute-start.21
  65.0 6.3 %expert_set.4 = (bf16[64,2048]{1,0:T(8,128)(2,1)S(1)}, bf16[64,2048]{1,0:T(8,128)(2,1)S(1)}, bf16[64,2048]{1,0:T(8,128)(2,1)S(1)}, bf16[64,2048]{1,0:T(8,128)(2,...) custom-call(bf16[64,4224]{1,0:T(8,128)(2,1)S(1)} %pack_rows.1.refs_6, ...), custom_call_target="tpu_custom_call" | custom-call | tf_op jit(solution)/shard_map/expert_set/pallas_call | solution.py:91
  71.2 6.1 %expert_set.5 = (bf16[64,2048]{1,0:T(8,128)(2,1)S(1)}, bf16[64,2048]{1,0:T(8,128)(2,1)S(1)}, bf16[64,2048]{1,0:T(8,128)(2,1)S(1)}, bf16[64,2048]{1,0:T(8,128)(2,...) custom-call(bf16[64,4224]{1,0:T(8,128)(2,1)S(1)} %collective-permute, ...), custom_call_target="tpu_custom_call", output_to_operand_aliasing={{4}: (7, {}), {5}: (8, {}), {6}: (9, {}), {7}: (10, {})} | custom-call | tf_op jit(solution)/shard_map/expert_set/pallas_call | solution.py:91
  77.4 1.6 %collective-permute-start.20 = (bf16[32,4224]{1,0:T(8,128)(2,1)S(1)}, bf16[32,4224]{1,0:T(8,128)(2,1)S(1)}, u32[]{:S(2)}, u32[]{:S(2)}) collective-permute-start(bf16[32,4224]{1,0:T(8,128)(2,1)S(1)} %slice.18), channel_id=1, source_target_pairs={{0,4},{2,6},{4,0},{6,2},{8,12},{10,14},{12,8},{14,10},{16,20},{18,... | collective-permute-start | bytes 811016 | tf_op jit(solution)/shard_map/ppermute | solution.py:406
  79.0 0.5 collective-permute-start.28
  79.5 1.2 collective-permute-start.27
  80.6 0.6 collective-permute-start.30
  81.2 5.7 %collective-permute-done.20.refs_3_ = bf16[32,4224]{1,0:T(8,128)(2,1)S(1)} collective-permute-done((bf16[32,4224]{1,0:T(8,128)(2,1)S(1)}, bf16[32,4224]{1,0:T(8,128)(2,1)S(1)}, u32[]{:S(2)}, u32[]{:S(2)}) %collective-permute-start.20) | collective-permute-done | bytes 270368 | tf_op jit(solution)/shard_map/ppermute | solution.py:406
  86.9 0.6 collective-permute-start.29
  87.4 1.1 collective-permute-start.14
  88.6 5.4 %group_sums.4 = (f32[2,2,8,768]{3,2,1,0:T(8,128)S(1)}, f32[2,6,1024]{2,1,0:T(8,128)S(1)}) custom-call(bf16[512,2048]{1,0:T(8,128)(2,1)S(1)} %get-tuple-element.57.refs_0_, bf16[512,2048]{1,0:T(8,128)(2,1)S(1)} %get-tuple-element.58.refs_1_, bf16[512,768]{1,0:T(8,128)(2,1)S(1)} %get-tuple-element.59.refs_2_, ...), custom_call_target="tpu_custom_call" | custom-call | tf_op jit(solution)/shard_map/group_sums/pallas_call | solution.py:91
  94.0 6.1 %expert_set.6 = (bf16[64,2048]{1,0:T(8,128)(2,1)S(1)}, bf16[64,2048]{1,0:T(8,128)(2,1)S(1)}, bf16[64,2048]{1,0:T(8,128)(2,1)S(1)}, bf16[64,2048]{1,0:T(8,128)(2,...) custom-call(bf16[64,4224]{1,0:T(8,128)(2,1)S(1)} %collective-permute, ...), custom_call_target="tpu_custom_call" | custom-call | tf_op jit(solution)/shard_map/expert_set/pallas_call | solution.py:91
  100.1 1.0 collective-permute-start.22
  101.1 6.3 %expert_set.7 = (bf16[64,2048]{1,0:T(8,128)(2,1)S(1)}, bf16[64,2048]{1,0:T(8,128)(2,1)S(1)}, bf16[64,2048]{1,0:T(8,128)(2,1)S(1)}, bf16[64,2048]{1,0:T(8,128)(2,...) custom-call(bf16[64,4224]{1,0:T(8,128)(2,1)S(1)} %collective-permute, ...), custom_call_target="tpu_custom_call", output_to_operand_aliasing={{4}: (7, {}), {5}: (8, {}), {6}: (9, {}), {7}: (10, {})} | custom-call | tf_op jit(solution)/shard_map/expert_set/pallas_call | solution.py:91
  107.4 1.6 collective-permute-start.32
  109.0 0.5 collective-permute-start.5
  109.5 1.1 collective-permute-start.13
  110.6 0.1 add_rows.9
  110.7 1.0 collective-permute-start.15
  111.7 1.1 collective-permute-start.24
  112.8 0.1 add_rows.11
  112.8 5.4 %group_sums.5 = (f32[2,2,8,768]{3,2,1,0:T(8,128)S(1)}, f32[2,6,1024]{2,1,0:T(8,128)S(1)}) custom-call(bf16[512,2048]{1,0:T(8,128)(2,1)S(1)} %get-tuple-element.74.refs_0_, bf16[512,2048]{1,0:T(8,128)(2,1)S(1)} %get-tuple-element.75.refs_1_, bf16[512,768]{1,0:T(8,128)(2,1)S(1)} %get-tuple-element.76.refs_2_, ...), custom_call_target="tpu_custom_call" | custom-call | tf_op jit(solution)/shard_map/group_sums/pallas_call | solution.py:91
  118.2 0.9 collective-permute-start.23
  119.2 0.1 add_rows.13.refs_5_
  119.2 1.2 collective-permute-start.31
  120.5 1.6 %collective-permute-done.13.refs_1_ = bf16[64,2048]{1,0:T(8,128)(2,1)S(1)} collective-permute-done((bf16[64,2048]{1,0:T(8,128)(2,1)S(1)}, bf16[64,2048]{1,0:T(8,128)(2,1)S(1)}, u32[]{:S(2)}, u32[]{:S(2)}) %collective-permute-start.13) | collective-permute-done | bytes 262176 | tf_op jit(solution)/shard_map/ppermute | solution.py:406
  122.0 1.3 collective-permute-start.33
  123.3 2.1 %collective-permute-done.24.refs_2_ = bf16[64,2048]{1,0:T(8,128)(2,1)S(1)} collective-permute-done((bf16[64,2048]{1,0:T(8,128)(2,1)S(1)}, bf16[64,2048]{1,0:T(8,128)(2,1)S(1)}, u32[]{:S(2)}, u32[]{:S(2)}) %collective-permute-start.24) | collective-permute-done | bytes 262176 | tf_op jit(solution)/shard_map/ppermute | solution.py:406
  125.4 0.1 add_rows.8
  125.5 0.1 add_rows.10
  125.6 0.6 collective-permute-start.7
  126.2 0.1 add_rows.12
  126.3 5.4 %group_sums.6 = (f32[2,2,8,768]{3,2,1,0:T(8,128)S(1)}, f32[2,6,1024]{2,1,0:T(8,128)S(1)}) custom-call(bf16[512,2048]{1,0:T(8,128)(2,1)S(1)} %get-tuple-element.57.refs_0_, bf16[512,2048]{1,0:T(8,128)(2,1)S(1)} %get-tuple-element.58.refs_1_, bf16[512,768]{1,0:T(8,128)(2,1)S(1)} %get-tuple-element.59.refs_2_, ...), custom_call_target="tpu_custom_call" | custom-call | tf_op jit(solution)/shard_map/group_sums/pallas_call | solution.py:91
  131.7 1.3 collective-permute-start.6
  133.0 1.2 collective-permute-start.16
  134.2 0.1 add_rows.14.refs_7_
  134.3 1.8 %collective-permute-start.25 = (bf16[64,2048]{1,0:T(8,128)(2,1)S(1)}, bf16[64,2048]{1,0:T(8,128)(2,1)S(1)}, u32[]{:S(2)}, u32[]{:S(2)}) collective-permute-start(bf16[64,2048]{1,0:T(8,128)(2,1)S(1)} %add_rows.12), channel_id=1, source_target_pairs={{0,16},{2,18},{4,20},{6,22},{8,24},{10,26},{12,28},{14,30},{16,0},... | collective-permute-start | bytes 786440 | tf_op jit(solution)/shard_map/ppermute | solution.py:406
  136.1 1.4 collective-permute-start.34
  137.6 5.4 %group_sums.7 = (f32[2,2,8,768]{3,2,1,0:T(8,128)S(1)}, f32[2,6,1024]{2,1,0:T(8,128)S(1)}) custom-call(bf16[512,2048]{1,0:T(8,128)(2,1)S(1)} %get-tuple-element.74.refs_0_, bf16[512,2048]{1,0:T(8,128)(2,1)S(1)} %get-tuple-element.75.refs_1_, bf16[512,768]{1,0:T(8,128)(2,1)S(1)} %get-tuple-element.76.refs_2_, ...), custom_call_target="tpu_custom_call" | custom-call | tf_op jit(solution)/shard_map/group_sums/pallas_call | solution.py:91
  142.9 2.9 %clip_gradients.1 = (f32[2,2,8,768]{3,2,1,0:T(8,128)}, f32[6,2,1024]{2,1,0:T(2,128)}) custom-call(f32[2,2,16,768]{3,2,1,0:T(8,128)} %bitcast.19, f32[2,2,16,768]{3,2,1,0:T(8,128)} %bitcast.21, f32[6,2,2048]{2,1,0:T(2,128)} %bitcast.23, f32[6,2,2048]{2,1,0:T(2,128)} %bitcast.25, f32[2,2,8,768]{3,2,1,0:T(8,128)S(1)} %get-tuple-element.82.refs_4_, ...), custom_call_target="tpu_custom_call" | custom-call | tf_op jit(solution)/shard_map/clip_gradients/pallas_call | solution.py:91
  145.8 0.1 collective-permute-done.16.refs_3_
  145.9 9.8 %collective-permute-done.25.refs_4_ = bf16[64,2048]{1,0:T(8,128)(2,1)S(1)} collective-permute-done((bf16[64,2048]{1,0:T(8,128)(2,1)S(1)}, bf16[64,2048]{1,0:T(8,128)(2,1)S(1)}, u32[]{:S(2)}, u32[]{:S(2)}) %collective-permute-start.25) | collective-permute-done | bytes 262176 | tf_op jit(solution)/shard_map/ppermute | solution.py:406
  155.7 0.9 add_rows.15
  (39 shorter events, 0.3 us)
Async XLA Ops:
  7.6 30.2 %collective-permute-start.4 = (bf16[3,1024,768]{2,1,0:T(8,128)(2,1)S(1)}, bf16[3,1024,768]{2,1,0:T(8,128)(2,1)S(1)}, u32[]{:S(2)}, u32[]{:S(2)}) collective-permute-start(bf16[3,1024,768]{2,1,0:T(8,128)(2,1)S(1)} %make_weights.1.refs_5_.refs_4_), channel_id=1, source_target_pairs={{0,1},{1,0},{2,3},{3,2},{4,5},{5,4},{6,7},{7,6},{8,9},{9,8},{10,11... | collective-permute-start | bytes 14155784 | tf_op jit(solution)/shard_map/ppermute | solution.py:409
  8.1 15.5 %collective-permute-start.1 = (bf16[64,4224]{1,0:T(8,128)(2,1)S(1)}, bf16[64,4224]{1,0:T(8,128)(2,1)S(1)}, u32[]{:S(2)}, u32[]{:S(2)}) collective-permute-start(bf16[64,4224]{1,0:T(8,128)(2,1)S(1)} %pack_rows.1.refs_6_.refs_0_), channel_id=1, source_target_pairs={{0,4},{2,6},{4,0},{6,2},{8,12},{10,14},{12,8},{14,10},{16,20},{18,... | collective-permute-start | bytes 1622024 | tf_op jit(solution)/shard_map/ppermute | solution.py:406
  10.7 14.7 %collective-permute-start = (bf16[64,4224]{1,0:T(8,128)(2,1)S(1)}, bf16[64,4224]{1,0:T(8,128)(2,1)S(1)}, u32[]{:S(2)}, u32[]{:S(2)}) collective-permute-start(bf16[64,4224]{1,0:T(8,128)(2,1)S(1)} %pack_rows.1.refs_6_.refs_0_), channel_id=1, source_target_pairs={{0,2},{2,0},{4,6},{6,4},{8,10},{10,8},{12,14},{14,12},{16,18},{18,... | collective-permute-start | bytes 1622024 | tf_op jit(solution)/shard_map/ppermute | solution.py:406
  12.2 25.5 %collective-permute-start.8 = (bf16[64,4224]{1,0:T(8,128)(2,1)S(1)}, bf16[64,4224]{1,0:T(8,128)(2,1)S(1)}, u32[]{:S(2)}, u32[]{:S(2)}) collective-permute-start(bf16[64,4224]{1,0:T(8,128)(2,1)S(1)} %pack_rows.1.refs_6_.refs_0_), channel_id=1, source_target_pairs={{0,8},{2,10},{4,12},{6,14},{8,0},{10,2},{12,4},{14,6},{16,24},{18,... | collective-permute-start | bytes 1622024 | tf_op jit(solution)/shard_map/ppermute | solution.py:406
  13.8 27.0 %collective-permute-start.17 = (bf16[64,4224]{1,0:T(8,128)(2,1)S(1)}, bf16[64,4224]{1,0:T(8,128)(2,1)S(1)}, u32[]{:S(2)}, u32[]{:S(2)}) collective-permute-start(bf16[64,4224]{1,0:T(8,128)(2,1)S(1)} %pack_rows.1.refs_6_.refs_0_), channel_id=1, source_target_pairs={{0,16},{2,18},{4,20},{6,22},{8,24},{10,26},{12,28},{14,30},{16,0},... | collective-permute-start | bytes 1622024 | tf_op jit(solution)/shard_map/ppermute | solution.py:406
  23.6 15.1 %collective-permute-start.3 = (bf16[32,4224]{1,0:T(8,128)(2,1)S(1)}, bf16[32,4224]{1,0:T(8,128)(2,1)S(1)}, u32[]{:S(2)}, u32[]{:S(2)}) collective-permute-start(bf16[32,4224]{1,0:T(8,128)(2,1)S(1)} %slice.17), channel_id=1, source_target_pairs={{0,2},{2,0},{4,6},{6,4},{8,10},{10,8},{12,14},{14,12},{16,18},{18,... | collective-permute-start | bytes 811016 | tf_op jit(solution)/shard_map/ppermute | solution.py:406
  25.4 13.3 %collective-permute-start.2 = (bf16[32,4224]{1,0:T(8,128)(2,1)S(1)}, bf16[32,4224]{1,0:T(8,128)(2,1)S(1)}, u32[]{:S(2)}, u32[]{:S(2)}) collective-permute-start(bf16[32,4224]{1,0:T(8,128)(2,1)S(1)} %slice.16), channel_id=1, source_target_pairs={{0,4},{2,6},{4,0},{6,2},{8,12},{10,14},{12,8},{14,10},{16,20},{18,... | collective-permute-start | bytes 811016 | tf_op jit(solution)/shard_map/ppermute | solution.py:406
  37.8 13.9 %collective-permute-start.10 = (bf16[64,4224]{1,0:T(8,128)(2,1)S(1)}, bf16[64,4224]{1,0:T(8,128)(2,1)S(1)}, u32[]{:S(2)}, u32[]{:S(2)}) collective-permute-start(bf16[64,4224]{1,0:T(8,128)(2,1)S(1)} %hold.3), channel_id=1, source_target_pairs={{0,4},{2,6},{4,0},{6,2},{8,12},{10,14},{12,8},{14,10},{16,20},{18,... | collective-permute-start | bytes 1622024 | tf_op jit(solution)/shard_map/ppermute | solution.py:406
  38.4 13.3 %collective-permute-start.9 = (bf16[64,4224]{1,0:T(8,128)(2,1)S(1)}, bf16[64,4224]{1,0:T(8,128)(2,1)S(1)}, u32[]{:S(2)}, u32[]{:S(2)}) collective-permute-start(bf16[64,4224]{1,0:T(8,128)(2,1)S(1)} %hold.3), channel_id=1, source_target_pairs={{0,2},{2,0},{4,6},{6,4},{8,10},{10,8},{12,14},{14,12},{16,18},{18,... | collective-permute-start | bytes 1622024 | tf_op jit(solution)/shard_map/ppermute | solution.py:406
  38.7 9.4 %collective-permute-start.12 = (bf16[32,4224]{1,0:T(8,128)(2,1)S(1)}, bf16[32,4224]{1,0:T(8,128)(2,1)S(1)}, u32[]{:S(2)}, u32[]{:S(2)}) collective-permute-start(bf16[32,4224]{1,0:T(8,128)(2,1)S(1)} %collective-permute-done.3.refs_4_), channel_id=1, source_target_pairs={{0,8},{2,10},{4,12},{6,14},{8,0},{10,2},{12,4},{14,6},{16,24},{18,... | collective-permute-start | bytes 811016 | tf_op jit(solution)/shard_map/ppermute | solution.py:406
  38.8 12.9 %collective-permute-start.11 = (bf16[32,4224]{1,0:T(8,128)(2,1)S(1)}, bf16[32,4224]{1,0:T(8,128)(2,1)S(1)}, u32[]{:S(2)}, u32[]{:S(2)}) collective-permute-start(bf16[32,4224]{1,0:T(8,128)(2,1)S(1)} %collective-permute-done.2.refs_3_), channel_id=1, source_target_pairs={{0,8},{2,10},{4,12},{6,14},{8,0},{10,2},{12,4},{14,6},{16,24},{18,... | collective-permute-start | bytes 811016 | tf_op jit(solution)/shard_map/ppermute | solution.py:406
  51.7 12.1 %collective-permute-start.19 = (bf16[64,4224]{1,0:T(8,128)(2,1)S(1)}, bf16[64,4224]{1,0:T(8,128)(2,1)S(1)}, u32[]{:S(2)}, u32[]{:S(2)}) collective-permute-start(bf16[64,4224]{1,0:T(8,128)(2,1)S(1)} %hold.4), channel_id=1, source_target_pairs={{0,4},{2,6},{4,0},{6,2},{8,12},{10,14},{12,8},{14,10},{16,20},{18,... | collective-permute-start | bytes 1622024 | tf_op jit(solution)/shard_map/ppermute | solution.py:406
  53.1 11.8 %collective-permute-start.26 = (bf16[64,4224]{1,0:T(8,128)(2,1)S(1)}, bf16[64,4224]{1,0:T(8,128)(2,1)S(1)}, u32[]{:S(2)}, u32[]{:S(2)}) collective-permute-start(bf16[64,4224]{1,0:T(8,128)(2,1)S(1)} %collective-permute-done.17.refs_0_), channel_id=1, source_target_pairs={{0,8},{2,10},{4,12},{6,14},{8,0},{10,2},{12,4},{14,6},{16,24},{18,... | collective-permute-start | bytes 1622024 | tf_op jit(solution)/shard_map/ppermute | solution.py:406
  53.4 23.9 %collective-permute-start.18 = (bf16[64,4224]{1,0:T(8,128)(2,1)S(1)}, bf16[64,4224]{1,0:T(8,128)(2,1)S(1)}, u32[]{:S(2)}, u32[]{:S(2)}) collective-permute-start(bf16[64,4224]{1,0:T(8,128)(2,1)S(1)} %hold.4), channel_id=1, source_target_pairs={{0,2},{2,0},{4,6},{6,4},{8,10},{10,8},{12,14},{14,12},{16,18},{18,... | collective-permute-start | bytes 1622024 | tf_op jit(solution)/shard_map/ppermute | solution.py:406
  63.8 16.8 %collective-permute-start.21 = (bf16[32,4224]{1,0:T(8,128)(2,1)S(1)}, bf16[32,4224]{1,0:T(8,128)(2,1)S(1)}, u32[]{:S(2)}, u32[]{:S(2)}) collective-permute-start(bf16[32,4224]{1,0:T(8,128)(2,1)S(1)} %slice.19), channel_id=1, source_target_pairs={{0,2},{2,0},{4,6},{6,4},{8,10},{10,8},{12,14},{14,12},{16,18},{18,... | collective-permute-start | bytes 811016 | tf_op jit(solution)/shard_map/ppermute | solution.py:406
  77.4 9.5 %collective-permute-start.20 = (bf16[32,4224]{1,0:T(8,128)(2,1)S(1)}, bf16[32,4224]{1,0:T(8,128)(2,1)S(1)}, u32[]{:S(2)}, u32[]{:S(2)}) collective-permute-start(bf16[32,4224]{1,0:T(8,128)(2,1)S(1)} %slice.18), channel_id=1, source_target_pairs={{0,4},{2,6},{4,0},{6,2},{8,12},{10,14},{12,8},{14,10},{16,20},{18,... | collective-permute-start | bytes 811016 | tf_op jit(solution)/shard_map/ppermute | solution.py:406
  79.0 22.1 %collective-permute-start.28 = (bf16[64,4224]{1,0:T(8,128)(2,1)S(1)}, bf16[64,4224]{1,0:T(8,128)(2,1)S(1)}, u32[]{:S(2)}, u32[]{:S(2)}) collective-permute-start(bf16[64,4224]{1,0:T(8,128)(2,1)S(1)} %hold.5), channel_id=1, source_target_pairs={{0,4},{2,6},{4,0},{6,2},{8,12},{10,14},{12,8},{14,10},{16,20},{18,... | collective-permute-start | bytes 1622024 | tf_op jit(solution)/shard_map/ppermute | solution.py:406
  79.5 21.6 %collective-permute-start.27 = (bf16[64,4224]{1,0:T(8,128)(2,1)S(1)}, bf16[64,4224]{1,0:T(8,128)(2,1)S(1)}, u32[]{:S(2)}, u32[]{:S(2)}) collective-permute-start(bf16[64,4224]{1,0:T(8,128)(2,1)S(1)} %hold.5), channel_id=1, source_target_pairs={{0,2},{2,0},{4,6},{6,4},{8,10},{10,8},{12,14},{14,12},{16,18},{18,... | collective-permute-start | bytes 1622024 | tf_op jit(solution)/shard_map/ppermute | solution.py:406
  80.6 19.5 %collective-permute-start.30 = (bf16[32,4224]{1,0:T(8,128)(2,1)S(1)}, bf16[32,4224]{1,0:T(8,128)(2,1)S(1)}, u32[]{:S(2)}, u32[]{:S(2)}) collective-permute-start(bf16[32,4224]{1,0:T(8,128)(2,1)S(1)} %collective-permute-done.21.refs_4_), channel_id=1, source_target_pairs={{0,8},{2,10},{4,12},{6,14},{8,0},{10,2},{12,4},{14,6},{16,24},{18,... | collective-permute-start | bytes 811016 | tf_op jit(solution)/shard_map/ppermute | solution.py:406
  86.9 14.2 %collective-permute-start.29 = (bf16[32,4224]{1,0:T(8,128)(2,1)S(1)}, bf16[32,4224]{1,0:T(8,128)(2,1)S(1)}, u32[]{:S(2)}, u32[]{:S(2)}) collective-permute-start(bf16[32,4224]{1,0:T(8,128)(2,1)S(1)} %collective-permute-done.20.refs_3_), channel_id=1, source_target_pairs={{0,8},{2,10},{4,12},{6,14},{8,0},{10,2},{12,4},{14,6},{16,24},{18,... | collective-permute-start | bytes 811016 | tf_op jit(solution)/shard_map/ppermute | solution.py:406
  87.4 23.2 %collective-permute-start.14 = (bf16[64,2048]{1,0:T(8,128)(2,1)S(1)}, bf16[64,2048]{1,0:T(8,128)(2,1)S(1)}, u32[]{:S(2)}, u32[]{:S(2)}) collective-permute-start(bf16[64,2048]{1,0:T(8,128)(2,1)S(1)} %get-tuple-element.56), channel_id=1, source_target_pairs={{0,2},{2,0},{4,6},{6,4},{8,10},{10,8},{12,14},{14,12},{16,18},{18,... | collective-permute-start | bytes 786440 | tf_op jit(solution)/shard_map/ppermute | solution.py:406
  100.1 11.6 %collective-permute-start.22 = (bf16[64,2048]{1,0:T(8,128)(2,1)S(1)}, bf16[64,2048]{1,0:T(8,128)(2,1)S(1)}, u32[]{:S(2)}, u32[]{:S(2)}) collective-permute-start(bf16[64,2048]{1,0:T(8,128)(2,1)S(1)} %get-tuple-element.64), channel_id=1, source_target_pairs={{0,4},{2,6},{4,0},{6,2},{8,12},{10,14},{12,8},{14,10},{16,20},{18,... | collective-permute-start | bytes 786440 | tf_op jit(solution)/shard_map/ppermute | solution.py:406
  107.4 10.8 %collective-permute-start.32 = (bf16[64,2048]{1,0:T(8,128)(2,1)S(1)}, bf16[64,2048]{1,0:T(8,128)(2,1)S(1)}, u32[]{:S(2)}, u32[]{:S(2)}) collective-permute-start(bf16[64,2048]{1,0:T(8,128)(2,1)S(1)} %get-tuple-element.73), channel_id=1, source_target_pairs={{0,2},{2,0},{4,6},{6,4},{8,10},{10,8},{12,14},{14,12},{16,18},{18,... | collective-permute-start | bytes 786440 | tf_op jit(solution)/shard_map/ppermute | solution.py:406
  109.0 10.3 %collective-permute-start.5 = (bf16[64,2048]{1,0:T(8,128)(2,1)S(1)}, bf16[64,2048]{1,0:T(8,128)(2,1)S(1)}, u32[]{:S(2)}, u32[]{:S(2)}) collective-permute-start(bf16[64,2048]{1,0:T(8,128)(2,1)S(1)} %get-tuple-element.47), channel_id=1, source_target_pairs={{0,4},{2,6},{4,0},{6,2},{8,12},{10,14},{12,8},{14,10},{16,20},{18,... | collective-permute-start | bytes 786440 | tf_op jit(solution)/shard_map/ppermute | solution.py:406
  109.5 12.6 %collective-permute-start.13 = (bf16[64,2048]{1,0:T(8,128)(2,1)S(1)}, bf16[64,2048]{1,0:T(8,128)(2,1)S(1)}, u32[]{:S(2)}, u32[]{:S(2)}) collective-permute-start(bf16[64,2048]{1,0:T(8,128)(2,1)S(1)} %get-tuple-element.54), channel_id=1, source_target_pairs={{0,2},{2,0},{4,6},{6,4},{8,10},{10,8},{12,14},{14,12},{16,18},{18,... | collective-permute-start | bytes 786440 | tf_op jit(solution)/shard_map/ppermute | solution.py:406
  110.7 12.6 %collective-permute-start.15 = (bf16[64,2048]{1,0:T(8,128)(2,1)S(1)}, bf16[64,2048]{1,0:T(8,128)(2,1)S(1)}, u32[]{:S(2)}, u32[]{:S(2)}) collective-permute-start(bf16[64,2048]{1,0:T(8,128)(2,1)S(1)} %add_rows.9), channel_id=1, source_target_pairs={{0,4},{2,6},{4,0},{6,2},{8,12},{10,14},{12,8},{14,10},{16,20},{18,... | collective-permute-start | bytes 786440 | tf_op jit(solution)/shard_map/ppermute | solution.py:406
  111.7 13.8 %collective-permute-start.24 = (bf16[64,2048]{1,0:T(8,128)(2,1)S(1)}, bf16[64,2048]{1,0:T(8,128)(2,1)S(1)}, u32[]{:S(2)}, u32[]{:S(2)}) collective-permute-start(bf16[64,2048]{1,0:T(8,128)(2,1)S(1)} %get-tuple-element.65), channel_id=1, source_target_pairs={{0,4},{2,6},{4,0},{6,2},{8,12},{10,14},{12,8},{14,10},{16,20},{18,... | collective-permute-start | bytes 786440 | tf_op jit(solution)/shard_map/ppermute | solution.py:406
  118.2 7.4 %collective-permute-start.23 = (bf16[64,2048]{1,0:T(8,128)(2,1)S(1)}, bf16[64,2048]{1,0:T(8,128)(2,1)S(1)}, u32[]{:S(2)}, u32[]{:S(2)}) collective-permute-start(bf16[64,2048]{1,0:T(8,128)(2,1)S(1)} %add_rows.11), channel_id=1, source_target_pairs={{0,2},{2,0},{4,6},{6,4},{8,10},{10,8},{12,14},{14,12},{16,18},{18,... | collective-permute-start | bytes 786440 | tf_op jit(solution)/shard_map/ppermute | solution.py:406
  119.2 12.4 %collective-permute-start.31 = (bf16[64,2048]{1,0:T(8,128)(2,1)S(1)}, bf16[64,2048]{1,0:T(8,128)(2,1)S(1)}, u32[]{:S(2)}, u32[]{:S(2)}) collective-permute-start(bf16[64,2048]{1,0:T(8,128)(2,1)S(1)} %get-tuple-element.71), channel_id=1, source_target_pairs={{0,2},{2,0},{4,6},{6,4},{8,10},{10,8},{12,14},{14,12},{16,18},{18,... | collective-permute-start | bytes 786440 | tf_op jit(solution)/shard_map/ppermute | solution.py:406
  122.0 11.0 %collective-permute-start.33 = (bf16[64,2048]{1,0:T(8,128)(2,1)S(1)}, bf16[64,2048]{1,0:T(8,128)(2,1)S(1)}, u32[]{:S(2)}, u32[]{:S(2)}) collective-permute-start(bf16[64,2048]{1,0:T(8,128)(2,1)S(1)} %add_rows.13.refs_5_), channel_id=1, source_target_pairs={{0,4},{2,6},{4,0},{6,2},{8,12},{10,14},{12,8},{14,10},{16,20},{18,... | collective-permute-start | bytes 786440 | tf_op jit(solution)/shard_map/ppermute | solution.py:406
  123.3 12.8 %collective-permute-start.35 = (f32[2,2,8,768]{3,2,1,0:T(8,128)S(1)}, f32[2,2,8,768]{3,2,1,0:T(8,128)S(1)}, u32[]{:S(2)}, u32[]{:S(2)}) collective-permute-start(f32[2,2,8,768]{3,2,1,0:T(8,128)S(1)} %get-tuple-element.79.refs_2_), channel_id=1, source_target_pairs={{0,1},{1,0},{2,3},{3,2},{4,5},{5,4},{6,7},{7,6},{8,9},{9,8},{10,11... | collective-permute-start | bytes 294920 | tf_op jit(solution)/shard_map/ppermute | solution.py:409
  125.4 8.9 %collective-permute-start.36 = (f32[2,6,1024]{2,1,0:T(8,128)S(1)}, f32[2,6,1024]{2,1,0:T(8,128)S(1)}, u32[]{:S(2)}, u32[]{:S(2)}) collective-permute-start(f32[2,6,1024]{2,1,0:T(8,128)S(1)} %get-tuple-element.84), channel_id=1, source_target_pairs={{0,1},{1,0},{2,3},{3,2},{4,5},{5,4},{6,7},{7,6},{8,9},{9,8},{10,11... | collective-permute-start | bytes 147464 | tf_op jit(solution)/shard_map/ppermute | solution.py:409
  125.6 20.2 %collective-permute-start.7 = (bf16[64,2048]{1,0:T(8,128)(2,1)S(1)}, bf16[64,2048]{1,0:T(8,128)(2,1)S(1)}, u32[]{:S(2)}, u32[]{:S(2)}) collective-permute-start(bf16[64,2048]{1,0:T(8,128)(2,1)S(1)} %get-tuple-element.48), channel_id=1, source_target_pairs={{0,4},{2,6},{4,0},{6,2},{8,12},{10,14},{12,8},{14,10},{16,20},{18,... | collective-permute-start | bytes 786440 | tf_op jit(solution)/shard_map/ppermute | solution.py:406
  131.7 14.2 %collective-permute-start.6 = (bf16[64,2048]{1,0:T(8,128)(2,1)S(1)}, bf16[64,2048]{1,0:T(8,128)(2,1)S(1)}, u32[]{:S(2)}, u32[]{:S(2)}) collective-permute-start(bf16[64,2048]{1,0:T(8,128)(2,1)S(1)} %add_rows.8), channel_id=1, source_target_pairs={{0,2},{2,0},{4,6},{6,4},{8,10},{10,8},{12,14},{14,12},{16,18},{18,... | collective-permute-start | bytes 786440 | tf_op jit(solution)/shard_map/ppermute | solution.py:406
  133.0 12.9 %collective-permute-start.16 = (bf16[64,2048]{1,0:T(8,128)(2,1)S(1)}, bf16[64,2048]{1,0:T(8,128)(2,1)S(1)}, u32[]{:S(2)}, u32[]{:S(2)}) collective-permute-start(bf16[64,2048]{1,0:T(8,128)(2,1)S(1)} %add_rows.10), channel_id=1, source_target_pairs={{0,8},{2,10},{4,12},{6,14},{8,0},{10,2},{12,4},{14,6},{16,24},{18,... | collective-permute-start | bytes 786440 | tf_op jit(solution)/shard_map/ppermute | solution.py:406
  134.3 21.4 %collective-permute-start.25 = (bf16[64,2048]{1,0:T(8,128)(2,1)S(1)}, bf16[64,2048]{1,0:T(8,128)(2,1)S(1)}, u32[]{:S(2)}, u32[]{:S(2)}) collective-permute-start(bf16[64,2048]{1,0:T(8,128)(2,1)S(1)} %add_rows.12), channel_id=1, source_target_pairs={{0,16},{2,18},{4,20},{6,22},{8,24},{10,26},{12,28},{14,30},{16,0},... | collective-permute-start | bytes 786440 | tf_op jit(solution)/shard_map/ppermute | solution.py:406
  136.1 19.6 %collective-permute-start.34 = (bf16[64,2048]{1,0:T(8,128)(2,1)S(1)}, bf16[64,2048]{1,0:T(8,128)(2,1)S(1)}, u32[]{:S(2)}, u32[]{:S(2)}) collective-permute-start(bf16[64,2048]{1,0:T(8,128)(2,1)S(1)} %add_rows.14.refs_7_), channel_id=1, source_target_pairs={{0,24},{2,26},{4,28},{6,30},{8,16},{10,18},{12,20},{14,22},{16,8},... | collective-permute-start | bytes 786440 | tf_op jit(solution)/shard_map/ppermute | solution.py:406

commit v4 on v3

--- a/solution.py
+++ b/solution.py
@@ -13,7 +13,6 @@
 TILE = 256
 LIMIT = 24 * 1024 * 1024
 SMALL = 8 * 1024 * 1024
-TINY = 1024 * 1024
 F32 = jnp.float32
 BF16 = jnp.bfloat16
 
@@ -71,7 +70,7 @@
     def out(self, shape, dtype):
         return pltpu.VMEM(shape, dtype) if self.keep else jax.ShapeDtypeStruct(shape, dtype)
 
-    def run(self, kernel, name, inputs, outputs, after=(), alias=None, limit=LIMIT, raw=(), late=0, free=()):
+    def run(self, kernel, name, inputs, outputs, after=(), alias=None, limit=LIMIT, raw=(), free=(), flops=0):
         count, given = len(inputs), len(raw)
 
         def wrapped(*refs):
@@ -82,10 +81,9 @@
             ]
             for copy in copies:
                 copy.start()
-            for copy in copies[late:]:
+            for copy in copies:
                 copy.wait()
-            waits = [copy.wait for copy in copies[:late]]
-            kernel(*waits, *scratch, *refs[given : given + count], *outs)
+            kernel(*scratch, *refs[given : given + count], *outs)
 
         scratch = [pltpu.VMEM(a.shape, a.dtype) for a in raw]
         return pl.pallas_call(
@@ -99,7 +97,7 @@
             scratch_shapes=scratch + ([pltpu.SemaphoreType.DMA((given,))] if raw else []),
             input_output_aliases=alias or {},
             compiler_params=pltpu.CompilerParams(vmem_limit_bytes=limit),
-            cost_estimate=pl.CostEstimate(flops=0, bytes_accessed=0, transcendentals=0),
+            cost_estimate=pl.CostEstimate(flops=int(flops), bytes_accessed=0, transcendentals=0),
             name=name,
         )(*[pltpu.with_memory_space_constraint(a, pltpu.HBM) for a in raw], *[self.pin(a) for a in inputs], *after)
 
@@ -125,7 +123,7 @@
     out_ref[:, 2 * width :] = dot_tn(split, same.astype(F32).astype(BF16)).astype(BF16)
 
 
-def weight_kernel(wait_in, wait_out, codes_in, codes_out, clip_in, range_in, clip_out, range_out, w_ref):
+def weight_kernel(codes_in, codes_out, clip_in, range_in, clip_out, range_out, w_ref):
     dp = lax.axis_index("dp")
     depth, third = codes_in.shape[1:]
     hidden = clip_in.shape[3]
@@ -136,8 +134,6 @@
         upper = sigmoid(clip_in[p, 0, own, :]) * range_in[p, 0, own, :]
         lower = sigmoid(clip_in[p, 1, own, :]) * range_in[p, 1, own, :]
         ends = placed(jnp.concatenate([(upper + lower) / 15.0, lower], axis=0), order)
-        if p == 0:
-            wait_in()
         for g in range(groups):
             packed = codes_in[p, g * GROUP : (g + 1) * GROUP, :]
             for j in range(PACK):
@@ -154,7 +150,6 @@
         step.append((upper_end + lower_end) / 15.0)
         lower.append(lower_end)
     row = lax.broadcasted_iota(jnp.int32, (CHUNK, 1), 0)
-    wait_out()
     for start in range(0, third, CHUNK):
         packed = codes_out[start : start + CHUNK, :]
         for j in range(PACK):
@@ -247,6 +242,7 @@
         [*blocks, *weights, *(pair or ())],
         [((rows, width), BF16)] * 4 + stored,
         after=after,
+        flops=40 * rows * width * hidden,
         alias=None if pair is None else {len(blocks) + 2 + i: 4 + i for i in range(4)},
     )
     return list(out[:4]), list(out[4:])
@@ -330,6 +326,7 @@
         [*stored, side, *(before or ())],
         [(shape, F32) for shape in shapes],
         after=after,
+        flops=24 * stored[0].shape[0] * weights[0].size // 8,
     )
 
 
@@ -379,8 +376,12 @@
     refs[-1][...] = total.astype(refs[-1].dtype)
 
 
-def hold_kernel(*refs):
-    pass
+def part_kernel(first, old, new):
+    new[...] = old[first : first + new.shape[0], :]
+
+
+def hold_kernel(old, new):
+    new[...] = old[...]
 
 
 def body(
@@ -414,16 +415,7 @@
         )[0]
 
     def held(array, *after):
-        return pl.pallas_call(
-            hold_kernel,
-            in_specs=[ANYWHERE] * (1 + len(after)),
-            out_specs=ANYWHERE,
-            out_shape=calls.out(array.shape, array.dtype),
-            input_output_aliases={0: 0},
-            compiler_params=pltpu.CompilerParams(vmem_limit_bytes=TINY),
-            cost_estimate=pl.CostEstimate(flops=0, bytes_accessed=0, transcendentals=0),
-            name="hold",
-        )(calls.pin(array), *after)
+        return calls.run(hold_kernel, "hold", [array], [(array.shape, array.dtype)], after, limit=SMALL)[0]
 
     packed = calls.run(
         functools.partial(pack_kernel, experts),
@@ -445,53 +437,59 @@
             [],
             [((3, depth, hidden), BF16)],
             raw=(codes_in[0], codes_out[0], *clips),
-            late=2,
             after=after,
         )
         return own_weights, swap_core(own_weights)
 
     cut = rows // 2
 
-    def crossed(over_x, over_y):
-        return swap(over_x[:cut], 2), swap(over_y[cut:], 1)
+    def part(array, first, after):
+        shape = (rows - cut if first else cut, array.shape[1])
+        return calls.run(
+            functools.partial(part_kernel, first), "part", [array], [(shape, array.dtype)], after, limit=SMALL
+        )[0]
+
+    def crossed(over_x, over_y, *after):
+        return swap(part(over_x, 0, after), 2), swap(part(over_y, cut, after), 1)
 
     def quad(head, weights, after):
-        near, far = swap(head, 4), swap(head, 8)
+        near = swap(head, 4)
         x0, y0 = swap(head, 1), swap(head, 2)
+        far = swap(near, 12)
         if weights is None:
             weights = dequantized(head)
         d0 = crossed(x0, y0)
-        last = swap(far, 4)
         ready = held(near, x0, y0, weights[1])
         x1, y1 = swap(ready, 1), swap(ready, 2)
-        d1 = tuple(swap(part, 4) for part in d0)
-        ready = held(far, x1, y1, *d0, *d1)
-        x2, y2 = swap(ready, 1), swap(ready, 2)
-        d2 = crossed(x2, y2)
-        d3 = tuple(swap(part, 4) for part in d2)
+        d1 = tuple(swap(half, 4) for half in d0)
         p0, stored = run_set(calls, (head, x0, y0, *d0), weights, experts, after=after)
+        ready = held(far, x1, y1, *d1, p0[0])
+        x2, y2, last = swap(ready, 1), swap(ready, 2), swap(ready, 4)
         p1, stored = run_set(calls, (near, x1, y1, *d1), weights, experts, stored)
-        ready = held(last, x2, y2, p0[0], p1[0])
+        ready = held(last, x2, y2)
         x3, y3 = swap(ready, 1), swap(ready, 2)
         other = run_sums(calls, stored, weights, True, sums[True], shapes)
-        p2, later = run_set(calls, (far, x2, y2, *d2), weights, experts, after=(other[0],))
-        p3, later = run_set(calls, (last, x3, y3, *d3), weights, experts, later)
-        sums[True] = run_sums(calls, later, weights, True, other, shapes)
+        d2 = crossed(x2, y2, other[0])
+        d3 = tuple(swap(half, 4) for half in d2)
+        p2, later = run_set(calls, (far, x2, y2, *d2), weights, experts)
+        mine = run_sums(calls, stored, weights, False, sums[False], shapes, (p2[0],))
+        x_sum2 = added(p2[1], swap(p2[3], 2))
+        p3, later = run_set(calls, (last, x3, y3, *d3), weights, experts, later, (x_sum2,))
+        total2 = added(p2[0], swap(x_sum2, 1), swap(p2[2], 2))
+        sums[True] = run_sums(calls, later, weights, True, other, shapes, (total2,))
         y_sum3 = added(p3[2], swap(p3[3], 1), after=(sums[True][0],))
-        mine = run_sums(calls, stored, weights, False, sums[False], shapes, (y_sum3,))
-        x_sum2 = added(p2[1], swap(p2[3], 2))
-        total2 = added(p2[0], swap(x_sum2, 1), swap(p2[2], 2))
-        total3 = added(p3[0], swap(p3[1], 1), swap(y_sum3, 2), after=(mine[0],))
+        far_sum = swap(total2, 8)
+        total3 = added(p3[0], swap(p3[1], 1), swap(y_sum3, 2), after=(far_sum,))
         sums[False] = run_sums(calls, later, weights, False, mine, shapes, (total3,))
-        y_sum1 = added(p1[2], swap(p1[3], 1))
+        y_sum1 = added(p1[2], swap(held(p1[3], x3, y3), 1))
         total1 = added(p1[0], swap(p1[1], 1), swap(y_sum1, 2))
-        x_sum0 = added(p0[1], swap(p0[3], 2))
+        x_sum0 = added(p0[1], swap(held(p0[3], x3, y3), 2))
         parts = (
             p0[0],
             swap(x_sum0, 1),
             swap(p0[2], 2),
             swap(total1, 4),
-            swap(total2, 8),
+            far_sum,
             swap(total3, 12),
         )
         return parts, weights

time: 159 us -> 154 us (0.969); the launches traced: 157 us -> 154 us
  waiting for transfers between devices: 56.9 us -> 50.9 us
  starting transfers between devices: 41 us -> 45.7 us
    ppermute x34, waiting for transfers between devices: 56.9 us -> 50.9 us  [swap(): lax.ppermute(array, 'expert', [(i, i ^ mask) for i in range(experts)])]
    ppermute x34, starting transfers between devices: 40.5 us -> 45.1 us  [swap(): lax.ppermute(array, 'expert', [(i, i ^ mask) for i in range(experts)])]
    pallas_call x19 -> x28, Pallas kernels: 57.5 us -> 56.8 us  [run(): pl.pallas_call(wrapped, in_specs=[ANYWHERE] * given + [INSIDE] * count +...]
  transfers between devices with their start and end apart: 37 -> 37, of which waited for: 10 -> 12; matrix products, arithmetic and copies ran while one was open for 0% -> 0% of each run, Pallas kernels for 32% -> 32%
where the time goes in v4:
time: 154 us
  Pallas kernels  56.8 us (37%)
  waiting for transfers between devices  50.9 us (33%)
  starting transfers between devices  45.7 us (30%)
    pallas_call x28, Pallas kernels, run(): pl.pallas_call(wrapped, in_specs=[ANYWHERE] * given + [INSIDE] * count +...  56.8 us
    ppermute x34, waiting for transfers between devices, swap(): lax.ppermute(array, 'expert', [(i, i ^ mask) for i in range(experts)])  50.9 us
    ppermute x34, starting transfers between devices, swap(): lax.ppermute(array, 'expert', [(i, i ^ mask) for i in range(experts)])  45.1 us
  transfers between devices with their start and end apart: 37, of which 12 were waited for; matrix products, arithmetic and copies ran while one was open for 0% of the time, Pallas kernels for 32%

profile of v4, /device:TPU:0, one launch (start us, length us, event | category | flops | bytes accessed | tf_op | source)
XLA Modules:
  0.0 154.3 jit_solution(15331135851308476978)
XLA Ops:
  0.6 1.3 pack_rows.1.refs_6_.refs_0_
  1.9 4.7 %make_weights.1.refs_5_.refs_4_ = bf16[3,1024,768]{2,1,0:T(8,128)(2,1)S(1)} custom-call(s32[2,1024,256]{2,1,0:T(8,128)} %bitcast.16, s32[256,1024]{1,0:T(8,128)} %bitcast.17, f32[2,2,16,768]{3,2,1,0:T(8,128)} %bitcast.18, f32[2,2,16,768]{3,2,1,0:T(8,128)} %bitcast.20, f32[6,2,2048]{2,1,0:T(2,128)} %bitcast.22, f32[6,2,2048]{2,1,0:T(2,128)} %bitcast.24, ...), custom_call_target="tpu_custom_call" | custom-call | tf_op jit(solution)/shard_map/make_weights/pallas_call | solution.py:89
  6.6 0.5 collective-permute-start.4
  7.1 2.6 %collective-permute-start.1 = (bf16[64,4224]{1,0:T(8,128)(2,1)S(1)}, bf16[64,4224]{1,0:T(8,128)(2,1)S(1)}, u32[]{:S(2)}, u32[]{:S(2)}) collective-permute-start(bf16[64,4224]{1,0:T(8,128)(2,1)S(1)} %pack_rows.1.refs_6_.refs_0_), channel_id=1, source_target_pairs={{0,4},{2,6},{4,0},{6,2},{8,12},{10,14},{12,8},{14,10},{16,20},{18,... | collective-permute-start | bytes 1622024 | tf_op jit(solution)/shard_map/ppermute | solution.py:407
  9.7 1.5 collective-permute-start
  11.2 1.6 %collective-permute-start.5 = (bf16[64,4224]{1,0:T(8,128)(2,1)S(1)}, bf16[64,4224]{1,0:T(8,128)(2,1)S(1)}, u32[]{:S(2)}, u32[]{:S(2)}) collective-permute-start(bf16[64,4224]{1,0:T(8,128)(2,1)S(1)} %pack_rows.1.refs_6_.refs_0_), channel_id=1, source_target_pairs={{0,8},{2,10},{4,12},{6,14},{8,0},{10,2},{12,4},{14,6},{16,24},{18,... | collective-permute-start | bytes 1622024 | tf_op jit(solution)/shard_map/ppermute | solution.py:407
  12.8 9.8 %collective-permute-done.1.refs_0_.refs_2_ = bf16[64,4224]{1,0:T(8,128)(2,1)S(1)} collective-permute-done((bf16[64,4224]{1,0:T(8,128)(2,1)S(1)}, bf16[64,4224]{1,0:T(8,128)(2,1)S(1)}, u32[]{:S(2)}, u32[]{:S(2)}) %collective-permute-start.1) | collective-permute-done | bytes 540704 | tf_op jit(solution)/shard_map/ppermute | solution.py:407
  22.6 1.8 %collective-permute-start.3 = (bf16[32,4224]{1,0:T(8,128)(2,1)S(1)}, bf16[32,4224]{1,0:T(8,128)(2,1)S(1)}, u32[]{:S(2)}, u32[]{:S(2)}) collective-permute-start(bf16[32,4224]{1,0:T(8,128)(2,1)S(1)} %part.5), channel_id=1, source_target_pairs={{0,2},{2,0},{4,6},{6,4},{8,10},{10,8},{12,14},{14,12},{16,18},{18,... | collective-permute-start | bytes 811016 | tf_op jit(solution)/shard_map/ppermute | solution.py:407
  24.4 1.6 %collective-permute-start.2 = (bf16[32,4224]{1,0:T(8,128)(2,1)S(1)}, bf16[32,4224]{1,0:T(8,128)(2,1)S(1)}, u32[]{:S(2)}, u32[]{:S(2)}) collective-permute-start(bf16[32,4224]{1,0:T(8,128)(2,1)S(1)} %part.4), channel_id=1, source_target_pairs={{0,4},{2,6},{4,0},{6,2},{8,12},{10,14},{12,8},{14,10},{16,20},{18,... | collective-permute-start | bytes 811016 | tf_op jit(solution)/shard_map/ppermute | solution.py:407
  26.0 3.6 %collective-permute-start.6 = (bf16[64,4224]{1,0:T(8,128)(2,1)S(1)}, bf16[64,4224]{1,0:T(8,128)(2,1)S(1)}, u32[]{:S(2)}, u32[]{:S(2)}) collective-permute-start(bf16[64,4224]{1,0:T(8,128)(2,1)S(1)} %collective-permute-done.5.refs_0_), channel_id=1, source_target_pairs={{0,24},{2,26},{4,28},{6,30},{8,16},{10,18},{12,20},{14,22},{16,8},... | collective-permute-start | bytes 1622024 | tf_op jit(solution)/shard_map/ppermute | solution.py:407
  29.7 0.6 collective-permute-start.7
  30.3 1.1 collective-permute-start.8
  31.4 2.5 %collective-permute-start.10 = (bf16[32,4224]{1,0:T(8,128)(2,1)S(1)}, bf16[32,4224]{1,0:T(8,128)(2,1)S(1)}, u32[]{:S(2)}, u32[]{:S(2)}) collective-permute-start(bf16[32,4224]{1,0:T(8,128)(2,1)S(1)} %collective-permute-done.3.refs_4_), channel_id=1, source_target_pairs={{0,8},{2,10},{4,12},{6,14},{8,0},{10,2},{12,4},{14,6},{16,24},{18,... | collective-permute-start | bytes 811016 | tf_op jit(solution)/shard_map/ppermute | solution.py:407
  33.9 1.6 %collective-permute-start.9 = (bf16[32,4224]{1,0:T(8,128)(2,1)S(1)}, bf16[32,4224]{1,0:T(8,128)(2,1)S(1)}, u32[]{:S(2)}, u32[]{:S(2)}) collective-permute-start(bf16[32,4224]{1,0:T(8,128)(2,1)S(1)} %collective-permute-done.2.refs_3_), channel_id=1, source_target_pairs={{0,8},{2,10},{4,12},{6,14},{8,0},{10,2},{12,4},{14,6},{16,24},{18,... | collective-permute-start | bytes 811016 | tf_op jit(solution)/shard_map/ppermute | solution.py:407
  35.5 6.3 %expert_set.4 = (bf16[64,2048]{1,0:T(8,128)(2,1)S(1)}, bf16[64,2048]{1,0:T(8,128)(2,1)S(1)}, bf16[64,2048]{1,0:T(8,128)(2,1)S(1)}, bf16[64,2048]{1,0:T(8,128)(2,...) custom-call(bf16[64,4224]{1,0:T(8,128)(2,1)S(1)} %pack_rows.1.refs_6, ...), custom_call_target="tpu_custom_call" | custom-call | flops 4026531840 | tf_op jit(solution)/shard_map/expert_set/pallas_call | solution.py:89
  41.8 6.4 %collective-permute-done.10.refs_4_ = bf16[32,4224]{1,0:T(8,128)(2,1)S(1)} collective-permute-done((bf16[32,4224]{1,0:T(8,128)(2,1)S(1)}, bf16[32,4224]{1,0:T(8,128)(2,1)S(1)}, u32[]{:S(2)}, u32[]{:S(2)}) %collective-permute-start.10) | collective-permute-done | bytes 270368 | tf_op jit(solution)/shard_map/ppermute | solution.py:407
  48.2 4.7 %collective-permute-done.9.refs_3_ = bf16[32,4224]{1,0:T(8,128)(2,1)S(1)} collective-permute-done((bf16[32,4224]{1,0:T(8,128)(2,1)S(1)}, bf16[32,4224]{1,0:T(8,128)(2,1)S(1)}, u32[]{:S(2)}, u32[]{:S(2)}) %collective-permute-start.9) | collective-permute-done | bytes 270368 | tf_op jit(solution)/shard_map/ppermute | solution.py:407
  52.9 0.6 collective-permute-start.13
  53.5 1.1 collective-permute-start.12
  54.6 1.7 %collective-permute-start.11 = (bf16[64,4224]{1,0:T(8,128)(2,1)S(1)}, bf16[64,4224]{1,0:T(8,128)(2,1)S(1)}, u32[]{:S(2)}, u32[]{:S(2)}) collective-permute-start(bf16[64,4224]{1,0:T(8,128)(2,1)S(1)} %hold.6), channel_id=1, source_target_pairs={{0,8},{2,10},{4,12},{6,14},{8,0},{10,2},{12,4},{14,6},{16,24},{18,... | collective-permute-start | bytes 1622024 | tf_op jit(solution)/shard_map/ppermute | solution.py:407
  56.3 6.1 %expert_set.5 = (bf16[64,2048]{1,0:T(8,128)(2,1)S(1)}, bf16[64,2048]{1,0:T(8,128)(2,1)S(1)}, bf16[64,2048]{1,0:T(8,128)(2,1)S(1)}, bf16[64,2048]{1,0:T(8,128)(2,...) custom-call(bf16[64,4224]{1,0:T(8,128)(2,1)S(1)} %collective-permute, ...), custom_call_target="tpu_custom_call", output_to_operand_aliasing={{4}: (7, {}), {5}: (8, {}), {6}: (9, {}), {7}: (10, {})} | custom-call | flops 4026531840 | tf_op jit(solution)/shard_map/expert_set/pallas_call | solution.py:89
  62.4 5.4 %group_sums.4 = (f32[2,2,8,768]{3,2,1,0:T(8,128)S(1)}, f32[2,6,1024]{2,1,0:T(8,128)S(1)}) custom-call(bf16[512,2048]{1,0:T(8,128)(2,1)S(1)} %get-tuple-element.57.refs_0_, bf16[512,2048]{1,0:T(8,128)(2,1)S(1)} %get-tuple-element.58.refs_1_, bf16[512,768]{1,0:T(8,128)(2,1)S(1)} %get-tuple-element.59.refs_2_, ...), custom_call_target="tpu_custom_call" | custom-call | flops 3623878656 | tf_op jit(solution)/shard_map/group_sums/pallas_call | solution.py:89
  67.9 1.0 collective-permute-start.24
  68.9 1.6 %collective-permute-start.23 = (bf16[32,4224]{1,0:T(8,128)(2,1)S(1)}, bf16[32,4224]{1,0:T(8,128)(2,1)S(1)}, u32[]{:S(2)}, u32[]{:S(2)}) collective-permute-start(bf16[32,4224]{1,0:T(8,128)(2,1)S(1)} %part.6), channel_id=1, source_target_pairs={{0,4},{2,6},{4,0},{6,2},{8,12},{10,14},{12,8},{14,10},{16,20},{18,... | collective-permute-start | bytes 811016 | tf_op jit(solution)/shard_map/ppermute | solution.py:407
  70.5 0.6 collective-permute-start.14
  71.1 1.1 collective-permute-start.15
  72.2 5.2 %collective-permute-done.24.refs_4_ = bf16[32,4224]{1,0:T(8,128)(2,1)S(1)} collective-permute-done((bf16[32,4224]{1,0:T(8,128)(2,1)S(1)}, bf16[32,4224]{1,0:T(8,128)(2,1)S(1)}, u32[]{:S(2)}, u32[]{:S(2)}) %collective-permute-start.24) | collective-permute-done | bytes 270368 | tf_op jit(solution)/shard_map/ppermute | solution.py:407
  77.3 0.3 collective-permute-start.30
  77.6 0.7 collective-permute-done.23.refs_3_
  78.4 1.0 collective-permute-start.29
  79.4 6.3 %expert_set.6 = (bf16[64,2048]{1,0:T(8,128)(2,1)S(1)}, bf16[64,2048]{1,0:T(8,128)(2,1)S(1)}, bf16[64,2048]{1,0:T(8,128)(2,1)S(1)}, bf16[64,2048]{1,0:T(8,128)(2,...) custom-call(bf16[64,4224]{1,0:T(8,128)(2,1)S(1)} %collective-permute, ...), custom_call_target="tpu_custom_call" | custom-call | flops 4026531840 | tf_op jit(solution)/shard_map/expert_set/pallas_call | solution.py:89
  85.7 1.0 collective-permute-start.25
  86.7 5.7 %collective-permute-done.25.refs_1_ = bf16[64,2048]{1,0:T(8,128)(2,1)S(1)} collective-permute-done((bf16[64,2048]{1,0:T(8,128)(2,1)S(1)}, bf16[64,2048]{1,0:T(8,128)(2,1)S(1)}, u32[]{:S(2)}, u32[]{:S(2)}) %collective-permute-start.25) | collective-permute-done | bytes 262176 | tf_op jit(solution)/shard_map/ppermute | solution.py:407
  92.4 1.5 collective-permute-start.19
  93.9 0.8 collective-permute-start.27
  94.7 0.9 collective-permute-start.26
  95.7 6.1 %expert_set.7 = (bf16[64,2048]{1,0:T(8,128)(2,1)S(1)}, bf16[64,2048]{1,0:T(8,128)(2,1)S(1)}, bf16[64,2048]{1,0:T(8,128)(2,1)S(1)}, bf16[64,2048]{1,0:T(8,128)(2,...) custom-call(bf16[64,4224]{1,0:T(8,128)(2,1)S(1)} %collective-permute, ...), custom_call_target="tpu_custom_call", output_to_operand_aliasing={{4}: (7, {}), {5}: (8, {}), {6}: (9, {}), {7}: (10, {})} | custom-call | flops 4026531840 | tf_op jit(solution)/shard_map/expert_set/pallas_call | solution.py:89
  101.8 1.2 collective-permute-start.32
  102.9 0.9 collective-permute-start.31
  103.9 1.2 collective-permute-start.20
  105.1 0.8 collective-permute-done.26.refs_1_
  105.8 1.2 collective-permute-start.16
  107.0 0.1 add_rows.12.refs_7_
  107.1 5.4 %group_sums.5 = (f32[2,2,8,768]{3,2,1,0:T(8,128)S(1)}, f32[2,6,1024]{2,1,0:T(8,128)S(1)}) custom-call(bf16[512,2048]{1,0:T(8,128)(2,1)S(1)} %get-tuple-element.74.refs_0_, bf16[512,2048]{1,0:T(8,128)(2,1)S(1)} %get-tuple-element.75.refs_1_, bf16[512,768]{1,0:T(8,128)(2,1)S(1)} %get-tuple-element.76.refs_2_, ...), custom_call_target="tpu_custom_call" | custom-call | flops 3623878656 | tf_op jit(solution)/shard_map/group_sums/pallas_call | solution.py:89
  112.5 7.6 %collective-permute-done.20.refs_1_ = bf16[64,2048]{1,0:T(8,128)(2,1)S(1)} collective-permute-done((bf16[64,2048]{1,0:T(8,128)(2,1)S(1)}, bf16[64,2048]{1,0:T(8,128)(2,1)S(1)}, u32[]{:S(2)}, u32[]{:S(2)}) %collective-permute-start.20) | collective-permute-done | bytes 262176 | tf_op jit(solution)/shard_map/ppermute | solution.py:407
  120.1 4.3 %collective-permute-start.28 = (bf16[64,2048]{1,0:T(8,128)(2,1)S(1)}, bf16[64,2048]{1,0:T(8,128)(2,1)S(1)}, u32[]{:S(2)}, u32[]{:S(2)}) collective-permute-start(bf16[64,2048]{1,0:T(8,128)(2,1)S(1)} %add_rows.12.refs_7_), channel_id=1, source_target_pairs={{0,16},{2,18},{4,20},{6,22},{8,24},{10,26},{12,28},{14,30},{16,0},... | collective-permute-start | bytes 786440 | tf_op jit(solution)/shard_map/ppermute | solution.py:407
  124.5 0.1 collective-permute-start.36
  124.7 1.6 %collective-permute-start.33 = (bf16[64,2048]{1,0:T(8,128)(2,1)S(1)}, bf16[64,2048]{1,0:T(8,128)(2,1)S(1)}, u32[]{:S(2)}, u32[]{:S(2)}) collective-permute-start(bf16[64,2048]{1,0:T(8,128)(2,1)S(1)} %add_rows.13), channel_id=1, source_target_pairs={{0,4},{2,6},{4,0},{6,2},{8,12},{10,14},{12,8},{14,10},{16,20},{18,... | collective-permute-start | bytes 786440 | tf_op jit(solution)/shard_map/ppermute | solution.py:407
  126.3 0.5 collective-permute-start.21
  126.8 5.4 %group_sums.6 = (f32[2,2,8,768]{3,2,1,0:T(8,128)S(1)}, f32[2,6,1024]{2,1,0:T(8,128)S(1)}) custom-call(bf16[512,2048]{1,0:T(8,128)(2,1)S(1)} %get-tuple-element.57.refs_0_, bf16[512,2048]{1,0:T(8,128)(2,1)S(1)} %get-tuple-element.58.refs_1_, bf16[512,768]{1,0:T(8,128)(2,1)S(1)} %get-tuple-element.59.refs_2_, ...), custom_call_target="tpu_custom_call" | custom-call | flops 3623878656 | tf_op jit(solution)/shard_map/group_sums/pallas_call | solution.py:89
  132.2 0.1 add_rows.8
  132.3 2.1 %collective-permute-done.28.refs_3_.refs_4_ = bf16[64,2048]{1,0:T(8,128)(2,1)S(1)} collective-permute-done((bf16[64,2048]{1,0:T(8,128)(2,1)S(1)}, bf16[64,2048]{1,0:T(8,128)(2,1)S(1)}, u32[]{:S(2)}, u32[]{:S(2)}) %collective-permute-start.28) | collective-permute-done | bytes 262176 | tf_op jit(solution)/shard_map/ppermute | solution.py:407
  134.3 0.8 collective-permute-start.18
  135.1 0.1 add_rows.14.refs_7_
  135.2 1.1 collective-permute-start.17
  136.3 3.2 %collective-permute-done.21.refs_2_ = bf16[64,2048]{1,0:T(8,128)(2,1)S(1)} collective-permute-done((bf16[64,2048]{1,0:T(8,128)(2,1)S(1)}, bf16[64,2048]{1,0:T(8,128)(2,1)S(1)}, u32[]{:S(2)}, u32[]{:S(2)}) %collective-permute-start.21) | collective-permute-done | bytes 262176 | tf_op jit(solution)/shard_map/ppermute | solution.py:407
  139.5 0.1 collective-permute-start.34
  139.6 0.1 add_rows.10
  139.7 0.6 collective-permute-start.22
  140.3 5.4 %group_sums.7 = (f32[2,2,8,768]{3,2,1,0:T(8,128)S(1)}, f32[2,6,1024]{2,1,0:T(8,128)S(1)}) custom-call(bf16[512,2048]{1,0:T(8,128)(2,1)S(1)} %get-tuple-element.74.refs_0_, bf16[512,2048]{1,0:T(8,128)(2,1)S(1)} %get-tuple-element.75.refs_1_, bf16[512,768]{1,0:T(8,128)(2,1)S(1)} %get-tuple-element.76.refs_2_, ...), custom_call_target="tpu_custom_call" | custom-call | flops 3623878656 | tf_op jit(solution)/shard_map/group_sums/pallas_call | solution.py:89
  145.7 2.9 %clip_gradients.1 = (f32[2,2,8,768]{3,2,1,0:T(8,128)}, f32[6,2,1024]{2,1,0:T(2,128)}) custom-call(f32[2,2,16,768]{3,2,1,0:T(8,128)} %bitcast.19, f32[2,2,16,768]{3,2,1,0:T(8,128)} %bitcast.21, f32[6,2,2048]{2,1,0:T(2,128)} %bitcast.23, f32[6,2,2048]{2,1,0:T(2,128)} %bitcast.25, f32[2,2,8,768]{3,2,1,0:T(8,128)S(1)} %get-tuple-element.82.refs_4_, ...), custom_call_target="tpu_custom_call" | custom-call | tf_op jit(solution)/shard_map/clip_gradients/pallas_call | solution.py:89
  148.6 1.9 %collective-permute-done.34.refs_5_ = bf16[64,2048]{1,0:T(8,128)(2,1)S(1)} collective-permute-done((bf16[64,2048]{1,0:T(8,128)(2,1)S(1)}, bf16[64,2048]{1,0:T(8,128)(2,1)S(1)}, u32[]{:S(2)}, u32[]{:S(2)}) %collective-permute-start.34) | collective-permute-done | bytes 262176 | tf_op jit(solution)/shard_map/ppermute | solution.py:407
  150.5 2.9 %collective-permute-done.22.refs_3_ = bf16[64,2048]{1,0:T(8,128)(2,1)S(1)} collective-permute-done((bf16[64,2048]{1,0:T(8,128)(2,1)S(1)}, bf16[64,2048]{1,0:T(8,128)(2,1)S(1)}, u32[]{:S(2)}, u32[]{:S(2)}) %collective-permute-start.22) | collective-permute-done | bytes 262176 | tf_op jit(solution)/shard_map/ppermute | solution.py:407
  153.4 0.9 add_rows.15
  (38 shorter events, 0.5 us)
Async XLA Ops:
  6.6 23.0 %collective-permute-start.4 = (bf16[3,1024,768]{2,1,0:T(8,128)(2,1)S(1)}, bf16[3,1024,768]{2,1,0:T(8,128)(2,1)S(1)}, u32[]{:S(2)}, u32[]{:S(2)}) collective-permute-start(bf16[3,1024,768]{2,1,0:T(8,128)(2,1)S(1)} %make_weights.1.refs_5_.refs_4_), channel_id=1, source_target_pairs={{0,1},{1,0},{2,3},{3,2},{4,5},{5,4},{6,7},{7,6},{8,9},{9,8},{10,11... | collective-permute-start | bytes 14155784 | tf_op jit(solution)/shard_map/ppermute | solution.py:410
  7.1 15.5 %collective-permute-start.1 = (bf16[64,4224]{1,0:T(8,128)(2,1)S(1)}, bf16[64,4224]{1,0:T(8,128)(2,1)S(1)}, u32[]{:S(2)}, u32[]{:S(2)}) collective-permute-start(bf16[64,4224]{1,0:T(8,128)(2,1)S(1)} %pack_rows.1.refs_6_.refs_0_), channel_id=1, source_target_pairs={{0,4},{2,6},{4,0},{6,2},{8,12},{10,14},{12,8},{14,10},{16,20},{18,... | collective-permute-start | bytes 1622024 | tf_op jit(solution)/shard_map/ppermute | solution.py:407
  9.7 14.7 %collective-permute-start = (bf16[64,4224]{1,0:T(8,128)(2,1)S(1)}, bf16[64,4224]{1,0:T(8,128)(2,1)S(1)}, u32[]{:S(2)}, u32[]{:S(2)}) collective-permute-start(bf16[64,4224]{1,0:T(8,128)(2,1)S(1)} %pack_rows.1.refs_6_.refs_0_), channel_id=1, source_target_pairs={{0,2},{2,0},{4,6},{6,4},{8,10},{10,8},{12,14},{14,12},{16,18},{18,... | collective-permute-start | bytes 1622024 | tf_op jit(solution)/shard_map/ppermute | solution.py:407
  11.2 14.8 %collective-permute-start.5 = (bf16[64,4224]{1,0:T(8,128)(2,1)S(1)}, bf16[64,4224]{1,0:T(8,128)(2,1)S(1)}, u32[]{:S(2)}, u32[]{:S(2)}) collective-permute-start(bf16[64,4224]{1,0:T(8,128)(2,1)S(1)} %pack_rows.1.refs_6_.refs_0_), channel_id=1, source_target_pairs={{0,8},{2,10},{4,12},{6,14},{8,0},{10,2},{12,4},{14,6},{16,24},{18,... | collective-permute-start | bytes 1622024 | tf_op jit(solution)/shard_map/ppermute | solution.py:407
  22.6 8.8 %collective-permute-start.3 = (bf16[32,4224]{1,0:T(8,128)(2,1)S(1)}, bf16[32,4224]{1,0:T(8,128)(2,1)S(1)}, u32[]{:S(2)}, u32[]{:S(2)}) collective-permute-start(bf16[32,4224]{1,0:T(8,128)(2,1)S(1)} %part.5), channel_id=1, source_target_pairs={{0,2},{2,0},{4,6},{6,4},{8,10},{10,8},{12,14},{14,12},{16,18},{18,... | collective-permute-start | bytes 811016 | tf_op jit(solution)/shard_map/ppermute | solution.py:407
  24.4 9.5 %collective-permute-start.2 = (bf16[32,4224]{1,0:T(8,128)(2,1)S(1)}, bf16[32,4224]{1,0:T(8,128)(2,1)S(1)}, u32[]{:S(2)}, u32[]{:S(2)}) collective-permute-start(bf16[32,4224]{1,0:T(8,128)(2,1)S(1)} %part.4), channel_id=1, source_target_pairs={{0,4},{2,6},{4,0},{6,2},{8,12},{10,14},{12,8},{14,10},{16,20},{18,... | collective-permute-start | bytes 811016 | tf_op jit(solution)/shard_map/ppermute | solution.py:407
  26.0 26.8 %collective-permute-start.6 = (bf16[64,4224]{1,0:T(8,128)(2,1)S(1)}, bf16[64,4224]{1,0:T(8,128)(2,1)S(1)}, u32[]{:S(2)}, u32[]{:S(2)}) collective-permute-start(bf16[64,4224]{1,0:T(8,128)(2,1)S(1)} %collective-permute-done.5.refs_0_), channel_id=1, source_target_pairs={{0,24},{2,26},{4,28},{6,30},{8,16},{10,18},{12,20},{14,22},{16,8},... | collective-permute-start | bytes 1622024 | tf_op jit(solution)/shard_map/ppermute | solution.py:407
  29.7 23.2 %collective-permute-start.7 = (bf16[64,4224]{1,0:T(8,128)(2,1)S(1)}, bf16[64,4224]{1,0:T(8,128)(2,1)S(1)}, u32[]{:S(2)}, u32[]{:S(2)}) collective-permute-start(bf16[64,4224]{1,0:T(8,128)(2,1)S(1)} %hold.5), channel_id=1, source_target_pairs={{0,2},{2,0},{4,6},{6,4},{8,10},{10,8},{12,14},{14,12},{16,18},{18,... | collective-permute-start | bytes 1622024 | tf_op jit(solution)/shard_map/ppermute | solution.py:407
  30.3 22.6 %collective-permute-start.8 = (bf16[64,4224]{1,0:T(8,128)(2,1)S(1)}, bf16[64,4224]{1,0:T(8,128)(2,1)S(1)}, u32[]{:S(2)}, u32[]{:S(2)}) collective-permute-start(bf16[64,4224]{1,0:T(8,128)(2,1)S(1)} %hold.5), channel_id=1, source_target_pairs={{0,4},{2,6},{4,0},{6,2},{8,12},{10,14},{12,8},{14,10},{16,20},{18,... | collective-permute-start | bytes 1622024 | tf_op jit(solution)/shard_map/ppermute | solution.py:407
  31.4 16.8 %collective-permute-start.10 = (bf16[32,4224]{1,0:T(8,128)(2,1)S(1)}, bf16[32,4224]{1,0:T(8,128)(2,1)S(1)}, u32[]{:S(2)}, u32[]{:S(2)}) collective-permute-start(bf16[32,4224]{1,0:T(8,128)(2,1)S(1)} %collective-permute-done.3.refs_4_), channel_id=1, source_target_pairs={{0,8},{2,10},{4,12},{6,14},{8,0},{10,2},{12,4},{14,6},{16,24},{18,... | collective-permute-start | bytes 811016 | tf_op jit(solution)/shard_map/ppermute | solution.py:407
  33.9 19.0 %collective-permute-start.9 = (bf16[32,4224]{1,0:T(8,128)(2,1)S(1)}, bf16[32,4224]{1,0:T(8,128)(2,1)S(1)}, u32[]{:S(2)}, u32[]{:S(2)}) collective-permute-start(bf16[32,4224]{1,0:T(8,128)(2,1)S(1)} %collective-permute-done.2.refs_3_), channel_id=1, source_target_pairs={{0,8},{2,10},{4,12},{6,14},{8,0},{10,2},{12,4},{14,6},{16,24},{18,... | collective-permute-start | bytes 811016 | tf_op jit(solution)/shard_map/ppermute | solution.py:407
  52.9 14.9 %collective-permute-start.13 = (bf16[64,4224]{1,0:T(8,128)(2,1)S(1)}, bf16[64,4224]{1,0:T(8,128)(2,1)S(1)}, u32[]{:S(2)}, u32[]{:S(2)}) collective-permute-start(bf16[64,4224]{1,0:T(8,128)(2,1)S(1)} %hold.6), channel_id=1, source_target_pairs={{0,4},{2,6},{4,0},{6,2},{8,12},{10,14},{12,8},{14,10},{16,20},{18,... | collective-permute-start | bytes 1622024 | tf_op jit(solution)/shard_map/ppermute | solution.py:407
  53.5 15.4 %collective-permute-start.12 = (bf16[64,4224]{1,0:T(8,128)(2,1)S(1)}, bf16[64,4224]{1,0:T(8,128)(2,1)S(1)}, u32[]{:S(2)}, u32[]{:S(2)}) collective-permute-start(bf16[64,4224]{1,0:T(8,128)(2,1)S(1)} %hold.6), channel_id=1, source_target_pairs={{0,2},{2,0},{4,6},{6,4},{8,10},{10,8},{12,14},{14,12},{16,18},{18,... | collective-permute-start | bytes 1622024 | tf_op jit(solution)/shard_map/ppermute | solution.py:407
  54.6 15.9 %collective-permute-start.11 = (bf16[64,4224]{1,0:T(8,128)(2,1)S(1)}, bf16[64,4224]{1,0:T(8,128)(2,1)S(1)}, u32[]{:S(2)}, u32[]{:S(2)}) collective-permute-start(bf16[64,4224]{1,0:T(8,128)(2,1)S(1)} %hold.6), channel_id=1, source_target_pairs={{0,8},{2,10},{4,12},{6,14},{8,0},{10,2},{12,4},{14,6},{16,24},{18,... | collective-permute-start | bytes 1622024 | tf_op jit(solution)/shard_map/ppermute | solution.py:407
  67.9 9.5 %collective-permute-start.24 = (bf16[32,4224]{1,0:T(8,128)(2,1)S(1)}, bf16[32,4224]{1,0:T(8,128)(2,1)S(1)}, u32[]{:S(2)}, u32[]{:S(2)}) collective-permute-start(bf16[32,4224]{1,0:T(8,128)(2,1)S(1)} %part.7), channel_id=1, source_target_pairs={{0,2},{2,0},{4,6},{6,4},{8,10},{10,8},{12,14},{14,12},{16,18},{18,... | collective-permute-start | bytes 811016 | tf_op jit(solution)/shard_map/ppermute | solution.py:407
  68.9 9.5 %collective-permute-start.23 = (bf16[32,4224]{1,0:T(8,128)(2,1)S(1)}, bf16[32,4224]{1,0:T(8,128)(2,1)S(1)}, u32[]{:S(2)}, u32[]{:S(2)}) collective-permute-start(bf16[32,4224]{1,0:T(8,128)(2,1)S(1)} %part.6), channel_id=1, source_target_pairs={{0,4},{2,6},{4,0},{6,2},{8,12},{10,14},{12,8},{14,10},{16,20},{18,... | collective-permute-start | bytes 811016 | tf_op jit(solution)/shard_map/ppermute | solution.py:407
  70.5 25.2 %collective-permute-start.14 = (bf16[64,4224]{1,0:T(8,128)(2,1)S(1)}, bf16[64,4224]{1,0:T(8,128)(2,1)S(1)}, u32[]{:S(2)}, u32[]{:S(2)}) collective-permute-start(bf16[64,4224]{1,0:T(8,128)(2,1)S(1)} %hold.7), channel_id=1, source_target_pairs={{0,2},{2,0},{4,6},{6,4},{8,10},{10,8},{12,14},{14,12},{16,18},{18,... | collective-permute-start | bytes 1622024 | tf_op jit(solution)/shard_map/ppermute | solution.py:407
  71.1 24.6 %collective-permute-start.15 = (bf16[64,4224]{1,0:T(8,128)(2,1)S(1)}, bf16[64,4224]{1,0:T(8,128)(2,1)S(1)}, u32[]{:S(2)}, u32[]{:S(2)}) collective-permute-start(bf16[64,4224]{1,0:T(8,128)(2,1)S(1)} %hold.7), channel_id=1, source_target_pairs={{0,4},{2,6},{4,0},{6,2},{8,12},{10,14},{12,8},{14,10},{16,20},{18,... | collective-permute-start | bytes 1622024 | tf_op jit(solution)/shard_map/ppermute | solution.py:407
  77.3 16.6 %collective-permute-start.30 = (bf16[32,4224]{1,0:T(8,128)(2,1)S(1)}, bf16[32,4224]{1,0:T(8,128)(2,1)S(1)}, u32[]{:S(2)}, u32[]{:S(2)}) collective-permute-start(bf16[32,4224]{1,0:T(8,128)(2,1)S(1)} %collective-permute-done.24.refs_4_), channel_id=1, source_target_pairs={{0,8},{2,10},{4,12},{6,14},{8,0},{10,2},{12,4},{14,6},{16,24},{18,... | collective-permute-start | bytes 811016 | tf_op jit(solution)/shard_map/ppermute | solution.py:407
  78.4 16.4 %collective-permute-start.29 = (bf16[32,4224]{1,0:T(8,128)(2,1)S(1)}, bf16[32,4224]{1,0:T(8,128)(2,1)S(1)}, u32[]{:S(2)}, u32[]{:S(2)}) collective-permute-start(bf16[32,4224]{1,0:T(8,128)(2,1)S(1)} %collective-permute-done.23.refs_3_), channel_id=1, source_target_pairs={{0,8},{2,10},{4,12},{6,14},{8,0},{10,2},{12,4},{14,6},{16,24},{18,... | collective-permute-start | bytes 811016 | tf_op jit(solution)/shard_map/ppermute | solution.py:407
  85.7 6.7 %collective-permute-start.25 = (bf16[64,2048]{1,0:T(8,128)(2,1)S(1)}, bf16[64,2048]{1,0:T(8,128)(2,1)S(1)}, u32[]{:S(2)}, u32[]{:S(2)}) collective-permute-start(bf16[64,2048]{1,0:T(8,128)(2,1)S(1)} %get-tuple-element.64), channel_id=1, source_target_pairs={{0,4},{2,6},{4,0},{6,2},{8,12},{10,14},{12,8},{14,10},{16,20},{18,... | collective-permute-start | bytes 786440 | tf_op jit(solution)/shard_map/ppermute | solution.py:407
  92.4 42.9 %collective-permute-start.19 = (bf16[64,2048]{1,0:T(8,128)(2,1)S(1)}, bf16[64,2048]{1,0:T(8,128)(2,1)S(1)}, u32[]{:S(2)}, u32[]{:S(2)}) collective-permute-start(bf16[64,2048]{1,0:T(8,128)(2,1)S(1)} %get-tuple-element.54), channel_id=1, source_target_pairs={{0,2},{2,0},{4,6},{6,4},{8,10},{10,8},{12,14},{14,12},{16,18},{18,... | collective-permute-start | bytes 786440 | tf_op jit(solution)/shard_map/ppermute | solution.py:407
  93.9 10.0 %collective-permute-start.27 = (bf16[64,2048]{1,0:T(8,128)(2,1)S(1)}, bf16[64,2048]{1,0:T(8,128)(2,1)S(1)}, u32[]{:S(2)}, u32[]{:S(2)}) collective-permute-start(bf16[64,2048]{1,0:T(8,128)(2,1)S(1)} %get-tuple-element.65), channel_id=1, source_target_pairs={{0,4},{2,6},{4,0},{6,2},{8,12},{10,14},{12,8},{14,10},{16,20},{18,... | collective-permute-start | bytes 786440 | tf_op jit(solution)/shard_map/ppermute | solution.py:407
  94.7 11.1 %collective-permute-start.26 = (bf16[64,2048]{1,0:T(8,128)(2,1)S(1)}, bf16[64,2048]{1,0:T(8,128)(2,1)S(1)}, u32[]{:S(2)}, u32[]{:S(2)}) collective-permute-start(bf16[64,2048]{1,0:T(8,128)(2,1)S(1)} %add_rows.11.refs_11_), channel_id=1, source_target_pairs={{0,2},{2,0},{4,6},{6,4},{8,10},{10,8},{12,14},{14,12},{16,18},{18,... | collective-permute-start | bytes 786440 | tf_op jit(solution)/shard_map/ppermute | solution.py:407
  101.8 22.7 %collective-permute-start.32 = (bf16[64,2048]{1,0:T(8,128)(2,1)S(1)}, bf16[64,2048]{1,0:T(8,128)(2,1)S(1)}, u32[]{:S(2)}, u32[]{:S(2)}) collective-permute-start(bf16[64,2048]{1,0:T(8,128)(2,1)S(1)} %get-tuple-element.73), channel_id=1, source_target_pairs={{0,2},{2,0},{4,6},{6,4},{8,10},{10,8},{12,14},{14,12},{16,18},{18,... | collective-permute-start | bytes 786440 | tf_op jit(solution)/shard_map/ppermute | solution.py:407
  102.9 21.8 %collective-permute-start.31 = (bf16[64,2048]{1,0:T(8,128)(2,1)S(1)}, bf16[64,2048]{1,0:T(8,128)(2,1)S(1)}, u32[]{:S(2)}, u32[]{:S(2)}) collective-permute-start(bf16[64,2048]{1,0:T(8,128)(2,1)S(1)} %get-tuple-element.71), channel_id=1, source_target_pairs={{0,2},{2,0},{4,6},{6,4},{8,10},{10,8},{12,14},{14,12},{16,18},{18,... | collective-permute-start | bytes 786440 | tf_op jit(solution)/shard_map/ppermute | solution.py:407
  103.9 16.2 %collective-permute-start.20 = (bf16[64,2048]{1,0:T(8,128)(2,1)S(1)}, bf16[64,2048]{1,0:T(8,128)(2,1)S(1)}, u32[]{:S(2)}, u32[]{:S(2)}) collective-permute-start(bf16[64,2048]{1,0:T(8,128)(2,1)S(1)} %hold.9), channel_id=1, source_target_pairs={{0,2},{2,0},{4,6},{6,4},{8,10},{10,8},{12,14},{14,12},{16,18},{18,... | collective-permute-start | bytes 786440 | tf_op jit(solution)/shard_map/ppermute | solution.py:407
  105.8 20.4 %collective-permute-start.16 = (bf16[64,2048]{1,0:T(8,128)(2,1)S(1)}, bf16[64,2048]{1,0:T(8,128)(2,1)S(1)}, u32[]{:S(2)}, u32[]{:S(2)}) collective-permute-start(bf16[64,2048]{1,0:T(8,128)(2,1)S(1)} %hold.8), channel_id=1, source_target_pairs={{0,4},{2,6},{4,0},{6,2},{8,12},{10,14},{12,8},{14,10},{16,20},{18,... | collective-permute-start | bytes 786440 | tf_op jit(solution)/shard_map/ppermute | solution.py:407
  120.1 14.2 %collective-permute-start.28 = (bf16[64,2048]{1,0:T(8,128)(2,1)S(1)}, bf16[64,2048]{1,0:T(8,128)(2,1)S(1)}, u32[]{:S(2)}, u32[]{:S(2)}) collective-permute-start(bf16[64,2048]{1,0:T(8,128)(2,1)S(1)} %add_rows.12.refs_7_), channel_id=1, source_target_pairs={{0,16},{2,18},{4,20},{6,22},{8,24},{10,26},{12,28},{14,30},{16,0},... | collective-permute-start | bytes 786440 | tf_op jit(solution)/shard_map/ppermute | solution.py:407
  124.5 15.2 %collective-permute-start.36 = (f32[2,6,1024]{2,1,0:T(8,128)S(1)}, f32[2,6,1024]{2,1,0:T(8,128)S(1)}, u32[]{:S(2)}, u32[]{:S(2)}) collective-permute-start(f32[2,6,1024]{2,1,0:T(8,128)S(1)} %get-tuple-element.84), channel_id=1, source_target_pairs={{0,1},{1,0},{2,3},{3,2},{4,5},{5,4},{6,7},{7,6},{8,9},{9,8},{10,11... | collective-permute-start | bytes 147464 | tf_op jit(solution)/shard_map/ppermute | solution.py:410
  124.7 10.4 %collective-permute-start.33 = (bf16[64,2048]{1,0:T(8,128)(2,1)S(1)}, bf16[64,2048]{1,0:T(8,128)(2,1)S(1)}, u32[]{:S(2)}, u32[]{:S(2)}) collective-permute-start(bf16[64,2048]{1,0:T(8,128)(2,1)S(1)} %add_rows.13), channel_id=1, source_target_pairs={{0,4},{2,6},{4,0},{6,2},{8,12},{10,14},{12,8},{14,10},{16,20},{18,... | collective-permute-start | bytes 786440 | tf_op jit(solution)/shard_map/ppermute | solution.py:407
  126.3 13.2 %collective-permute-start.21 = (bf16[64,2048]{1,0:T(8,128)(2,1)S(1)}, bf16[64,2048]{1,0:T(8,128)(2,1)S(1)}, u32[]{:S(2)}, u32[]{:S(2)}) collective-permute-start(bf16[64,2048]{1,0:T(8,128)(2,1)S(1)} %add_rows.9), channel_id=1, source_target_pairs={{0,4},{2,6},{4,0},{6,2},{8,12},{10,14},{12,8},{14,10},{16,20},{18,... | collective-permute-start | bytes 786440 | tf_op jit(solution)/shard_map/ppermute | solution.py:407
  134.3 14.3 %collective-permute-start.18 = (bf16[64,2048]{1,0:T(8,128)(2,1)S(1)}, bf16[64,2048]{1,0:T(8,128)(2,1)S(1)}, u32[]{:S(2)}, u32[]{:S(2)}) collective-permute-start(bf16[64,2048]{1,0:T(8,128)(2,1)S(1)} %get-tuple-element.48), channel_id=1, source_target_pairs={{0,4},{2,6},{4,0},{6,2},{8,12},{10,14},{12,8},{14,10},{16,20},{18,... | collective-permute-start | bytes 786440 | tf_op jit(solution)/shard_map/ppermute | solution.py:407
  135.1 10.6 %collective-permute-start.35 = (f32[2,2,8,768]{3,2,1,0:T(8,128)S(1)}, f32[2,2,8,768]{3,2,1,0:T(8,128)S(1)}, u32[]{:S(2)}, u32[]{:S(2)}) collective-permute-start(f32[2,2,8,768]{3,2,1,0:T(8,128)S(1)} %get-tuple-element.79.refs_2_), channel_id=1, source_target_pairs={{0,1},{1,0},{2,3},{3,2},{4,5},{5,4},{6,7},{7,6},{8,9},{9,8},{10,11... | collective-permute-start | bytes 294920 | tf_op jit(solution)/shard_map/ppermute | solution.py:410
  135.2 13.4 %collective-permute-start.17 = (bf16[64,2048]{1,0:T(8,128)(2,1)S(1)}, bf16[64,2048]{1,0:T(8,128)(2,1)S(1)}, u32[]{:S(2)}, u32[]{:S(2)}) collective-permute-start(bf16[64,2048]{1,0:T(8,128)(2,1)S(1)} %add_rows.8), channel_id=1, source_target_pairs={{0,2},{2,0},{4,6},{6,4},{8,10},{10,8},{12,14},{14,12},{16,18},{18,... | collective-permute-start | bytes 786440 | tf_op jit(solution)/shard_map/ppermute | solution.py:407
  139.5 11.0 %collective-permute-start.34 = (bf16[64,2048]{1,0:T(8,128)(2,1)S(1)}, bf16[64,2048]{1,0:T(8,128)(2,1)S(1)}, u32[]{:S(2)}, u32[]{:S(2)}) collective-permute-start(bf16[64,2048]{1,0:T(8,128)(2,1)S(1)} %add_rows.14.refs_7_), channel_id=1, source_target_pairs={{0,24},{2,26},{4,28},{6,30},{8,16},{10,18},{12,20},{14,22},{16,8},... | collective-permute-start | bytes 786440 | tf_op jit(solution)/shard_map/ppermute | solution.py:407
  139.7 13.7 %collective-permute-start.22 = (bf16[64,2048]{1,0:T(8,128)(2,1)S(1)}, bf16[64,2048]{1,0:T(8,128)(2,1)S(1)}, u32[]{:S(2)}, u32[]{:S(2)}) collective-permute-start(bf16[64,2048]{1,0:T(8,128)(2,1)S(1)} %add_rows.10), channel_id=1, source_target_pairs={{0,8},{2,10},{4,12},{6,14},{8,0},{10,2},{12,4},{14,6},{16,24},{18,... | collective-permute-start | bytes 786440 | tf_op jit(solution)/shard_map/ppermute | solution.py:407

commit v5 on v4

--- a/solution.py
+++ b/solution.py
@@ -472,37 +472,38 @@
         d2 = crossed(x2, y2, other[0])
         d3 = tuple(swap(half, 4) for half in d2)
         p2, later = run_set(calls, (far, x2, y2, *d2), weights, experts)
-        mine = run_sums(calls, stored, weights, False, sums[False], shapes, (p2[0],))
-        x_sum2 = added(p2[1], swap(p2[3], 2))
-        p3, later = run_set(calls, (last, x3, y3, *d3), weights, experts, later, (x_sum2,))
-        total2 = added(p2[0], swap(x_sum2, 1), swap(p2[2], 2))
-        sums[True] = run_sums(calls, later, weights, True, other, shapes, (total2,))
+        p3, later = run_set(calls, (last, x3, y3, *d3), weights, experts, later)
+        x_sum0 = added(p0[1], swap(held(p0[3], x3, y3), 2))
+        y_sum1 = added(p1[2], swap(held(p1[3], x3, y3), 1))
+        x_sum2 = added(p2[1], swap(p2[3], 2), after=(p3[0],))
+        sums[True] = run_sums(calls, later, weights, True, other, shapes, (x_sum2,))
+        total2 = added(p2[0], swap(x_sum2, 1), swap(p2[2], 2), after=(sums[True][0],))
+        far_sum = swap(total2, 8)
         y_sum3 = added(p3[2], swap(p3[3], 1), after=(sums[True][0],))
-        far_sum = swap(total2, 8)
-        total3 = added(p3[0], swap(p3[1], 1), swap(y_sum3, 2), after=(far_sum,))
+        mine = run_sums(calls, stored, weights, False, sums[False], shapes, (y_sum3, total2))
+        total3 = added(p3[0], swap(p3[1], 1), swap(y_sum3, 2), after=(mine[0], far_sum))
+        late0, late1 = held(p0[2], total2), held(p1[1], total2)
+        total1 = added(p1[0], swap(late1, 1), swap(held(y_sum1, total2), 2))
         sums[False] = run_sums(calls, later, weights, False, mine, shapes, (total3,))
-        y_sum1 = added(p1[2], swap(held(p1[3], x3, y3), 1))
-        total1 = added(p1[0], swap(p1[1], 1), swap(y_sum1, 2))
-        x_sum0 = added(p0[1], swap(held(p0[3], x3, y3), 2))
         parts = (
             p0[0],
-            swap(x_sum0, 1),
-            swap(p0[2], 2),
+            swap(held(x_sum0, total2), 1),
+            swap(late0, 2),
             swap(total1, 4),
             far_sum,
             swap(total3, 12),
         )
-        return parts, weights
+        return parts, weights, total3
 
     final, after, weights = [], (), None
     for base in range(0, experts, 16):
-        parts, weights = quad(swap(packed, base) if base else packed, weights, after)
+        parts, weights, last_sum = quad(swap(packed, base) if base else packed, weights, after)
         final += [swap(added(*parts), base)] if base else parts
         after = (sums[False][0],)
     grad_tokens = added(*final, free=(0,))
 
     mine_in, mine_out = sums[False]
-    got_in, got_out = (swap_core(a) for a in sums[True])
+    got_in, got_out = (swap_core(held(a, last_sum)) for a in sums[True])
     grad_in, grad_clip_out = calls.run(
         clip_kernel,
         "clip_gradients",

time: 154 us -> 145 us (0.942)
  waiting for transfers between devices: 50.9 us -> 39.4 us
  starting transfers between devices: 45.7 us -> 47.5 us
    ppermute x34, waiting for transfers between devices: 50.9 us -> 39.4 us  [swap(): lax.ppermute(array, 'expert', [(i, i ^ mask) for i in range(experts)])]
    ppermute x34, starting transfers between devices: 45.1 us -> 46.9 us  [swap(): lax.ppermute(array, 'expert', [(i, i ^ mask) for i in range(experts)])]
    pallas_call x28 -> x34, Pallas kernels: 56.8 us -> 56.9 us  [run(): pl.pallas_call(wrapped, in_specs=[ANYWHERE] * given + [INSIDE] * count +...]
  transfers between devices with their start and end apart: 37 -> 37, of which waited for: 12 -> 10; matrix products, arithmetic and copies ran while one was open for 0% -> 0% of each run, Pallas kernels for 32% -> 35%
where the time goes in v5:
time: 145 us
  Pallas kernels  56.9 us (39%)
  starting transfers between devices  47.5 us (33%)
  waiting for transfers between devices  39.4 us (27%)
    pallas_call x34, Pallas kernels, run(): pl.pallas_call(wrapped, in_specs=[ANYWHERE] * given + [INSIDE] * count +...  56.9 us
    ppermute x34, starting transfers between devices, swap(): lax.ppermute(array, 'expert', [(i, i ^ mask) for i in range(experts)])  46.9 us
    ppermute x34, waiting for transfers between devices, swap(): lax.ppermute(array, 'expert', [(i, i ^ mask) for i in range(experts)])  39.4 us
  transfers between devices with their start and end apart: 37, of which 10 were waited for; matrix products, arithmetic and copies ran while one was open for 0% of the time, Pallas kernels for 35%

profile of v5, /device:TPU:0, one launch (start us, length us, event | category | flops | bytes accessed | tf_op | source)
XLA Modules:
  0.0 144.8 jit_solution(12444771007047667205)
XLA Ops:
  0.6 1.3 pack_rows.1.refs_6_.refs_0_
  1.9 4.7 %make_weights.1.refs_5_.refs_4_ = bf16[3,1024,768]{2,1,0:T(8,128)(2,1)S(1)} custom-call(s32[2,1024,256]{2,1,0:T(8,128)} %bitcast.16, s32[256,1024]{1,0:T(8,128)} %bitcast.17, f32[2,2,16,768]{3,2,1,0:T(8,128)} %bitcast.18, f32[2,2,16,768]{3,2,1,0:T(8,128)} %bitcast.20, f32[6,2,2048]{2,1,0:T(2,128)} %bitcast.22, f32[6,2,2048]{2,1,0:T(2,128)} %bitcast.24, ...), custom_call_target="tpu_custom_call" | custom-call | tf_op jit(solution)/shard_map/make_weights/pallas_call | solution.py:89
  6.6 0.5 collective-permute-start.4
  7.1 2.6 %collective-permute-start.1 = (bf16[64,4224]{1,0:T(8,128)(2,1)S(1)}, bf16[64,4224]{1,0:T(8,128)(2,1)S(1)}, u32[]{:S(2)}, u32[]{:S(2)}) collective-permute-start(bf16[64,4224]{1,0:T(8,128)(2,1)S(1)} %pack_rows.1.refs_6_.refs_0_), channel_id=1, source_target_pairs={{0,4},{2,6},{4,0},{6,2},{8,12},{10,14},{12,8},{14,10},{16,20},{18,... | collective-permute-start | bytes 1622024 | tf_op jit(solution)/shard_map/ppermute | solution.py:407
  9.7 1.5 %collective-permute-start = (bf16[64,4224]{1,0:T(8,128)(2,1)S(1)}, bf16[64,4224]{1,0:T(8,128)(2,1)S(1)}, u32[]{:S(2)}, u32[]{:S(2)}) collective-permute-start(bf16[64,4224]{1,0:T(8,128)(2,1)S(1)} %pack_rows.1.refs_6_.refs_0_), channel_id=1, source_target_pairs={{0,2},{2,0},{4,6},{6,4},{8,10},{10,8},{12,14},{14,12},{16,18},{18,... | collective-permute-start | bytes 1622024 | tf_op jit(solution)/shard_map/ppermute | solution.py:407
  11.2 1.6 %collective-permute-start.5 = (bf16[64,4224]{1,0:T(8,128)(2,1)S(1)}, bf16[64,4224]{1,0:T(8,128)(2,1)S(1)}, u32[]{:S(2)}, u32[]{:S(2)}) collective-permute-start(bf16[64,4224]{1,0:T(8,128)(2,1)S(1)} %pack_rows.1.refs_6_.refs_0_), channel_id=1, source_target_pairs={{0,8},{2,10},{4,12},{6,14},{8,0},{10,2},{12,4},{14,6},{16,24},{18,... | collective-permute-start | bytes 1622024 | tf_op jit(solution)/shard_map/ppermute | solution.py:407
  12.8 9.8 %collective-permute-done.1.refs_0_.refs_2_ = bf16[64,4224]{1,0:T(8,128)(2,1)S(1)} collective-permute-done((bf16[64,4224]{1,0:T(8,128)(2,1)S(1)}, bf16[64,4224]{1,0:T(8,128)(2,1)S(1)}, u32[]{:S(2)}, u32[]{:S(2)}) %collective-permute-start.1) | collective-permute-done | bytes 540704 | tf_op jit(solution)/shard_map/ppermute | solution.py:407
  22.6 1.8 %collective-permute-start.3 = (bf16[32,4224]{1,0:T(8,128)(2,1)S(1)}, bf16[32,4224]{1,0:T(8,128)(2,1)S(1)}, u32[]{:S(2)}, u32[]{:S(2)}) collective-permute-start(bf16[32,4224]{1,0:T(8,128)(2,1)S(1)} %part.5), channel_id=1, source_target_pairs={{0,2},{2,0},{4,6},{6,4},{8,10},{10,8},{12,14},{14,12},{16,18},{18,... | collective-permute-start | bytes 811016 | tf_op jit(solution)/shard_map/ppermute | solution.py:407
  24.4 1.6 %collective-permute-start.2 = (bf16[32,4224]{1,0:T(8,128)(2,1)S(1)}, bf16[32,4224]{1,0:T(8,128)(2,1)S(1)}, u32[]{:S(2)}, u32[]{:S(2)}) collective-permute-start(bf16[32,4224]{1,0:T(8,128)(2,1)S(1)} %part.4), channel_id=1, source_target_pairs={{0,4},{2,6},{4,0},{6,2},{8,12},{10,14},{12,8},{14,10},{16,20},{18,... | collective-permute-start | bytes 811016 | tf_op jit(solution)/shard_map/ppermute | solution.py:407
  26.0 3.6 %collective-permute-start.6 = (bf16[64,4224]{1,0:T(8,128)(2,1)S(1)}, bf16[64,4224]{1,0:T(8,128)(2,1)S(1)}, u32[]{:S(2)}, u32[]{:S(2)}) collective-permute-start(bf16[64,4224]{1,0:T(8,128)(2,1)S(1)} %collective-permute-done.5.refs_0_), channel_id=1, source_target_pairs={{0,24},{2,26},{4,28},{6,30},{8,16},{10,18},{12,20},{14,22},{16,8},... | collective-permute-start | bytes 1622024 | tf_op jit(solution)/shard_map/ppermute | solution.py:407
  29.7 0.6 collective-permute-start.8
  30.2 1.1 collective-permute-start.7
  31.4 2.5 %collective-permute-start.10 = (bf16[32,4224]{1,0:T(8,128)(2,1)S(1)}, bf16[32,4224]{1,0:T(8,128)(2,1)S(1)}, u32[]{:S(2)}, u32[]{:S(2)}) collective-permute-start(bf16[32,4224]{1,0:T(8,128)(2,1)S(1)} %collective-permute-done.3.refs_4_), channel_id=1, source_target_pairs={{0,8},{2,10},{4,12},{6,14},{8,0},{10,2},{12,4},{14,6},{16,24},{18,... | collective-permute-start | bytes 811016 | tf_op jit(solution)/shard_map/ppermute | solution.py:407
  33.9 1.6 %collective-permute-start.9 = (bf16[32,4224]{1,0:T(8,128)(2,1)S(1)}, bf16[32,4224]{1,0:T(8,128)(2,1)S(1)}, u32[]{:S(2)}, u32[]{:S(2)}) collective-permute-start(bf16[32,4224]{1,0:T(8,128)(2,1)S(1)} %collective-permute-done.2.refs_3_), channel_id=1, source_target_pairs={{0,8},{2,10},{4,12},{6,14},{8,0},{10,2},{12,4},{14,6},{16,24},{18,... | collective-permute-start | bytes 811016 | tf_op jit(solution)/shard_map/ppermute | solution.py:407
  35.5 6.3 %expert_set.4 = (bf16[64,2048]{1,0:T(8,128)(2,1)S(1)}, bf16[64,2048]{1,0:T(8,128)(2,1)S(1)}, bf16[64,2048]{1,0:T(8,128)(2,1)S(1)}, bf16[64,2048]{1,0:T(8,128)(2,...) custom-call(bf16[64,4224]{1,0:T(8,128)(2,1)S(1)} %pack_rows.1.refs_6, ...), custom_call_target="tpu_custom_call" | custom-call | flops 4026531840 | tf_op jit(solution)/shard_map/expert_set/pallas_call | solution.py:89
  41.8 1.3 collective-permute-done.6.refs_0_
  43.1 5.1 %collective-permute-done.10.refs_4_ = bf16[32,4224]{1,0:T(8,128)(2,1)S(1)} collective-permute-done((bf16[32,4224]{1,0:T(8,128)(2,1)S(1)}, bf16[32,4224]{1,0:T(8,128)(2,1)S(1)}, u32[]{:S(2)}, u32[]{:S(2)}) %collective-permute-start.10) | collective-permute-done | bytes 270368 | tf_op jit(solution)/shard_map/ppermute | solution.py:407
  48.2 4.7 %collective-permute-done.9.refs_3_ = bf16[32,4224]{1,0:T(8,128)(2,1)S(1)} collective-permute-done((bf16[32,4224]{1,0:T(8,128)(2,1)S(1)}, bf16[32,4224]{1,0:T(8,128)(2,1)S(1)}, u32[]{:S(2)}, u32[]{:S(2)}) %collective-permute-start.9) | collective-permute-done | bytes 270368 | tf_op jit(solution)/shard_map/ppermute | solution.py:407
  52.9 0.6 collective-permute-start.13
  53.5 1.1 collective-permute-start.12
  54.6 1.7 %collective-permute-start.11 = (bf16[64,4224]{1,0:T(8,128)(2,1)S(1)}, bf16[64,4224]{1,0:T(8,128)(2,1)S(1)}, u32[]{:S(2)}, u32[]{:S(2)}) collective-permute-start(bf16[64,4224]{1,0:T(8,128)(2,1)S(1)} %hold.12), channel_id=1, source_target_pairs={{0,8},{2,10},{4,12},{6,14},{8,0},{10,2},{12,4},{14,6},{16,24},{18,... | collective-permute-start | bytes 1622024 | tf_op jit(solution)/shard_map/ppermute | solution.py:407
  56.3 6.1 %expert_set.5 = (bf16[64,2048]{1,0:T(8,128)(2,1)S(1)}, bf16[64,2048]{1,0:T(8,128)(2,1)S(1)}, bf16[64,2048]{1,0:T(8,128)(2,1)S(1)}, bf16[64,2048]{1,0:T(8,128)(2,...) custom-call(bf16[64,4224]{1,0:T(8,128)(2,1)S(1)} %collective-permute, ...), custom_call_target="tpu_custom_call", output_to_operand_aliasing={{4}: (7, {}), {5}: (8, {}), {6}: (9, {}), {7}: (10, {})} | custom-call | flops 4026531840 | tf_op jit(solution)/shard_map/expert_set/pallas_call | solution.py:89
  62.4 5.4 %group_sums.4 = (f32[2,2,8,768]{3,2,1,0:T(8,128)S(1)}, f32[2,6,1024]{2,1,0:T(8,128)S(1)}) custom-call(bf16[512,2048]{1,0:T(8,128)(2,1)S(1)} %get-tuple-element.52.refs_0_, bf16[512,2048]{1,0:T(8,128)(2,1)S(1)} %get-tuple-element.53.refs_1_, bf16[512,768]{1,0:T(8,128)(2,1)S(1)} %get-tuple-element.54.refs_2_, ...), custom_call_target="tpu_custom_call" | custom-call | flops 3623878656 | tf_op jit(solution)/shard_map/group_sums/pallas_call | solution.py:89
  67.8 1.0 collective-permute-start.18
  68.9 1.6 %collective-permute-start.17 = (bf16[32,4224]{1,0:T(8,128)(2,1)S(1)}, bf16[32,4224]{1,0:T(8,128)(2,1)S(1)}, u32[]{:S(2)}, u32[]{:S(2)}) collective-permute-start(bf16[32,4224]{1,0:T(8,128)(2,1)S(1)} %part.6), channel_id=1, source_target_pairs={{0,4},{2,6},{4,0},{6,2},{8,12},{10,14},{12,8},{14,10},{16,20},{18,... | collective-permute-start | bytes 811016 | tf_op jit(solution)/shard_map/ppermute | solution.py:407
  70.5 0.6 collective-permute-start.15
  71.1 1.1 collective-permute-start.14
  72.2 5.2 %collective-permute-done.18.refs_4_ = bf16[32,4224]{1,0:T(8,128)(2,1)S(1)} collective-permute-done((bf16[32,4224]{1,0:T(8,128)(2,1)S(1)}, bf16[32,4224]{1,0:T(8,128)(2,1)S(1)}, u32[]{:S(2)}, u32[]{:S(2)}) %collective-permute-start.18) | collective-permute-done | bytes 270368 | tf_op jit(solution)/shard_map/ppermute | solution.py:407
  77.3 0.3 collective-permute-start.21
  77.6 0.7 collective-permute-done.17.refs_3_
  78.3 1.0 collective-permute-start.20
  79.4 6.3 %expert_set.6 = (bf16[64,2048]{1,0:T(8,128)(2,1)S(1)}, bf16[64,2048]{1,0:T(8,128)(2,1)S(1)}, bf16[64,2048]{1,0:T(8,128)(2,1)S(1)}, bf16[64,2048]{1,0:T(8,128)(2,...) custom-call(bf16[64,4224]{1,0:T(8,128)(2,1)S(1)} %collective-permute, ...), custom_call_target="tpu_custom_call" | custom-call | flops 4026531840 | tf_op jit(solution)/shard_map/expert_set/pallas_call | solution.py:89
  85.7 1.0 collective-permute-start.19
  86.7 3.2 %collective-permute-done.15.refs_2_ = bf16[64,4224]{1,0:T(8,128)(2,1)S(1)} collective-permute-done((bf16[64,4224]{1,0:T(8,128)(2,1)S(1)}, bf16[64,4224]{1,0:T(8,128)(2,1)S(1)}, u32[]{:S(2)}, u32[]{:S(2)}) %collective-permute-start.15) | collective-permute-done | bytes 540704 | tf_op jit(solution)/shard_map/ppermute | solution.py:407
  89.9 1.0 collective-permute-start.23
  91.0 1.1 collective-permute-start.27
  92.1 6.1 %expert_set.7 = (bf16[64,2048]{1,0:T(8,128)(2,1)S(1)}, bf16[64,2048]{1,0:T(8,128)(2,1)S(1)}, bf16[64,2048]{1,0:T(8,128)(2,1)S(1)}, bf16[64,2048]{1,0:T(8,128)(2,...) custom-call(bf16[64,4224]{1,0:T(8,128)(2,1)S(1)} %collective-permute, ...), custom_call_target="tpu_custom_call", output_to_operand_aliasing={{4}: (7, {}), {5}: (8, {}), {6}: (9, {}), {7}: (10, {})} | custom-call | flops 4026531840 | tf_op jit(solution)/shard_map/expert_set/pallas_call | solution.py:89
  98.2 1.1 collective-permute-start.31
  99.2 1.0 collective-permute-start.32
  100.3 0.1 add_rows.9.refs_7_
  100.3 1.1 collective-permute-start.22
  101.4 5.4 %group_sums.5 = (f32[2,2,8,768]{3,2,1,0:T(8,128)S(1)}, f32[2,6,1024]{2,1,0:T(8,128)S(1)}) custom-call(bf16[512,2048]{1,0:T(8,128)(2,1)S(1)} %get-tuple-element.66.refs_0_, bf16[512,2048]{1,0:T(8,128)(2,1)S(1)} %get-tuple-element.67.refs_1_, bf16[512,768]{1,0:T(8,128)(2,1)S(1)} %get-tuple-element.68.refs_2_, ...), custom_call_target="tpu_custom_call" | custom-call | flops 3623878656 | tf_op jit(solution)/shard_map/group_sums/pallas_call | solution.py:89
  106.8 4.2 %collective-permute-done.32.refs_1_ = bf16[64,2048]{1,0:T(8,128)(2,1)S(1)} collective-permute-done((bf16[64,2048]{1,0:T(8,128)(2,1)S(1)}, bf16[64,2048]{1,0:T(8,128)(2,1)S(1)}, u32[]{:S(2)}, u32[]{:S(2)}) %collective-permute-start.32) | collective-permute-done | bytes 262176 | tf_op jit(solution)/shard_map/ppermute | solution.py:407
  111.0 1.5 %collective-permute-start.16 = (bf16[64,2048]{1,0:T(8,128)(2,1)S(1)}, bf16[64,2048]{1,0:T(8,128)(2,1)S(1)}, u32[]{:S(2)}, u32[]{:S(2)}) collective-permute-start(bf16[64,2048]{1,0:T(8,128)(2,1)S(1)} %hold.14), channel_id=1, source_target_pairs={{0,4},{2,6},{4,0},{6,2},{8,12},{10,14},{12,8},{14,10},{16,20},{18,... | collective-permute-start | bytes 786440 | tf_op jit(solution)/shard_map/ppermute | solution.py:407
  112.5 0.6 collective-permute-start.33
  113.1 0.6 collective-permute-done.22.refs_1_
  113.8 0.1 add_rows.10.refs_1_.refs_6_
  113.9 4.2 %collective-permute-start.30 = (bf16[64,2048]{1,0:T(8,128)(2,1)S(1)}, bf16[64,2048]{1,0:T(8,128)(2,1)S(1)}, u32[]{:S(2)}, u32[]{:S(2)}) collective-permute-start(bf16[64,2048]{1,0:T(8,128)(2,1)S(1)} %add_rows.10.refs_1_.refs_6_), channel_id=1, source_target_pairs={{0,16},{2,18},{4,20},{6,22},{8,24},{10,26},{12,28},{14,30},{16,0},... | collective-permute-start | bytes 786440 | tf_op jit(solution)/shard_map/ppermute | solution.py:407
  118.2 0.9 collective-permute-start.26
  119.1 1.2 collective-permute-start.28
  120.3 5.4 %group_sums.6 = (f32[2,2,8,768]{3,2,1,0:T(8,128)S(1)}, f32[2,6,1024]{2,1,0:T(8,128)S(1)}) custom-call(bf16[512,2048]{1,0:T(8,128)(2,1)S(1)} %get-tuple-element.52.refs_0_, bf16[512,2048]{1,0:T(8,128)(2,1)S(1)} %get-tuple-element.53.refs_1_, bf16[512,768]{1,0:T(8,128)(2,1)S(1)} %get-tuple-element.54.refs_2_, ...), custom_call_target="tpu_custom_call" | custom-call | flops 3623878656 | tf_op jit(solution)/shard_map/group_sums/pallas_call | solution.py:89
  125.7 0.1 add_rows.14.refs_7_.refs_1_
  125.8 0.1 collective-permute-start.36
  126.0 0.1 add_rows.8.refs_0_
  126.1 0.9 collective-permute-start.24
  127.0 1.2 collective-permute-start.25
  128.2 2.6 %collective-permute-start.34 = (bf16[64,2048]{1,0:T(8,128)(2,1)S(1)}, bf16[64,2048]{1,0:T(8,128)(2,1)S(1)}, u32[]{:S(2)}, u32[]{:S(2)}) collective-permute-start(bf16[64,2048]{1,0:T(8,128)(2,1)S(1)} %add_rows.14.refs_7_.refs_1_), channel_id=1, source_target_pairs={{0,24},{2,26},{4,28},{6,30},{8,16},{10,18},{12,20},{14,22},{16,8},... | collective-permute-start | bytes 786440 | tf_op jit(solution)/shard_map/ppermute | solution.py:407
  130.8 0.1 add_rows.12
  130.9 0.1 collective-permute-start.29
  131.0 0.1 collective-permute-start.35
  131.1 5.4 %group_sums.7 = (f32[2,2,8,768]{3,2,1,0:T(8,128)S(1)}, f32[2,6,1024]{2,1,0:T(8,128)S(1)}) custom-call(bf16[512,2048]{1,0:T(8,128)(2,1)S(1)} %get-tuple-element.66.refs_0_, bf16[512,2048]{1,0:T(8,128)(2,1)S(1)} %get-tuple-element.67.refs_1_, bf16[512,768]{1,0:T(8,128)(2,1)S(1)} %get-tuple-element.68.refs_2_, ...), custom_call_target="tpu_custom_call" | custom-call | flops 3623878656 | tf_op jit(solution)/shard_map/group_sums/pallas_call | solution.py:89
  136.4 2.9 %clip_gradients.1 = (f32[2,2,8,768]{3,2,1,0:T(8,128)}, f32[6,2,1024]{2,1,0:T(2,128)}) custom-call(f32[2,2,16,768]{3,2,1,0:T(8,128)} %bitcast.19, f32[2,2,16,768]{3,2,1,0:T(8,128)} %bitcast.21, f32[6,2,2048]{2,1,0:T(2,128)} %bitcast.23, f32[6,2,2048]{2,1,0:T(2,128)} %bitcast.25, f32[2,2,8,768]{3,2,1,0:T(8,128)S(1)} %get-tuple-element.82.refs_4_, ...), custom_call_target="tpu_custom_call" | custom-call | tf_op jit(solution)/shard_map/clip_gradients/pallas_call | solution.py:89
  139.3 4.6 %collective-permute-done.29.refs_3_ = bf16[64,2048]{1,0:T(8,128)(2,1)S(1)} collective-permute-done((bf16[64,2048]{1,0:T(8,128)(2,1)S(1)}, bf16[64,2048]{1,0:T(8,128)(2,1)S(1)}, u32[]{:S(2)}, u32[]{:S(2)}) %collective-permute-start.29) | collective-permute-done | bytes 262176 | tf_op jit(solution)/shard_map/ppermute | solution.py:407
  143.9 0.9 add_rows.15
  (44 shorter events, 0.5 us)
Async XLA Ops:
  6.6 23.0 %collective-permute-start.4 = (bf16[3,1024,768]{2,1,0:T(8,128)(2,1)S(1)}, bf16[3,1024,768]{2,1,0:T(8,128)(2,1)S(1)}, u32[]{:S(2)}, u32[]{:S(2)}) collective-permute-start(bf16[3,1024,768]{2,1,0:T(8,128)(2,1)S(1)} %make_weights.1.refs_5_.refs_4_), channel_id=1, source_target_pairs={{0,1},{1,0},{2,3},{3,2},{4,5},{5,4},{6,7},{7,6},{8,9},{9,8},{10,11... | collective-permute-start | bytes 14155784 | tf_op jit(solution)/shard_map/ppermute | solution.py:410
  7.1 15.5 %collective-permute-start.1 = (bf16[64,4224]{1,0:T(8,128)(2,1)S(1)}, bf16[64,4224]{1,0:T(8,128)(2,1)S(1)}, u32[]{:S(2)}, u32[]{:S(2)}) collective-permute-start(bf16[64,4224]{1,0:T(8,128)(2,1)S(1)} %pack_rows.1.refs_6_.refs_0_), channel_id=1, source_target_pairs={{0,4},{2,6},{4,0},{6,2},{8,12},{10,14},{12,8},{14,10},{16,20},{18,... | collective-permute-start | bytes 1622024 | tf_op jit(solution)/shard_map/ppermute | solution.py:407
  9.7 14.7 %collective-permute-start = (bf16[64,4224]{1,0:T(8,128)(2,1)S(1)}, bf16[64,4224]{1,0:T(8,128)(2,1)S(1)}, u32[]{:S(2)}, u32[]{:S(2)}) collective-permute-start(bf16[64,4224]{1,0:T(8,128)(2,1)S(1)} %pack_rows.1.refs_6_.refs_0_), channel_id=1, source_target_pairs={{0,2},{2,0},{4,6},{6,4},{8,10},{10,8},{12,14},{14,12},{16,18},{18,... | collective-permute-start | bytes 1622024 | tf_op jit(solution)/shard_map/ppermute | solution.py:407
  11.2 14.8 %collective-permute-start.5 = (bf16[64,4224]{1,0:T(8,128)(2,1)S(1)}, bf16[64,4224]{1,0:T(8,128)(2,1)S(1)}, u32[]{:S(2)}, u32[]{:S(2)}) collective-permute-start(bf16[64,4224]{1,0:T(8,128)(2,1)S(1)} %pack_rows.1.refs_6_.refs_0_), channel_id=1, source_target_pairs={{0,8},{2,10},{4,12},{6,14},{8,0},{10,2},{12,4},{14,6},{16,24},{18,... | collective-permute-start | bytes 1622024 | tf_op jit(solution)/shard_map/ppermute | solution.py:407
  22.6 8.8 %collective-permute-start.3 = (bf16[32,4224]{1,0:T(8,128)(2,1)S(1)}, bf16[32,4224]{1,0:T(8,128)(2,1)S(1)}, u32[]{:S(2)}, u32[]{:S(2)}) collective-permute-start(bf16[32,4224]{1,0:T(8,128)(2,1)S(1)} %part.5), channel_id=1, source_target_pairs={{0,2},{2,0},{4,6},{6,4},{8,10},{10,8},{12,14},{14,12},{16,18},{18,... | collective-permute-start | bytes 811016 | tf_op jit(solution)/shard_map/ppermute | solution.py:407
  24.4 9.5 %collective-permute-start.2 = (bf16[32,4224]{1,0:T(8,128)(2,1)S(1)}, bf16[32,4224]{1,0:T(8,128)(2,1)S(1)}, u32[]{:S(2)}, u32[]{:S(2)}) collective-permute-start(bf16[32,4224]{1,0:T(8,128)(2,1)S(1)} %part.4), channel_id=1, source_target_pairs={{0,4},{2,6},{4,0},{6,2},{8,12},{10,14},{12,8},{14,10},{16,20},{18,... | collective-permute-start | bytes 811016 | tf_op jit(solution)/shard_map/ppermute | solution.py:407
  26.0 17.1 %collective-permute-start.6 = (bf16[64,4224]{1,0:T(8,128)(2,1)S(1)}, bf16[64,4224]{1,0:T(8,128)(2,1)S(1)}, u32[]{:S(2)}, u32[]{:S(2)}) collective-permute-start(bf16[64,4224]{1,0:T(8,128)(2,1)S(1)} %collective-permute-done.5.refs_0_), channel_id=1, source_target_pairs={{0,24},{2,26},{4,28},{6,30},{8,16},{10,18},{12,20},{14,22},{16,8},... | collective-permute-start | bytes 1622024 | tf_op jit(solution)/shard_map/ppermute | solution.py:407
  29.7 23.2 %collective-permute-start.8 = (bf16[64,4224]{1,0:T(8,128)(2,1)S(1)}, bf16[64,4224]{1,0:T(8,128)(2,1)S(1)}, u32[]{:S(2)}, u32[]{:S(2)}) collective-permute-start(bf16[64,4224]{1,0:T(8,128)(2,1)S(1)} %hold.11), channel_id=1, source_target_pairs={{0,4},{2,6},{4,0},{6,2},{8,12},{10,14},{12,8},{14,10},{16,20},{18,... | collective-permute-start | bytes 1622024 | tf_op jit(solution)/shard_map/ppermute | solution.py:407
  30.2 22.6 %collective-permute-start.7 = (bf16[64,4224]{1,0:T(8,128)(2,1)S(1)}, bf16[64,4224]{1,0:T(8,128)(2,1)S(1)}, u32[]{:S(2)}, u32[]{:S(2)}) collective-permute-start(bf16[64,4224]{1,0:T(8,128)(2,1)S(1)} %hold.11), channel_id=1, source_target_pairs={{0,2},{2,0},{4,6},{6,4},{8,10},{10,8},{12,14},{14,12},{16,18},{18,... | collective-permute-start | bytes 1622024 | tf_op jit(solution)/shard_map/ppermute | solution.py:407
  31.4 16.8 %collective-permute-start.10 = (bf16[32,4224]{1,0:T(8,128)(2,1)S(1)}, bf16[32,4224]{1,0:T(8,128)(2,1)S(1)}, u32[]{:S(2)}, u32[]{:S(2)}) collective-permute-start(bf16[32,4224]{1,0:T(8,128)(2,1)S(1)} %collective-permute-done.3.refs_4_), channel_id=1, source_target_pairs={{0,8},{2,10},{4,12},{6,14},{8,0},{10,2},{12,4},{14,6},{16,24},{18,... | collective-permute-start | bytes 811016 | tf_op jit(solution)/shard_map/ppermute | solution.py:407
  33.9 19.0 %collective-permute-start.9 = (bf16[32,4224]{1,0:T(8,128)(2,1)S(1)}, bf16[32,4224]{1,0:T(8,128)(2,1)S(1)}, u32[]{:S(2)}, u32[]{:S(2)}) collective-permute-start(bf16[32,4224]{1,0:T(8,128)(2,1)S(1)} %collective-permute-done.2.refs_3_), channel_id=1, source_target_pairs={{0,8},{2,10},{4,12},{6,14},{8,0},{10,2},{12,4},{14,6},{16,24},{18,... | collective-permute-start | bytes 811016 | tf_op jit(solution)/shard_map/ppermute | solution.py:407
  52.9 14.9 %collective-permute-start.13 = (bf16[64,4224]{1,0:T(8,128)(2,1)S(1)}, bf16[64,4224]{1,0:T(8,128)(2,1)S(1)}, u32[]{:S(2)}, u32[]{:S(2)}) collective-permute-start(bf16[64,4224]{1,0:T(8,128)(2,1)S(1)} %hold.12), channel_id=1, source_target_pairs={{0,4},{2,6},{4,0},{6,2},{8,12},{10,14},{12,8},{14,10},{16,20},{18,... | collective-permute-start | bytes 1622024 | tf_op jit(solution)/shard_map/ppermute | solution.py:407
  53.5 15.4 %collective-permute-start.12 = (bf16[64,4224]{1,0:T(8,128)(2,1)S(1)}, bf16[64,4224]{1,0:T(8,128)(2,1)S(1)}, u32[]{:S(2)}, u32[]{:S(2)}) collective-permute-start(bf16[64,4224]{1,0:T(8,128)(2,1)S(1)} %hold.12), channel_id=1, source_target_pairs={{0,2},{2,0},{4,6},{6,4},{8,10},{10,8},{12,14},{14,12},{16,18},{18,... | collective-permute-start | bytes 1622024 | tf_op jit(solution)/shard_map/ppermute | solution.py:407
  54.6 15.9 %collective-permute-start.11 = (bf16[64,4224]{1,0:T(8,128)(2,1)S(1)}, bf16[64,4224]{1,0:T(8,128)(2,1)S(1)}, u32[]{:S(2)}, u32[]{:S(2)}) collective-permute-start(bf16[64,4224]{1,0:T(8,128)(2,1)S(1)} %hold.12), channel_id=1, source_target_pairs={{0,8},{2,10},{4,12},{6,14},{8,0},{10,2},{12,4},{14,6},{16,24},{18,... | collective-permute-start | bytes 1622024 | tf_op jit(solution)/shard_map/ppermute | solution.py:407
  67.8 9.5 %collective-permute-start.18 = (bf16[32,4224]{1,0:T(8,128)(2,1)S(1)}, bf16[32,4224]{1,0:T(8,128)(2,1)S(1)}, u32[]{:S(2)}, u32[]{:S(2)}) collective-permute-start(bf16[32,4224]{1,0:T(8,128)(2,1)S(1)} %part.7), channel_id=1, source_target_pairs={{0,2},{2,0},{4,6},{6,4},{8,10},{10,8},{12,14},{14,12},{16,18},{18,... | collective-permute-start | bytes 811016 | tf_op jit(solution)/shard_map/ppermute | solution.py:407
  68.9 9.5 %collective-permute-start.17 = (bf16[32,4224]{1,0:T(8,128)(2,1)S(1)}, bf16[32,4224]{1,0:T(8,128)(2,1)S(1)}, u32[]{:S(2)}, u32[]{:S(2)}) collective-permute-start(bf16[32,4224]{1,0:T(8,128)(2,1)S(1)} %part.6), channel_id=1, source_target_pairs={{0,4},{2,6},{4,0},{6,2},{8,12},{10,14},{12,8},{14,10},{16,20},{18,... | collective-permute-start | bytes 811016 | tf_op jit(solution)/shard_map/ppermute | solution.py:407
  70.5 19.4 %collective-permute-start.15 = (bf16[64,4224]{1,0:T(8,128)(2,1)S(1)}, bf16[64,4224]{1,0:T(8,128)(2,1)S(1)}, u32[]{:S(2)}, u32[]{:S(2)}) collective-permute-start(bf16[64,4224]{1,0:T(8,128)(2,1)S(1)} %hold.13), channel_id=1, source_target_pairs={{0,4},{2,6},{4,0},{6,2},{8,12},{10,14},{12,8},{14,10},{16,20},{18,... | collective-permute-start | bytes 1622024 | tf_op jit(solution)/shard_map/ppermute | solution.py:407
  71.1 19.9 %collective-permute-start.14 = (bf16[64,4224]{1,0:T(8,128)(2,1)S(1)}, bf16[64,4224]{1,0:T(8,128)(2,1)S(1)}, u32[]{:S(2)}, u32[]{:S(2)}) collective-permute-start(bf16[64,4224]{1,0:T(8,128)(2,1)S(1)} %hold.13), channel_id=1, source_target_pairs={{0,2},{2,0},{4,6},{6,4},{8,10},{10,8},{12,14},{14,12},{16,18},{18,... | collective-permute-start | bytes 1622024 | tf_op jit(solution)/shard_map/ppermute | solution.py:407
  77.3 14.7 %collective-permute-start.21 = (bf16[32,4224]{1,0:T(8,128)(2,1)S(1)}, bf16[32,4224]{1,0:T(8,128)(2,1)S(1)}, u32[]{:S(2)}, u32[]{:S(2)}) collective-permute-start(bf16[32,4224]{1,0:T(8,128)(2,1)S(1)} %collective-permute-done.18.refs_4_), channel_id=1, source_target_pairs={{0,8},{2,10},{4,12},{6,14},{8,0},{10,2},{12,4},{14,6},{16,24},{18,... | collective-permute-start | bytes 811016 | tf_op jit(solution)/shard_map/ppermute | solution.py:407
  78.3 13.7 %collective-permute-start.20 = (bf16[32,4224]{1,0:T(8,128)(2,1)S(1)}, bf16[32,4224]{1,0:T(8,128)(2,1)S(1)}, u32[]{:S(2)}, u32[]{:S(2)}) collective-permute-start(bf16[32,4224]{1,0:T(8,128)(2,1)S(1)} %collective-permute-done.17.refs_3_), channel_id=1, source_target_pairs={{0,8},{2,10},{4,12},{6,14},{8,0},{10,2},{12,4},{14,6},{16,24},{18,... | collective-permute-start | bytes 811016 | tf_op jit(solution)/shard_map/ppermute | solution.py:407
  85.7 14.6 %collective-permute-start.19 = (bf16[64,2048]{1,0:T(8,128)(2,1)S(1)}, bf16[64,2048]{1,0:T(8,128)(2,1)S(1)}, u32[]{:S(2)}, u32[]{:S(2)}) collective-permute-start(bf16[64,2048]{1,0:T(8,128)(2,1)S(1)} %get-tuple-element.59), channel_id=1, source_target_pairs={{0,4},{2,6},{4,0},{6,2},{8,12},{10,14},{12,8},{14,10},{16,20},{18,... | collective-permute-start | bytes 786440 | tf_op jit(solution)/shard_map/ppermute | solution.py:407
  89.9 22.6 %collective-permute-start.23 = (bf16[64,2048]{1,0:T(8,128)(2,1)S(1)}, bf16[64,2048]{1,0:T(8,128)(2,1)S(1)}, u32[]{:S(2)}, u32[]{:S(2)}) collective-permute-start(bf16[64,2048]{1,0:T(8,128)(2,1)S(1)} %get-tuple-element.65), channel_id=1, source_target_pairs={{0,4},{2,6},{4,0},{6,2},{8,12},{10,14},{12,8},{14,10},{16,20},{18,... | collective-permute-start | bytes 786440 | tf_op jit(solution)/shard_map/ppermute | solution.py:407
  91.0 27.1 %collective-permute-start.27 = (bf16[64,2048]{1,0:T(8,128)(2,1)S(1)}, bf16[64,2048]{1,0:T(8,128)(2,1)S(1)}, u32[]{:S(2)}, u32[]{:S(2)}) collective-permute-start(bf16[64,2048]{1,0:T(8,128)(2,1)S(1)} %hold.18), channel_id=1, source_target_pairs={{0,2},{2,0},{4,6},{6,4},{8,10},{10,8},{12,14},{14,12},{16,18},{18,... | collective-permute-start | bytes 786440 | tf_op jit(solution)/shard_map/ppermute | solution.py:407
  98.2 20.9 %collective-permute-start.31 = (bf16[64,2048]{1,0:T(8,128)(2,1)S(1)}, bf16[64,2048]{1,0:T(8,128)(2,1)S(1)}, u32[]{:S(2)}, u32[]{:S(2)}) collective-permute-start(bf16[64,2048]{1,0:T(8,128)(2,1)S(1)} %get-tuple-element.77), channel_id=1, source_target_pairs={{0,2},{2,0},{4,6},{6,4},{8,10},{10,8},{12,14},{14,12},{16,18},{18,... | collective-permute-start | bytes 786440 | tf_op jit(solution)/shard_map/ppermute | solution.py:407
  99.2 11.7 %collective-permute-start.32 = (bf16[64,2048]{1,0:T(8,128)(2,1)S(1)}, bf16[64,2048]{1,0:T(8,128)(2,1)S(1)}, u32[]{:S(2)}, u32[]{:S(2)}) collective-permute-start(bf16[64,2048]{1,0:T(8,128)(2,1)S(1)} %get-tuple-element.79), channel_id=1, source_target_pairs={{0,2},{2,0},{4,6},{6,4},{8,10},{10,8},{12,14},{14,12},{16,18},{18,... | collective-permute-start | bytes 786440 | tf_op jit(solution)/shard_map/ppermute | solution.py:407
  100.3 13.4 %collective-permute-start.22 = (bf16[64,2048]{1,0:T(8,128)(2,1)S(1)}, bf16[64,2048]{1,0:T(8,128)(2,1)S(1)}, u32[]{:S(2)}, u32[]{:S(2)}) collective-permute-start(bf16[64,2048]{1,0:T(8,128)(2,1)S(1)} %add_rows.9.refs_7_), channel_id=1, source_target_pairs={{0,2},{2,0},{4,6},{6,4},{8,10},{10,8},{12,14},{14,12},{16,18},{18,... | collective-permute-start | bytes 786440 | tf_op jit(solution)/shard_map/ppermute | solution.py:407
  111.0 15.0 %collective-permute-start.16 = (bf16[64,2048]{1,0:T(8,128)(2,1)S(1)}, bf16[64,2048]{1,0:T(8,128)(2,1)S(1)}, u32[]{:S(2)}, u32[]{:S(2)}) collective-permute-start(bf16[64,2048]{1,0:T(8,128)(2,1)S(1)} %hold.14), channel_id=1, source_target_pairs={{0,4},{2,6},{4,0},{6,2},{8,12},{10,14},{12,8},{14,10},{16,20},{18,... | collective-permute-start | bytes 786440 | tf_op jit(solution)/shard_map/ppermute | solution.py:407
  112.5 13.2 %collective-permute-start.33 = (bf16[64,2048]{1,0:T(8,128)(2,1)S(1)}, bf16[64,2048]{1,0:T(8,128)(2,1)S(1)}, u32[]{:S(2)}, u32[]{:S(2)}) collective-permute-start(bf16[64,2048]{1,0:T(8,128)(2,1)S(1)} %add_rows.13.refs_5_), channel_id=1, source_target_pairs={{0,4},{2,6},{4,0},{6,2},{8,12},{10,14},{12,8},{14,10},{16,20},{18,... | collective-permute-start | bytes 786440 | tf_op jit(solution)/shard_map/ppermute | solution.py:407
  113.9 11.8 %collective-permute-start.30 = (bf16[64,2048]{1,0:T(8,128)(2,1)S(1)}, bf16[64,2048]{1,0:T(8,128)(2,1)S(1)}, u32[]{:S(2)}, u32[]{:S(2)}) collective-permute-start(bf16[64,2048]{1,0:T(8,128)(2,1)S(1)} %add_rows.10.refs_1_.refs_6_), channel_id=1, source_target_pairs={{0,16},{2,18},{4,20},{6,22},{8,24},{10,26},{12,28},{14,30},{16,0},... | collective-permute-start | bytes 786440 | tf_op jit(solution)/shard_map/ppermute | solution.py:407
  118.2 10.0 %collective-permute-start.26 = (bf16[64,2048]{1,0:T(8,128)(2,1)S(1)}, bf16[64,2048]{1,0:T(8,128)(2,1)S(1)}, u32[]{:S(2)}, u32[]{:S(2)}) collective-permute-start(bf16[64,2048]{1,0:T(8,128)(2,1)S(1)} %hold.17), channel_id=1, source_target_pairs={{0,2},{2,0},{4,6},{6,4},{8,10},{10,8},{12,14},{14,12},{16,18},{18,... | collective-permute-start | bytes 786440 | tf_op jit(solution)/shard_map/ppermute | solution.py:407
  119.1 11.7 %collective-permute-start.28 = (bf16[64,2048]{1,0:T(8,128)(2,1)S(1)}, bf16[64,2048]{1,0:T(8,128)(2,1)S(1)}, u32[]{:S(2)}, u32[]{:S(2)}) collective-permute-start(bf16[64,2048]{1,0:T(8,128)(2,1)S(1)} %hold.19), channel_id=1, source_target_pairs={{0,4},{2,6},{4,0},{6,2},{8,12},{10,14},{12,8},{14,10},{16,20},{18,... | collective-permute-start | bytes 786440 | tf_op jit(solution)/shard_map/ppermute | solution.py:407
  125.8 5.1 %collective-permute-start.36 = (f32[2,6,1024]{2,1,0:T(8,128)S(1)}, f32[2,6,1024]{2,1,0:T(8,128)S(1)}, u32[]{:S(2)}, u32[]{:S(2)}) collective-permute-start(f32[2,6,1024]{2,1,0:T(8,128)S(1)} %hold.21), channel_id=1, source_target_pairs={{0,1},{1,0},{2,3},{3,2},{4,5},{5,4},{6,7},{7,6},{8,9},{9,8},{10,11... | collective-permute-start | bytes 147464 | tf_op jit(solution)/shard_map/ppermute | solution.py:410
  126.1 13.3 %collective-permute-start.24 = (bf16[64,2048]{1,0:T(8,128)(2,1)S(1)}, bf16[64,2048]{1,0:T(8,128)(2,1)S(1)}, u32[]{:S(2)}, u32[]{:S(2)}) collective-permute-start(bf16[64,2048]{1,0:T(8,128)(2,1)S(1)} %hold.15), channel_id=1, source_target_pairs={{0,2},{2,0},{4,6},{6,4},{8,10},{10,8},{12,14},{14,12},{16,18},{18,... | collective-permute-start | bytes 786440 | tf_op jit(solution)/shard_map/ppermute | solution.py:407
  127.0 12.3 %collective-permute-start.25 = (bf16[64,2048]{1,0:T(8,128)(2,1)S(1)}, bf16[64,2048]{1,0:T(8,128)(2,1)S(1)}, u32[]{:S(2)}, u32[]{:S(2)}) collective-permute-start(bf16[64,2048]{1,0:T(8,128)(2,1)S(1)} %hold.16), channel_id=1, source_target_pairs={{0,4},{2,6},{4,0},{6,2},{8,12},{10,14},{12,8},{14,10},{16,20},{18,... | collective-permute-start | bytes 786440 | tf_op jit(solution)/shard_map/ppermute | solution.py:407
  128.2 15.7 %collective-permute-start.34 = (bf16[64,2048]{1,0:T(8,128)(2,1)S(1)}, bf16[64,2048]{1,0:T(8,128)(2,1)S(1)}, u32[]{:S(2)}, u32[]{:S(2)}) collective-permute-start(bf16[64,2048]{1,0:T(8,128)(2,1)S(1)} %add_rows.14.refs_7_.refs_1_), channel_id=1, source_target_pairs={{0,24},{2,26},{4,28},{6,30},{8,16},{10,18},{12,20},{14,22},{16,8},... | collective-permute-start | bytes 786440 | tf_op jit(solution)/shard_map/ppermute | solution.py:407
  130.9 13.0 %collective-permute-start.29 = (bf16[64,2048]{1,0:T(8,128)(2,1)S(1)}, bf16[64,2048]{1,0:T(8,128)(2,1)S(1)}, u32[]{:S(2)}, u32[]{:S(2)}) collective-permute-start(bf16[64,2048]{1,0:T(8,128)(2,1)S(1)} %add_rows.12), channel_id=1, source_target_pairs={{0,8},{2,10},{4,12},{6,14},{8,0},{10,2},{12,4},{14,6},{16,24},{18,... | collective-permute-start | bytes 786440 | tf_op jit(solution)/shard_map/ppermute | solution.py:407
  131.0 5.5 %collective-permute-start.35 = (f32[2,2,8,768]{3,2,1,0:T(8,128)S(1)}, f32[2,2,8,768]{3,2,1,0:T(8,128)S(1)}, u32[]{:S(2)}, u32[]{:S(2)}) collective-permute-start(f32[2,2,8,768]{3,2,1,0:T(8,128)S(1)} %hold.20), channel_id=1, source_target_pairs={{0,1},{1,0},{2,3},{3,2},{4,5},{5,4},{6,7},{7,6},{8,9},{9,8},{10,11... | collective-permute-start | bytes 294920 | tf_op jit(solution)/shard_map/ppermute | solution.py:410

commit v6 on v5

--- a/solution.py
+++ b/solution.py
@@ -449,8 +449,8 @@
             functools.partial(part_kernel, first), "part", [array], [(shape, array.dtype)], after, limit=SMALL
         )[0]
 
-    def crossed(over_x, over_y, *after):
-        return swap(part(over_x, 0, after), 2), swap(part(over_y, cut, after), 1)
+    def crossed(over_x, over_y):
+        return swap(part(over_x, 0, ()), 2), swap(part(over_y, cut, ()), 1)
 
     def quad(head, weights, after):
         near = swap(head, 4)
@@ -463,16 +463,18 @@
         x1, y1 = swap(ready, 1), swap(ready, 2)
         d1 = tuple(swap(half, 4) for half in d0)
         p0, stored = run_set(calls, (head, x0, y0, *d0), weights, experts, after=after)
-        ready = held(far, x1, y1, *d1, p0[0])
+        ready = held(far, x1, y1, p0[0])
         x2, y2, last = swap(ready, 1), swap(ready, 2), swap(ready, 4)
         p1, stored = run_set(calls, (near, x1, y1, *d1), weights, experts, stored)
-        ready = held(last, x2, y2)
+        halves = part(x2, 0, (p1[0],)), part(y2, cut, (p1[0],))
+        d2 = swap(halves[0], 2), swap(halves[1], 1)
+        ready = held(last, *halves)
         x3, y3 = swap(ready, 1), swap(ready, 2)
-        other = run_sums(calls, stored, weights, True, sums[True], shapes)
-        d2 = crossed(x2, y2, other[0])
+        other = run_sums(calls, stored, weights, True, sums[True], shapes, (ready,))
         d3 = tuple(swap(half, 4) for half in d2)
-        p2, later = run_set(calls, (far, x2, y2, *d2), weights, experts)
-        p3, later = run_set(calls, (last, x3, y3, *d3), weights, experts, later)
+        p2, later = run_set(calls, (far, x2, y2, *d2), weights, experts, after=(other[0],))
+        mine = run_sums(calls, stored, weights, False, sums[False], shapes, (p2[0],))
+        p3, later = run_set(calls, (last, x3, y3, *d3), weights, experts, later, (mine[0],))
         x_sum0 = added(p0[1], swap(held(p0[3], x3, y3), 2))
         y_sum1 = added(p1[2], swap(held(p1[3], x3, y3), 1))
         x_sum2 = added(p2[1], swap(p2[3], 2), after=(p3[0],))
@@ -480,11 +482,10 @@
         total2 = added(p2[0], swap(x_sum2, 1), swap(p2[2], 2), after=(sums[True][0],))
         far_sum = swap(total2, 8)
         y_sum3 = added(p3[2], swap(p3[3], 1), after=(sums[True][0],))
-        mine = run_sums(calls, stored, weights, False, sums[False], shapes, (y_sum3, total2))
-        total3 = added(p3[0], swap(p3[1], 1), swap(y_sum3, 2), after=(mine[0], far_sum))
+        sums[False] = run_sums(calls, later, weights, False, mine, shapes, (y_sum3, total2))
+        total3 = added(p3[0], swap(p3[1], 1), swap(y_sum3, 2), after=(sums[False][0], far_sum))
         late0, late1 = held(p0[2], total2), held(p1[1], total2)
         total1 = added(p1[0], swap(late1, 1), swap(held(y_sum1, total2), 2))
-        sums[False] = run_sums(calls, later, weights, False, mine, shapes, (total3,))
         parts = (
             p0[0],
             swap(held(x_sum0, total2), 1),

time: 145 us -> 140 us (0.966)
  waiting for transfers between devices: 39.4 us -> 25.7 us
  starting transfers between devices: 47.5 us -> 56.3 us
    ppermute x34, waiting for transfers between devices: 39.4 us -> 23.3 us  [swap(): lax.ppermute(array, 'expert', [(i, i ^ mask) for i in range(experts)])]
    ppermute x34, starting transfers between devices: 46.9 us -> 55.5 us  [swap(): lax.ppermute(array, 'expert', [(i, i ^ mask) for i in range(experts)])]
    ppermute x3, waiting for transfers between devices: 0.01 us -> 2.37 us  [swap_core(): return lax.ppermute(array, 'dp', [(0, 1), (1, 0)])]
  transfers between devices with their start and end apart: 37 -> 37, of which waited for: 10 -> 11; matrix products, arithmetic and copies ran while one was open for 0% -> 0% of each run, Pallas kernels for 35% -> 36%
where the time goes in v6:
time: 140 us
  Pallas kernels  56.9 us (41%)
  starting transfers between devices  56.3 us (40%)
  waiting for transfers between devices  25.7 us (18%)
    pallas_call x34, Pallas kernels, run(): pl.pallas_call(wrapped, in_specs=[ANYWHERE] * given + [INSIDE] * count +...  56.9 us
    ppermute x34, starting transfers between devices, swap(): lax.ppermute(array, 'expert', [(i, i ^ mask) for i in range(experts)])  55.5 us
    ppermute x34, waiting for transfers between devices, swap(): lax.ppermute(array, 'expert', [(i, i ^ mask) for i in range(experts)])  23.3 us
  transfers between devices with their start and end apart: 37, of which 11 were waited for; matrix products, arithmetic and copies ran while one was open for 0% of the time, Pallas kernels for 36%

profile of v6, /device:TPU:0, one launch (start us, length us, event | category | flops | bytes accessed | tf_op | source)
XLA Modules:
  0.0 139.8 jit_solution(2200962762422864844)
XLA Ops:
  0.6 1.3 pack_rows.1.refs_6_.refs_0_
  1.9 4.7 %make_weights.1.refs_5_.refs_4_ = bf16[3,1024,768]{2,1,0:T(8,128)(2,1)S(1)} custom-call(s32[2,1024,256]{2,1,0:T(8,128)} %bitcast.16, s32[256,1024]{1,0:T(8,128)} %bitcast.17, f32[2,2,16,768]{3,2,1,0:T(8,128)} %bitcast.18, f32[2,2,16,768]{3,2,1,0:T(8,128)} %bitcast.20, f32[6,2,2048]{2,1,0:T(2,128)} %bitcast.22, f32[6,2,2048]{2,1,0:T(2,128)} %bitcast.24, ...), custom_call_target="tpu_custom_call" | custom-call | tf_op jit(solution)/shard_map/make_weights/pallas_call | solution.py:89
  6.6 0.5 collective-permute-start.4
  7.1 2.6 %collective-permute-start = (bf16[64,4224]{1,0:T(8,128)(2,1)S(1)}, bf16[64,4224]{1,0:T(8,128)(2,1)S(1)}, u32[]{:S(2)}, u32[]{:S(2)}) collective-permute-start(bf16[64,4224]{1,0:T(8,128)(2,1)S(1)} %pack_rows.1.refs_6_.refs_0_), channel_id=1, source_target_pairs={{0,2},{2,0},{4,6},{6,4},{8,10},{10,8},{12,14},{14,12},{16,18},{18,... | collective-permute-start | bytes 1622024 | tf_op jit(solution)/shard_map/ppermute | solution.py:407
  9.7 1.5 %collective-permute-start.1 = (bf16[64,4224]{1,0:T(8,128)(2,1)S(1)}, bf16[64,4224]{1,0:T(8,128)(2,1)S(1)}, u32[]{:S(2)}, u32[]{:S(2)}) collective-permute-start(bf16[64,4224]{1,0:T(8,128)(2,1)S(1)} %pack_rows.1.refs_6_.refs_0_), channel_id=1, source_target_pairs={{0,4},{2,6},{4,0},{6,2},{8,12},{10,14},{12,8},{14,10},{16,20},{18,... | collective-permute-start | bytes 1622024 | tf_op jit(solution)/shard_map/ppermute | solution.py:407
  11.2 1.6 %collective-permute-start.5 = (bf16[64,4224]{1,0:T(8,128)(2,1)S(1)}, bf16[64,4224]{1,0:T(8,128)(2,1)S(1)}, u32[]{:S(2)}, u32[]{:S(2)}) collective-permute-start(bf16[64,4224]{1,0:T(8,128)(2,1)S(1)} %pack_rows.1.refs_6_.refs_0_), channel_id=1, source_target_pairs={{0,8},{2,10},{4,12},{6,14},{8,0},{10,2},{12,4},{14,6},{16,24},{18,... | collective-permute-start | bytes 1622024 | tf_op jit(solution)/shard_map/ppermute | solution.py:407
  12.8 9.8 %collective-permute-done.refs_0_.refs_1_ = bf16[64,4224]{1,0:T(8,128)(2,1)S(1)} collective-permute-done((bf16[64,4224]{1,0:T(8,128)(2,1)S(1)}, bf16[64,4224]{1,0:T(8,128)(2,1)S(1)}, u32[]{:S(2)}, u32[]{:S(2)}) %collective-permute-start) | collective-permute-done | bytes 540704 | tf_op jit(solution)/shard_map/ppermute | solution.py:407
  22.6 1.9 %collective-permute-start.2 = (bf16[32,4224]{1,0:T(8,128)(2,1)S(1)}, bf16[32,4224]{1,0:T(8,128)(2,1)S(1)}, u32[]{:S(2)}, u32[]{:S(2)}) collective-permute-start(bf16[32,4224]{1,0:T(8,128)(2,1)S(1)} %part.4), channel_id=1, source_target_pairs={{0,4},{2,6},{4,0},{6,2},{8,12},{10,14},{12,8},{14,10},{16,20},{18,... | collective-permute-start | bytes 811016 | tf_op jit(solution)/shard_map/ppermute | solution.py:407
  24.5 1.6 %collective-permute-start.3 = (bf16[32,4224]{1,0:T(8,128)(2,1)S(1)}, bf16[32,4224]{1,0:T(8,128)(2,1)S(1)}, u32[]{:S(2)}, u32[]{:S(2)}) collective-permute-start(bf16[32,4224]{1,0:T(8,128)(2,1)S(1)} %part.5), channel_id=1, source_target_pairs={{0,2},{2,0},{4,6},{6,4},{8,10},{10,8},{12,14},{14,12},{16,18},{18,... | collective-permute-start | bytes 811016 | tf_op jit(solution)/shard_map/ppermute | solution.py:407
  26.0 3.6 %collective-permute-start.6 = (bf16[64,4224]{1,0:T(8,128)(2,1)S(1)}, bf16[64,4224]{1,0:T(8,128)(2,1)S(1)}, u32[]{:S(2)}, u32[]{:S(2)}) collective-permute-start(bf16[64,4224]{1,0:T(8,128)(2,1)S(1)} %collective-permute-done.5.refs_0_), channel_id=1, source_target_pairs={{0,24},{2,26},{4,28},{6,30},{8,16},{10,18},{12,20},{14,22},{16,8},... | collective-permute-start | bytes 1622024 | tf_op jit(solution)/shard_map/ppermute | solution.py:407
  29.7 0.6 collective-permute-start.7
  30.3 1.1 collective-permute-start.8
  31.4 2.5 %collective-permute-start.11 = (bf16[32,4224]{1,0:T(8,128)(2,1)S(1)}, bf16[32,4224]{1,0:T(8,128)(2,1)S(1)}, u32[]{:S(2)}, u32[]{:S(2)}) collective-permute-start(bf16[32,4224]{1,0:T(8,128)(2,1)S(1)} %collective-permute-done.2.refs_3_), channel_id=1, source_target_pairs={{0,8},{2,10},{4,12},{6,14},{8,0},{10,2},{12,4},{14,6},{16,24},{18,... | collective-permute-start | bytes 811016 | tf_op jit(solution)/shard_map/ppermute | solution.py:407
  33.9 1.6 %collective-permute-start.12 = (bf16[32,4224]{1,0:T(8,128)(2,1)S(1)}, bf16[32,4224]{1,0:T(8,128)(2,1)S(1)}, u32[]{:S(2)}, u32[]{:S(2)}) collective-permute-start(bf16[32,4224]{1,0:T(8,128)(2,1)S(1)} %collective-permute-done.3.refs_4_), channel_id=1, source_target_pairs={{0,8},{2,10},{4,12},{6,14},{8,0},{10,2},{12,4},{14,6},{16,24},{18,... | collective-permute-start | bytes 811016 | tf_op jit(solution)/shard_map/ppermute | solution.py:407
  35.5 6.3 %expert_set.4 = (bf16[64,2048]{1,0:T(8,128)(2,1)S(1)}, bf16[64,2048]{1,0:T(8,128)(2,1)S(1)}, bf16[64,2048]{1,0:T(8,128)(2,1)S(1)}, bf16[64,2048]{1,0:T(8,128)(2,...) custom-call(bf16[64,4224]{1,0:T(8,128)(2,1)S(1)} %pack_rows.1.refs_6, ...), custom_call_target="tpu_custom_call" | custom-call | flops 4026531840 | tf_op jit(solution)/shard_map/expert_set/pallas_call | solution.py:89
  41.8 1.3 collective-permute-done.6.refs_0_
  43.1 0.8 collective-permute-done.7.refs_1_
  43.9 1.1 collective-permute-start.13
  45.1 0.9 collective-permute-start.10
  46.0 8.2 %collective-permute-start.9 = (bf16[64,4224]{1,0:T(8,128)(2,1)S(1)}, bf16[64,4224]{1,0:T(8,128)(2,1)S(1)}, u32[]{:S(2)}, u32[]{:S(2)}) collective-permute-start(bf16[64,4224]{1,0:T(8,128)(2,1)S(1)} %hold.12), channel_id=1, source_target_pairs={{0,8},{2,10},{4,12},{6,14},{8,0},{10,2},{12,4},{14,6},{16,24},{18,... | collective-permute-start | bytes 1622024 | tf_op jit(solution)/shard_map/ppermute | solution.py:407
  54.2 6.1 %expert_set.5 = (bf16[64,2048]{1,0:T(8,128)(2,1)S(1)}, bf16[64,2048]{1,0:T(8,128)(2,1)S(1)}, bf16[64,2048]{1,0:T(8,128)(2,1)S(1)}, bf16[64,2048]{1,0:T(8,128)(2,...) custom-call(bf16[64,4224]{1,0:T(8,128)(2,1)S(1)} %collective-permute, ...), custom_call_target="tpu_custom_call", output_to_operand_aliasing={{4}: (7, {}), {5}: (8, {}), {6}: (9, {}), {7}: (10, {})} | custom-call | flops 4026531840 | tf_op jit(solution)/shard_map/expert_set/pallas_call | solution.py:89
  60.3 1.0 collective-permute-start.18
  61.4 1.6 %collective-permute-start.17 = (bf16[32,4224]{1,0:T(8,128)(2,1)S(1)}, bf16[32,4224]{1,0:T(8,128)(2,1)S(1)}, u32[]{:S(2)}, u32[]{:S(2)}) collective-permute-start(bf16[32,4224]{1,0:T(8,128)(2,1)S(1)} %part.6.refs_1_), channel_id=1, source_target_pairs={{0,4},{2,6},{4,0},{6,2},{8,12},{10,14},{12,8},{14,10},{16,20},{18,... | collective-permute-start | bytes 811016 | tf_op jit(solution)/shard_map/ppermute | solution.py:407
  62.9 2.2 %collective-permute-done.9.refs_0_ = bf16[64,4224]{1,0:T(8,128)(2,1)S(1)} collective-permute-done((bf16[64,4224]{1,0:T(8,128)(2,1)S(1)}, bf16[64,4224]{1,0:T(8,128)(2,1)S(1)}, u32[]{:S(2)}, u32[]{:S(2)}) %collective-permute-start.9) | collective-permute-done | bytes 540704 | tf_op jit(solution)/shard_map/ppermute | solution.py:407
  65.2 1.0 collective-permute-start.14
  66.2 1.5 %collective-permute-start.15 = (bf16[64,4224]{1,0:T(8,128)(2,1)S(1)}, bf16[64,4224]{1,0:T(8,128)(2,1)S(1)}, u32[]{:S(2)}, u32[]{:S(2)}) collective-permute-start(bf16[64,4224]{1,0:T(8,128)(2,1)S(1)} %hold.13.refs_5_), channel_id=1, source_target_pairs={{0,4},{2,6},{4,0},{6,2},{8,12},{10,14},{12,8},{14,10},{16,20},{18,... | collective-permute-start | bytes 1622024 | tf_op jit(solution)/shard_map/ppermute | solution.py:407
  67.7 5.4 %group_sums.4 = (f32[2,2,8,768]{3,2,1,0:T(8,128)S(1)}, f32[2,6,1024]{2,1,0:T(8,128)S(1)}) custom-call(bf16[512,2048]{1,0:T(8,128)(2,1)S(1)} %get-tuple-element.53.refs_0_, bf16[512,2048]{1,0:T(8,128)(2,1)S(1)} %get-tuple-element.54.refs_1_, bf16[512,768]{1,0:T(8,128)(2,1)S(1)} %get-tuple-element.55.refs_2_, ...), custom_call_target="tpu_custom_call" | custom-call | flops 3623878656 | tf_op jit(solution)/shard_map/group_sums/pallas_call | solution.py:89
  73.1 6.1 %expert_set.6 = (bf16[64,2048]{1,0:T(8,128)(2,1)S(1)}, bf16[64,2048]{1,0:T(8,128)(2,1)S(1)}, bf16[64,2048]{1,0:T(8,128)(2,1)S(1)}, bf16[64,2048]{1,0:T(8,128)(2,...) custom-call(bf16[64,4224]{1,0:T(8,128)(2,1)S(1)} %collective-permute, ...), custom_call_target="tpu_custom_call" | custom-call | flops 4026531840 | tf_op jit(solution)/shard_map/expert_set/pallas_call | solution.py:89
  79.2 0.6 collective-permute-start.19
  79.8 3.8 %collective-permute-start.21 = (bf16[32,4224]{1,0:T(8,128)(2,1)S(1)}, bf16[32,4224]{1,0:T(8,128)(2,1)S(1)}, u32[]{:S(2)}, u32[]{:S(2)}) collective-permute-start(bf16[32,4224]{1,0:T(8,128)(2,1)S(1)} %collective-permute-done.18.refs_4_), channel_id=1, source_target_pairs={{0,8},{2,10},{4,12},{6,14},{8,0},{10,2},{12,4},{14,6},{16,24},{18,... | collective-permute-start | bytes 811016 | tf_op jit(solution)/shard_map/ppermute | solution.py:407
  83.6 5.6 %group_sums.5 = (f32[2,2,8,768]{3,2,1,0:T(8,128)S(1)}, f32[2,6,1024]{2,1,0:T(8,128)S(1)}) custom-call(bf16[512,2048]{1,0:T(8,128)(2,1)S(1)} %get-tuple-element.53.refs_0_, bf16[512,2048]{1,0:T(8,128)(2,1)S(1)} %get-tuple-element.54.refs_1_, bf16[512,768]{1,0:T(8,128)(2,1)S(1)} %get-tuple-element.55.refs_2_, ...), custom_call_target="tpu_custom_call" | custom-call | flops 3623878656 | tf_op jit(solution)/shard_map/group_sums/pallas_call | solution.py:89
  89.2 0.7 collective-permute-start.23
  89.9 1.6 %collective-permute-done.20.refs_3_ = bf16[32,4224]{1,0:T(8,128)(2,1)S(1)} collective-permute-done((bf16[32,4224]{1,0:T(8,128)(2,1)S(1)}, bf16[32,4224]{1,0:T(8,128)(2,1)S(1)}, u32[]{:S(2)}, u32[]{:S(2)}) %collective-permute-start.20) | collective-permute-done | bytes 270368 | tf_op jit(solution)/shard_map/ppermute | solution.py:407
  91.5 6.1 %expert_set.7 = (bf16[64,2048]{1,0:T(8,128)(2,1)S(1)}, bf16[64,2048]{1,0:T(8,128)(2,1)S(1)}, bf16[64,2048]{1,0:T(8,128)(2,1)S(1)}, bf16[64,2048]{1,0:T(8,128)(2,...) custom-call(bf16[64,4224]{1,0:T(8,128)(2,1)S(1)} %collective-permute, ...), custom_call_target="tpu_custom_call", output_to_operand_aliasing={{4}: (7, {}), {5}: (8, {}), {6}: (9, {}), {7}: (10, {})} | custom-call | flops 4026531840 | tf_op jit(solution)/shard_map/expert_set/pallas_call | solution.py:89
  97.6 1.2 collective-permute-start.32
  98.8 0.1 add_rows.9.refs_7_
  98.9 0.9 collective-permute-start.22
  99.8 1.2 collective-permute-start.27
  101.1 1.0 collective-permute-start.16
  102.1 5.4 %group_sums.6 = (f32[2,2,8,768]{3,2,1,0:T(8,128)S(1)}, f32[2,6,1024]{2,1,0:T(8,128)S(1)}) custom-call(bf16[512,2048]{1,0:T(8,128)(2,1)S(1)} %get-tuple-element.68.refs_0_, bf16[512,2048]{1,0:T(8,128)(2,1)S(1)} %get-tuple-element.69.refs_1_, bf16[512,768]{1,0:T(8,128)(2,1)S(1)} %get-tuple-element.70.refs_2_, ...), custom_call_target="tpu_custom_call" | custom-call | flops 3623878656 | tf_op jit(solution)/shard_map/group_sums/pallas_call | solution.py:89
  107.4 1.6 %collective-permute-start.31 = (bf16[64,2048]{1,0:T(8,128)(2,1)S(1)}, bf16[64,2048]{1,0:T(8,128)(2,1)S(1)}, u32[]{:S(2)}, u32[]{:S(2)}) collective-permute-start(bf16[64,2048]{1,0:T(8,128)(2,1)S(1)} %get-tuple-element.78), channel_id=1, source_target_pairs={{0,2},{2,0},{4,6},{6,4},{8,10},{10,8},{12,14},{14,12},{16,18},{18,... | collective-permute-start | bytes 786440 | tf_op jit(solution)/shard_map/ppermute | solution.py:407
  109.1 0.6 collective-permute-start.33
  109.6 2.3 %collective-permute-done.22.refs_1_ = bf16[64,2048]{1,0:T(8,128)(2,1)S(1)} collective-permute-done((bf16[64,2048]{1,0:T(8,128)(2,1)S(1)}, bf16[64,2048]{1,0:T(8,128)(2,1)S(1)}, u32[]{:S(2)}, u32[]{:S(2)}) %collective-permute-start.22) | collective-permute-done | bytes 262176 | tf_op jit(solution)/shard_map/ppermute | solution.py:407
  112.0 0.1 add_rows.10.refs_1_.refs_8_
  112.1 3.1 %collective-permute-start.30 = (bf16[64,2048]{1,0:T(8,128)(2,1)S(1)}, bf16[64,2048]{1,0:T(8,128)(2,1)S(1)}, u32[]{:S(2)}, u32[]{:S(2)}) collective-permute-start(bf16[64,2048]{1,0:T(8,128)(2,1)S(1)} %add_rows.10.refs_1_.refs_8_), channel_id=1, source_target_pairs={{0,16},{2,18},{4,20},{6,22},{8,24},{10,26},{12,28},{14,30},{16,0},... | collective-permute-start | bytes 786440 | tf_op jit(solution)/shard_map/ppermute | solution.py:407
  115.2 2.4 %collective-permute-done.27.refs_1_ = bf16[64,2048]{1,0:T(8,128)(2,1)S(1)} collective-permute-done((bf16[64,2048]{1,0:T(8,128)(2,1)S(1)}, bf16[64,2048]{1,0:T(8,128)(2,1)S(1)}, u32[]{:S(2)}, u32[]{:S(2)}) %collective-permute-start.27) | collective-permute-done | bytes 262176 | tf_op jit(solution)/shard_map/ppermute | solution.py:407
  117.7 2.2 %collective-permute-start.28 = (bf16[64,2048]{1,0:T(8,128)(2,1)S(1)}, bf16[64,2048]{1,0:T(8,128)(2,1)S(1)}, u32[]{:S(2)}, u32[]{:S(2)}) collective-permute-start(bf16[64,2048]{1,0:T(8,128)(2,1)S(1)} %hold.19), channel_id=1, source_target_pairs={{0,4},{2,6},{4,0},{6,2},{8,12},{10,14},{12,8},{14,10},{16,20},{18,... | collective-permute-start | bytes 786440 | tf_op jit(solution)/shard_map/ppermute | solution.py:407
  119.9 0.6 collective-permute-start.26
  120.5 0.1 add_rows.8.refs_0_
  120.6 5.4 %group_sums.7 = (f32[2,2,8,768]{3,2,1,0:T(8,128)S(1)}, f32[2,6,1024]{2,1,0:T(8,128)S(1)}) custom-call(bf16[512,2048]{1,0:T(8,128)(2,1)S(1)} %get-tuple-element.68.refs_0_, bf16[512,2048]{1,0:T(8,128)(2,1)S(1)} %get-tuple-element.69.refs_1_, bf16[512,768]{1,0:T(8,128)(2,1)S(1)} %get-tuple-element.70.refs_2_, ...), custom_call_target="tpu_custom_call" | custom-call | flops 3623878656 | tf_op jit(solution)/shard_map/group_sums/pallas_call | solution.py:89
  126.0 1.2 collective-permute-start.25
  127.2 0.5 collective-permute-start.24
  127.6 0.1 add_rows.14.refs_1_
  127.7 2.6 %collective-permute-start.34 = (bf16[64,2048]{1,0:T(8,128)(2,1)S(1)}, bf16[64,2048]{1,0:T(8,128)(2,1)S(1)}, u32[]{:S(2)}, u32[]{:S(2)}) collective-permute-start(bf16[64,2048]{1,0:T(8,128)(2,1)S(1)} %add_rows.14.refs_1_), channel_id=1, source_target_pairs={{0,24},{2,26},{4,28},{6,30},{8,16},{10,18},{12,20},{14,22},{16,8},... | collective-permute-start | bytes 786440 | tf_op jit(solution)/shard_map/ppermute | solution.py:407
  130.3 0.1 add_rows.12
  130.4 0.1 collective-permute-start.29
  130.5 0.1 collective-permute-start.36
  130.6 1.2 collective-permute-done.36.refs_7_
  131.8 0.2 collective-permute-start.35
  132.0 1.1 collective-permute-done.35.refs_5_
  133.1 2.9 %clip_gradients.1 = (f32[2,2,8,768]{3,2,1,0:T(8,128)}, f32[6,2,1024]{2,1,0:T(2,128)}) custom-call(f32[2,2,16,768]{3,2,1,0:T(8,128)} %bitcast.19, f32[2,2,16,768]{3,2,1,0:T(8,128)} %bitcast.21, f32[6,2,2048]{2,1,0:T(2,128)} %bitcast.23, f32[6,2,2048]{2,1,0:T(2,128)} %bitcast.25, f32[2,2,8,768]{3,2,1,0:T(8,128)S(1)} %get-tuple-element.82.refs_3_.refs_4_, ...), custom_call_target="tpu_custom_call" | custom-call | tf_op jit(solution)/shard_map/clip_gradients/pallas_call | solution.py:89
  136.0 0.1 collective-permute-done.34.refs_5_
  136.2 2.7 %collective-permute-done.29.refs_3_ = bf16[64,2048]{1,0:T(8,128)(2,1)S(1)} collective-permute-done((bf16[64,2048]{1,0:T(8,128)(2,1)S(1)}, bf16[64,2048]{1,0:T(8,128)(2,1)S(1)}, u32[]{:S(2)}, u32[]{:S(2)}) %collective-permute-start.29) | collective-permute-done | bytes 262176 | tf_op jit(solution)/shard_map/ppermute | solution.py:407
  138.9 0.9 add_rows.15
  (44 shorter events, 0.5 us)
Async XLA Ops:
  6.6 23.0 %collective-permute-start.4 = (bf16[3,1024,768]{2,1,0:T(8,128)(2,1)S(1)}, bf16[3,1024,768]{2,1,0:T(8,128)(2,1)S(1)}, u32[]{:S(2)}, u32[]{:S(2)}) collective-permute-start(bf16[3,1024,768]{2,1,0:T(8,128)(2,1)S(1)} %make_weights.1.refs_5_.refs_4_), channel_id=1, source_target_pairs={{0,1},{1,0},{2,3},{3,2},{4,5},{5,4},{6,7},{7,6},{8,9},{9,8},{10,11... | collective-permute-start | bytes 14155784 | tf_op jit(solution)/shard_map/ppermute | solution.py:410
  7.1 15.4 %collective-permute-start = (bf16[64,4224]{1,0:T(8,128)(2,1)S(1)}, bf16[64,4224]{1,0:T(8,128)(2,1)S(1)}, u32[]{:S(2)}, u32[]{:S(2)}) collective-permute-start(bf16[64,4224]{1,0:T(8,128)(2,1)S(1)} %pack_rows.1.refs_6_.refs_0_), channel_id=1, source_target_pairs={{0,2},{2,0},{4,6},{6,4},{8,10},{10,8},{12,14},{14,12},{16,18},{18,... | collective-permute-start | bytes 1622024 | tf_op jit(solution)/shard_map/ppermute | solution.py:407
  9.7 14.7 %collective-permute-start.1 = (bf16[64,4224]{1,0:T(8,128)(2,1)S(1)}, bf16[64,4224]{1,0:T(8,128)(2,1)S(1)}, u32[]{:S(2)}, u32[]{:S(2)}) collective-permute-start(bf16[64,4224]{1,0:T(8,128)(2,1)S(1)} %pack_rows.1.refs_6_.refs_0_), channel_id=1, source_target_pairs={{0,4},{2,6},{4,0},{6,2},{8,12},{10,14},{12,8},{14,10},{16,20},{18,... | collective-permute-start | bytes 1622024 | tf_op jit(solution)/shard_map/ppermute | solution.py:407
  11.2 14.8 %collective-permute-start.5 = (bf16[64,4224]{1,0:T(8,128)(2,1)S(1)}, bf16[64,4224]{1,0:T(8,128)(2,1)S(1)}, u32[]{:S(2)}, u32[]{:S(2)}) collective-permute-start(bf16[64,4224]{1,0:T(8,128)(2,1)S(1)} %pack_rows.1.refs_6_.refs_0_), channel_id=1, source_target_pairs={{0,8},{2,10},{4,12},{6,14},{8,0},{10,2},{12,4},{14,6},{16,24},{18,... | collective-permute-start | bytes 1622024 | tf_op jit(solution)/shard_map/ppermute | solution.py:407
  22.6 8.8 %collective-permute-start.2 = (bf16[32,4224]{1,0:T(8,128)(2,1)S(1)}, bf16[32,4224]{1,0:T(8,128)(2,1)S(1)}, u32[]{:S(2)}, u32[]{:S(2)}) collective-permute-start(bf16[32,4224]{1,0:T(8,128)(2,1)S(1)} %part.4), channel_id=1, source_target_pairs={{0,4},{2,6},{4,0},{6,2},{8,12},{10,14},{12,8},{14,10},{16,20},{18,... | collective-permute-start | bytes 811016 | tf_op jit(solution)/shard_map/ppermute | solution.py:407
  24.5 9.4 %collective-permute-start.3 = (bf16[32,4224]{1,0:T(8,128)(2,1)S(1)}, bf16[32,4224]{1,0:T(8,128)(2,1)S(1)}, u32[]{:S(2)}, u32[]{:S(2)}) collective-permute-start(bf16[32,4224]{1,0:T(8,128)(2,1)S(1)} %part.5), channel_id=1, source_target_pairs={{0,2},{2,0},{4,6},{6,4},{8,10},{10,8},{12,14},{14,12},{16,18},{18,... | collective-permute-start | bytes 811016 | tf_op jit(solution)/shard_map/ppermute | solution.py:407
  26.0 17.1 %collective-permute-start.6 = (bf16[64,4224]{1,0:T(8,128)(2,1)S(1)}, bf16[64,4224]{1,0:T(8,128)(2,1)S(1)}, u32[]{:S(2)}, u32[]{:S(2)}) collective-permute-start(bf16[64,4224]{1,0:T(8,128)(2,1)S(1)} %collective-permute-done.5.refs_0_), channel_id=1, source_target_pairs={{0,24},{2,26},{4,28},{6,30},{8,16},{10,18},{12,20},{14,22},{16,8},... | collective-permute-start | bytes 1622024 | tf_op jit(solution)/shard_map/ppermute | solution.py:407
  29.7 14.2 %collective-permute-start.7 = (bf16[64,4224]{1,0:T(8,128)(2,1)S(1)}, bf16[64,4224]{1,0:T(8,128)(2,1)S(1)}, u32[]{:S(2)}, u32[]{:S(2)}) collective-permute-start(bf16[64,4224]{1,0:T(8,128)(2,1)S(1)} %hold.11), channel_id=1, source_target_pairs={{0,2},{2,0},{4,6},{6,4},{8,10},{10,8},{12,14},{14,12},{16,18},{18,... | collective-permute-start | bytes 1622024 | tf_op jit(solution)/shard_map/ppermute | solution.py:407
  30.3 13.6 %collective-permute-start.8 = (bf16[64,4224]{1,0:T(8,128)(2,1)S(1)}, bf16[64,4224]{1,0:T(8,128)(2,1)S(1)}, u32[]{:S(2)}, u32[]{:S(2)}) collective-permute-start(bf16[64,4224]{1,0:T(8,128)(2,1)S(1)} %hold.11), channel_id=1, source_target_pairs={{0,4},{2,6},{4,0},{6,2},{8,12},{10,14},{12,8},{14,10},{16,20},{18,... | collective-permute-start | bytes 1622024 | tf_op jit(solution)/shard_map/ppermute | solution.py:407
  31.4 22.8 %collective-permute-start.11 = (bf16[32,4224]{1,0:T(8,128)(2,1)S(1)}, bf16[32,4224]{1,0:T(8,128)(2,1)S(1)}, u32[]{:S(2)}, u32[]{:S(2)}) collective-permute-start(bf16[32,4224]{1,0:T(8,128)(2,1)S(1)} %collective-permute-done.2.refs_3_), channel_id=1, source_target_pairs={{0,8},{2,10},{4,12},{6,14},{8,0},{10,2},{12,4},{14,6},{16,24},{18,... | collective-permute-start | bytes 811016 | tf_op jit(solution)/shard_map/ppermute | solution.py:407
  33.9 20.3 %collective-permute-start.12 = (bf16[32,4224]{1,0:T(8,128)(2,1)S(1)}, bf16[32,4224]{1,0:T(8,128)(2,1)S(1)}, u32[]{:S(2)}, u32[]{:S(2)}) collective-permute-start(bf16[32,4224]{1,0:T(8,128)(2,1)S(1)} %collective-permute-done.3.refs_4_), channel_id=1, source_target_pairs={{0,8},{2,10},{4,12},{6,14},{8,0},{10,2},{12,4},{14,6},{16,24},{18,... | collective-permute-start | bytes 811016 | tf_op jit(solution)/shard_map/ppermute | solution.py:407
  43.9 16.4 %collective-permute-start.13 = (bf16[64,4224]{1,0:T(8,128)(2,1)S(1)}, bf16[64,4224]{1,0:T(8,128)(2,1)S(1)}, u32[]{:S(2)}, u32[]{:S(2)}) collective-permute-start(bf16[64,4224]{1,0:T(8,128)(2,1)S(1)} %hold.12), channel_id=1, source_target_pairs={{0,4},{2,6},{4,0},{6,2},{8,12},{10,14},{12,8},{14,10},{16,20},{18,... | collective-permute-start | bytes 1622024 | tf_op jit(solution)/shard_map/ppermute | solution.py:407
  45.1 16.3 %collective-permute-start.10 = (bf16[64,4224]{1,0:T(8,128)(2,1)S(1)}, bf16[64,4224]{1,0:T(8,128)(2,1)S(1)}, u32[]{:S(2)}, u32[]{:S(2)}) collective-permute-start(bf16[64,4224]{1,0:T(8,128)(2,1)S(1)} %hold.12), channel_id=1, source_target_pairs={{0,2},{2,0},{4,6},{6,4},{8,10},{10,8},{12,14},{14,12},{16,18},{18,... | collective-permute-start | bytes 1622024 | tf_op jit(solution)/shard_map/ppermute | solution.py:407
  46.0 19.2 %collective-permute-start.9 = (bf16[64,4224]{1,0:T(8,128)(2,1)S(1)}, bf16[64,4224]{1,0:T(8,128)(2,1)S(1)}, u32[]{:S(2)}, u32[]{:S(2)}) collective-permute-start(bf16[64,4224]{1,0:T(8,128)(2,1)S(1)} %hold.12), channel_id=1, source_target_pairs={{0,8},{2,10},{4,12},{6,14},{8,0},{10,2},{12,4},{14,6},{16,24},{18,... | collective-permute-start | bytes 1622024 | tf_op jit(solution)/shard_map/ppermute | solution.py:407
  60.3 12.8 %collective-permute-start.18 = (bf16[32,4224]{1,0:T(8,128)(2,1)S(1)}, bf16[32,4224]{1,0:T(8,128)(2,1)S(1)}, u32[]{:S(2)}, u32[]{:S(2)}) collective-permute-start(bf16[32,4224]{1,0:T(8,128)(2,1)S(1)} %part.7.refs_2_), channel_id=1, source_target_pairs={{0,2},{2,0},{4,6},{6,4},{8,10},{10,8},{12,14},{14,12},{16,18},{18,... | collective-permute-start | bytes 811016 | tf_op jit(solution)/shard_map/ppermute | solution.py:407
  61.4 11.8 %collective-permute-start.17 = (bf16[32,4224]{1,0:T(8,128)(2,1)S(1)}, bf16[32,4224]{1,0:T(8,128)(2,1)S(1)}, u32[]{:S(2)}, u32[]{:S(2)}) collective-permute-start(bf16[32,4224]{1,0:T(8,128)(2,1)S(1)} %part.6.refs_1_), channel_id=1, source_target_pairs={{0,4},{2,6},{4,0},{6,2},{8,12},{10,14},{12,8},{14,10},{16,20},{18,... | collective-permute-start | bytes 811016 | tf_op jit(solution)/shard_map/ppermute | solution.py:407
  65.2 24.0 %collective-permute-start.14 = (bf16[64,4224]{1,0:T(8,128)(2,1)S(1)}, bf16[64,4224]{1,0:T(8,128)(2,1)S(1)}, u32[]{:S(2)}, u32[]{:S(2)}) collective-permute-start(bf16[64,4224]{1,0:T(8,128)(2,1)S(1)} %hold.13.refs_5_), channel_id=1, source_target_pairs={{0,2},{2,0},{4,6},{6,4},{8,10},{10,8},{12,14},{14,12},{16,18},{18,... | collective-permute-start | bytes 1622024 | tf_op jit(solution)/shard_map/ppermute | solution.py:407
  66.2 23.7 %collective-permute-start.15 = (bf16[64,4224]{1,0:T(8,128)(2,1)S(1)}, bf16[64,4224]{1,0:T(8,128)(2,1)S(1)}, u32[]{:S(2)}, u32[]{:S(2)}) collective-permute-start(bf16[64,4224]{1,0:T(8,128)(2,1)S(1)} %hold.13.refs_5_), channel_id=1, source_target_pairs={{0,4},{2,6},{4,0},{6,2},{8,12},{10,14},{12,8},{14,10},{16,20},{18,... | collective-permute-start | bytes 1622024 | tf_op jit(solution)/shard_map/ppermute | solution.py:407
  79.2 19.6 %collective-permute-start.19 = (bf16[64,2048]{1,0:T(8,128)(2,1)S(1)}, bf16[64,2048]{1,0:T(8,128)(2,1)S(1)}, u32[]{:S(2)}, u32[]{:S(2)}) collective-permute-start(bf16[64,2048]{1,0:T(8,128)(2,1)S(1)} %get-tuple-element.60), channel_id=1, source_target_pairs={{0,4},{2,6},{4,0},{6,2},{8,12},{10,14},{12,8},{14,10},{16,20},{18,... | collective-permute-start | bytes 786440 | tf_op jit(solution)/shard_map/ppermute | solution.py:407
  79.8 10.1 %collective-permute-start.21 = (bf16[32,4224]{1,0:T(8,128)(2,1)S(1)}, bf16[32,4224]{1,0:T(8,128)(2,1)S(1)}, u32[]{:S(2)}, u32[]{:S(2)}) collective-permute-start(bf16[32,4224]{1,0:T(8,128)(2,1)S(1)} %collective-permute-done.18.refs_4_), channel_id=1, source_target_pairs={{0,8},{2,10},{4,12},{6,14},{8,0},{10,2},{12,4},{14,6},{16,24},{18,... | collective-permute-start | bytes 811016 | tf_op jit(solution)/shard_map/ppermute | solution.py:407
  83.6 7.9 %collective-permute-start.20 = (bf16[32,4224]{1,0:T(8,128)(2,1)S(1)}, bf16[32,4224]{1,0:T(8,128)(2,1)S(1)}, u32[]{:S(2)}, u32[]{:S(2)}) collective-permute-start(bf16[32,4224]{1,0:T(8,128)(2,1)S(1)} %collective-permute-done.17.refs_3_), channel_id=1, source_target_pairs={{0,8},{2,10},{4,12},{6,14},{8,0},{10,2},{12,4},{14,6},{16,24},{18,... | collective-permute-start | bytes 811016 | tf_op jit(solution)/shard_map/ppermute | solution.py:407
  89.2 19.8 %collective-permute-start.23 = (bf16[64,2048]{1,0:T(8,128)(2,1)S(1)}, bf16[64,2048]{1,0:T(8,128)(2,1)S(1)}, u32[]{:S(2)}, u32[]{:S(2)}) collective-permute-start(bf16[64,2048]{1,0:T(8,128)(2,1)S(1)} %get-tuple-element.67), channel_id=1, source_target_pairs={{0,4},{2,6},{4,0},{6,2},{8,12},{10,14},{12,8},{14,10},{16,20},{18,... | collective-permute-start | bytes 786440 | tf_op jit(solution)/shard_map/ppermute | solution.py:407
  97.6 9.8 %collective-permute-start.32 = (bf16[64,2048]{1,0:T(8,128)(2,1)S(1)}, bf16[64,2048]{1,0:T(8,128)(2,1)S(1)}, u32[]{:S(2)}, u32[]{:S(2)}) collective-permute-start(bf16[64,2048]{1,0:T(8,128)(2,1)S(1)} %get-tuple-element.80), channel_id=1, source_target_pairs={{0,2},{2,0},{4,6},{6,4},{8,10},{10,8},{12,14},{14,12},{16,18},{18,... | collective-permute-start | bytes 786440 | tf_op jit(solution)/shard_map/ppermute | solution.py:407
  98.9 13.1 %collective-permute-start.22 = (bf16[64,2048]{1,0:T(8,128)(2,1)S(1)}, bf16[64,2048]{1,0:T(8,128)(2,1)S(1)}, u32[]{:S(2)}, u32[]{:S(2)}) collective-permute-start(bf16[64,2048]{1,0:T(8,128)(2,1)S(1)} %add_rows.9.refs_7_), channel_id=1, source_target_pairs={{0,2},{2,0},{4,6},{6,4},{8,10},{10,8},{12,14},{14,12},{16,18},{18,... | collective-permute-start | bytes 786440 | tf_op jit(solution)/shard_map/ppermute | solution.py:407
  99.8 17.7 %collective-permute-start.27 = (bf16[64,2048]{1,0:T(8,128)(2,1)S(1)}, bf16[64,2048]{1,0:T(8,128)(2,1)S(1)}, u32[]{:S(2)}, u32[]{:S(2)}) collective-permute-start(bf16[64,2048]{1,0:T(8,128)(2,1)S(1)} %hold.18), channel_id=1, source_target_pairs={{0,2},{2,0},{4,6},{6,4},{8,10},{10,8},{12,14},{14,12},{16,18},{18,... | collective-permute-start | bytes 786440 | tf_op jit(solution)/shard_map/ppermute | solution.py:407
  101.1 18.8 %collective-permute-start.16 = (bf16[64,2048]{1,0:T(8,128)(2,1)S(1)}, bf16[64,2048]{1,0:T(8,128)(2,1)S(1)}, u32[]{:S(2)}, u32[]{:S(2)}) collective-permute-start(bf16[64,2048]{1,0:T(8,128)(2,1)S(1)} %hold.14), channel_id=1, source_target_pairs={{0,4},{2,6},{4,0},{6,2},{8,12},{10,14},{12,8},{14,10},{16,20},{18,... | collective-permute-start | bytes 786440 | tf_op jit(solution)/shard_map/ppermute | solution.py:407
  107.4 18.5 %collective-permute-start.31 = (bf16[64,2048]{1,0:T(8,128)(2,1)S(1)}, bf16[64,2048]{1,0:T(8,128)(2,1)S(1)}, u32[]{:S(2)}, u32[]{:S(2)}) collective-permute-start(bf16[64,2048]{1,0:T(8,128)(2,1)S(1)} %get-tuple-element.78), channel_id=1, source_target_pairs={{0,2},{2,0},{4,6},{6,4},{8,10},{10,8},{12,14},{14,12},{16,18},{18,... | collective-permute-start | bytes 786440 | tf_op jit(solution)/shard_map/ppermute | solution.py:407
  109.1 18.1 %collective-permute-start.33 = (bf16[64,2048]{1,0:T(8,128)(2,1)S(1)}, bf16[64,2048]{1,0:T(8,128)(2,1)S(1)}, u32[]{:S(2)}, u32[]{:S(2)}) collective-permute-start(bf16[64,2048]{1,0:T(8,128)(2,1)S(1)} %add_rows.13.refs_7_), channel_id=1, source_target_pairs={{0,4},{2,6},{4,0},{6,2},{8,12},{10,14},{12,8},{14,10},{16,20},{18,... | collective-permute-start | bytes 786440 | tf_op jit(solution)/shard_map/ppermute | solution.py:407
  112.1 15.5 %collective-permute-start.30 = (bf16[64,2048]{1,0:T(8,128)(2,1)S(1)}, bf16[64,2048]{1,0:T(8,128)(2,1)S(1)}, u32[]{:S(2)}, u32[]{:S(2)}) collective-permute-start(bf16[64,2048]{1,0:T(8,128)(2,1)S(1)} %add_rows.10.refs_1_.refs_8_), channel_id=1, source_target_pairs={{0,16},{2,18},{4,20},{6,22},{8,24},{10,26},{12,28},{14,30},{16,0},... | collective-permute-start | bytes 786440 | tf_op jit(solution)/shard_map/ppermute | solution.py:407
  117.7 12.7 %collective-permute-start.28 = (bf16[64,2048]{1,0:T(8,128)(2,1)S(1)}, bf16[64,2048]{1,0:T(8,128)(2,1)S(1)}, u32[]{:S(2)}, u32[]{:S(2)}) collective-permute-start(bf16[64,2048]{1,0:T(8,128)(2,1)S(1)} %hold.19), channel_id=1, source_target_pairs={{0,4},{2,6},{4,0},{6,2},{8,12},{10,14},{12,8},{14,10},{16,20},{18,... | collective-permute-start | bytes 786440 | tf_op jit(solution)/shard_map/ppermute | solution.py:407
  119.9 10.4 %collective-permute-start.26 = (bf16[64,2048]{1,0:T(8,128)(2,1)S(1)}, bf16[64,2048]{1,0:T(8,128)(2,1)S(1)}, u32[]{:S(2)}, u32[]{:S(2)}) collective-permute-start(bf16[64,2048]{1,0:T(8,128)(2,1)S(1)} %hold.17), channel_id=1, source_target_pairs={{0,2},{2,0},{4,6},{6,4},{8,10},{10,8},{12,14},{14,12},{16,18},{18,... | collective-permute-start | bytes 786440 | tf_op jit(solution)/shard_map/ppermute | solution.py:407
  126.0 10.1 %collective-permute-start.25 = (bf16[64,2048]{1,0:T(8,128)(2,1)S(1)}, bf16[64,2048]{1,0:T(8,128)(2,1)S(1)}, u32[]{:S(2)}, u32[]{:S(2)}) collective-permute-start(bf16[64,2048]{1,0:T(8,128)(2,1)S(1)} %hold.16), channel_id=1, source_target_pairs={{0,4},{2,6},{4,0},{6,2},{8,12},{10,14},{12,8},{14,10},{16,20},{18,... | collective-permute-start | bytes 786440 | tf_op jit(solution)/shard_map/ppermute | solution.py:407
  127.2 8.9 %collective-permute-start.24 = (bf16[64,2048]{1,0:T(8,128)(2,1)S(1)}, bf16[64,2048]{1,0:T(8,128)(2,1)S(1)}, u32[]{:S(2)}, u32[]{:S(2)}) collective-permute-start(bf16[64,2048]{1,0:T(8,128)(2,1)S(1)} %hold.15), channel_id=1, source_target_pairs={{0,2},{2,0},{4,6},{6,4},{8,10},{10,8},{12,14},{14,12},{16,18},{18,... | collective-permute-start | bytes 786440 | tf_op jit(solution)/shard_map/ppermute | solution.py:407
  127.7 8.4 %collective-permute-start.34 = (bf16[64,2048]{1,0:T(8,128)(2,1)S(1)}, bf16[64,2048]{1,0:T(8,128)(2,1)S(1)}, u32[]{:S(2)}, u32[]{:S(2)}) collective-permute-start(bf16[64,2048]{1,0:T(8,128)(2,1)S(1)} %add_rows.14.refs_1_), channel_id=1, source_target_pairs={{0,24},{2,26},{4,28},{6,30},{8,16},{10,18},{12,20},{14,22},{16,8},... | collective-permute-start | bytes 786440 | tf_op jit(solution)/shard_map/ppermute | solution.py:407
  130.4 8.4 %collective-permute-start.29 = (bf16[64,2048]{1,0:T(8,128)(2,1)S(1)}, bf16[64,2048]{1,0:T(8,128)(2,1)S(1)}, u32[]{:S(2)}, u32[]{:S(2)}) collective-permute-start(bf16[64,2048]{1,0:T(8,128)(2,1)S(1)} %add_rows.12), channel_id=1, source_target_pairs={{0,8},{2,10},{4,12},{6,14},{8,0},{10,2},{12,4},{14,6},{16,24},{18,... | collective-permute-start | bytes 786440 | tf_op jit(solution)/shard_map/ppermute | solution.py:407
  130.5 1.3 collective-permute-start.36
  131.8 1.3 collective-permute-start.35

commit v7 on v6

--- a/solution.py
+++ b/solution.py
@@ -477,12 +477,12 @@
         p3, later = run_set(calls, (last, x3, y3, *d3), weights, experts, later, (mine[0],))
         x_sum0 = added(p0[1], swap(held(p0[3], x3, y3), 2))
         y_sum1 = added(p1[2], swap(held(p1[3], x3, y3), 1))
-        x_sum2 = added(p2[1], swap(p2[3], 2), after=(p3[0],))
-        sums[True] = run_sums(calls, later, weights, True, other, shapes, (x_sum2,))
-        total2 = added(p2[0], swap(x_sum2, 1), swap(p2[2], 2), after=(sums[True][0],))
+        x_sum2 = added(p2[1], swap(p2[3], 2), after=(mine[0],))
+        total2 = added(p2[0], swap(x_sum2, 1), swap(p2[2], 2), after=(p3[0],))
         far_sum = swap(total2, 8)
+        sums[True] = run_sums(calls, later, weights, True, other, shapes, (total2,))
         y_sum3 = added(p3[2], swap(p3[3], 1), after=(sums[True][0],))
-        sums[False] = run_sums(calls, later, weights, False, mine, shapes, (y_sum3, total2))
+        sums[False] = run_sums(calls, later, weights, False, mine, shapes, (y_sum3,))
         total3 = added(p3[0], swap(p3[1], 1), swap(y_sum3, 2), after=(sums[False][0], far_sum))
         late0, late1 = held(p0[2], total2), held(p1[1], total2)
         total1 = added(p1[0], swap(late1, 1), swap(held(y_sum1, total2), 2))

time: 140 us -> 138 us (0.986)
  waiting for transfers between devices: 25.7 us -> 24.1 us
    ppermute x34, waiting for transfers between devices: 23.3 us -> 21.7 us  [swap(): lax.ppermute(array, 'expert', [(i, i ^ mask) for i in range(experts)])]
  transfers between devices with their start and end apart: 37 -> 37, of which waited for: 11 -> 8; matrix products, arithmetic and copies ran while one was open for 0% -> 0% of each run, Pallas kernels for 36% -> 36%
where the time goes in v7:
time: 138 us
  Pallas kernels  56.9 us (41%)
  starting transfers between devices  56.1 us (41%)
  waiting for transfers between devices  24.1 us (17%)
    pallas_call x34, Pallas kernels, run(): pl.pallas_call(wrapped, in_specs=[ANYWHERE] * given + [INSIDE] * count +...  56.9 us
    ppermute x34, starting transfers between devices, swap(): lax.ppermute(array, 'expert', [(i, i ^ mask) for i in range(experts)])  55.4 us
    ppermute x34, waiting for transfers between devices, swap(): lax.ppermute(array, 'expert', [(i, i ^ mask) for i in range(experts)])  21.7 us
  transfers between devices with their start and end apart: 37, of which 8 were waited for; matrix products, arithmetic and copies ran while one was open for 0% of the time, Pallas kernels for 36%

profile of v7, /device:TPU:0, one launch (start us, length us, event | category | flops | bytes accessed | tf_op | source)
XLA Modules:
  0.0 138.0 jit_solution(6404122909033925299)
XLA Ops:
  0.6 1.3 pack_rows.1.refs_6_.refs_0_
  1.9 4.7 %make_weights.1.refs_5_.refs_4_ = bf16[3,1024,768]{2,1,0:T(8,128)(2,1)S(1)} custom-call(s32[2,1024,256]{2,1,0:T(8,128)} %bitcast.16, s32[256,1024]{1,0:T(8,128)} %bitcast.17, f32[2,2,16,768]{3,2,1,0:T(8,128)} %bitcast.18, f32[2,2,16,768]{3,2,1,0:T(8,128)} %bitcast.20, f32[6,2,2048]{2,1,0:T(2,128)} %bitcast.22, f32[6,2,2048]{2,1,0:T(2,128)} %bitcast.24, ...), custom_call_target="tpu_custom_call" | custom-call | tf_op jit(solution)/shard_map/make_weights/pallas_call | solution.py:89
  6.6 0.5 collective-permute-start.4
  7.1 2.6 %collective-permute-start = (bf16[64,4224]{1,0:T(8,128)(2,1)S(1)}, bf16[64,4224]{1,0:T(8,128)(2,1)S(1)}, u32[]{:S(2)}, u32[]{:S(2)}) collective-permute-start(bf16[64,4224]{1,0:T(8,128)(2,1)S(1)} %pack_rows.1.refs_6_.refs_0_), channel_id=1, source_target_pairs={{0,2},{2,0},{4,6},{6,4},{8,10},{10,8},{12,14},{14,12},{16,18},{18,... | collective-permute-start | bytes 1622024 | tf_op jit(solution)/shard_map/ppermute | solution.py:407
  9.7 1.5 %collective-permute-start.1 = (bf16[64,4224]{1,0:T(8,128)(2,1)S(1)}, bf16[64,4224]{1,0:T(8,128)(2,1)S(1)}, u32[]{:S(2)}, u32[]{:S(2)}) collective-permute-start(bf16[64,4224]{1,0:T(8,128)(2,1)S(1)} %pack_rows.1.refs_6_.refs_0_), channel_id=1, source_target_pairs={{0,4},{2,6},{4,0},{6,2},{8,12},{10,14},{12,8},{14,10},{16,20},{18,... | collective-permute-start | bytes 1622024 | tf_op jit(solution)/shard_map/ppermute | solution.py:407
  11.2 1.6 %collective-permute-start.5 = (bf16[64,4224]{1,0:T(8,128)(2,1)S(1)}, bf16[64,4224]{1,0:T(8,128)(2,1)S(1)}, u32[]{:S(2)}, u32[]{:S(2)}) collective-permute-start(bf16[64,4224]{1,0:T(8,128)(2,1)S(1)} %pack_rows.1.refs_6_.refs_0_), channel_id=1, source_target_pairs={{0,8},{2,10},{4,12},{6,14},{8,0},{10,2},{12,4},{14,6},{16,24},{18,... | collective-permute-start | bytes 1622024 | tf_op jit(solution)/shard_map/ppermute | solution.py:407
  12.8 9.8 %collective-permute-done.refs_0_.refs_1_ = bf16[64,4224]{1,0:T(8,128)(2,1)S(1)} collective-permute-done((bf16[64,4224]{1,0:T(8,128)(2,1)S(1)}, bf16[64,4224]{1,0:T(8,128)(2,1)S(1)}, u32[]{:S(2)}, u32[]{:S(2)}) %collective-permute-start) | collective-permute-done | bytes 540704 | tf_op jit(solution)/shard_map/ppermute | solution.py:407
  22.6 1.9 %collective-permute-start.2 = (bf16[32,4224]{1,0:T(8,128)(2,1)S(1)}, bf16[32,4224]{1,0:T(8,128)(2,1)S(1)}, u32[]{:S(2)}, u32[]{:S(2)}) collective-permute-start(bf16[32,4224]{1,0:T(8,128)(2,1)S(1)} %part.4), channel_id=1, source_target_pairs={{0,4},{2,6},{4,0},{6,2},{8,12},{10,14},{12,8},{14,10},{16,20},{18,... | collective-permute-start | bytes 811016 | tf_op jit(solution)/shard_map/ppermute | solution.py:407
  24.4 0.0 collective-permute-done.1.refs_0_.refs_2_
  24.5 1.6 %collective-permute-start.3 = (bf16[32,4224]{1,0:T(8,128)(2,1)S(1)}, bf16[32,4224]{1,0:T(8,128)(2,1)S(1)}, u32[]{:S(2)}, u32[]{:S(2)}) collective-permute-start(bf16[32,4224]{1,0:T(8,128)(2,1)S(1)} %part.5), channel_id=1, source_target_pairs={{0,2},{2,0},{4,6},{6,4},{8,10},{10,8},{12,14},{14,12},{16,18},{18,... | collective-permute-start | bytes 811016 | tf_op jit(solution)/shard_map/ppermute | solution.py:407
  26.0 3.6 %collective-permute-start.6 = (bf16[64,4224]{1,0:T(8,128)(2,1)S(1)}, bf16[64,4224]{1,0:T(8,128)(2,1)S(1)}, u32[]{:S(2)}, u32[]{:S(2)}) collective-permute-start(bf16[64,4224]{1,0:T(8,128)(2,1)S(1)} %collective-permute-done.5.refs_0_), channel_id=1, source_target_pairs={{0,24},{2,26},{4,28},{6,30},{8,16},{10,18},{12,20},{14,22},{16,8},... | collective-permute-start | bytes 1622024 | tf_op jit(solution)/shard_map/ppermute | solution.py:407
  29.7 0.6 collective-permute-start.7
  30.3 1.1 collective-permute-start.8
  31.4 2.5 %collective-permute-start.11 = (bf16[32,4224]{1,0:T(8,128)(2,1)S(1)}, bf16[32,4224]{1,0:T(8,128)(2,1)S(1)}, u32[]{:S(2)}, u32[]{:S(2)}) collective-permute-start(bf16[32,4224]{1,0:T(8,128)(2,1)S(1)} %collective-permute-done.2.refs_3_), channel_id=1, source_target_pairs={{0,8},{2,10},{4,12},{6,14},{8,0},{10,2},{12,4},{14,6},{16,24},{18,... | collective-permute-start | bytes 811016 | tf_op jit(solution)/shard_map/ppermute | solution.py:407
  33.9 1.6 %collective-permute-start.12 = (bf16[32,4224]{1,0:T(8,128)(2,1)S(1)}, bf16[32,4224]{1,0:T(8,128)(2,1)S(1)}, u32[]{:S(2)}, u32[]{:S(2)}) collective-permute-start(bf16[32,4224]{1,0:T(8,128)(2,1)S(1)} %collective-permute-done.3.refs_4_), channel_id=1, source_target_pairs={{0,8},{2,10},{4,12},{6,14},{8,0},{10,2},{12,4},{14,6},{16,24},{18,... | collective-permute-start | bytes 811016 | tf_op jit(solution)/shard_map/ppermute | solution.py:407
  35.5 6.3 %expert_set.4 = (bf16[64,2048]{1,0:T(8,128)(2,1)S(1)}, bf16[64,2048]{1,0:T(8,128)(2,1)S(1)}, bf16[64,2048]{1,0:T(8,128)(2,1)S(1)}, bf16[64,2048]{1,0:T(8,128)(2,...) custom-call(bf16[64,4224]{1,0:T(8,128)(2,1)S(1)} %pack_rows.1.refs_6, ...), custom_call_target="tpu_custom_call" | custom-call | flops 4026531840 | tf_op jit(solution)/shard_map/expert_set/pallas_call | solution.py:89
  41.8 1.3 collective-permute-done.6.refs_0_
  43.1 0.8 collective-permute-done.7.refs_1_
  43.9 1.1 collective-permute-start.13
  45.1 0.9 collective-permute-start.10
  46.0 8.2 %collective-permute-start.9 = (bf16[64,4224]{1,0:T(8,128)(2,1)S(1)}, bf16[64,4224]{1,0:T(8,128)(2,1)S(1)}, u32[]{:S(2)}, u32[]{:S(2)}) collective-permute-start(bf16[64,4224]{1,0:T(8,128)(2,1)S(1)} %hold.12), channel_id=1, source_target_pairs={{0,8},{2,10},{4,12},{6,14},{8,0},{10,2},{12,4},{14,6},{16,24},{18,... | collective-permute-start | bytes 1622024 | tf_op jit(solution)/shard_map/ppermute | solution.py:407
  54.2 6.1 %expert_set.5 = (bf16[64,2048]{1,0:T(8,128)(2,1)S(1)}, bf16[64,2048]{1,0:T(8,128)(2,1)S(1)}, bf16[64,2048]{1,0:T(8,128)(2,1)S(1)}, bf16[64,2048]{1,0:T(8,128)(2,...) custom-call(bf16[64,4224]{1,0:T(8,128)(2,1)S(1)} %collective-permute, ...), custom_call_target="tpu_custom_call", output_to_operand_aliasing={{4}: (7, {}), {5}: (8, {}), {6}: (9, {}), {7}: (10, {})} | custom-call | flops 4026531840 | tf_op jit(solution)/shard_map/expert_set/pallas_call | solution.py:89
  60.3 1.0 collective-permute-start.18
  61.4 1.6 %collective-permute-start.17 = (bf16[32,4224]{1,0:T(8,128)(2,1)S(1)}, bf16[32,4224]{1,0:T(8,128)(2,1)S(1)}, u32[]{:S(2)}, u32[]{:S(2)}) collective-permute-start(bf16[32,4224]{1,0:T(8,128)(2,1)S(1)} %part.6.refs_1_), channel_id=1, source_target_pairs={{0,4},{2,6},{4,0},{6,2},{8,12},{10,14},{12,8},{14,10},{16,20},{18,... | collective-permute-start | bytes 811016 | tf_op jit(solution)/shard_map/ppermute | solution.py:407
  62.9 2.2 %collective-permute-done.9.refs_0_ = bf16[64,4224]{1,0:T(8,128)(2,1)S(1)} collective-permute-done((bf16[64,4224]{1,0:T(8,128)(2,1)S(1)}, bf16[64,4224]{1,0:T(8,128)(2,1)S(1)}, u32[]{:S(2)}, u32[]{:S(2)}) %collective-permute-start.9) | collective-permute-done | bytes 540704 | tf_op jit(solution)/shard_map/ppermute | solution.py:407
  65.2 1.0 collective-permute-start.14
  66.2 1.5 %collective-permute-start.15 = (bf16[64,4224]{1,0:T(8,128)(2,1)S(1)}, bf16[64,4224]{1,0:T(8,128)(2,1)S(1)}, u32[]{:S(2)}, u32[]{:S(2)}) collective-permute-start(bf16[64,4224]{1,0:T(8,128)(2,1)S(1)} %hold.13.refs_5_), channel_id=1, source_target_pairs={{0,4},{2,6},{4,0},{6,2},{8,12},{10,14},{12,8},{14,10},{16,20},{18,... | collective-permute-start | bytes 1622024 | tf_op jit(solution)/shard_map/ppermute | solution.py:407
  67.7 5.4 %group_sums.4 = (f32[2,2,8,768]{3,2,1,0:T(8,128)S(1)}, f32[2,6,1024]{2,1,0:T(8,128)S(1)}) custom-call(bf16[512,2048]{1,0:T(8,128)(2,1)S(1)} %get-tuple-element.53.refs_0_, bf16[512,2048]{1,0:T(8,128)(2,1)S(1)} %get-tuple-element.54.refs_1_, bf16[512,768]{1,0:T(8,128)(2,1)S(1)} %get-tuple-element.55.refs_2_, ...), custom_call_target="tpu_custom_call" | custom-call | flops 3623878656 | tf_op jit(solution)/shard_map/group_sums/pallas_call | solution.py:89
  73.1 6.1 %expert_set.6 = (bf16[64,2048]{1,0:T(8,128)(2,1)S(1)}, bf16[64,2048]{1,0:T(8,128)(2,1)S(1)}, bf16[64,2048]{1,0:T(8,128)(2,1)S(1)}, bf16[64,2048]{1,0:T(8,128)(2,...) custom-call(bf16[64,4224]{1,0:T(8,128)(2,1)S(1)} %collective-permute, ...), custom_call_target="tpu_custom_call" | custom-call | flops 4026531840 | tf_op jit(solution)/shard_map/expert_set/pallas_call | solution.py:89
  79.2 0.6 collective-permute-start.19
  79.8 3.8 %collective-permute-start.23 = (bf16[32,4224]{1,0:T(8,128)(2,1)S(1)}, bf16[32,4224]{1,0:T(8,128)(2,1)S(1)}, u32[]{:S(2)}, u32[]{:S(2)}) collective-permute-start(bf16[32,4224]{1,0:T(8,128)(2,1)S(1)} %collective-permute-done.18.refs_4_), channel_id=1, source_target_pairs={{0,8},{2,10},{4,12},{6,14},{8,0},{10,2},{12,4},{14,6},{16,24},{18,... | collective-permute-start | bytes 811016 | tf_op jit(solution)/shard_map/ppermute | solution.py:407
  83.6 0.0 collective-permute-start.22
  83.6 5.6 %group_sums.5 = (f32[2,2,8,768]{3,2,1,0:T(8,128)S(1)}, f32[2,6,1024]{2,1,0:T(8,128)S(1)}) custom-call(bf16[512,2048]{1,0:T(8,128)(2,1)S(1)} %get-tuple-element.53.refs_0_, bf16[512,2048]{1,0:T(8,128)(2,1)S(1)} %get-tuple-element.54.refs_1_, bf16[512,768]{1,0:T(8,128)(2,1)S(1)} %get-tuple-element.55.refs_2_, ...), custom_call_target="tpu_custom_call" | custom-call | flops 3623878656 | tf_op jit(solution)/shard_map/group_sums/pallas_call | solution.py:89
  89.2 0.7 collective-permute-start.21
  89.9 0.1 add_rows.9
  90.0 1.6 %collective-permute-start.20 = (bf16[64,2048]{1,0:T(8,128)(2,1)S(1)}, bf16[64,2048]{1,0:T(8,128)(2,1)S(1)}, u32[]{:S(2)}, u32[]{:S(2)}) collective-permute-start(bf16[64,2048]{1,0:T(8,128)(2,1)S(1)} %add_rows.9), channel_id=1, source_target_pairs={{0,2},{2,0},{4,6},{6,4},{8,10},{10,8},{12,14},{14,12},{16,18},{18,... | collective-permute-start | bytes 786440 | tf_op jit(solution)/shard_map/ppermute | solution.py:407
  91.6 6.1 %expert_set.7 = (bf16[64,2048]{1,0:T(8,128)(2,1)S(1)}, bf16[64,2048]{1,0:T(8,128)(2,1)S(1)}, bf16[64,2048]{1,0:T(8,128)(2,1)S(1)}, bf16[64,2048]{1,0:T(8,128)(2,...) custom-call(bf16[64,4224]{1,0:T(8,128)(2,1)S(1)} %collective-permute, ...), custom_call_target="tpu_custom_call", output_to_operand_aliasing={{4}: (7, {}), {5}: (8, {}), {6}: (9, {}), {7}: (10, {})} | custom-call | flops 4026531840 | tf_op jit(solution)/shard_map/expert_set/pallas_call | solution.py:89
  97.7 1.2 collective-permute-start.32
  98.8 0.9 collective-permute-start.31
  99.8 1.2 collective-permute-start.27
  101.0 1.0 collective-permute-start.16
  101.9 0.1 add_rows.10.refs_1_.refs_7_
  102.0 3.0 %collective-permute-start.30 = (bf16[64,2048]{1,0:T(8,128)(2,1)S(1)}, bf16[64,2048]{1,0:T(8,128)(2,1)S(1)}, u32[]{:S(2)}, u32[]{:S(2)}) collective-permute-start(bf16[64,2048]{1,0:T(8,128)(2,1)S(1)} %add_rows.10.refs_1_.refs_7_), channel_id=1, source_target_pairs={{0,16},{2,18},{4,20},{6,22},{8,24},{10,26},{12,28},{14,30},{16,0},... | collective-permute-start | bytes 786440 | tf_op jit(solution)/shard_map/ppermute | solution.py:407
  105.1 5.4 %group_sums.6 = (f32[2,2,8,768]{3,2,1,0:T(8,128)S(1)}, f32[2,6,1024]{2,1,0:T(8,128)S(1)}) custom-call(bf16[512,2048]{1,0:T(8,128)(2,1)S(1)} %get-tuple-element.75.refs_0_, bf16[512,2048]{1,0:T(8,128)(2,1)S(1)} %get-tuple-element.76.refs_1_, bf16[512,768]{1,0:T(8,128)(2,1)S(1)} %get-tuple-element.77.refs_2_, ...), custom_call_target="tpu_custom_call" | custom-call | flops 3623878656 | tf_op jit(solution)/shard_map/group_sums/pallas_call | solution.py:89
  110.5 0.2 collective-permute-start.26
  110.8 0.1 add_rows.13.refs_7_
  110.8 5.3 %collective-permute-done.27.refs_1_ = bf16[64,2048]{1,0:T(8,128)(2,1)S(1)} collective-permute-done((bf16[64,2048]{1,0:T(8,128)(2,1)S(1)}, bf16[64,2048]{1,0:T(8,128)(2,1)S(1)}, u32[]{:S(2)}, u32[]{:S(2)}) %collective-permute-start.27) | collective-permute-done | bytes 262176 | tf_op jit(solution)/shard_map/ppermute | solution.py:407
  116.1 1.4 %collective-permute-start.33 = (bf16[64,2048]{1,0:T(8,128)(2,1)S(1)}, bf16[64,2048]{1,0:T(8,128)(2,1)S(1)}, u32[]{:S(2)}, u32[]{:S(2)}) collective-permute-start(bf16[64,2048]{1,0:T(8,128)(2,1)S(1)} %add_rows.13.refs_7_), channel_id=1, source_target_pairs={{0,4},{2,6},{4,0},{6,2},{8,12},{10,14},{12,8},{14,10},{16,20},{18,... | collective-permute-start | bytes 786440 | tf_op jit(solution)/shard_map/ppermute | solution.py:407
  117.5 0.1 add_rows.11.refs_0_
  117.6 0.7 collective-permute-start.28
  118.3 0.1 add_rows.8.refs_0_
  118.4 5.4 %group_sums.7 = (f32[2,2,8,768]{3,2,1,0:T(8,128)S(1)}, f32[2,6,1024]{2,1,0:T(8,128)S(1)}) custom-call(bf16[512,2048]{1,0:T(8,128)(2,1)S(1)} %get-tuple-element.75.refs_0_, bf16[512,2048]{1,0:T(8,128)(2,1)S(1)} %get-tuple-element.76.refs_1_, bf16[512,768]{1,0:T(8,128)(2,1)S(1)} %get-tuple-element.77.refs_2_, ...), custom_call_target="tpu_custom_call" | custom-call | flops 3623878656 | tf_op jit(solution)/shard_map/group_sums/pallas_call | solution.py:89
  123.8 1.5 %collective-permute-start.25 = (bf16[64,2048]{1,0:T(8,128)(2,1)S(1)}, bf16[64,2048]{1,0:T(8,128)(2,1)S(1)}, u32[]{:S(2)}, u32[]{:S(2)}) collective-permute-start(bf16[64,2048]{1,0:T(8,128)(2,1)S(1)} %hold.16), channel_id=1, source_target_pairs={{0,4},{2,6},{4,0},{6,2},{8,12},{10,14},{12,8},{14,10},{16,20},{18,... | collective-permute-start | bytes 786440 | tf_op jit(solution)/shard_map/ppermute | solution.py:407
  125.3 0.6 collective-permute-start.24
  125.8 0.1 add_rows.14.refs_1_
  125.9 2.1 %collective-permute-start.34 = (bf16[64,2048]{1,0:T(8,128)(2,1)S(1)}, bf16[64,2048]{1,0:T(8,128)(2,1)S(1)}, u32[]{:S(2)}, u32[]{:S(2)}) collective-permute-start(bf16[64,2048]{1,0:T(8,128)(2,1)S(1)} %add_rows.14.refs_1_), channel_id=1, source_target_pairs={{0,24},{2,26},{4,28},{6,30},{8,16},{10,18},{12,20},{14,22},{16,8},... | collective-permute-start | bytes 786440 | tf_op jit(solution)/shard_map/ppermute | solution.py:407
  128.1 0.1 add_rows.12
  128.2 1.2 collective-permute-start.29
  129.4 1.2 collective-permute-done.36.refs_7_
  130.6 0.2 collective-permute-start.35
  130.8 1.1 collective-permute-done.35.refs_5_
  131.9 2.9 %clip_gradients.1 = (f32[2,2,8,768]{3,2,1,0:T(8,128)}, f32[6,2,1024]{2,1,0:T(2,128)}) custom-call(f32[2,2,16,768]{3,2,1,0:T(8,128)} %bitcast.19, f32[2,2,16,768]{3,2,1,0:T(8,128)} %bitcast.21, f32[6,2,2048]{2,1,0:T(2,128)} %bitcast.23, f32[6,2,2048]{2,1,0:T(2,128)} %bitcast.25, f32[2,2,8,768]{3,2,1,0:T(8,128)S(1)} %get-tuple-element.82.refs_3_.refs_4_, ...), custom_call_target="tpu_custom_call" | custom-call | tf_op jit(solution)/shard_map/clip_gradients/pallas_call | solution.py:89
  134.8 2.3 %collective-permute-done.29.refs_3_ = bf16[64,2048]{1,0:T(8,128)(2,1)S(1)} collective-permute-done((bf16[64,2048]{1,0:T(8,128)(2,1)S(1)}, bf16[64,2048]{1,0:T(8,128)(2,1)S(1)}, u32[]{:S(2)}, u32[]{:S(2)}) %collective-permute-start.29) | collective-permute-done | bytes 262176 | tf_op jit(solution)/shard_map/ppermute | solution.py:407
  137.1 0.9 add_rows.15
  (44 shorter events, 0.4 us)
Async XLA Ops:
  6.6 23.0 %collective-permute-start.4 = (bf16[3,1024,768]{2,1,0:T(8,128)(2,1)S(1)}, bf16[3,1024,768]{2,1,0:T(8,128)(2,1)S(1)}, u32[]{:S(2)}, u32[]{:S(2)}) collective-permute-start(bf16[3,1024,768]{2,1,0:T(8,128)(2,1)S(1)} %make_weights.1.refs_5_.refs_4_), channel_id=1, source_target_pairs={{0,1},{1,0},{2,3},{3,2},{4,5},{5,4},{6,7},{7,6},{8,9},{9,8},{10,11... | collective-permute-start | bytes 14155784 | tf_op jit(solution)/shard_map/ppermute | solution.py:410
  7.1 15.4 %collective-permute-start = (bf16[64,4224]{1,0:T(8,128)(2,1)S(1)}, bf16[64,4224]{1,0:T(8,128)(2,1)S(1)}, u32[]{:S(2)}, u32[]{:S(2)}) collective-permute-start(bf16[64,4224]{1,0:T(8,128)(2,1)S(1)} %pack_rows.1.refs_6_.refs_0_), channel_id=1, source_target_pairs={{0,2},{2,0},{4,6},{6,4},{8,10},{10,8},{12,14},{14,12},{16,18},{18,... | collective-permute-start | bytes 1622024 | tf_op jit(solution)/shard_map/ppermute | solution.py:407
  9.7 14.7 %collective-permute-start.1 = (bf16[64,4224]{1,0:T(8,128)(2,1)S(1)}, bf16[64,4224]{1,0:T(8,128)(2,1)S(1)}, u32[]{:S(2)}, u32[]{:S(2)}) collective-permute-start(bf16[64,4224]{1,0:T(8,128)(2,1)S(1)} %pack_rows.1.refs_6_.refs_0_), channel_id=1, source_target_pairs={{0,4},{2,6},{4,0},{6,2},{8,12},{10,14},{12,8},{14,10},{16,20},{18,... | collective-permute-start | bytes 1622024 | tf_op jit(solution)/shard_map/ppermute | solution.py:407
  11.2 14.8 %collective-permute-start.5 = (bf16[64,4224]{1,0:T(8,128)(2,1)S(1)}, bf16[64,4224]{1,0:T(8,128)(2,1)S(1)}, u32[]{:S(2)}, u32[]{:S(2)}) collective-permute-start(bf16[64,4224]{1,0:T(8,128)(2,1)S(1)} %pack_rows.1.refs_6_.refs_0_), channel_id=1, source_target_pairs={{0,8},{2,10},{4,12},{6,14},{8,0},{10,2},{12,4},{14,6},{16,24},{18,... | collective-permute-start | bytes 1622024 | tf_op jit(solution)/shard_map/ppermute | solution.py:407
  22.6 8.8 %collective-permute-start.2 = (bf16[32,4224]{1,0:T(8,128)(2,1)S(1)}, bf16[32,4224]{1,0:T(8,128)(2,1)S(1)}, u32[]{:S(2)}, u32[]{:S(2)}) collective-permute-start(bf16[32,4224]{1,0:T(8,128)(2,1)S(1)} %part.4), channel_id=1, source_target_pairs={{0,4},{2,6},{4,0},{6,2},{8,12},{10,14},{12,8},{14,10},{16,20},{18,... | collective-permute-start | bytes 811016 | tf_op jit(solution)/shard_map/ppermute | solution.py:407
  24.5 9.4 %collective-permute-start.3 = (bf16[32,4224]{1,0:T(8,128)(2,1)S(1)}, bf16[32,4224]{1,0:T(8,128)(2,1)S(1)}, u32[]{:S(2)}, u32[]{:S(2)}) collective-permute-start(bf16[32,4224]{1,0:T(8,128)(2,1)S(1)} %part.5), channel_id=1, source_target_pairs={{0,2},{2,0},{4,6},{6,4},{8,10},{10,8},{12,14},{14,12},{16,18},{18,... | collective-permute-start | bytes 811016 | tf_op jit(solution)/shard_map/ppermute | solution.py:407
  26.0 17.1 %collective-permute-start.6 = (bf16[64,4224]{1,0:T(8,128)(2,1)S(1)}, bf16[64,4224]{1,0:T(8,128)(2,1)S(1)}, u32[]{:S(2)}, u32[]{:S(2)}) collective-permute-start(bf16[64,4224]{1,0:T(8,128)(2,1)S(1)} %collective-permute-done.5.refs_0_), channel_id=1, source_target_pairs={{0,24},{2,26},{4,28},{6,30},{8,16},{10,18},{12,20},{14,22},{16,8},... | collective-permute-start | bytes 1622024 | tf_op jit(solution)/shard_map/ppermute | solution.py:407
  29.7 14.2 %collective-permute-start.7 = (bf16[64,4224]{1,0:T(8,128)(2,1)S(1)}, bf16[64,4224]{1,0:T(8,128)(2,1)S(1)}, u32[]{:S(2)}, u32[]{:S(2)}) collective-permute-start(bf16[64,4224]{1,0:T(8,128)(2,1)S(1)} %hold.11), channel_id=1, source_target_pairs={{0,2},{2,0},{4,6},{6,4},{8,10},{10,8},{12,14},{14,12},{16,18},{18,... | collective-permute-start | bytes 1622024 | tf_op jit(solution)/shard_map/ppermute | solution.py:407
  30.3 13.6 %collective-permute-start.8 = (bf16[64,4224]{1,0:T(8,128)(2,1)S(1)}, bf16[64,4224]{1,0:T(8,128)(2,1)S(1)}, u32[]{:S(2)}, u32[]{:S(2)}) collective-permute-start(bf16[64,4224]{1,0:T(8,128)(2,1)S(1)} %hold.11), channel_id=1, source_target_pairs={{0,4},{2,6},{4,0},{6,2},{8,12},{10,14},{12,8},{14,10},{16,20},{18,... | collective-permute-start | bytes 1622024 | tf_op jit(solution)/shard_map/ppermute | solution.py:407
  31.4 22.8 %collective-permute-start.11 = (bf16[32,4224]{1,0:T(8,128)(2,1)S(1)}, bf16[32,4224]{1,0:T(8,128)(2,1)S(1)}, u32[]{:S(2)}, u32[]{:S(2)}) collective-permute-start(bf16[32,4224]{1,0:T(8,128)(2,1)S(1)} %collective-permute-done.2.refs_3_), channel_id=1, source_target_pairs={{0,8},{2,10},{4,12},{6,14},{8,0},{10,2},{12,4},{14,6},{16,24},{18,... | collective-permute-start | bytes 811016 | tf_op jit(solution)/shard_map/ppermute | solution.py:407
  33.9 20.3 %collective-permute-start.12 = (bf16[32,4224]{1,0:T(8,128)(2,1)S(1)}, bf16[32,4224]{1,0:T(8,128)(2,1)S(1)}, u32[]{:S(2)}, u32[]{:S(2)}) collective-permute-start(bf16[32,4224]{1,0:T(8,128)(2,1)S(1)} %collective-permute-done.3.refs_4_), channel_id=1, source_target_pairs={{0,8},{2,10},{4,12},{6,14},{8,0},{10,2},{12,4},{14,6},{16,24},{18,... | collective-permute-start | bytes 811016 | tf_op jit(solution)/shard_map/ppermute | solution.py:407
  43.9 16.4 %collective-permute-start.13 = (bf16[64,4224]{1,0:T(8,128)(2,1)S(1)}, bf16[64,4224]{1,0:T(8,128)(2,1)S(1)}, u32[]{:S(2)}, u32[]{:S(2)}) collective-permute-start(bf16[64,4224]{1,0:T(8,128)(2,1)S(1)} %hold.12), channel_id=1, source_target_pairs={{0,4},{2,6},{4,0},{6,2},{8,12},{10,14},{12,8},{14,10},{16,20},{18,... | collective-permute-start | bytes 1622024 | tf_op jit(solution)/shard_map/ppermute | solution.py:407
  45.1 16.3 %collective-permute-start.10 = (bf16[64,4224]{1,0:T(8,128)(2,1)S(1)}, bf16[64,4224]{1,0:T(8,128)(2,1)S(1)}, u32[]{:S(2)}, u32[]{:S(2)}) collective-permute-start(bf16[64,4224]{1,0:T(8,128)(2,1)S(1)} %hold.12), channel_id=1, source_target_pairs={{0,2},{2,0},{4,6},{6,4},{8,10},{10,8},{12,14},{14,12},{16,18},{18,... | collective-permute-start | bytes 1622024 | tf_op jit(solution)/shard_map/ppermute | solution.py:407
  46.0 19.2 %collective-permute-start.9 = (bf16[64,4224]{1,0:T(8,128)(2,1)S(1)}, bf16[64,4224]{1,0:T(8,128)(2,1)S(1)}, u32[]{:S(2)}, u32[]{:S(2)}) collective-permute-start(bf16[64,4224]{1,0:T(8,128)(2,1)S(1)} %hold.12), channel_id=1, source_target_pairs={{0,8},{2,10},{4,12},{6,14},{8,0},{10,2},{12,4},{14,6},{16,24},{18,... | collective-permute-start | bytes 1622024 | tf_op jit(solution)/shard_map/ppermute | solution.py:407
  60.3 12.8 %collective-permute-start.18 = (bf16[32,4224]{1,0:T(8,128)(2,1)S(1)}, bf16[32,4224]{1,0:T(8,128)(2,1)S(1)}, u32[]{:S(2)}, u32[]{:S(2)}) collective-permute-start(bf16[32,4224]{1,0:T(8,128)(2,1)S(1)} %part.7.refs_2_), channel_id=1, source_target_pairs={{0,2},{2,0},{4,6},{6,4},{8,10},{10,8},{12,14},{14,12},{16,18},{18,... | collective-permute-start | bytes 811016 | tf_op jit(solution)/shard_map/ppermute | solution.py:407
  61.4 11.8 %collective-permute-start.17 = (bf16[32,4224]{1,0:T(8,128)(2,1)S(1)}, bf16[32,4224]{1,0:T(8,128)(2,1)S(1)}, u32[]{:S(2)}, u32[]{:S(2)}) collective-permute-start(bf16[32,4224]{1,0:T(8,128)(2,1)S(1)} %part.6.refs_1_), channel_id=1, source_target_pairs={{0,4},{2,6},{4,0},{6,2},{8,12},{10,14},{12,8},{14,10},{16,20},{18,... | collective-permute-start | bytes 811016 | tf_op jit(solution)/shard_map/ppermute | solution.py:407
  65.2 24.8 %collective-permute-start.14 = (bf16[64,4224]{1,0:T(8,128)(2,1)S(1)}, bf16[64,4224]{1,0:T(8,128)(2,1)S(1)}, u32[]{:S(2)}, u32[]{:S(2)}) collective-permute-start(bf16[64,4224]{1,0:T(8,128)(2,1)S(1)} %hold.13.refs_5_), channel_id=1, source_target_pairs={{0,2},{2,0},{4,6},{6,4},{8,10},{10,8},{12,14},{14,12},{16,18},{18,... | collective-permute-start | bytes 1622024 | tf_op jit(solution)/shard_map/ppermute | solution.py:407
  66.2 25.4 %collective-permute-start.15 = (bf16[64,4224]{1,0:T(8,128)(2,1)S(1)}, bf16[64,4224]{1,0:T(8,128)(2,1)S(1)}, u32[]{:S(2)}, u32[]{:S(2)}) collective-permute-start(bf16[64,4224]{1,0:T(8,128)(2,1)S(1)} %hold.13.refs_5_), channel_id=1, source_target_pairs={{0,4},{2,6},{4,0},{6,2},{8,12},{10,14},{12,8},{14,10},{16,20},{18,... | collective-permute-start | bytes 1622024 | tf_op jit(solution)/shard_map/ppermute | solution.py:407
  79.2 10.0 %collective-permute-start.19 = (bf16[64,2048]{1,0:T(8,128)(2,1)S(1)}, bf16[64,2048]{1,0:T(8,128)(2,1)S(1)}, u32[]{:S(2)}, u32[]{:S(2)}) collective-permute-start(bf16[64,2048]{1,0:T(8,128)(2,1)S(1)} %get-tuple-element.60), channel_id=1, source_target_pairs={{0,4},{2,6},{4,0},{6,2},{8,12},{10,14},{12,8},{14,10},{16,20},{18,... | collective-permute-start | bytes 786440 | tf_op jit(solution)/shard_map/ppermute | solution.py:407
  79.8 11.7 %collective-permute-start.23 = (bf16[32,4224]{1,0:T(8,128)(2,1)S(1)}, bf16[32,4224]{1,0:T(8,128)(2,1)S(1)}, u32[]{:S(2)}, u32[]{:S(2)}) collective-permute-start(bf16[32,4224]{1,0:T(8,128)(2,1)S(1)} %collective-permute-done.18.refs_4_), channel_id=1, source_target_pairs={{0,8},{2,10},{4,12},{6,14},{8,0},{10,2},{12,4},{14,6},{16,24},{18,... | collective-permute-start | bytes 811016 | tf_op jit(solution)/shard_map/ppermute | solution.py:407
  83.6 8.0 %collective-permute-start.22 = (bf16[32,4224]{1,0:T(8,128)(2,1)S(1)}, bf16[32,4224]{1,0:T(8,128)(2,1)S(1)}, u32[]{:S(2)}, u32[]{:S(2)}) collective-permute-start(bf16[32,4224]{1,0:T(8,128)(2,1)S(1)} %collective-permute-done.17.refs_3_), channel_id=1, source_target_pairs={{0,8},{2,10},{4,12},{6,14},{8,0},{10,2},{12,4},{14,6},{16,24},{18,... | collective-permute-start | bytes 811016 | tf_op jit(solution)/shard_map/ppermute | solution.py:407
  89.2 11.7 %collective-permute-start.21 = (bf16[64,2048]{1,0:T(8,128)(2,1)S(1)}, bf16[64,2048]{1,0:T(8,128)(2,1)S(1)}, u32[]{:S(2)}, u32[]{:S(2)}) collective-permute-start(bf16[64,2048]{1,0:T(8,128)(2,1)S(1)} %get-tuple-element.62), channel_id=1, source_target_pairs={{0,4},{2,6},{4,0},{6,2},{8,12},{10,14},{12,8},{14,10},{16,20},{18,... | collective-permute-start | bytes 786440 | tf_op jit(solution)/shard_map/ppermute | solution.py:407
  90.0 12.0 %collective-permute-start.20 = (bf16[64,2048]{1,0:T(8,128)(2,1)S(1)}, bf16[64,2048]{1,0:T(8,128)(2,1)S(1)}, u32[]{:S(2)}, u32[]{:S(2)}) collective-permute-start(bf16[64,2048]{1,0:T(8,128)(2,1)S(1)} %add_rows.9), channel_id=1, source_target_pairs={{0,2},{2,0},{4,6},{6,4},{8,10},{10,8},{12,14},{14,12},{16,18},{18,... | collective-permute-start | bytes 786440 | tf_op jit(solution)/shard_map/ppermute | solution.py:407
  97.7 12.8 %collective-permute-start.32 = (bf16[64,2048]{1,0:T(8,128)(2,1)S(1)}, bf16[64,2048]{1,0:T(8,128)(2,1)S(1)}, u32[]{:S(2)}, u32[]{:S(2)}) collective-permute-start(bf16[64,2048]{1,0:T(8,128)(2,1)S(1)} %get-tuple-element.74), channel_id=1, source_target_pairs={{0,2},{2,0},{4,6},{6,4},{8,10},{10,8},{12,14},{14,12},{16,18},{18,... | collective-permute-start | bytes 786440 | tf_op jit(solution)/shard_map/ppermute | solution.py:407
  98.8 24.9 %collective-permute-start.31 = (bf16[64,2048]{1,0:T(8,128)(2,1)S(1)}, bf16[64,2048]{1,0:T(8,128)(2,1)S(1)}, u32[]{:S(2)}, u32[]{:S(2)}) collective-permute-start(bf16[64,2048]{1,0:T(8,128)(2,1)S(1)} %get-tuple-element.72), channel_id=1, source_target_pairs={{0,2},{2,0},{4,6},{6,4},{8,10},{10,8},{12,14},{14,12},{16,18},{18,... | collective-permute-start | bytes 786440 | tf_op jit(solution)/shard_map/ppermute | solution.py:407
  99.8 16.3 %collective-permute-start.27 = (bf16[64,2048]{1,0:T(8,128)(2,1)S(1)}, bf16[64,2048]{1,0:T(8,128)(2,1)S(1)}, u32[]{:S(2)}, u32[]{:S(2)}) collective-permute-start(bf16[64,2048]{1,0:T(8,128)(2,1)S(1)} %hold.18), channel_id=1, source_target_pairs={{0,2},{2,0},{4,6},{6,4},{8,10},{10,8},{12,14},{14,12},{16,18},{18,... | collective-permute-start | bytes 786440 | tf_op jit(solution)/shard_map/ppermute | solution.py:407
  101.0 16.6 %collective-permute-start.16 = (bf16[64,2048]{1,0:T(8,128)(2,1)S(1)}, bf16[64,2048]{1,0:T(8,128)(2,1)S(1)}, u32[]{:S(2)}, u32[]{:S(2)}) collective-permute-start(bf16[64,2048]{1,0:T(8,128)(2,1)S(1)} %hold.14), channel_id=1, source_target_pairs={{0,4},{2,6},{4,0},{6,2},{8,12},{10,14},{12,8},{14,10},{16,20},{18,... | collective-permute-start | bytes 786440 | tf_op jit(solution)/shard_map/ppermute | solution.py:407
  102.0 23.2 %collective-permute-start.30 = (bf16[64,2048]{1,0:T(8,128)(2,1)S(1)}, bf16[64,2048]{1,0:T(8,128)(2,1)S(1)}, u32[]{:S(2)}, u32[]{:S(2)}) collective-permute-start(bf16[64,2048]{1,0:T(8,128)(2,1)S(1)} %add_rows.10.refs_1_.refs_7_), channel_id=1, source_target_pairs={{0,16},{2,18},{4,20},{6,22},{8,24},{10,26},{12,28},{14,30},{16,0},... | collective-permute-start | bytes 786440 | tf_op jit(solution)/shard_map/ppermute | solution.py:407
  110.5 17.6 %collective-permute-start.26 = (bf16[64,2048]{1,0:T(8,128)(2,1)S(1)}, bf16[64,2048]{1,0:T(8,128)(2,1)S(1)}, u32[]{:S(2)}, u32[]{:S(2)}) collective-permute-start(bf16[64,2048]{1,0:T(8,128)(2,1)S(1)} %hold.17), channel_id=1, source_target_pairs={{0,2},{2,0},{4,6},{6,4},{8,10},{10,8},{12,14},{14,12},{16,18},{18,... | collective-permute-start | bytes 786440 | tf_op jit(solution)/shard_map/ppermute | solution.py:407
  116.1 9.7 %collective-permute-start.33 = (bf16[64,2048]{1,0:T(8,128)(2,1)S(1)}, bf16[64,2048]{1,0:T(8,128)(2,1)S(1)}, u32[]{:S(2)}, u32[]{:S(2)}) collective-permute-start(bf16[64,2048]{1,0:T(8,128)(2,1)S(1)} %add_rows.13.refs_7_), channel_id=1, source_target_pairs={{0,4},{2,6},{4,0},{6,2},{8,12},{10,14},{12,8},{14,10},{16,20},{18,... | collective-permute-start | bytes 786440 | tf_op jit(solution)/shard_map/ppermute | solution.py:407
  117.6 10.5 %collective-permute-start.28 = (bf16[64,2048]{1,0:T(8,128)(2,1)S(1)}, bf16[64,2048]{1,0:T(8,128)(2,1)S(1)}, u32[]{:S(2)}, u32[]{:S(2)}) collective-permute-start(bf16[64,2048]{1,0:T(8,128)(2,1)S(1)} %hold.19), channel_id=1, source_target_pairs={{0,4},{2,6},{4,0},{6,2},{8,12},{10,14},{12,8},{14,10},{16,20},{18,... | collective-permute-start | bytes 786440 | tf_op jit(solution)/shard_map/ppermute | solution.py:407
  123.8 11.0 %collective-permute-start.25 = (bf16[64,2048]{1,0:T(8,128)(2,1)S(1)}, bf16[64,2048]{1,0:T(8,128)(2,1)S(1)}, u32[]{:S(2)}, u32[]{:S(2)}) collective-permute-start(bf16[64,2048]{1,0:T(8,128)(2,1)S(1)} %hold.16), channel_id=1, source_target_pairs={{0,4},{2,6},{4,0},{6,2},{8,12},{10,14},{12,8},{14,10},{16,20},{18,... | collective-permute-start | bytes 786440 | tf_op jit(solution)/shard_map/ppermute | solution.py:407
  125.3 9.5 %collective-permute-start.24 = (bf16[64,2048]{1,0:T(8,128)(2,1)S(1)}, bf16[64,2048]{1,0:T(8,128)(2,1)S(1)}, u32[]{:S(2)}, u32[]{:S(2)}) collective-permute-start(bf16[64,2048]{1,0:T(8,128)(2,1)S(1)} %hold.15), channel_id=1, source_target_pairs={{0,2},{2,0},{4,6},{6,4},{8,10},{10,8},{12,14},{14,12},{16,18},{18,... | collective-permute-start | bytes 786440 | tf_op jit(solution)/shard_map/ppermute | solution.py:407
  125.9 8.9 %collective-permute-start.34 = (bf16[64,2048]{1,0:T(8,128)(2,1)S(1)}, bf16[64,2048]{1,0:T(8,128)(2,1)S(1)}, u32[]{:S(2)}, u32[]{:S(2)}) collective-permute-start(bf16[64,2048]{1,0:T(8,128)(2,1)S(1)} %add_rows.14.refs_1_), channel_id=1, source_target_pairs={{0,24},{2,26},{4,28},{6,30},{8,16},{10,18},{12,20},{14,22},{16,8},... | collective-permute-start | bytes 786440 | tf_op jit(solution)/shard_map/ppermute | solution.py:407
  128.2 8.9 %collective-permute-start.29 = (bf16[64,2048]{1,0:T(8,128)(2,1)S(1)}, bf16[64,2048]{1,0:T(8,128)(2,1)S(1)}, u32[]{:S(2)}, u32[]{:S(2)}) collective-permute-start(bf16[64,2048]{1,0:T(8,128)(2,1)S(1)} %add_rows.12), channel_id=1, source_target_pairs={{0,8},{2,10},{4,12},{6,14},{8,0},{10,2},{12,4},{14,6},{16,24},{18,... | collective-permute-start | bytes 786440 | tf_op jit(solution)/shard_map/ppermute | solution.py:407
  129.3 1.3 collective-permute-start.36
  130.6 1.3 collective-permute-start.35

commit v8 on v7

--- a/solution.py
+++ b/solution.py
@@ -484,11 +484,11 @@
         y_sum3 = added(p3[2], swap(p3[3], 1), after=(sums[True][0],))
         sums[False] = run_sums(calls, later, weights, False, mine, shapes, (y_sum3,))
         total3 = added(p3[0], swap(p3[1], 1), swap(y_sum3, 2), after=(sums[False][0], far_sum))
-        late0, late1 = held(p0[2], total2), held(p1[1], total2)
-        total1 = added(p1[0], swap(late1, 1), swap(held(y_sum1, total2), 2))
+        late0, late1 = held(p0[2], y_sum3), held(p1[1], y_sum3)
+        total1 = added(p1[0], swap(late1, 1), swap(held(y_sum1, y_sum3), 2))
         parts = (
             p0[0],
-            swap(held(x_sum0, total2), 1),
+            swap(held(x_sum0, y_sum3), 1),
             swap(late0, 2),
             swap(total1, 4),
             far_sum,

time: 138 us -> 136 us (0.986)
  waiting for transfers between devices: 24.1 us -> 22.5 us
    ppermute x34, waiting for transfers between devices: 21.7 us -> 20.2 us  [swap(): lax.ppermute(array, 'expert', [(i, i ^ mask) for i in range(experts)])]
  transfers between devices with their start and end apart: 37 -> 37, of which waited for: 8 -> 9; matrix products, arithmetic and copies ran while one was open for 0% -> 0% of each run, Pallas kernels for 36% -> 37%
where the time goes in v8:
time: 136 us
  Pallas kernels  56.9 us (42%)
  starting transfers between devices  55.7 us (41%)
  waiting for transfers between devices  22.5 us (17%)
    pallas_call x34, Pallas kernels, run(): pl.pallas_call(wrapped, in_specs=[ANYWHERE] * given + [INSIDE] * count +...  56.9 us
    ppermute x34, starting transfers between devices, swap(): lax.ppermute(array, 'expert', [(i, i ^ mask) for i in range(experts)])  55.1 us
    ppermute x34, waiting for transfers between devices, swap(): lax.ppermute(array, 'expert', [(i, i ^ mask) for i in range(experts)])  20.2 us
  transfers between devices with their start and end apart: 37, of which 9 were waited for; matrix products, arithmetic and copies ran while one was open for 0% of the time, Pallas kernels for 37%

profile of v8, /device:TPU:0, one launch (start us, length us, event | category | flops | bytes accessed | tf_op | source)
XLA Modules:
  0.0 136.1 jit_solution(11309529620101959811)
XLA Ops:
  0.6 1.3 pack_rows.1.refs_6_.refs_0_
  1.9 4.7 %make_weights.1.refs_5_.refs_4_ = bf16[3,1024,768]{2,1,0:T(8,128)(2,1)S(1)} custom-call(s32[2,1024,256]{2,1,0:T(8,128)} %bitcast.16, s32[256,1024]{1,0:T(8,128)} %bitcast.17, f32[2,2,16,768]{3,2,1,0:T(8,128)} %bitcast.18, f32[2,2,16,768]{3,2,1,0:T(8,128)} %bitcast.20, f32[6,2,2048]{2,1,0:T(2,128)} %bitcast.22, f32[6,2,2048]{2,1,0:T(2,128)} %bitcast.24, ...), custom_call_target="tpu_custom_call" | custom-call | tf_op jit(solution)/shard_map/make_weights/pallas_call | solution.py:89
  6.6 0.5 collective-permute-start.4
  7.1 2.6 %collective-permute-start = (bf16[64,4224]{1,0:T(8,128)(2,1)S(1)}, bf16[64,4224]{1,0:T(8,128)(2,1)S(1)}, u32[]{:S(2)}, u32[]{:S(2)}) collective-permute-start(bf16[64,4224]{1,0:T(8,128)(2,1)S(1)} %pack_rows.1.refs_6_.refs_0_), channel_id=1, source_target_pairs={{0,2},{2,0},{4,6},{6,4},{8,10},{10,8},{12,14},{14,12},{16,18},{18,... | collective-permute-start | bytes 1622024 | tf_op jit(solution)/shard_map/ppermute | solution.py:407
  9.7 1.5 %collective-permute-start.1 = (bf16[64,4224]{1,0:T(8,128)(2,1)S(1)}, bf16[64,4224]{1,0:T(8,128)(2,1)S(1)}, u32[]{:S(2)}, u32[]{:S(2)}) collective-permute-start(bf16[64,4224]{1,0:T(8,128)(2,1)S(1)} %pack_rows.1.refs_6_.refs_0_), channel_id=1, source_target_pairs={{0,4},{2,6},{4,0},{6,2},{8,12},{10,14},{12,8},{14,10},{16,20},{18,... | collective-permute-start | bytes 1622024 | tf_op jit(solution)/shard_map/ppermute | solution.py:407
  11.2 1.6 %collective-permute-start.5 = (bf16[64,4224]{1,0:T(8,128)(2,1)S(1)}, bf16[64,4224]{1,0:T(8,128)(2,1)S(1)}, u32[]{:S(2)}, u32[]{:S(2)}) collective-permute-start(bf16[64,4224]{1,0:T(8,128)(2,1)S(1)} %pack_rows.1.refs_6_.refs_0_), channel_id=1, source_target_pairs={{0,8},{2,10},{4,12},{6,14},{8,0},{10,2},{12,4},{14,6},{16,24},{18,... | collective-permute-start | bytes 1622024 | tf_op jit(solution)/shard_map/ppermute | solution.py:407
  12.8 9.8 %collective-permute-done.refs_0_.refs_1_ = bf16[64,4224]{1,0:T(8,128)(2,1)S(1)} collective-permute-done((bf16[64,4224]{1,0:T(8,128)(2,1)S(1)}, bf16[64,4224]{1,0:T(8,128)(2,1)S(1)}, u32[]{:S(2)}, u32[]{:S(2)}) %collective-permute-start) | collective-permute-done | bytes 540704 | tf_op jit(solution)/shard_map/ppermute | solution.py:407
  22.6 1.9 %collective-permute-start.2 = (bf16[32,4224]{1,0:T(8,128)(2,1)S(1)}, bf16[32,4224]{1,0:T(8,128)(2,1)S(1)}, u32[]{:S(2)}, u32[]{:S(2)}) collective-permute-start(bf16[32,4224]{1,0:T(8,128)(2,1)S(1)} %part.4), channel_id=1, source_target_pairs={{0,4},{2,6},{4,0},{6,2},{8,12},{10,14},{12,8},{14,10},{16,20},{18,... | collective-permute-start | bytes 811016 | tf_op jit(solution)/shard_map/ppermute | solution.py:407
  24.5 1.6 %collective-permute-start.3 = (bf16[32,4224]{1,0:T(8,128)(2,1)S(1)}, bf16[32,4224]{1,0:T(8,128)(2,1)S(1)}, u32[]{:S(2)}, u32[]{:S(2)}) collective-permute-start(bf16[32,4224]{1,0:T(8,128)(2,1)S(1)} %part.5), channel_id=1, source_target_pairs={{0,2},{2,0},{4,6},{6,4},{8,10},{10,8},{12,14},{14,12},{16,18},{18,... | collective-permute-start | bytes 811016 | tf_op jit(solution)/shard_map/ppermute | solution.py:407
  26.0 3.6 %collective-permute-start.6 = (bf16[64,4224]{1,0:T(8,128)(2,1)S(1)}, bf16[64,4224]{1,0:T(8,128)(2,1)S(1)}, u32[]{:S(2)}, u32[]{:S(2)}) collective-permute-start(bf16[64,4224]{1,0:T(8,128)(2,1)S(1)} %collective-permute-done.5.refs_0_), channel_id=1, source_target_pairs={{0,24},{2,26},{4,28},{6,30},{8,16},{10,18},{12,20},{14,22},{16,8},... | collective-permute-start | bytes 1622024 | tf_op jit(solution)/shard_map/ppermute | solution.py:407
  29.7 0.6 collective-permute-start.7
  30.3 1.1 collective-permute-start.8
  31.4 2.5 %collective-permute-start.11 = (bf16[32,4224]{1,0:T(8,128)(2,1)S(1)}, bf16[32,4224]{1,0:T(8,128)(2,1)S(1)}, u32[]{:S(2)}, u32[]{:S(2)}) collective-permute-start(bf16[32,4224]{1,0:T(8,128)(2,1)S(1)} %collective-permute-done.2.refs_3_), channel_id=1, source_target_pairs={{0,8},{2,10},{4,12},{6,14},{8,0},{10,2},{12,4},{14,6},{16,24},{18,... | collective-permute-start | bytes 811016 | tf_op jit(solution)/shard_map/ppermute | solution.py:407
  33.9 1.6 %collective-permute-start.12 = (bf16[32,4224]{1,0:T(8,128)(2,1)S(1)}, bf16[32,4224]{1,0:T(8,128)(2,1)S(1)}, u32[]{:S(2)}, u32[]{:S(2)}) collective-permute-start(bf16[32,4224]{1,0:T(8,128)(2,1)S(1)} %collective-permute-done.3.refs_4_), channel_id=1, source_target_pairs={{0,8},{2,10},{4,12},{6,14},{8,0},{10,2},{12,4},{14,6},{16,24},{18,... | collective-permute-start | bytes 811016 | tf_op jit(solution)/shard_map/ppermute | solution.py:407
  35.5 6.3 %expert_set.4 = (bf16[64,2048]{1,0:T(8,128)(2,1)S(1)}, bf16[64,2048]{1,0:T(8,128)(2,1)S(1)}, bf16[64,2048]{1,0:T(8,128)(2,1)S(1)}, bf16[64,2048]{1,0:T(8,128)(2,...) custom-call(bf16[64,4224]{1,0:T(8,128)(2,1)S(1)} %pack_rows.1.refs_6, ...), custom_call_target="tpu_custom_call" | custom-call | flops 4026531840 | tf_op jit(solution)/shard_map/expert_set/pallas_call | solution.py:89
  41.8 1.3 collective-permute-done.6.refs_0_
  43.1 0.8 collective-permute-done.7.refs_1_
  43.9 1.1 collective-permute-start.13
  45.1 0.9 collective-permute-start.10
  46.0 8.2 %collective-permute-start.9 = (bf16[64,4224]{1,0:T(8,128)(2,1)S(1)}, bf16[64,4224]{1,0:T(8,128)(2,1)S(1)}, u32[]{:S(2)}, u32[]{:S(2)}) collective-permute-start(bf16[64,4224]{1,0:T(8,128)(2,1)S(1)} %hold.12), channel_id=1, source_target_pairs={{0,8},{2,10},{4,12},{6,14},{8,0},{10,2},{12,4},{14,6},{16,24},{18,... | collective-permute-start | bytes 1622024 | tf_op jit(solution)/shard_map/ppermute | solution.py:407
  54.2 6.1 %expert_set.5 = (bf16[64,2048]{1,0:T(8,128)(2,1)S(1)}, bf16[64,2048]{1,0:T(8,128)(2,1)S(1)}, bf16[64,2048]{1,0:T(8,128)(2,1)S(1)}, bf16[64,2048]{1,0:T(8,128)(2,...) custom-call(bf16[64,4224]{1,0:T(8,128)(2,1)S(1)} %collective-permute, ...), custom_call_target="tpu_custom_call", output_to_operand_aliasing={{4}: (7, {}), {5}: (8, {}), {6}: (9, {}), {7}: (10, {})} | custom-call | flops 4026531840 | tf_op jit(solution)/shard_map/expert_set/pallas_call | solution.py:89
  60.3 1.0 collective-permute-start.19
  61.4 1.6 %collective-permute-start.17 = (bf16[32,4224]{1,0:T(8,128)(2,1)S(1)}, bf16[32,4224]{1,0:T(8,128)(2,1)S(1)}, u32[]{:S(2)}, u32[]{:S(2)}) collective-permute-start(bf16[32,4224]{1,0:T(8,128)(2,1)S(1)} %part.6.refs_1_), channel_id=1, source_target_pairs={{0,4},{2,6},{4,0},{6,2},{8,12},{10,14},{12,8},{14,10},{16,20},{18,... | collective-permute-start | bytes 811016 | tf_op jit(solution)/shard_map/ppermute | solution.py:407
  62.9 2.2 %collective-permute-done.9.refs_0_ = bf16[64,4224]{1,0:T(8,128)(2,1)S(1)} collective-permute-done((bf16[64,4224]{1,0:T(8,128)(2,1)S(1)}, bf16[64,4224]{1,0:T(8,128)(2,1)S(1)}, u32[]{:S(2)}, u32[]{:S(2)}) %collective-permute-start.9) | collective-permute-done | bytes 540704 | tf_op jit(solution)/shard_map/ppermute | solution.py:407
  65.2 1.0 collective-permute-start.14
  66.2 1.5 %collective-permute-start.15 = (bf16[64,4224]{1,0:T(8,128)(2,1)S(1)}, bf16[64,4224]{1,0:T(8,128)(2,1)S(1)}, u32[]{:S(2)}, u32[]{:S(2)}) collective-permute-start(bf16[64,4224]{1,0:T(8,128)(2,1)S(1)} %hold.13.refs_5_), channel_id=1, source_target_pairs={{0,4},{2,6},{4,0},{6,2},{8,12},{10,14},{12,8},{14,10},{16,20},{18,... | collective-permute-start | bytes 1622024 | tf_op jit(solution)/shard_map/ppermute | solution.py:407
  67.7 5.4 %group_sums.4 = (f32[2,2,8,768]{3,2,1,0:T(8,128)S(1)}, f32[2,6,1024]{2,1,0:T(8,128)S(1)}) custom-call(bf16[512,2048]{1,0:T(8,128)(2,1)S(1)} %get-tuple-element.53.refs_0_, bf16[512,2048]{1,0:T(8,128)(2,1)S(1)} %get-tuple-element.54.refs_1_, bf16[512,768]{1,0:T(8,128)(2,1)S(1)} %get-tuple-element.55.refs_2_, ...), custom_call_target="tpu_custom_call" | custom-call | flops 3623878656 | tf_op jit(solution)/shard_map/group_sums/pallas_call | solution.py:89
  73.1 6.1 %expert_set.6 = (bf16[64,2048]{1,0:T(8,128)(2,1)S(1)}, bf16[64,2048]{1,0:T(8,128)(2,1)S(1)}, bf16[64,2048]{1,0:T(8,128)(2,1)S(1)}, bf16[64,2048]{1,0:T(8,128)(2,...) custom-call(bf16[64,4224]{1,0:T(8,128)(2,1)S(1)} %collective-permute, ...), custom_call_target="tpu_custom_call" | custom-call | flops 4026531840 | tf_op jit(solution)/shard_map/expert_set/pallas_call | solution.py:89
  79.2 0.6 collective-permute-start.22
  79.8 3.8 %collective-permute-start.20 = (bf16[32,4224]{1,0:T(8,128)(2,1)S(1)}, bf16[32,4224]{1,0:T(8,128)(2,1)S(1)}, u32[]{:S(2)}, u32[]{:S(2)}) collective-permute-start(bf16[32,4224]{1,0:T(8,128)(2,1)S(1)} %collective-permute-done.19.refs_4_), channel_id=1, source_target_pairs={{0,8},{2,10},{4,12},{6,14},{8,0},{10,2},{12,4},{14,6},{16,24},{18,... | collective-permute-start | bytes 811016 | tf_op jit(solution)/shard_map/ppermute | solution.py:407
  83.6 0.0 collective-permute-start.18
  83.6 5.6 %group_sums.5 = (f32[2,2,8,768]{3,2,1,0:T(8,128)S(1)}, f32[2,6,1024]{2,1,0:T(8,128)S(1)}) custom-call(bf16[512,2048]{1,0:T(8,128)(2,1)S(1)} %get-tuple-element.53.refs_0_, bf16[512,2048]{1,0:T(8,128)(2,1)S(1)} %get-tuple-element.54.refs_1_, bf16[512,768]{1,0:T(8,128)(2,1)S(1)} %get-tuple-element.55.refs_2_, ...), custom_call_target="tpu_custom_call" | custom-call | flops 3623878656 | tf_op jit(solution)/shard_map/group_sums/pallas_call | solution.py:89
  89.2 0.7 collective-permute-start.24
  89.9 0.1 add_rows.9
  90.0 1.6 %collective-permute-start.23 = (bf16[64,2048]{1,0:T(8,128)(2,1)S(1)}, bf16[64,2048]{1,0:T(8,128)(2,1)S(1)}, u32[]{:S(2)}, u32[]{:S(2)}) collective-permute-start(bf16[64,2048]{1,0:T(8,128)(2,1)S(1)} %add_rows.9), channel_id=1, source_target_pairs={{0,2},{2,0},{4,6},{6,4},{8,10},{10,8},{12,14},{14,12},{16,18},{18,... | collective-permute-start | bytes 786440 | tf_op jit(solution)/shard_map/ppermute | solution.py:407
  91.6 6.1 %expert_set.7 = (bf16[64,2048]{1,0:T(8,128)(2,1)S(1)}, bf16[64,2048]{1,0:T(8,128)(2,1)S(1)}, bf16[64,2048]{1,0:T(8,128)(2,1)S(1)}, bf16[64,2048]{1,0:T(8,128)(2,...) custom-call(bf16[64,4224]{1,0:T(8,128)(2,1)S(1)} %collective-permute, ...), custom_call_target="tpu_custom_call", output_to_operand_aliasing={{4}: (7, {}), {5}: (8, {}), {6}: (9, {}), {7}: (10, {})} | custom-call | flops 4026531840 | tf_op jit(solution)/shard_map/expert_set/pallas_call | solution.py:89
  97.7 1.2 collective-permute-start.21
  98.8 0.9 collective-permute-start.32
  99.8 1.2 collective-permute-start.28
  101.0 1.0 collective-permute-start.16
  101.9 0.1 add_rows.10.refs_7_
  102.0 3.0 %collective-permute-start.31 = (bf16[64,2048]{1,0:T(8,128)(2,1)S(1)}, bf16[64,2048]{1,0:T(8,128)(2,1)S(1)}, u32[]{:S(2)}, u32[]{:S(2)}) collective-permute-start(bf16[64,2048]{1,0:T(8,128)(2,1)S(1)} %add_rows.10.refs_7_), channel_id=1, source_target_pairs={{0,16},{2,18},{4,20},{6,22},{8,24},{10,26},{12,28},{14,30},{16,0},... | collective-permute-start | bytes 786440 | tf_op jit(solution)/shard_map/ppermute | solution.py:407
  105.1 5.4 %group_sums.6 = (f32[2,2,8,768]{3,2,1,0:T(8,128)S(1)}, f32[2,6,1024]{2,1,0:T(8,128)S(1)}) custom-call(bf16[512,2048]{1,0:T(8,128)(2,1)S(1)} %get-tuple-element.66.refs_0_, bf16[512,2048]{1,0:T(8,128)(2,1)S(1)} %get-tuple-element.67.refs_1_, bf16[512,768]{1,0:T(8,128)(2,1)S(1)} %get-tuple-element.68.refs_2_, ...), custom_call_target="tpu_custom_call" | custom-call | flops 3623878656 | tf_op jit(solution)/shard_map/group_sums/pallas_call | solution.py:89
  110.5 0.1 add_rows.11.refs_1_.refs_7_
  110.5 0.1 collective-permute-start.33
  110.7 3.4 %collective-permute-done.28.refs_1_ = bf16[64,2048]{1,0:T(8,128)(2,1)S(1)} collective-permute-done((bf16[64,2048]{1,0:T(8,128)(2,1)S(1)}, bf16[64,2048]{1,0:T(8,128)(2,1)S(1)}, u32[]{:S(2)}, u32[]{:S(2)}) %collective-permute-start.28) | collective-permute-done | bytes 262176 | tf_op jit(solution)/shard_map/ppermute | solution.py:407
  114.0 0.1 add_rows.12.refs_0_
  114.1 2.1 %collective-permute-start.29 = (bf16[64,2048]{1,0:T(8,128)(2,1)S(1)}, bf16[64,2048]{1,0:T(8,128)(2,1)S(1)}, u32[]{:S(2)}, u32[]{:S(2)}) collective-permute-start(bf16[64,2048]{1,0:T(8,128)(2,1)S(1)} %hold.19), channel_id=1, source_target_pairs={{0,4},{2,6},{4,0},{6,2},{8,12},{10,14},{12,8},{14,10},{16,20},{18,... | collective-permute-start | bytes 786440 | tf_op jit(solution)/shard_map/ppermute | solution.py:407
  116.3 0.2 collective-permute-start.27
  116.5 0.1 add_rows.8.refs_0_
  116.6 5.4 %group_sums.7 = (f32[2,2,8,768]{3,2,1,0:T(8,128)S(1)}, f32[2,6,1024]{2,1,0:T(8,128)S(1)}) custom-call(bf16[512,2048]{1,0:T(8,128)(2,1)S(1)} %get-tuple-element.66.refs_0_, bf16[512,2048]{1,0:T(8,128)(2,1)S(1)} %get-tuple-element.67.refs_1_, bf16[512,768]{1,0:T(8,128)(2,1)S(1)} %get-tuple-element.68.refs_2_, ...), custom_call_target="tpu_custom_call" | custom-call | flops 3623878656 | tf_op jit(solution)/shard_map/group_sums/pallas_call | solution.py:89
  122.0 2.1 %collective-permute-start.26 = (bf16[64,2048]{1,0:T(8,128)(2,1)S(1)}, bf16[64,2048]{1,0:T(8,128)(2,1)S(1)}, u32[]{:S(2)}, u32[]{:S(2)}) collective-permute-start(bf16[64,2048]{1,0:T(8,128)(2,1)S(1)} %hold.16), channel_id=1, source_target_pairs={{0,4},{2,6},{4,0},{6,2},{8,12},{10,14},{12,8},{14,10},{16,20},{18,... | collective-permute-start | bytes 786440 | tf_op jit(solution)/shard_map/ppermute | solution.py:407
  124.1 0.0 collective-permute-start.25
  124.1 0.1 add_rows.14.refs_1_
  124.2 1.6 %collective-permute-start.34 = (bf16[64,2048]{1,0:T(8,128)(2,1)S(1)}, bf16[64,2048]{1,0:T(8,128)(2,1)S(1)}, u32[]{:S(2)}, u32[]{:S(2)}) collective-permute-start(bf16[64,2048]{1,0:T(8,128)(2,1)S(1)} %add_rows.14.refs_1_), channel_id=1, source_target_pairs={{0,24},{2,26},{4,28},{6,30},{8,16},{10,18},{12,20},{14,22},{16,8},... | collective-permute-start | bytes 786440 | tf_op jit(solution)/shard_map/ppermute | solution.py:407
  125.8 0.1 add_rows.13
  125.9 1.2 collective-permute-start.30
  127.1 1.2 collective-permute-done.36.refs_7_
  128.4 0.2 collective-permute-start.35
  128.5 1.1 collective-permute-done.35.refs_5_
  129.7 2.9 %clip_gradients.1 = (f32[2,2,8,768]{3,2,1,0:T(8,128)}, f32[6,2,1024]{2,1,0:T(2,128)}) custom-call(f32[2,2,16,768]{3,2,1,0:T(8,128)} %bitcast.19, f32[2,2,16,768]{3,2,1,0:T(8,128)} %bitcast.21, f32[6,2,2048]{2,1,0:T(2,128)} %bitcast.23, f32[6,2,2048]{2,1,0:T(2,128)} %bitcast.25, f32[2,2,8,768]{3,2,1,0:T(8,128)S(1)} %get-tuple-element.82.refs_3_.refs_4_, ...), custom_call_target="tpu_custom_call" | custom-call | tf_op jit(solution)/shard_map/clip_gradients/pallas_call | solution.py:89
  132.5 0.1 collective-permute-done.34.refs_5_
  132.6 2.6 %collective-permute-done.30.refs_3_ = bf16[64,2048]{1,0:T(8,128)(2,1)S(1)} collective-permute-done((bf16[64,2048]{1,0:T(8,128)(2,1)S(1)}, bf16[64,2048]{1,0:T(8,128)(2,1)S(1)}, u32[]{:S(2)}, u32[]{:S(2)}) %collective-permute-start.30) | collective-permute-done | bytes 262176 | tf_op jit(solution)/shard_map/ppermute | solution.py:407
  135.2 0.9 add_rows.15
  (44 shorter events, 0.4 us)
Async XLA Ops:
  6.6 23.0 %collective-permute-start.4 = (bf16[3,1024,768]{2,1,0:T(8,128)(2,1)S(1)}, bf16[3,1024,768]{2,1,0:T(8,128)(2,1)S(1)}, u32[]{:S(2)}, u32[]{:S(2)}) collective-permute-start(bf16[3,1024,768]{2,1,0:T(8,128)(2,1)S(1)} %make_weights.1.refs_5_.refs_4_), channel_id=1, source_target_pairs={{0,1},{1,0},{2,3},{3,2},{4,5},{5,4},{6,7},{7,6},{8,9},{9,8},{10,11... | collective-permute-start | bytes 14155784 | tf_op jit(solution)/shard_map/ppermute | solution.py:410
  7.1 15.4 %collective-permute-start = (bf16[64,4224]{1,0:T(8,128)(2,1)S(1)}, bf16[64,4224]{1,0:T(8,128)(2,1)S(1)}, u32[]{:S(2)}, u32[]{:S(2)}) collective-permute-start(bf16[64,4224]{1,0:T(8,128)(2,1)S(1)} %pack_rows.1.refs_6_.refs_0_), channel_id=1, source_target_pairs={{0,2},{2,0},{4,6},{6,4},{8,10},{10,8},{12,14},{14,12},{16,18},{18,... | collective-permute-start | bytes 1622024 | tf_op jit(solution)/shard_map/ppermute | solution.py:407
  9.7 14.7 %collective-permute-start.1 = (bf16[64,4224]{1,0:T(8,128)(2,1)S(1)}, bf16[64,4224]{1,0:T(8,128)(2,1)S(1)}, u32[]{:S(2)}, u32[]{:S(2)}) collective-permute-start(bf16[64,4224]{1,0:T(8,128)(2,1)S(1)} %pack_rows.1.refs_6_.refs_0_), channel_id=1, source_target_pairs={{0,4},{2,6},{4,0},{6,2},{8,12},{10,14},{12,8},{14,10},{16,20},{18,... | collective-permute-start | bytes 1622024 | tf_op jit(solution)/shard_map/ppermute | solution.py:407
  11.2 14.8 %collective-permute-start.5 = (bf16[64,4224]{1,0:T(8,128)(2,1)S(1)}, bf16[64,4224]{1,0:T(8,128)(2,1)S(1)}, u32[]{:S(2)}, u32[]{:S(2)}) collective-permute-start(bf16[64,4224]{1,0:T(8,128)(2,1)S(1)} %pack_rows.1.refs_6_.refs_0_), channel_id=1, source_target_pairs={{0,8},{2,10},{4,12},{6,14},{8,0},{10,2},{12,4},{14,6},{16,24},{18,... | collective-permute-start | bytes 1622024 | tf_op jit(solution)/shard_map/ppermute | solution.py:407
  22.6 8.8 %collective-permute-start.2 = (bf16[32,4224]{1,0:T(8,128)(2,1)S(1)}, bf16[32,4224]{1,0:T(8,128)(2,1)S(1)}, u32[]{:S(2)}, u32[]{:S(2)}) collective-permute-start(bf16[32,4224]{1,0:T(8,128)(2,1)S(1)} %part.4), channel_id=1, source_target_pairs={{0,4},{2,6},{4,0},{6,2},{8,12},{10,14},{12,8},{14,10},{16,20},{18,... | collective-permute-start | bytes 811016 | tf_op jit(solution)/shard_map/ppermute | solution.py:407
  24.5 9.4 %collective-permute-start.3 = (bf16[32,4224]{1,0:T(8,128)(2,1)S(1)}, bf16[32,4224]{1,0:T(8,128)(2,1)S(1)}, u32[]{:S(2)}, u32[]{:S(2)}) collective-permute-start(bf16[32,4224]{1,0:T(8,128)(2,1)S(1)} %part.5), channel_id=1, source_target_pairs={{0,2},{2,0},{4,6},{6,4},{8,10},{10,8},{12,14},{14,12},{16,18},{18,... | collective-permute-start | bytes 811016 | tf_op jit(solution)/shard_map/ppermute | solution.py:407
  26.0 17.1 %collective-permute-start.6 = (bf16[64,4224]{1,0:T(8,128)(2,1)S(1)}, bf16[64,4224]{1,0:T(8,128)(2,1)S(1)}, u32[]{:S(2)}, u32[]{:S(2)}) collective-permute-start(bf16[64,4224]{1,0:T(8,128)(2,1)S(1)} %collective-permute-done.5.refs_0_), channel_id=1, source_target_pairs={{0,24},{2,26},{4,28},{6,30},{8,16},{10,18},{12,20},{14,22},{16,8},... | collective-permute-start | bytes 1622024 | tf_op jit(solution)/shard_map/ppermute | solution.py:407
  29.7 14.2 %collective-permute-start.7 = (bf16[64,4224]{1,0:T(8,128)(2,1)S(1)}, bf16[64,4224]{1,0:T(8,128)(2,1)S(1)}, u32[]{:S(2)}, u32[]{:S(2)}) collective-permute-start(bf16[64,4224]{1,0:T(8,128)(2,1)S(1)} %hold.11), channel_id=1, source_target_pairs={{0,2},{2,0},{4,6},{6,4},{8,10},{10,8},{12,14},{14,12},{16,18},{18,... | collective-permute-start | bytes 1622024 | tf_op jit(solution)/shard_map/ppermute | solution.py:407
  30.3 13.6 %collective-permute-start.8 = (bf16[64,4224]{1,0:T(8,128)(2,1)S(1)}, bf16[64,4224]{1,0:T(8,128)(2,1)S(1)}, u32[]{:S(2)}, u32[]{:S(2)}) collective-permute-start(bf16[64,4224]{1,0:T(8,128)(2,1)S(1)} %hold.11), channel_id=1, source_target_pairs={{0,4},{2,6},{4,0},{6,2},{8,12},{10,14},{12,8},{14,10},{16,20},{18,... | collective-permute-start | bytes 1622024 | tf_op jit(solution)/shard_map/ppermute | solution.py:407
  31.4 22.8 %collective-permute-start.11 = (bf16[32,4224]{1,0:T(8,128)(2,1)S(1)}, bf16[32,4224]{1,0:T(8,128)(2,1)S(1)}, u32[]{:S(2)}, u32[]{:S(2)}) collective-permute-start(bf16[32,4224]{1,0:T(8,128)(2,1)S(1)} %collective-permute-done.2.refs_3_), channel_id=1, source_target_pairs={{0,8},{2,10},{4,12},{6,14},{8,0},{10,2},{12,4},{14,6},{16,24},{18,... | collective-permute-start | bytes 811016 | tf_op jit(solution)/shard_map/ppermute | solution.py:407
  33.9 20.3 %collective-permute-start.12 = (bf16[32,4224]{1,0:T(8,128)(2,1)S(1)}, bf16[32,4224]{1,0:T(8,128)(2,1)S(1)}, u32[]{:S(2)}, u32[]{:S(2)}) collective-permute-start(bf16[32,4224]{1,0:T(8,128)(2,1)S(1)} %collective-permute-done.3.refs_4_), channel_id=1, source_target_pairs={{0,8},{2,10},{4,12},{6,14},{8,0},{10,2},{12,4},{14,6},{16,24},{18,... | collective-permute-start | bytes 811016 | tf_op jit(solution)/shard_map/ppermute | solution.py:407
  43.9 16.4 %collective-permute-start.13 = (bf16[64,4224]{1,0:T(8,128)(2,1)S(1)}, bf16[64,4224]{1,0:T(8,128)(2,1)S(1)}, u32[]{:S(2)}, u32[]{:S(2)}) collective-permute-start(bf16[64,4224]{1,0:T(8,128)(2,1)S(1)} %hold.12), channel_id=1, source_target_pairs={{0,4},{2,6},{4,0},{6,2},{8,12},{10,14},{12,8},{14,10},{16,20},{18,... | collective-permute-start | bytes 1622024 | tf_op jit(solution)/shard_map/ppermute | solution.py:407
  45.1 16.3 %collective-permute-start.10 = (bf16[64,4224]{1,0:T(8,128)(2,1)S(1)}, bf16[64,4224]{1,0:T(8,128)(2,1)S(1)}, u32[]{:S(2)}, u32[]{:S(2)}) collective-permute-start(bf16[64,4224]{1,0:T(8,128)(2,1)S(1)} %hold.12), channel_id=1, source_target_pairs={{0,2},{2,0},{4,6},{6,4},{8,10},{10,8},{12,14},{14,12},{16,18},{18,... | collective-permute-start | bytes 1622024 | tf_op jit(solution)/shard_map/ppermute | solution.py:407
  46.0 19.2 %collective-permute-start.9 = (bf16[64,4224]{1,0:T(8,128)(2,1)S(1)}, bf16[64,4224]{1,0:T(8,128)(2,1)S(1)}, u32[]{:S(2)}, u32[]{:S(2)}) collective-permute-start(bf16[64,4224]{1,0:T(8,128)(2,1)S(1)} %hold.12), channel_id=1, source_target_pairs={{0,8},{2,10},{4,12},{6,14},{8,0},{10,2},{12,4},{14,6},{16,24},{18,... | collective-permute-start | bytes 1622024 | tf_op jit(solution)/shard_map/ppermute | solution.py:407
  60.3 12.8 %collective-permute-start.19 = (bf16[32,4224]{1,0:T(8,128)(2,1)S(1)}, bf16[32,4224]{1,0:T(8,128)(2,1)S(1)}, u32[]{:S(2)}, u32[]{:S(2)}) collective-permute-start(bf16[32,4224]{1,0:T(8,128)(2,1)S(1)} %part.7.refs_2_), channel_id=1, source_target_pairs={{0,2},{2,0},{4,6},{6,4},{8,10},{10,8},{12,14},{14,12},{16,18},{18,... | collective-permute-start | bytes 811016 | tf_op jit(solution)/shard_map/ppermute | solution.py:407
  61.4 11.8 %collective-permute-start.17 = (bf16[32,4224]{1,0:T(8,128)(2,1)S(1)}, bf16[32,4224]{1,0:T(8,128)(2,1)S(1)}, u32[]{:S(2)}, u32[]{:S(2)}) collective-permute-start(bf16[32,4224]{1,0:T(8,128)(2,1)S(1)} %part.6.refs_1_), channel_id=1, source_target_pairs={{0,4},{2,6},{4,0},{6,2},{8,12},{10,14},{12,8},{14,10},{16,20},{18,... | collective-permute-start | bytes 811016 | tf_op jit(solution)/shard_map/ppermute | solution.py:407
  65.2 24.8 %collective-permute-start.14 = (bf16[64,4224]{1,0:T(8,128)(2,1)S(1)}, bf16[64,4224]{1,0:T(8,128)(2,1)S(1)}, u32[]{:S(2)}, u32[]{:S(2)}) collective-permute-start(bf16[64,4224]{1,0:T(8,128)(2,1)S(1)} %hold.13.refs_5_), channel_id=1, source_target_pairs={{0,2},{2,0},{4,6},{6,4},{8,10},{10,8},{12,14},{14,12},{16,18},{18,... | collective-permute-start | bytes 1622024 | tf_op jit(solution)/shard_map/ppermute | solution.py:407
  66.2 25.4 %collective-permute-start.15 = (bf16[64,4224]{1,0:T(8,128)(2,1)S(1)}, bf16[64,4224]{1,0:T(8,128)(2,1)S(1)}, u32[]{:S(2)}, u32[]{:S(2)}) collective-permute-start(bf16[64,4224]{1,0:T(8,128)(2,1)S(1)} %hold.13.refs_5_), channel_id=1, source_target_pairs={{0,4},{2,6},{4,0},{6,2},{8,12},{10,14},{12,8},{14,10},{16,20},{18,... | collective-permute-start | bytes 1622024 | tf_op jit(solution)/shard_map/ppermute | solution.py:407
  79.2 10.0 %collective-permute-start.22 = (bf16[64,2048]{1,0:T(8,128)(2,1)S(1)}, bf16[64,2048]{1,0:T(8,128)(2,1)S(1)}, u32[]{:S(2)}, u32[]{:S(2)}) collective-permute-start(bf16[64,2048]{1,0:T(8,128)(2,1)S(1)} %get-tuple-element.72), channel_id=1, source_target_pairs={{0,4},{2,6},{4,0},{6,2},{8,12},{10,14},{12,8},{14,10},{16,20},{18,... | collective-permute-start | bytes 786440 | tf_op jit(solution)/shard_map/ppermute | solution.py:407
  79.8 11.7 %collective-permute-start.20 = (bf16[32,4224]{1,0:T(8,128)(2,1)S(1)}, bf16[32,4224]{1,0:T(8,128)(2,1)S(1)}, u32[]{:S(2)}, u32[]{:S(2)}) collective-permute-start(bf16[32,4224]{1,0:T(8,128)(2,1)S(1)} %collective-permute-done.19.refs_4_), channel_id=1, source_target_pairs={{0,8},{2,10},{4,12},{6,14},{8,0},{10,2},{12,4},{14,6},{16,24},{18,... | collective-permute-start | bytes 811016 | tf_op jit(solution)/shard_map/ppermute | solution.py:407
  83.6 8.0 %collective-permute-start.18 = (bf16[32,4224]{1,0:T(8,128)(2,1)S(1)}, bf16[32,4224]{1,0:T(8,128)(2,1)S(1)}, u32[]{:S(2)}, u32[]{:S(2)}) collective-permute-start(bf16[32,4224]{1,0:T(8,128)(2,1)S(1)} %collective-permute-done.17.refs_3_), channel_id=1, source_target_pairs={{0,8},{2,10},{4,12},{6,14},{8,0},{10,2},{12,4},{14,6},{16,24},{18,... | collective-permute-start | bytes 811016 | tf_op jit(solution)/shard_map/ppermute | solution.py:407
  89.2 11.7 %collective-permute-start.24 = (bf16[64,2048]{1,0:T(8,128)(2,1)S(1)}, bf16[64,2048]{1,0:T(8,128)(2,1)S(1)}, u32[]{:S(2)}, u32[]{:S(2)}) collective-permute-start(bf16[64,2048]{1,0:T(8,128)(2,1)S(1)} %get-tuple-element.73), channel_id=1, source_target_pairs={{0,4},{2,6},{4,0},{6,2},{8,12},{10,14},{12,8},{14,10},{16,20},{18,... | collective-permute-start | bytes 786440 | tf_op jit(solution)/shard_map/ppermute | solution.py:407
  90.0 12.0 %collective-permute-start.23 = (bf16[64,2048]{1,0:T(8,128)(2,1)S(1)}, bf16[64,2048]{1,0:T(8,128)(2,1)S(1)}, u32[]{:S(2)}, u32[]{:S(2)}) collective-permute-start(bf16[64,2048]{1,0:T(8,128)(2,1)S(1)} %add_rows.9), channel_id=1, source_target_pairs={{0,2},{2,0},{4,6},{6,4},{8,10},{10,8},{12,14},{14,12},{16,18},{18,... | collective-permute-start | bytes 786440 | tf_op jit(solution)/shard_map/ppermute | solution.py:407
  97.7 12.8 %collective-permute-start.21 = (bf16[64,2048]{1,0:T(8,128)(2,1)S(1)}, bf16[64,2048]{1,0:T(8,128)(2,1)S(1)}, u32[]{:S(2)}, u32[]{:S(2)}) collective-permute-start(bf16[64,2048]{1,0:T(8,128)(2,1)S(1)} %get-tuple-element.65), channel_id=1, source_target_pairs={{0,2},{2,0},{4,6},{6,4},{8,10},{10,8},{12,14},{14,12},{16,18},{18,... | collective-permute-start | bytes 786440 | tf_op jit(solution)/shard_map/ppermute | solution.py:407
  98.8 23.2 %collective-permute-start.32 = (bf16[64,2048]{1,0:T(8,128)(2,1)S(1)}, bf16[64,2048]{1,0:T(8,128)(2,1)S(1)}, u32[]{:S(2)}, u32[]{:S(2)}) collective-permute-start(bf16[64,2048]{1,0:T(8,128)(2,1)S(1)} %get-tuple-element.80), channel_id=1, source_target_pairs={{0,2},{2,0},{4,6},{6,4},{8,10},{10,8},{12,14},{14,12},{16,18},{18,... | collective-permute-start | bytes 786440 | tf_op jit(solution)/shard_map/ppermute | solution.py:407
  99.8 14.3 %collective-permute-start.28 = (bf16[64,2048]{1,0:T(8,128)(2,1)S(1)}, bf16[64,2048]{1,0:T(8,128)(2,1)S(1)}, u32[]{:S(2)}, u32[]{:S(2)}) collective-permute-start(bf16[64,2048]{1,0:T(8,128)(2,1)S(1)} %hold.18), channel_id=1, source_target_pairs={{0,2},{2,0},{4,6},{6,4},{8,10},{10,8},{12,14},{14,12},{16,18},{18,... | collective-permute-start | bytes 786440 | tf_op jit(solution)/shard_map/ppermute | solution.py:407
  101.0 15.4 %collective-permute-start.16 = (bf16[64,2048]{1,0:T(8,128)(2,1)S(1)}, bf16[64,2048]{1,0:T(8,128)(2,1)S(1)}, u32[]{:S(2)}, u32[]{:S(2)}) collective-permute-start(bf16[64,2048]{1,0:T(8,128)(2,1)S(1)} %hold.14), channel_id=1, source_target_pairs={{0,4},{2,6},{4,0},{6,2},{8,12},{10,14},{12,8},{14,10},{16,20},{18,... | collective-permute-start | bytes 786440 | tf_op jit(solution)/shard_map/ppermute | solution.py:407
  102.0 22.0 %collective-permute-start.31 = (bf16[64,2048]{1,0:T(8,128)(2,1)S(1)}, bf16[64,2048]{1,0:T(8,128)(2,1)S(1)}, u32[]{:S(2)}, u32[]{:S(2)}) collective-permute-start(bf16[64,2048]{1,0:T(8,128)(2,1)S(1)} %add_rows.10.refs_7_), channel_id=1, source_target_pairs={{0,16},{2,18},{4,20},{6,22},{8,24},{10,26},{12,28},{14,30},{16,0},... | collective-permute-start | bytes 786440 | tf_op jit(solution)/shard_map/ppermute | solution.py:407
  110.5 13.6 %collective-permute-start.33 = (bf16[64,2048]{1,0:T(8,128)(2,1)S(1)}, bf16[64,2048]{1,0:T(8,128)(2,1)S(1)}, u32[]{:S(2)}, u32[]{:S(2)}) collective-permute-start(bf16[64,2048]{1,0:T(8,128)(2,1)S(1)} %add_rows.11.refs_1_.refs_7_), channel_id=1, source_target_pairs={{0,4},{2,6},{4,0},{6,2},{8,12},{10,14},{12,8},{14,10},{16,20},{18,... | collective-permute-start | bytes 786440 | tf_op jit(solution)/shard_map/ppermute | solution.py:407
  114.1 11.7 %collective-permute-start.29 = (bf16[64,2048]{1,0:T(8,128)(2,1)S(1)}, bf16[64,2048]{1,0:T(8,128)(2,1)S(1)}, u32[]{:S(2)}, u32[]{:S(2)}) collective-permute-start(bf16[64,2048]{1,0:T(8,128)(2,1)S(1)} %hold.19), channel_id=1, source_target_pairs={{0,4},{2,6},{4,0},{6,2},{8,12},{10,14},{12,8},{14,10},{16,20},{18,... | collective-permute-start | bytes 786440 | tf_op jit(solution)/shard_map/ppermute | solution.py:407
  116.3 9.5 %collective-permute-start.27 = (bf16[64,2048]{1,0:T(8,128)(2,1)S(1)}, bf16[64,2048]{1,0:T(8,128)(2,1)S(1)}, u32[]{:S(2)}, u32[]{:S(2)}) collective-permute-start(bf16[64,2048]{1,0:T(8,128)(2,1)S(1)} %hold.17), channel_id=1, source_target_pairs={{0,2},{2,0},{4,6},{6,4},{8,10},{10,8},{12,14},{14,12},{16,18},{18,... | collective-permute-start | bytes 786440 | tf_op jit(solution)/shard_map/ppermute | solution.py:407
  122.0 10.5 %collective-permute-start.26 = (bf16[64,2048]{1,0:T(8,128)(2,1)S(1)}, bf16[64,2048]{1,0:T(8,128)(2,1)S(1)}, u32[]{:S(2)}, u32[]{:S(2)}) collective-permute-start(bf16[64,2048]{1,0:T(8,128)(2,1)S(1)} %hold.16), channel_id=1, source_target_pairs={{0,4},{2,6},{4,0},{6,2},{8,12},{10,14},{12,8},{14,10},{16,20},{18,... | collective-permute-start | bytes 786440 | tf_op jit(solution)/shard_map/ppermute | solution.py:407
  124.1 8.4 %collective-permute-start.25 = (bf16[64,2048]{1,0:T(8,128)(2,1)S(1)}, bf16[64,2048]{1,0:T(8,128)(2,1)S(1)}, u32[]{:S(2)}, u32[]{:S(2)}) collective-permute-start(bf16[64,2048]{1,0:T(8,128)(2,1)S(1)} %hold.15), channel_id=1, source_target_pairs={{0,2},{2,0},{4,6},{6,4},{8,10},{10,8},{12,14},{14,12},{16,18},{18,... | collective-permute-start | bytes 786440 | tf_op jit(solution)/shard_map/ppermute | solution.py:407
  124.2 8.4 %collective-permute-start.34 = (bf16[64,2048]{1,0:T(8,128)(2,1)S(1)}, bf16[64,2048]{1,0:T(8,128)(2,1)S(1)}, u32[]{:S(2)}, u32[]{:S(2)}) collective-permute-start(bf16[64,2048]{1,0:T(8,128)(2,1)S(1)} %add_rows.14.refs_1_), channel_id=1, source_target_pairs={{0,24},{2,26},{4,28},{6,30},{8,16},{10,18},{12,20},{14,22},{16,8},... | collective-permute-start | bytes 786440 | tf_op jit(solution)/shard_map/ppermute | solution.py:407
  125.9 9.2 %collective-permute-start.30 = (bf16[64,2048]{1,0:T(8,128)(2,1)S(1)}, bf16[64,2048]{1,0:T(8,128)(2,1)S(1)}, u32[]{:S(2)}, u32[]{:S(2)}) collective-permute-start(bf16[64,2048]{1,0:T(8,128)(2,1)S(1)} %add_rows.13), channel_id=1, source_target_pairs={{0,8},{2,10},{4,12},{6,14},{8,0},{10,2},{12,4},{14,6},{16,24},{18,... | collective-permute-start | bytes 786440 | tf_op jit(solution)/shard_map/ppermute | solution.py:407
  127.1 1.3 collective-permute-start.36
  128.4 1.3 collective-permute-start.35
